TPU v7x, 32 devices: a whole 2x2x4 slice. The times are simulated.
32 devices in a mesh: tm: 4 (over z), det: 8 (over y, x, core).
Axes of the slice: x: 2, y: 2, z: 4, core: 2. Of those that a mesh axis runs over, the one named last changes fastest.
Arguments:
- noise: float32 [512, 16384], P('det', 'tm'), may hold values from -6 to 6
- factor: float32 [8, 512, 512], P('det', 'tm'), may hold values from -8 to 8, as said below
Outputs:
- correlated: float32 [512, 16384], P('det', 'tm')
Inputs may be any that keep to these rules, and one draw needn't show every extreme that they name: factor[b] is lower triangular with a positive diagonal, and factor[b] equals factor[7 - b].
All inputs are finite; a program needn't handle non-finite values.
Results may differ from a plain program's by a relative error of at most 0.00007.
Values sent between devices are 32-bit elements; how exact they have to be, the bound alone decides.
No kernel may reach another device: no remote copies, remote signals or barrier semaphores. Data moves between devices by JAX's collectives and lax.ppermute only.
A program may use at most 64 MiB of HBM per device.

v0:
```python
import math

import jax
import jax.numpy as jnp
from jax import lax
from jax.sharding import PartitionSpec as P

highest = lax.Precision.HIGHEST


def tables(length):
    counter = jnp.arange(length, dtype=jnp.int32)
    product = counter[:, None] * counter[None, :] % length
    angles = product.astype(jnp.float32) * (2.0 * math.pi / length)
    return (jnp.cos(angles), jnp.sin(angles))


def rotate(real_part, imag_part, angles):
    cosines = jnp.cos(angles)
    sines = jnp.sin(angles)
    if imag_part is None:
        return (real_part * cosines, -real_part * sines)
    return (real_part * cosines + imag_part * sines, imag_part * cosines - real_part * sines)


def direct_dft(real_part, imag_part):
    length = real_part.shape[-1]
    cosines, sines = tables(length)
    out_real = jnp.matmul(real_part, cosines, precision=highest)
    out_imag = -jnp.matmul(real_part, sines, precision=highest)
    if imag_part is not None:
        out_real = out_real + jnp.matmul(imag_part, sines, precision=highest)
        out_imag = out_imag + jnp.matmul(imag_part, cosines, precision=highest)
    return (out_real, out_imag)


def inner_factor(length):
    largest = 1
    for option in range(1, 513):
        if length % option == 0:
            largest = option
    return largest


def dft_last(real_part, imag_part):
    length = real_part.shape[-1]
    inner_len = inner_factor(length)
    if inner_len == length:
        return direct_dft(real_part, imag_part)
    outer_len = length // inner_len
    leading = real_part.shape[:-1]
    real_part = real_part.reshape(leading + (outer_len, inner_len))
    cosines, sines = tables(outer_len)
    mid_real = jnp.einsum("...tj,tk->...kj", real_part, cosines, precision=highest)
    mid_imag = -jnp.einsum("...tj,tk->...kj", real_part, sines, precision=highest)
    if imag_part is not None:
        imag_part = imag_part.reshape(leading + (outer_len, inner_len))
        mid_real = mid_real + jnp.einsum("...tj,tk->...kj", imag_part, sines, precision=highest)
        mid_imag = mid_imag + jnp.einsum("...tj,tk->...kj", imag_part, cosines, precision=highest)
    outer_count = jnp.arange(outer_len, dtype=jnp.int32)[:, None]
    inner_count = jnp.arange(inner_len, dtype=jnp.int32)[None, :]
    angles = (outer_count * inner_count % length).astype(jnp.float32) * (2.0 * math.pi / length)
    turn_real, turn_imag = rotate(mid_real, mid_imag, angles)
    fin_real, fin_imag = dft_last(turn_real, turn_imag)
    fin_real = jnp.swapaxes(fin_real, -1, -2).reshape(leading + (length,))
    fin_imag = jnp.swapaxes(fin_imag, -1, -2).reshape(leading + (length,))
    return (fin_real, fin_imag)


def hartley(real_part, imag_part):
    fin_real, fin_imag = dft_last(real_part, imag_part)
    return fin_real - fin_imag


def local(noise, factor):
    across = lax.axis_size("tm")
    groups = lax.axis_size("det")
    det_rows, span = noise.shape
    total = span * across
    series = lax.all_to_all(noise, "tm", split_axis=0, concat_axis=1, tiled=True)
    whole_index = jnp.arange(total, dtype=jnp.int32)[None, :]
    half_angles = whole_index.astype(jnp.float32) * (math.pi / total)
    twist_real, twist_imag = rotate(series, None, half_angles)
    spectrum = hartley(twist_real, twist_imag)
    spread = lax.all_to_all(spectrum, "det", split_axis=1, concat_axis=0, tiled=True)
    local_bins = lax.all_to_all(spread, "tm", split_axis=1, concat_axis=0, tiled=True)
    width = local_bins.shape[1]
    grouped = local_bins.reshape(across, groups, det_rows // across, width)
    rows_block = lax.all_gather(factor, "tm", axis=1, tiled=True)[0]
    count = rows_block.shape[0]
    shaped = rows_block.reshape(count, groups, across, det_rows // across)
    mixed = jnp.einsum("idar,adrk->ik", shaped, grouped, precision=highest)
    width = mixed.shape[1]
    ordered = (
        mixed.reshape(groups, across, det_rows // across, width)
        .transpose(1, 0, 2, 3)
        .reshape(-1, width)
    )
    back = lax.all_to_all(
        lax.all_to_all(ordered, "tm", split_axis=0, concat_axis=1, tiled=True),
        "det",
        split_axis=0,
        concat_axis=1,
        tiled=True,
    )
    back_real, back_imag = dft_last(back, None)
    back_real, back_imag = rotate(back_real, back_imag, half_angles)
    signal = (back_real - back_imag) / total
    result = lax.all_to_all(signal, "tm", split_axis=1, concat_axis=0, tiled=True)
    return result


def solution(mesh):
    in_specs = (P("det", "tm"), P("det", "tm", None))
    out_specs = P("det", "tm")
    return jax.shard_map(local, mesh=mesh, in_specs=in_specs, out_specs=out_specs, check_vma=False)
```

profile of v0, /device:TPU:0, one launch (start us, length us, event | category | flops | bytes accessed | tf_op | source)
XLA Modules:
  0.0 270.0 jit_solution(4828197326093208848)
XLA Ops:
  6.5 6.3 %all-to-all-start = ((f32[4,16,4096]{2,1,0:T(8,128)}), f32[4,16,4096]{2,1,0:T(8,128)S(1)}, u32[]{:S(2)}, u32[]{:S(2)}) async-start(f32[4,16,4096]{2,1,0:T(8,128)} %bitcast.92), calls=%async_computation | async-start | bytes 2097152 | tf_op jit(solution)/shard_map/all_to_all | solution.py:80
  13.6 25.0 %all-to-all-done = f32[4,16,4096]{2,1,0:T(8,128)S(1)} async-done(((f32[4,16,4096]{2,1,0:T(8,128)}), f32[4,16,4096]{2,1,0:T(8,128)S(1)}, u32[]{:S(2)}, u32[]{:S(2)}) %all-to-all-start) | async-done | bytes 1048608 | tf_op jit(solution)/shard_map/all_to_all | solution.py:80
  44.4 6.1 %convolution_negate_fusion.2 = f32[16,32,512]{2,1,0:T(8,128)S(1)} fusion(f32[32,16,512]{2,0,1:T(8,128)S(1)} %convolution_add_fusion.4, f32[32,16,512]{2,0,1:T(8,128)S(1)} %convolution_add_fusion.5, f32[32,512]{1,0:T(8,128)S(1)} %get-tuple-element.5, f32[32,512]{1,0:T(8,128)S(1)} %get-tuple-element.6), kind=kOutput, calls=%fused_computation.12 | convolution fusion | flops 1615331328 | bytes 3276800 | tf_op jit(solution)/shard_map/dot_general | solution.py:30
  50.5 5.8 %fusion.21 = f32[16,32,512]{2,1,0:T(8,128)S(1)} fusion(f32[32,16,512]{2,0,1:T(8,128)S(1)} %convolution_add_fusion.4, f32[32,16,512]{2,0,1:T(8,128)S(1)} %convolution_add_fusion.5, f32[32,512]{1,0:T(8,128)S(1)} %get-tuple-element.5, f32[32,512]{1,0:T(8,128)S(1)} %get-tuple-element.6), kind=kOutput, calls=%fused_computation.34 | convolution fusion | flops 1615069184 | bytes 3276800 | tf_op jit(solution)/shard_map/dot_general | solution.py:29
  56.3 15.6 %convolution_add_fusion.3 = f32[16,32,512]{2,1,0:T(8,128)S(1)} fusion(f32[16,32,512]{2,1,0:T(8,128)S(1)} %fusion.21, f32[32,16,512]{2,0,1:T(8,128)S(1)} %convolution_add_fusion.5, f32[32,16,512]{2,0,1:T(8,128)S(1)} %convolution_add_fusion.4, f32[32,512]{1,0:T(8,128)S(1)} %get-tuple-element.5, f32[32,512]{1,0:T(8,128)S(1)} %get-tuple-element.6), kind=kOutput, calls=%fused_computation.13 | convolution fusion | flops 1615331328 | bytes 4325376 | tf_op jit(solution)/shard_map/dot_general | solution.py:32
  71.9 5.9 %fusion.3 = f32[16,512,32]{1,2,0:T(8,128)S(1)} fusion(f32[16,32,512]{2,1,0:T(8,128)S(1)} %convolution_add_fusion.3, f32[16,32,512]{2,1,0:T(8,128)S(1)} %convolution_negate_fusion.2, f32[32,16,512]{2,0,1:T(8,128)S(1)} %convolution_add_fusion.5, f32[32,16,512]{2,0,1:T(8,128)S(1)} %convolution_add_fusion.4, f32[32,512]{1,0:T(8,128)S(1)} %get-tuple-element.5, ...), kind=kOutput, calls=%fused_computation.11 | convolution fusion | flops 1615593472 | bytes 5373952 | tf_op jit(solution)/shard_map/dot_general | solution.py:33
  77.8 2.6 copy.28
  80.4 3.7 %sub.34 = f32[16,8,2048]{2,1,0:T(8,128)S(1)} reshape(f32[16,512,32]{2,1,0:T(8,128)} %copy.28) | data formatting | bytes 2097152 | tf_op jit(solution)/shard_map/sub | solution.py:72
  85.7 3.7 %all-to-all-start.1 = ((f32[16,8,2048]{2,0,1:T(8,128)}), f32[16,8,2048]{2,0,1:T(8,128)S(1)}, u32[]{:S(2)}, u32[]{:S(2)}) async-start(f32[16,8,2048]{2,0,1:T(8,128)} %copy.29), calls=%async_computation.1 | async-start | bytes 2097152 | tf_op jit(solution)/shard_map/all_to_all | solution.py:85
  90.3 14.5 %all-to-all-done.1 = f32[16,8,2048]{2,0,1:T(8,128)S(1)} async-done(((f32[16,8,2048]{2,0,1:T(8,128)}), f32[16,8,2048]{2,0,1:T(8,128)S(1)}, u32[]{:S(2)}, u32[]{:S(2)}) %all-to-all-start.1) | async-done | bytes 1048608 | tf_op jit(solution)/shard_map/all_to_all | solution.py:85
  106.8 3.5 %all-to-all-start.2 = ((f32[128,4,512]{2,0,1:T(8,128)}), f32[128,4,512]{2,0,1:T(8,128)S(1)}, u32[]{:S(2)}, u32[]{:S(2)}) async-start(f32[128,4,512]{2,0,1:T(8,128)} %copy.30), calls=%async_computation.2 | async-start | bytes 2097152 | tf_op jit(solution)/shard_map/all_to_all | solution.py:86
  110.4 27.5 %all-gather.2.cloned.1.call-done = f32[1,512,512]{1,2,0:T(8,128)} async-done(((f32[1,128,512]{1,2,0:T(8,128)}), f32[1,512,512]{1,2,0:T(8,128)}) %all-gather.2.cloned.1.call-update) | async-done | bytes 1048592 | tf_op jit(solution)/shard_map/all_gather | solution.py:89
  137.9 5.2 %all-to-all-done.2 = f32[128,4,512]{2,0,1:T(8,128)S(1)} async-done(((f32[128,4,512]{2,0,1:T(8,128)}), f32[128,4,512]{2,0,1:T(8,128)S(1)}, u32[]{:S(2)}, u32[]{:S(2)}) %all-to-all-start.2) | async-done | bytes 1048608 | tf_op jit(solution)/shard_map/all_to_all | solution.py:86
  143.1 3.1 %fusion.25 = f32[512,512,1,1]{0,1,3,2:T(8,128)S(1)} fusion(f32[4,8,16,512]{3,2,1,0:T(8,128)S(1)} %bitcast.83, f32[512,8,4,16]{0,3,2,1:T(8,128)} %bitcast.91), kind=kOutput, calls=%fused_computation.38 | convolution fusion | flops 1610612736 | bytes 3145728 | tf_op jit(solution)/shard_map/idar,adrk->ik/dot_general | solution.py:92
  146.3 28.2 %all_to_all.96 = f32[4,128,512]{2,1,0:T(8,128)S(1)} all-to-all(f32[4,128,512]{2,1,0:T(8,128)S(1)} %bitcast.88), channel_id=1, replica_groups=mesh['tm'=4,'det'=8] {'tm'}, dimensions={0} | all-to-all | bytes 2097152 | tf_op jit(solution)/shard_map/all_to_all | solution.py:100
  176.8 4.0 %all-to-all-start.4 = ((f32[8,16,2048]{2,1,0:T(8,128)}), f32[8,16,2048]{2,1,0:T(8,128)S(1)}, u32[]{:S(2)}, u32[]{:S(2)}) async-start(f32[8,16,2048]{2,1,0:T(8,128)} %all_to_all.84), calls=%async_computation.4 | async-start | bytes 2097152 | tf_op jit(solution)/shard_map/all_to_all | solution.py:99
  181.3 14.5 %all-to-all-done.4 = f32[8,16,2048]{2,1,0:T(8,128)S(1)} async-done(((f32[8,16,2048]{2,1,0:T(8,128)}), f32[8,16,2048]{2,1,0:T(8,128)S(1)}, u32[]{:S(2)}, u32[]{:S(2)}) %all-to-all-start.4) | async-done | bytes 1048608 | tf_op jit(solution)/shard_map/all_to_all | solution.py:99
  198.9 5.8 %convolution_negate_fusion = f32[16,32,512]{2,1,0:T(8,128)S(1)} fusion(f32[32,16,512]{2,0,1:T(8,128)S(1)} %convolution_negate_fusion.1, f32[32,16,512]{2,0,1:T(8,128)S(1)} %fusion.65, f32[32,512]{1,0:T(8,128)S(1)} %get-tuple-element.5, f32[32,512]{1,0:T(8,128)S(1)} %get-tuple-element.6), kind=kOutput, calls=%fused_computation.5 | convolution fusion | flops 1615331328 | bytes 3276800 | tf_op jit(solution)/shard_map/dot_general | solution.py:30
  204.7 5.9 %fusion.10 = f32[16,32,512]{2,1,0:T(8,128)S(1)} fusion(f32[32,16,512]{2,0,1:T(8,128)S(1)} %convolution_negate_fusion.1, f32[32,16,512]{2,0,1:T(8,128)S(1)} %fusion.65, f32[32,512]{1,0:T(8,128)S(1)} %get-tuple-element.5, f32[32,512]{1,0:T(8,128)S(1)} %get-tuple-element.6), kind=kOutput, calls=%fused_computation.23 | convolution fusion | flops 1615069184 | bytes 3276800 | tf_op jit(solution)/shard_map/dot_general | solution.py:29
  210.6 5.8 %fusion = f32[16,512,32]{1,2,0:T(8,128)S(1)} fusion(f32[16,32,512]{2,1,0:T(8,128)S(1)} %convolution_negate_fusion, f32[32,16,512]{2,0,1:T(8,128)S(1)} %fusion.65, f32[32,16,512]{2,0,1:T(8,128)S(1)} %convolution_negate_fusion.1, f32[32,512]{1,0:T(8,128)S(1)} %get-tuple-element.5, f32[32,512]{1,0:T(8,128)S(1)} %get-tuple-element.6), kind=kOutput, calls=%fused_computation.4 | convolution fusion | flops 1615331328 | bytes 4325376 | tf_op jit(solution)/shard_map/dot_general | solution.py:33
  216.4 6.0 %fusion.1 = f32[16,512,32]{1,2,0:T(8,128)S(1)} fusion(f32[16,32,512]{2,1,0:T(8,128)S(1)} %fusion.10, f32[32,16,512]{2,0,1:T(8,128)S(1)} %fusion.65, f32[32,16,512]{2,0,1:T(8,128)S(1)} %convolution_negate_fusion.1, f32[32,512]{1,0:T(8,128)S(1)} %get-tuple-element.5, f32[32,512]{1,0:T(8,128)S(1)} %get-tuple-element.6), kind=kOutput, calls=%fused_computation.7 | convolution fusion | flops 1615331328 | bytes 4325376 | tf_op jit(solution)/shard_map/dot_general | solution.py:32
  225.1 3.7 %reshape.133 = f32[16,4,4096]{2,1,0:T(4,128)S(1)} reshape(f32[16,512,32]{2,1,0:T(8,128)} %copy.36) | data formatting | bytes 2097152 | tf_op jit(solution)/shard_map/reshape | solution.py:65
  231.4 3.7 %reshape.134 = f32[16,4,4096]{2,1,0:T(4,128)S(1)} reshape(f32[16,512,32]{2,1,0:T(8,128)} %copy.37) | data formatting | bytes 2097152 | tf_op jit(solution)/shard_map/reshape | solution.py:66
  236.3 25.6 %all_to_all.97 = f32[16,4,4096]{2,0,1:T(8,128)S(1)} all-to-all(f32[16,4,4096]{2,0,1:T(8,128)S(1)} %copy.38), channel_id=1, replica_groups=mesh['tm'=4,'det'=8] {'tm'}, dimensions={1} | all-to-all | bytes 2097152 | tf_op jit(solution)/shard_map/all_to_all | solution.py:109
  (30 shorter events, 24.4 us)
Async XLA Ops:
  6.5 32.0 %all-to-all-start = ((f32[4,16,4096]{2,1,0:T(8,128)}), f32[4,16,4096]{2,1,0:T(8,128)S(1)}, u32[]{:S(2)}, u32[]{:S(2)}) async-start(f32[4,16,4096]{2,1,0:T(8,128)} %bitcast.92), calls=%async_computation | async-start | bytes 2097152 | tf_op jit(solution)/shard_map/all_to_all | solution.py:80
  80.4 9.1 %copy-start = (f32[1,128,512]{2,1,0:T(8,128)S(1)}, f32[1,128,512]{2,1,0:T(8,128)}, u32[]{:S(2)}) copy-start(f32[1,128,512]{2,1,0:T(8,128)} %param.3) | copy-start | bytes 786436
  85.7 19.2 %all-to-all-start.1 = ((f32[16,8,2048]{2,0,1:T(8,128)}), f32[16,8,2048]{2,0,1:T(8,128)S(1)}, u32[]{:S(2)}, u32[]{:S(2)}) async-start(f32[16,8,2048]{2,0,1:T(8,128)} %copy.29), calls=%async_computation.1 | async-start | bytes 2097152 | tf_op jit(solution)/shard_map/all_to_all | solution.py:85
  89.4 48.4 %all-gather.2.cloned.1.call-start = ((), (), s32[]{:S(2)}) async-start(), calls=%async_computation.6 | async-start | bytes 1310720 | tf_op jit(solution)/shard_map/all_gather | solution.py:89
  106.8 36.3 %all-to-all-start.2 = ((f32[128,4,512]{2,0,1:T(8,128)}), f32[128,4,512]{2,0,1:T(8,128)S(1)}, u32[]{:S(2)}, u32[]{:S(2)}) async-start(f32[128,4,512]{2,0,1:T(8,128)} %copy.30), calls=%async_computation.2 | async-start | bytes 2097152 | tf_op jit(solution)/shard_map/all_to_all | solution.py:86
  176.8 18.9 %all-to-all-start.4 = ((f32[8,16,2048]{2,1,0:T(8,128)}), f32[8,16,2048]{2,1,0:T(8,128)S(1)}, u32[]{:S(2)}, u32[]{:S(2)}) async-start(f32[8,16,2048]{2,1,0:T(8,128)} %all_to_all.84), calls=%async_computation.4 | async-start | bytes 2097152 | tf_op jit(solution)/shard_map/all_to_all | solution.py:99
Sparse Core Ops, SparseCore 0:
  91.8 46.0 all-gather.1
where the time goes:
time: 275 us; the launch traced here: 270 us
  waiting for transfers between devices  86.7 us (32%)
  matrix products  66.5 us (24%)
  blocking collectives  53.8 us (20%)
  local copies, waits for them, and re-layouts  29.7 us (11%)
  starting transfers between devices  17.6 us (6%)
  between operations  13.9 us (5%)
    all_to_all x1, blocking collectives, local(): lax.all_to_all(ordered, 'tm', split_axis=0, concat_axis=1, tiled=True)  28.2 us
    all_gather x1, waiting for transfers between devices, local(): rows_block = lax.all_gather(factor, 'tm', axis=1, tiled=True)[0]  27.5 us
    all_to_all x1, blocking collectives, local(): lax.all_to_all(signal, 'tm', split_axis=1, concat_axis=0, tiled=True)  25.6 us
    all_to_all x1, waiting for transfers between devices, local(): lax.all_to_all(noise, 'tm', split_axis=0, concat_axis=1, tiled=True)  25 us
    dot_general x2, matrix products, direct_dft(): out_real = out_real + jnp.matmul(imag_part, sines, precision=highest)  21.6 us
    all_to_all x1, waiting for transfers between devices, local(): lax.all_to_all(spectrum, 'det', split_axis=1, concat_axis=0, tiled=True)  14.5 us
    all_to_all x1, waiting for transfers between devices, local(): lax.all_to_all(lax.all_to_all(ordered, 'tm', split_axis=0, concat_axis=1,...  14.5 us
    dot_general x2, matrix products, direct_dft(): out_imag = -jnp.matmul(real_part, sines, precision=highest)  11.9 us
  transfers between devices with their start and end apart: 5, of which 5 were waited for; matrix products, arithmetic and copies ran while one was open for 1% of the time, Pallas kernels for 0%

commit v1 on v0

v1 whole, which is shorter than its diff:
```python
import math

import jax
import jax.numpy as jnp
import ml_dtypes
import numpy as np
from jax import lax
from jax.experimental import pallas as pl
from jax.experimental.pallas import tpu as pltpu
from jax.sharding import PartitionSpec as P


LANES = 128
VMEM_LIMIT = 48 * 1024 * 1024


def fourier_matrix(n2, planes):
    share = n2 // (2 * planes)
    order = []
    for plane in range(planes):
        low = np.arange(plane * share, (plane + 1) * share)
        order.append(np.concatenate([low, n2 - 1 - low[::-1]]))
    order = np.stack(order)
    angle = 2.0 * np.pi / n2 * (np.arange(n2)[:, None, None] * order[None] % n2)
    cosine, sine = np.cos(angle), np.sin(angle)
    matrix = np.stack([np.stack([cosine, -sine], 2), np.stack([sine, cosine], 2)])
    matrix = matrix.reshape(2 * n2, 2 * n2).astype(np.float32)
    high = matrix.astype(ml_dtypes.bfloat16)
    low = (matrix - high.astype(np.float32)).astype(ml_dtypes.bfloat16)
    return high, low


def twiddles(n1, n2):
    angle = 2.0 * np.pi / (n1 * n2) * (np.arange(n1)[:, None] + 0.25) * np.arange(n2)[None, :]
    return np.cos(angle).astype(np.float32), np.sin(angle).astype(np.float32)


def forward_butterflies(parts, shift):
    count = len(parts)
    if count == 1:
        return parts
    half = count // 2
    turn_re, turn_im = math.cos(math.pi * shift), -math.sin(math.pi * shift)
    even, odd = [], []
    for (a_re, a_im), (b_re, b_im) in zip(parts[:half], parts[half:]):
        c_re = b_re * turn_re - b_im * turn_im
        c_im = b_re * turn_im + b_im * turn_re
        even.append((a_re + c_re, a_im + c_im))
        odd.append((a_re - c_re, a_im - c_im))
    even = forward_butterflies(even, shift / 2)
    odd = forward_butterflies(odd, (1 + shift) / 2)
    return [part for pair in zip(even, odd) for part in pair]


def inverse_butterflies(parts, shift):
    if len(parts) == 1:
        return parts
    turn_re, turn_im = math.cos(math.pi * shift), math.sin(math.pi * shift)
    even = inverse_butterflies(parts[0::2], shift / 2)
    odd = inverse_butterflies(parts[1::2], (1 + shift) / 2)
    first, second = [], []
    for (a_re, a_im), (b_re, b_im) in zip(even, odd):
        d_re, d_im = a_re - b_re, a_im - b_im
        first.append((a_re + b_re, a_im + b_im))
        second.append((d_re * turn_re - d_im * turn_im, d_re * turn_im + d_im * turn_re))
    return first + second


def split(value):
    high = value.astype(jnp.bfloat16)
    return high, (value - high.astype(jnp.float32)).astype(jnp.bfloat16)


def product(left, right, contract=((1,), (0,))):
    def dot(a, b):
        return lax.dot_general(a, b, (contract, ((), ())), preferred_element_type=jnp.float32)

    return dot(left[0], right[0]) + (dot(left[0], right[1]) + dot(left[1], right[0]))


def tiles(rows, lanes):
    step = min(8, rows)
    for row in range(0, rows, step):
        for lane in range(0, lanes, LANES):
            yield slice(row, row + step), lane


def forward_kernel(n1, n2, x_ref, cos_ref, sin_ref, high_ref, low_ref, out_ref, mid_ref):
    blocks, dets, span = x_ref.shape
    per = span // n2
    for rows, lane in tiles(dets, n2):

        def load(index):
            start = (index % per) * n2 + lane
            return x_ref[index // per, rows, start : start + LANES]

        parts = [(load(t1), -load(t1 + n1)) for t1 in range(n1)]
        for k1, (re, im) in enumerate(forward_butterflies(parts, 0.25)):
            cosine = cos_ref[k1 : k1 + 1, lane : lane + LANES]
            sine = sin_ref[k1 : k1 + 1, lane : lane + LANES]
            place = slice(k1 * dets + rows.start, k1 * dets + rows.stop)
            mid_ref[place, lane : lane + LANES] = re * cosine + im * sine
            mid_ref[place, n2 + lane : n2 + lane + LANES] = im * cosine - re * sine
    spectrum = product(split(mid_ref[...]), (high_ref[...], low_ref[...]))
    planes, _, width = out_ref.shape
    for plane in range(planes):
        out_ref[plane] = spectrum[:, plane * width : (plane + 1) * width]


def inverse_kernel(n1, n2, y_ref, cos_ref, sin_ref, high_ref, low_ref, out_ref, mid_ref):
    blocks, dets, span = out_ref.shape
    per = span // n2
    scale = 1.0 / (n1 * n2)
    bins = jnp.concatenate([y_ref[plane] for plane in range(y_ref.shape[0])], axis=1)
    mid_ref[...] = product(split(bins), (high_ref[...], low_ref[...]), ((1,), (1,)))
    for rows, lane in tiles(dets, n2):
        parts = []
        for k1 in range(n1):
            cosine = cos_ref[k1 : k1 + 1, lane : lane + LANES] * scale
            sine = sin_ref[k1 : k1 + 1, lane : lane + LANES] * scale
            place = slice(k1 * dets + rows.start, k1 * dets + rows.stop)
            re = mid_ref[place, lane : lane + LANES]
            im = mid_ref[place, n2 + lane : n2 + lane + LANES]
            parts.append((re * cosine - im * sine, im * cosine + re * sine))
        for t1, (re, im) in enumerate(inverse_butterflies(parts, 0.25)):
            for index, value in ((t1, re), (t1 + n1, -im)):
                start = (index % per) * n2 + lane
                out_ref[index // per, rows, start : start + LANES] = value


def mix_kernel(x_ref, factor_ref, out_ref, x_mid, y_mid):
    planes, groups, pieces, dets, width = x_ref.shape
    places = [
        (plane, group, piece, slice((group * planes + plane) * dets, (group * planes + plane + 1) * dets),
         slice(piece * width, (piece + 1) * width))
        for plane in range(planes) for group in range(groups) for piece in range(pieces)
    ]
    for plane, group, piece, rows, lanes in places:
        x_mid[rows, lanes] = x_ref[plane, group, piece]
    count = factor_ref.shape[0]
    half = count // 2
    f_high, f_low = split(factor_ref[...])
    x_high, x_low = split(x_mid[...])
    y_mid[:half] = product((f_high[:half, :half], f_low[:half, :half]), (x_high[:half], x_low[:half]))
    y_mid[half:] = product((f_high[half:], f_low[half:]), (x_high, x_low))
    for plane, group, piece, rows, lanes in places:
        out_ref[plane, group, piece] = y_mid[rows, lanes]


def call(kernel, out_shape, scratch, flops, *args):
    whole = pl.BlockSpec(memory_space=pltpu.VMEM)
    count = sum(math.prod(arg.shape) * arg.dtype.itemsize for arg in args) + math.prod(out_shape) * 4
    return pl.pallas_call(
        kernel,
        out_shape=jax.ShapeDtypeStruct(out_shape, jnp.float32),
        in_specs=[whole] * len(args),
        out_specs=whole,
        scratch_shapes=[pltpu.VMEM(shape, jnp.float32) for shape in scratch],
        compiler_params=pltpu.CompilerParams(vmem_limit_bytes=VMEM_LIMIT),
        cost_estimate=pl.CostEstimate(flops=flops, bytes_accessed=count, transcendentals=0),
    )(*args)


def band_factor(factor, planes, groups):
    half = factor.shape[1] // 2
    upper = lax.axis_index("det") >= groups // 2
    mine = lax.dynamic_slice_in_dim(factor[0], jnp.where(upper, half, 0), half, 0)
    pairs = []
    for plane in range(planes):
        for group in range(groups):
            target = min(group, groups - 1 - group)
            pairs.append((plane * groups + group, target * groups + 2 * plane + (group >= groups // 2)))
    share = lax.ppermute(mine, ("tm", "det"), pairs)
    return lax.all_gather(share, "det", axis=0, tiled=True)


def local(noise, factor):
    planes = lax.axis_size("tm")
    groups = lax.axis_size("det")
    rows, span = noise.shape
    dets = rows // planes
    n2 = LANES // 2 * planes
    n1 = span * planes // 2 // n2
    pieces = n1 // groups
    high, low = fourier_matrix(n2, planes)
    cosine, sine = twiddles(n1, n2)
    flops = 3 * 2 * n1 * dets * (2 * n2) ** 2

    matrix = band_factor(factor, planes, groups)
    series = lax.all_to_all(noise, "tm", split_axis=0, concat_axis=0, tiled=True).reshape(planes, dets, span)
    spectrum = call(
        lambda *refs: forward_kernel(n1, n2, *refs), (planes, n1 * dets, LANES), [(n1 * dets, 2 * n2)], flops,
        series, cosine, sine, high, low,
    )
    spread = lax.all_to_all(
        spectrum.reshape(planes * groups, pieces * dets, LANES), ("tm", "det"), split_axis=0, concat_axis=0, tiled=True
    )
    count = matrix.shape[0]
    mixed = call(
        mix_kernel, (planes, groups, pieces, dets, LANES), [(count, pieces * LANES)] * 2,
        2 * 3 * count * count * pieces * LANES,
        spread.reshape(planes, groups, pieces, dets, LANES), matrix,
    )
    back = lax.all_to_all(
        mixed.reshape(planes * groups, pieces * dets, LANES), ("tm", "det"), split_axis=0, concat_axis=0, tiled=True
    )
    signal = call(
        lambda *refs: inverse_kernel(n1, n2, *refs), (planes, dets, span), [(n1 * dets, 2 * n2)], flops,
        back.reshape(planes, n1 * dets, LANES), cosine, sine, high, low,
    )
    return lax.all_to_all(signal.reshape(rows, span), "tm", split_axis=0, concat_axis=0, tiled=True)


def solution(mesh):
    in_specs = (P("det", "tm"), P("det", "tm", None))
    return jax.shard_map(local, mesh=mesh, in_specs=in_specs, out_specs=P("det", "tm"), check_vma=False)
```

time: 275 us -> 170 us (0.62); the launches traced: 270 us -> 170 us
  matrix products: 66.5 us -> 0 us
  local copies, waits for them, and re-layouts: 29.7 us -> 2.88 us
  waiting for transfers between devices: 86.7 us -> 79 us
  starting transfers between devices: 17.6 us -> 10.9 us
  blocking collectives: 53.8 us -> 59.1 us
  Pallas kernels: 0 us -> 4.71 us
    dot_general x15 -> x0, matrix products: 66.5 us -> none  [the longest x2 21.6 us: direct_dft(): out_real = out_real + jnp.matmul(imag_part, sines, precision=highest)]
    all_to_all x4 -> x2, waiting for transfers between devices: 59.2 us -> 25.7 us  [the longest x1 25.7 us: local(): lax.all_to_all(noise, 'tm', split_axis=0, concat_axis=0, tiled=True)]
    all_gather x1, waiting for transfers between devices: 27.5 us -> 53.3 us  [band_factor(): return lax.all_gather(share, 'det', axis=0, tiled=True)]
    sub x3 -> x0, local copies, waits for them, and re-layouts: 7.91 us -> none  [hartley(): return fin_real - fin_imag]
    reshape x4 -> x0, local copies, waits for them, and re-layouts: 7.73 us -> none  [the longest x1 3.68 us: dft_last(): fin_real = jnp.swapaxes(fin_real, -1, -2).reshape(leading + (length,))]
    all_to_all x4 -> x2, starting transfers between devices: 17.5 us -> 10.2 us  [the longest x1 6.46 us: local(): lax.all_to_all(noise, 'tm', split_axis=0, concat_axis=0, tiled=True)]
    all_to_all x7 -> x0, local copies, waits for them, and re-layouts: 6.38 us -> none  [the longest x2 2.3 us: local(): lax.all_to_all(lax.all_to_all(ordered, 'tm', split_axis=0, concat_axis=1,...]
    add x2 -> x0, local copies, waits for them, and re-layouts: 5.3 us -> none  [the longest x1 2.65 us: direct_dft(): out_real = out_real + jnp.matmul(imag_part, sines, precision=highest)]
  transfers between devices with their start and end apart: 5 -> 4, of which waited for: 5 -> 2; matrix products, arithmetic and copies ran while one was open for 1% -> 0% of each run, Pallas kernels for 0% -> 0%
where the time goes in v1:
time: 170 us
  waiting for transfers between devices  79 us (46%)
  blocking collectives  59.1 us (35%)
  between operations  13.5 us (8%)
  starting transfers between devices  10.9 us (6%)
  Pallas kernels  4.71 us (3%)
  local copies, waits for them, and re-layouts  2.88 us (2%)
    all_gather x1, waiting for transfers between devices, band_factor(): return lax.all_gather(share, 'det', axis=0, tiled=True)  53.3 us
    all_to_all x1, blocking collectives, local(): lax.all_to_all(mixed.reshape(planes * groups, pieces * dets, LANES), ('tm...  30.6 us
    all_to_all x1, blocking collectives, local(): lax.all_to_all(signal.reshape(rows, span), 'tm', split_axis=0, concat_axi...  28.5 us
    all_to_all x1, waiting for transfers between devices, local(): lax.all_to_all(noise, 'tm', split_axis=0, concat_axis=0, tiled=True)  25.7 us
    all_to_all x1, starting transfers between devices, local(): lax.all_to_all(noise, 'tm', split_axis=0, concat_axis=0, tiled=True)  6.46 us
    pallas_call x3, Pallas kernels, call(): pl.pallas_call(kernel, out_shape=jax.ShapeDtypeStruct(out_shape, jnp.floa...  4.71 us
    all_to_all x1, starting transfers between devices, local(): lax.all_to_all(spectrum.reshape(planes * groups, pieces * dets, LANES), (...  3.71 us
  transfers between devices with their start and end apart: 4, of which 2 were waited for; matrix products, arithmetic and copies ran while one was open for 0% of the time, Pallas kernels for 0%

profile of v1, /device:TPU:0, one launch (start us, length us, event | category | flops | bytes accessed | tf_op | source)
XLA Modules:
  0.0 170.1 jit_solution(10334906773605652313)
XLA Ops:
  6.5 0.0 copy-start
  6.6 6.5 %all-to-all-start = ((f32[4,16,4096]{2,1,0:T(8,128)}), f32[4,16,4096]{2,1,0:T(8,128)S(1)}, u32[]{:S(2)}, u32[]{:S(2)}) async-start(f32[4,16,4096]{2,1,0:T(8,128)} %bitcast.12), calls=%async_computation | async-start | bytes 2097152 | tf_op jit(solution)/shard_map/all_to_all | solution.py:190
  13.0 25.7 %all-to-all-done.refs_0_ = f32[4,16,4096]{2,1,0:T(8,128)S(1)} async-done(((f32[4,16,4096]{2,1,0:T(8,128)}), f32[4,16,4096]{2,1,0:T(8,128)S(1)}, u32[]{:S(2)}, u32[]{:S(2)}) %all-to-all-start) | async-done | bytes 1048608 | tf_op jit(solution)/shard_map/all_to_all | solution.py:190
  38.7 0.0 copy-done.1
  38.7 0.0 copy-done.2
  38.7 0.0 copy-done.4
  38.8 0.0 copy-done.5
  38.8 2.4 %shard_map.64 = f32[4,512,128]{2,1,0:T(8,128)} custom-call(f32[4,16,4096]{2,1,0:T(8,128)S(1)} %all-to-all-done.refs_0_, f32[32,256]{1,0:T(8,128)S(1)} %copy-done.5, f32[32,256]{1,0:T(8,128)S(1)} %copy-done.4, bf16[512,512]{1,0:T(8,128)(2,1)S(1)} %copy-done.2, bf16[512,512]{1,0:T(8,128)(2,1)S(1)} %copy-done.1), custom_call_target="tpu_custom_call" | custom-call | flops 805306368 | bytes 3211264 | tf_op jit(solution)/shard_map/pallas_call | solution.py:153
  41.2 3.7 %all-to-all-start.1 = ((f32[32,64,128]{2,1,0:T(8,128)}), f32[32,64,128]{2,1,0:T(8,128)S(1)}, u32[]{:S(2)}, u32[]{:S(2)}) async-start(f32[32,64,128]{2,1,0:T(8,128)} %bitcast.1), calls=%async_computation.1 | async-start | bytes 2097152 | tf_op jit(solution)/shard_map/all_to_all | solution.py:195
  44.9 0.0 all-gather.2.cloned.1.call-start
  45.0 0.0 copy-done
  45.0 0.7 collective-permute-start
  45.7 0.0 collective-permute-done
  45.7 0.0 copy-start.6
  45.7 0.6 copy-done.6
  46.3 0.0 all-gather.2.cloned.1.call-update
  46.4 53.3 %all-gather.2.cloned.1.call-done.factor_ref = f32[512,512]{1,0:T(8,128)} async-done(((f32[64,512]{1,0:T(8,128)}), f32[512,512]{1,0:T(8,128)}) %all-gather.2.cloned.1.call-update) | async-done | bytes 1048592 | tf_op jit(solution)/shard_map/all_gather | solution.py:174
  99.6 0.0 all-to-all-done.1
  99.6 1.2 copy-done.3
  100.9 0.8 shard_map.65
  101.7 30.6 %all_to_all.28 = f32[32,64,128]{2,1,0:T(8,128)S(1)} all-to-all(f32[32,64,128]{2,1,0:T(8,128)S(1)} %bitcast.10), channel_id=1, replica_groups=mesh['tm'=4,'det'=8] {'tm','det'}, dimensions={0} | all-to-all | bytes 2097152 | tf_op jit(solution)/shard_map/all_to_all | solution.py:204
  132.3 1.5 shard_map.66
  133.8 28.5 %all_to_all.29 = f32[4,16,4096]{2,1,0:T(8,128)S(1)} all-to-all(f32[4,16,4096]{2,1,0:T(8,128)S(1)} %shard_map.66), channel_id=1, replica_groups=mesh['tm'=4,'det'=8] {'tm'}, dimensions={0} | all-to-all | bytes 2097152 | tf_op jit(solution)/shard_map/all_to_all | solution.py:211
  162.3 1.0 copy.8
  (6 shorter events, 0.0 us)
Async XLA Ops:
  6.5 38.4 %copy-start = (f32[1,128,512]{2,1,0:T(8,128)S(1)}, f32[1,128,512]{2,1,0:T(8,128)}, u32[]{:S(2)}) copy-start(f32[1,128,512]{2,1,0:T(8,128)} %param.7) | copy-start | bytes 786436
  6.5 32.2 %copy-start.1 = (bf16[512,512]{1,0:T(8,128)(2,1)S(1)}, bf16[512,512]{1,0:T(8,128)(2,1)}, u32[]{:S(2)}) copy-start(bf16[512,512]{1,0:T(8,128)(2,1)} %constant.24.clone.refs_4_) | copy-start | bytes 1572868
  6.5 32.2 %copy-start.2 = (bf16[512,512]{1,0:T(8,128)(2,1)S(1)}, bf16[512,512]{1,0:T(8,128)(2,1)}, u32[]{:S(2)}) copy-start(bf16[512,512]{1,0:T(8,128)(2,1)} %constant.23.clone.refs_3_) | copy-start | bytes 1572868
  6.5 32.2 %copy-start.4 = (f32[32,256]{1,0:T(8,128)S(1)}, f32[32,256]{1,0:T(8,128)}, u32[]{:S(2)}) copy-start(f32[32,256]{1,0:T(8,128)} %constant.22.clone.refs_2_) | copy-start | bytes 98308
  6.5 32.2 %copy-start.5 = (f32[32,256]{1,0:T(8,128)S(1)}, f32[32,256]{1,0:T(8,128)}, u32[]{:S(2)}) copy-start(f32[32,256]{1,0:T(8,128)} %constant.21.clone.refs_1_) | copy-start | bytes 98308
  6.6 32.2 %all-to-all-start = ((f32[4,16,4096]{2,1,0:T(8,128)}), f32[4,16,4096]{2,1,0:T(8,128)S(1)}, u32[]{:S(2)}, u32[]{:S(2)}) async-start(f32[4,16,4096]{2,1,0:T(8,128)} %bitcast.12), calls=%async_computation | async-start | bytes 2097152 | tf_op jit(solution)/shard_map/all_to_all | solution.py:190
  41.2 58.4 %all-to-all-start.1 = ((f32[32,64,128]{2,1,0:T(8,128)}), f32[32,64,128]{2,1,0:T(8,128)S(1)}, u32[]{:S(2)}, u32[]{:S(2)}) async-start(f32[32,64,128]{2,1,0:T(8,128)} %bitcast.1), calls=%async_computation.1 | async-start | bytes 2097152 | tf_op jit(solution)/shard_map/all_to_all | solution.py:195
  44.9 54.7 %all-gather.2.cloned.1.call-start = ((), (), s32[]{:S(2)}) async-start(), calls=%async_computation.4 | async-start | bytes 1179648 | tf_op jit(solution)/shard_map/all_gather | solution.py:174
  45.0 0.7 collective-permute-start
  45.7 0.7 copy-start.6
  99.6 1.2 copy-start.3
Sparse Core Ops, SparseCore 0:
  47.6 51.9 all-gather.1

commit v2 on v1

--- a/solution.py
+++ b/solution.py
@@ -85,8 +85,13 @@
             yield slice(row, row + step), lane
 
 
-def forward_kernel(n1, n2, x_ref, cos_ref, sin_ref, high_ref, low_ref, out_ref, mid_ref):
-    blocks, dets, span = x_ref.shape
+def forward_kernel(n1, n2, noise_ref, *refs):
+    here = lax.axis_index("tm")
+    blocks, dets, span = noise_ref.shape
+    others, (cos_ref, sin_ref, high_ref, low_ref, out_ref, x_ref, mid_ref) = refs[: blocks - 1], refs[blocks - 1 :]
+    x_ref[here] = noise_ref[here]
+    for step, other in enumerate(others, 1):
+        x_ref[here ^ step] = other[...]
     per = span // n2
     for rows, lane in tiles(dets, n2):
 
@@ -107,7 +112,9 @@
         out_ref[plane] = spectrum[:, plane * width : (plane + 1) * width]
 
 
-def inverse_kernel(n1, n2, y_ref, cos_ref, sin_ref, high_ref, low_ref, out_ref, mid_ref):
+def inverse_kernel(n1, n2, y_ref, cos_ref, sin_ref, high_ref, low_ref, *refs):
+    here = lax.axis_index("tm")
+    outs, (out_ref, mid_ref) = refs[:-2], refs[-2:]
     blocks, dets, span = out_ref.shape
     per = span // n2
     scale = 1.0 / (n1 * n2)
@@ -126,9 +133,22 @@
             for index, value in ((t1, re), (t1 + n1, -im)):
                 start = (index % per) * n2 + lane
                 out_ref[index // per, rows, start : start + LANES] = value
-
-
-def mix_kernel(x_ref, factor_ref, out_ref, x_mid, y_mid):
+    for step, out in enumerate(outs):
+        out[...] = out_ref[here ^ step]
+
+
+def factor_kernel(masks, factor_ref, high_ref, low_ref):
+    here = lax.axis_index("det")
+    shares, rows, _ = factor_ref.shape
+    for share in range(shares):
+        source = here
+        for bit, mask in enumerate(masks):
+            source = source ^ (mask if share >> bit & 1 else 0)
+        place = pl.ds(pl.multiple_of(source * rows, rows), rows)
+        high_ref[place], low_ref[place] = split(factor_ref[share])
+
+
+def mix_kernel(x_ref, f_high, f_low, out_ref, x_mid, y_mid):
     planes, groups, pieces, dets, width = x_ref.shape
     places = [
         (plane, group, piece, slice((group * planes + plane) * dets, (group * planes + plane + 1) * dets),
@@ -137,28 +157,34 @@
     ]
     for plane, group, piece, rows, lanes in places:
         x_mid[rows, lanes] = x_ref[plane, group, piece]
-    count = factor_ref.shape[0]
-    half = count // 2
-    f_high, f_low = split(factor_ref[...])
+    half = f_high.shape[0] // 2
     x_high, x_low = split(x_mid[...])
     y_mid[:half] = product((f_high[:half, :half], f_low[:half, :half]), (x_high[:half], x_low[:half]))
-    y_mid[half:] = product((f_high[half:], f_low[half:]), (x_high, x_low))
+    y_mid[half:] = product((f_high[half:, :], f_low[half:, :]), (x_high, x_low))
     for plane, group, piece, rows, lanes in places:
         out_ref[plane, group, piece] = y_mid[rows, lanes]
 
 
-def call(kernel, out_shape, scratch, flops, *args):
+def call(kernel, outs, scratch, flops, *args):
     whole = pl.BlockSpec(memory_space=pltpu.VMEM)
-    count = sum(math.prod(arg.shape) * arg.dtype.itemsize for arg in args) + math.prod(out_shape) * 4
+    count = sum(math.prod(arg.shape) * arg.dtype.itemsize for arg in (*args, *outs))
     return pl.pallas_call(
         kernel,
-        out_shape=jax.ShapeDtypeStruct(out_shape, jnp.float32),
+        out_shape=outs,
         in_specs=[whole] * len(args),
-        out_specs=whole,
+        out_specs=[whole] * len(outs),
         scratch_shapes=[pltpu.VMEM(shape, jnp.float32) for shape in scratch],
         compiler_params=pltpu.CompilerParams(vmem_limit_bytes=VMEM_LIMIT),
         cost_estimate=pl.CostEstimate(flops=flops, bytes_accessed=count, transcendentals=0),
     )(*args)
+
+
+def array(*shape, dtype=jnp.float32):
+    return jax.ShapeDtypeStruct(shape, dtype)
+
+
+def swap(value, axis, mask):
+    return lax.ppermute(value, axis, [(place, place ^ mask) for place in range(lax.axis_size(axis))])
 
 
 def band_factor(factor, planes, groups):
@@ -170,13 +196,18 @@
         for group in range(groups):
             target = min(group, groups - 1 - group)
             pairs.append((plane * groups + group, target * groups + 2 * plane + (group >= groups // 2)))
-    share = lax.ppermute(mine, ("tm", "det"), pairs)
-    return lax.all_gather(share, "det", axis=0, tiled=True)
+    share = lax.ppermute(mine, ("tm", "det"), pairs)[None]
+    masks = [2**bit for bit in range(1, groups.bit_length() - 1)] + [1]
+    for mask in masks:
+        share = jnp.concatenate([share, swap(share, "det", mask)])
+    whole = array(groups * half, factor.shape[2], dtype=jnp.bfloat16)
+    return call(lambda *refs: factor_kernel(masks, *refs), [whole, whole], [], 0, share)
 
 
 def local(noise, factor):
     planes = lax.axis_size("tm")
     groups = lax.axis_size("det")
+    here = lax.axis_index("tm")
     rows, span = noise.shape
     dets = rows // planes
     n2 = LANES // 2 * planes
@@ -185,30 +216,37 @@
     high, low = fourier_matrix(n2, planes)
     cosine, sine = twiddles(n1, n2)
     flops = 3 * 2 * n1 * dets * (2 * n2) ** 2
-
-    matrix = band_factor(factor, planes, groups)
-    series = lax.all_to_all(noise, "tm", split_axis=0, concat_axis=0, tiled=True).reshape(planes, dets, span)
-    spectrum = call(
-        lambda *refs: forward_kernel(n1, n2, *refs), (planes, n1 * dets, LANES), [(n1 * dets, 2 * n2)], flops,
-        series, cosine, sine, high, low,
+    series = (planes, dets, span)
+    middle = (n1 * dets, 2 * n2)
+
+    blocks = noise.reshape(series)
+    others = [swap(lax.dynamic_index_in_dim(blocks, here ^ step, keepdims=False), "tm", step) for step in range(1, planes)]
+    f_high, f_low = band_factor(factor, planes, groups)
+    (spectrum,) = call(
+        lambda *refs: forward_kernel(n1, n2, *refs), [array(planes, n1 * dets, LANES)], [series, middle], flops,
+        blocks, *others, cosine, sine, high, low,
     )
     spread = lax.all_to_all(
         spectrum.reshape(planes * groups, pieces * dets, LANES), ("tm", "det"), split_axis=0, concat_axis=0, tiled=True
     )
-    count = matrix.shape[0]
-    mixed = call(
-        mix_kernel, (planes, groups, pieces, dets, LANES), [(count, pieces * LANES)] * 2,
+    count = f_high.shape[0]
+    (mixed,) = call(
+        mix_kernel, [array(planes, groups, pieces, dets, LANES)], [(count, pieces * LANES)] * 2,
         2 * 3 * count * count * pieces * LANES,
-        spread.reshape(planes, groups, pieces, dets, LANES), matrix,
+        spread.reshape(planes, groups, pieces, dets, LANES), f_high, f_low,
     )
     back = lax.all_to_all(
         mixed.reshape(planes * groups, pieces * dets, LANES), ("tm", "det"), split_axis=0, concat_axis=0, tiled=True
     )
-    signal = call(
-        lambda *refs: inverse_kernel(n1, n2, *refs), (planes, dets, span), [(n1 * dets, 2 * n2)], flops,
+    parts = call(
+        lambda *refs: inverse_kernel(n1, n2, *refs), [array(dets, span)] * planes, [series, middle], flops,
         back.reshape(planes, n1 * dets, LANES), cosine, sine, high, low,
     )
-    return lax.all_to_all(signal.reshape(rows, span), "tm", split_axis=0, concat_axis=0, tiled=True)
+    result = jnp.zeros(series, jnp.float32)
+    for step, part in enumerate(parts):
+        part = swap(part, "tm", step) if step else part
+        result = lax.dynamic_update_index_in_dim(result, part, here ^ step, 0)
+    return result.reshape(rows, span)
 
 
 def solution(mesh):

time: 170 us -> 145 us (0.85); the launches traced: 170 us -> 143 us
  blocking collectives: 59.1 us -> 0 us
  starting transfers between devices: 10.9 us -> 52.8 us
  between operations: 13.5 us -> 0.17 us
  local copies, waits for them, and re-layouts: 2.88 us -> 5.19 us
    all_to_all x2 -> x0, blocking collectives: 59.1 us -> none  [the longest x1 30.6 us: local(): lax.all_to_all(mixed.reshape(planes * groups, pieces * dets, LANES), ('tm...]
    all_gather x1 -> x0, waiting for transfers between devices: 53.3 us -> none  [band_factor(): return lax.all_gather(share, 'det', axis=0, tiled=True)]
    ppermute x1 -> x10, waiting for transfers between devices: 0.01 us -> 52.1 us  [the longest x9 52.1 us: swap(): lax.ppermute(value, axis, [(place, place ^ mask) for place in range(lax.a...]
    ppermute x1 -> x10, starting transfers between devices: 0.67 us -> 44.3 us  [the longest x9 43.6 us: swap(): lax.ppermute(value, axis, [(place, place ^ mask) for place in range(lax.a...]
    all_to_all x1, starting transfers between devices: 6.46 us -> 3.79 us  [local(): lax.all_to_all(mixed.reshape(planes * groups, pieces * dets, LANES), ('tm...]
    unnamed x15 -> x18, local copies, waits for them, and re-layouts: 2.86 us -> 3.75 us
  transfers between devices with their start and end apart: 4 -> 12, of which waited for: 2 -> 8; matrix products, arithmetic and copies ran while one was open for 0% -> 0% of each run, Pallas kernels for 0% -> 0%
where the time goes in v2:
time: 145 us; the launch traced here: 143 us
  waiting for transfers between devices  78.4 us (54%)
  starting transfers between devices  52.8 us (36%)
  local copies, waits for them, and re-layouts  5.19 us (4%)
  Pallas kernels  4.37 us (3%)
  other arithmetic  1.67 us (1%)
    ppermute x9, waiting for transfers between devices, swap(): lax.ppermute(value, axis, [(place, place ^ mask) for place in range(lax.a...  52.1 us
    ppermute x9, starting transfers between devices, swap(): lax.ppermute(value, axis, [(place, place ^ mask) for place in range(lax.a...  43.6 us
    all_to_all x1, waiting for transfers between devices, local(): lax.all_to_all(mixed.reshape(planes * groups, pieces * dets, LANES), ('tm...  26.2 us
    all_to_all x1, starting transfers between devices, local(): lax.all_to_all(spectrum.reshape(planes * groups, pieces * dets, LANES), (...  4.72 us
    pallas_call x3, Pallas kernels, call(): pl.pallas_call(kernel, out_shape=outs, in_specs=[whole] * len(args), out_...  4.37 us
    all_to_all x1, starting transfers between devices, local(): lax.all_to_all(mixed.reshape(planes * groups, pieces * dets, LANES), ('tm...  3.79 us
    unnamed x18, local copies, waits for them, and re-layouts  3.75 us
  transfers between devices with their start and end apart: 12, of which 8 were waited for; matrix products, arithmetic and copies ran while one was open for 0% of the time, Pallas kernels for 0%

profile of v2, /device:TPU:0, one launch (start us, length us, event | category | flops | bytes accessed | tf_op | source)
XLA Modules:
  0.0 142.6 jit_solution(12601012043102259804)
XLA Ops:
  0.0 1.3 dynamic-slice_bitcast_fusion
  1.3 5.1 %collective-permute-start.2 = (f32[16,4096]{1,0:T(8,128)S(1)}, f32[16,4096]{1,0:T(8,128)S(1)}, u32[]{:S(2)}, u32[]{:S(2)}) collective-permute-start(f32[16,4096]{1,0:T(8,128)S(1)} %get-tuple-element.25), channel_id=1, source_target_pairs={{0,24},{8,16},{16,8},{24,0},{1,25},{9,17},{17,9},{25,1},{2,26},{10... | collective-permute-start | bytes 786440 | tf_op jit(solution)/shard_map/ppermute | solution.py:187
  7.1 6.6 %collective-permute-done.2.refs_3_ = f32[16,4096]{1,0:T(8,128)S(1)} collective-permute-done((f32[16,4096]{1,0:T(8,128)S(1)}, f32[16,4096]{1,0:T(8,128)S(1)}, u32[]{:S(2)}, u32[]{:S(2)}) %collective-permute-start.2) | collective-permute-done | bytes 262176 | tf_op jit(solution)/shard_map/ppermute | solution.py:187
  13.7 15.0 %collective-permute-done.1.refs_2_ = f32[16,4096]{1,0:T(8,128)S(1)} collective-permute-done((f32[16,4096]{1,0:T(8,128)S(1)}, f32[16,4096]{1,0:T(8,128)S(1)}, u32[]{:S(2)}, u32[]{:S(2)}) %collective-permute-start.1) | collective-permute-done | bytes 262176 | tf_op jit(solution)/shard_map/ppermute | solution.py:187
  28.8 1.0 copy-done.3
  29.8 0.8 copy-done.6
  30.6 2.5 %shard_map.64 = f32[4,512,128]{2,1,0:T(8,128)} custom-call(f32[4,16,4096]{2,1,0:T(8,128)S(1)} %bitcast.25, f32[16,4096]{1,0:T(8,128)S(1)} %collective-permute-done.refs_1_, f32[16,4096]{1,0:T(8,128)S(1)} %collective-permute-done.1.refs_2_, f32[16,4096]{1,0:T(8,128)S(1)} %collective-permute-done.2.refs_3_, f32[32,256]{1,0:T(8,128)S(1)} %copy-done.6, ...), custom_call_target="tpu_custom_call" | custom-call | flops 805306368 | bytes 3997696 | tf_op jit(solution)/shard_map/pallas_call | solution.py:171
  33.0 4.7 %all-to-all-start = ((f32[32,64,128]{2,1,0:T(8,128)}), f32[32,64,128]{2,1,0:T(8,128)S(1)}, u32[]{:S(2)}, u32[]{:S(2)}) async-start(f32[32,64,128]{2,1,0:T(8,128)} %bitcast.4), calls=%async_computation | async-start | bytes 2097152 | tf_op jit(solution)/shard_map/all_to_all | solution.py:229
  38.5 21.4 %collective-permute-start.4 = (f32[1,64,512]{2,1,0:T(8,128)S(1)}, f32[1,64,512]{2,1,0:T(8,128)S(1)}, u32[]{:S(2)}, u32[]{:S(2)}) collective-permute-start(f32[1,64,512]{2,1,0:T(8,128)S(1)} %bitcast.27), channel_id=1, source_target_pairs={{0,2},{1,3},{2,0},{3,1},{4,6},{5,7},{6,4},{7,5},{8,10},{9,11},{10,... | collective-permute-start | bytes 393224 | tf_op jit(solution)/shard_map/ppermute | solution.py:187
  59.9 5.0 %collective-permute-done.4 = f32[1,64,512]{2,1,0:T(8,128)S(1)} collective-permute-done((f32[1,64,512]{2,1,0:T(8,128)S(1)}, f32[1,64,512]{2,1,0:T(8,128)S(1)}, u32[]{:S(2)}, u32[]{:S(2)}) %collective-permute-start.4) | collective-permute-done | bytes 131104 | tf_op jit(solution)/shard_map/ppermute | solution.py:187
  64.9 12.0 %collective-permute-start.5 = (f32[2,64,512]{2,1,0:T(8,128)S(1)}, f32[2,64,512]{2,1,0:T(8,128)S(1)}, u32[]{:S(2)}, u32[]{:S(2)}) collective-permute-start(f32[2,64,512]{2,1,0:T(8,128)S(1)} %pad_maximum_fusion.2), channel_id=1, source_target_pairs={{0,4},{1,5},{2,6},{3,7},{4,0},{5,1},{6,2},{7,3},{8,12},{9,13},{10,... | collective-permute-start | bytes 786440 | tf_op jit(solution)/shard_map/ppermute | solution.py:187
  76.9 5.9 %collective-permute-done.5 = f32[2,64,512]{2,1,0:T(8,128)S(1)} collective-permute-done((f32[2,64,512]{2,1,0:T(8,128)S(1)}, f32[2,64,512]{2,1,0:T(8,128)S(1)}, u32[]{:S(2)}, u32[]{:S(2)}) %collective-permute-start.5) | collective-permute-done | bytes 262176 | tf_op jit(solution)/shard_map/ppermute | solution.py:187
  82.9 1.9 %collective-permute-done.6 = f32[4,64,512]{2,1,0:T(8,128)S(1)} collective-permute-done((f32[4,64,512]{2,1,0:T(8,128)S(1)}, f32[4,64,512]{2,1,0:T(8,128)S(1)}, u32[]{:S(2)}, u32[]{:S(2)}) %collective-permute-start.6) | collective-permute-done | bytes 524320 | tf_op jit(solution)/shard_map/ppermute | solution.py:187
  85.0 1.8 %shard_map.66 = f32[4,8,4,16,128]{4,3,2,1,0:T(8,128)} custom-call(f32[4,8,4,16,128]{4,3,2,1,0:T(8,128)S(1)} %bitcast.23, bf16[512,512]{1,0:T(8,128)(2,1)S(1)} %get-tuple-element.11.f_high, bf16[512,512]{1,0:T(8,128)(2,1)S(1)} %get-tuple-element.12.f_low), custom_call_target="tpu_custom_call" | custom-call | flops 805306368 | bytes 3145728 | tf_op jit(solution)/shard_map/pallas_call | solution.py:171
  86.8 3.8 %all-to-all-start.1 = ((f32[32,64,128]{2,1,0:T(8,128)}), f32[32,64,128]{2,1,0:T(8,128)S(1)}, u32[]{:S(2)}, u32[]{:S(2)}) async-start(f32[32,64,128]{2,1,0:T(8,128)} %bitcast.8), calls=%async_computation.1 | async-start | bytes 2097152 | tf_op jit(solution)/shard_map/all_to_all | solution.py:238
  90.6 26.2 %all-to-all-done.1 = f32[32,64,128]{2,1,0:T(8,128)S(1)} async-done(((f32[32,64,128]{2,1,0:T(8,128)}), f32[32,64,128]{2,1,0:T(8,128)S(1)}, u32[]{:S(2)}, u32[]{:S(2)}) %all-to-all-start.1) | async-done | bytes 1048608 | tf_op jit(solution)/shard_map/all_to_all | solution.py:238
  116.9 1.0 copy-done.4
  117.9 1.5 %shard_map.67 = (f32[4,16,4096]{2,1,0:T(8,128)S(1)}, f32[16,4096]{1,0:T(8,128)S(1)}, f32[16,4096]{1,0:T(8,128)S(1)}, f32[16,4096]{1,0:T(8,128)S(1)}) fusion(f32[4,16,4096]{2,1,0:T(8,128)S(1)} %broadcast_in_dim.19, s32[]{:T(128)S(6)} %select_n.26, f32[4,512,128]{2,1,0:T(8,128)S(1)} %bitcast.26, f32[32,256]{1,0:T(8,128)S(1)} %copy-done.7, ...), kind=kCustom, calls=%fused_computation.6 | custom fusion | flops 805306368 | bytes 3211268 | tf_op jit(solution)/shard_map/pallas_call | solution.py:171
  119.4 0.8 collective-permute-start.7
  120.3 1.1 collective-permute-start.8
  121.4 2.5 %collective-permute-start.9 = (f32[16,4096]{1,0:T(8,128)S(1)}, f32[16,4096]{1,0:T(8,128)S(1)}, u32[]{:S(2)}, u32[]{:S(2)}) collective-permute-start(f32[16,4096]{1,0:T(8,128)S(1)} %get-tuple-element.24), channel_id=1, source_target_pairs={{0,24},{8,16},{16,8},{24,0},{1,25},{9,17},{17,9},{25,1},{2,26},{10... | collective-permute-start | bytes 786440 | tf_op jit(solution)/shard_map/ppermute | solution.py:187
  123.9 8.0 %collective-permute-done.7 = f32[16,4096]{1,0:T(8,128)S(1)} collective-permute-done((f32[16,4096]{1,0:T(8,128)S(1)}, f32[16,4096]{1,0:T(8,128)S(1)}, u32[]{:S(2)}, u32[]{:S(2)}) %collective-permute-start.7) | collective-permute-done | bytes 262176 | tf_op jit(solution)/shard_map/ppermute | solution.py:187
  131.9 9.7 %collective-permute-done.8 = f32[16,4096]{1,0:T(8,128)S(1)} collective-permute-done((f32[16,4096]{1,0:T(8,128)S(1)}, f32[16,4096]{1,0:T(8,128)S(1)}, u32[]{:S(2)}, u32[]{:S(2)}) %collective-permute-start.8) | collective-permute-done | bytes 262176 | tf_op jit(solution)/shard_map/ppermute | solution.py:187
  141.6 1.0 copy-done.8
  (31 shorter events, 1.8 us)
Async XLA Ops:
  0.0 37.8 %copy-start = (f32[1,128,512]{2,1,0:T(8,128)S(1)}, f32[1,128,512]{2,1,0:T(8,128)}, u32[]{:S(2)}) copy-start(f32[1,128,512]{2,1,0:T(8,128)} %param.7) | copy-start | bytes 786436
  0.0 28.8 %copy-start.1 = (f32[64,4096]{1,0:T(8,128)S(1)}, f32[64,4096]{1,0:T(8,128)}, u32[]{:S(2)}) copy-start(f32[64,4096]{1,0:T(8,128)} %param.6) | copy-start | bytes 3145732
  0.0 28.8 %copy-start.2 = (bf16[512,512]{1,0:T(8,128)(2,1)S(1)}, bf16[512,512]{1,0:T(8,128)(2,1)}, u32[]{:S(2)}) copy-start(bf16[512,512]{1,0:T(8,128)(2,1)} %constant.54.clone.refs_7_) | copy-start | bytes 1572868
  0.0 28.8 %copy-start.5 = (f32[32,256]{1,0:T(8,128)S(1)}, f32[32,256]{1,0:T(8,128)}, u32[]{:S(2)}) copy-start(f32[32,256]{1,0:T(8,128)} %constant.52.clone.refs_5_) | copy-start | bytes 98308
  1.3 12.4 %collective-permute-start.2 = (f32[16,4096]{1,0:T(8,128)S(1)}, f32[16,4096]{1,0:T(8,128)S(1)}, u32[]{:S(2)}, u32[]{:S(2)}) collective-permute-start(f32[16,4096]{1,0:T(8,128)S(1)} %get-tuple-element.25), channel_id=1, source_target_pairs={{0,24},{8,16},{16,8},{24,0},{1,25},{9,17},{17,9},{25,1},{2,26},{10... | collective-permute-start | bytes 786440 | tf_op jit(solution)/shard_map/ppermute | solution.py:187
  6.4 22.3 %collective-permute-start.1 = (f32[16,4096]{1,0:T(8,128)S(1)}, f32[16,4096]{1,0:T(8,128)S(1)}, u32[]{:S(2)}, u32[]{:S(2)}) collective-permute-start(f32[16,4096]{1,0:T(8,128)S(1)} %get-tuple-element.26), channel_id=1, source_target_pairs={{0,16},{8,24},{16,0},{24,8},{1,17},{9,25},{17,1},{25,9},{2,18},{10... | collective-permute-start | bytes 786440 | tf_op jit(solution)/shard_map/ppermute | solution.py:187
  6.4 22.3 %collective-permute-start = (f32[16,4096]{1,0:T(8,128)S(1)}, f32[16,4096]{1,0:T(8,128)S(1)}, u32[]{:S(2)}, u32[]{:S(2)}) collective-permute-start(f32[16,4096]{1,0:T(8,128)S(1)} %get-tuple-element.27), channel_id=1, source_target_pairs={{0,8},{8,0},{16,24},{24,16},{1,9},{9,1},{17,25},{25,17},{2,10},{10... | collective-permute-start | bytes 786440 | tf_op jit(solution)/shard_map/ppermute | solution.py:187
  28.8 1.0 copy-start.3
  29.8 0.8 copy-start.6
  33.0 52.0 %all-to-all-start = ((f32[32,64,128]{2,1,0:T(8,128)}), f32[32,64,128]{2,1,0:T(8,128)S(1)}, u32[]{:S(2)}, u32[]{:S(2)}) async-start(f32[32,64,128]{2,1,0:T(8,128)} %bitcast.4), calls=%async_computation | async-start | bytes 2097152 | tf_op jit(solution)/shard_map/all_to_all | solution.py:229
  37.8 0.7 collective-permute-start.3
  38.5 26.4 %collective-permute-start.4 = (f32[1,64,512]{2,1,0:T(8,128)S(1)}, f32[1,64,512]{2,1,0:T(8,128)S(1)}, u32[]{:S(2)}, u32[]{:S(2)}) collective-permute-start(f32[1,64,512]{2,1,0:T(8,128)S(1)} %bitcast.27), channel_id=1, source_target_pairs={{0,2},{1,3},{2,0},{3,1},{4,6},{5,7},{6,4},{7,5},{8,10},{9,11},{10,... | collective-permute-start | bytes 393224 | tf_op jit(solution)/shard_map/ppermute | solution.py:187
  64.9 17.9 %collective-permute-start.5 = (f32[2,64,512]{2,1,0:T(8,128)S(1)}, f32[2,64,512]{2,1,0:T(8,128)S(1)}, u32[]{:S(2)}, u32[]{:S(2)}) collective-permute-start(f32[2,64,512]{2,1,0:T(8,128)S(1)} %pad_maximum_fusion.2), channel_id=1, source_target_pairs={{0,4},{1,5},{2,6},{3,7},{4,0},{5,1},{6,2},{7,3},{8,12},{9,13},{10,... | collective-permute-start | bytes 786440 | tf_op jit(solution)/shard_map/ppermute | solution.py:187
  82.8 2.0 %collective-permute-start.6 = (f32[4,64,512]{2,1,0:T(8,128)S(1)}, f32[4,64,512]{2,1,0:T(8,128)S(1)}, u32[]{:S(2)}, u32[]{:S(2)}) collective-permute-start(f32[4,64,512]{2,1,0:T(8,128)S(1)} %pad_maximum_fusion.1), channel_id=1, source_target_pairs={{0,1},{1,0},{2,3},{3,2},{4,5},{5,4},{6,7},{7,6},{8,9},{9,8},{10,11... | collective-permute-start | bytes 1572872 | tf_op jit(solution)/shard_map/ppermute | solution.py:187
  86.8 30.0 %all-to-all-start.1 = ((f32[32,64,128]{2,1,0:T(8,128)}), f32[32,64,128]{2,1,0:T(8,128)S(1)}, u32[]{:S(2)}, u32[]{:S(2)}) async-start(f32[32,64,128]{2,1,0:T(8,128)} %bitcast.8), calls=%async_computation.1 | async-start | bytes 2097152 | tf_op jit(solution)/shard_map/all_to_all | solution.py:238
  116.8 1.0 copy-start.4
  116.8 1.0 copy-start.7
  119.4 12.5 %collective-permute-start.7 = (f32[16,4096]{1,0:T(8,128)S(1)}, f32[16,4096]{1,0:T(8,128)S(1)}, u32[]{:S(2)}, u32[]{:S(2)}) collective-permute-start(f32[16,4096]{1,0:T(8,128)S(1)} %get-tuple-element.20), channel_id=1, source_target_pairs={{0,8},{8,0},{16,24},{24,16},{1,9},{9,1},{17,25},{25,17},{2,10},{10... | collective-permute-start | bytes 786440 | tf_op jit(solution)/shard_map/ppermute | solution.py:187
  120.3 21.3 %collective-permute-start.8 = (f32[16,4096]{1,0:T(8,128)S(1)}, f32[16,4096]{1,0:T(8,128)S(1)}, u32[]{:S(2)}, u32[]{:S(2)}) collective-permute-start(f32[16,4096]{1,0:T(8,128)S(1)} %get-tuple-element.22), channel_id=1, source_target_pairs={{0,16},{8,24},{16,0},{24,8},{1,17},{9,25},{17,1},{25,9},{2,18},{10... | collective-permute-start | bytes 786440 | tf_op jit(solution)/shard_map/ppermute | solution.py:187
  121.4 20.2 %collective-permute-start.9 = (f32[16,4096]{1,0:T(8,128)S(1)}, f32[16,4096]{1,0:T(8,128)S(1)}, u32[]{:S(2)}, u32[]{:S(2)}) collective-permute-start(f32[16,4096]{1,0:T(8,128)S(1)} %get-tuple-element.24), channel_id=1, source_target_pairs={{0,24},{8,16},{16,8},{24,0},{1,25},{9,17},{17,9},{25,1},{2,26},{10... | collective-permute-start | bytes 786440 | tf_op jit(solution)/shard_map/ppermute | solution.py:187
  141.6 1.0 copy-start.8

commit v3 on v2

v3 whole, which is shorter than its diff:
```python
import math

import jax
import jax.numpy as jnp
import ml_dtypes
import numpy as np
from jax import lax
from jax.experimental import pallas as pl
from jax.experimental.pallas import tpu as pltpu
from jax.sharding import PartitionSpec as P


LANES = 128
VMEM_LIMIT = 48 * 1024 * 1024
CHUNKS = 1


def fourier_matrix(n2, planes):
    share = n2 // (2 * planes)
    order = []
    for plane in range(planes):
        low = np.arange(plane * share, (plane + 1) * share)
        order.append(np.concatenate([low, n2 - 1 - low[::-1]]))
    order = np.stack(order)
    angle = 2.0 * np.pi / n2 * (np.arange(n2)[:, None, None] * order[None] % n2)
    cosine, sine = np.cos(angle), np.sin(angle)
    matrix = np.stack([np.stack([cosine, -sine], 2), np.stack([sine, cosine], 2)])
    matrix = matrix.reshape(2 * n2, 2 * n2).astype(np.float32)
    high = matrix.astype(ml_dtypes.bfloat16)
    low = (matrix - high.astype(np.float32)).astype(ml_dtypes.bfloat16)
    return high, low


def twiddles(n1, n2):
    angle = 2.0 * np.pi / (n1 * n2) * (np.arange(n1)[:, None] + 0.25) * np.arange(n2)[None, :]
    return np.stack([np.cos(angle), np.sin(angle)]).astype(np.float32)


def forward_butterflies(parts, shift):
    count = len(parts)
    if count == 1:
        return parts
    half = count // 2
    turn_re, turn_im = math.cos(math.pi * shift), -math.sin(math.pi * shift)
    even, odd = [], []
    for (a_re, a_im), (b_re, b_im) in zip(parts[:half], parts[half:]):
        c_re = b_re * turn_re - b_im * turn_im
        c_im = b_re * turn_im + b_im * turn_re
        even.append((a_re + c_re, a_im + c_im))
        odd.append((a_re - c_re, a_im - c_im))
    even = forward_butterflies(even, shift / 2)
    odd = forward_butterflies(odd, (1 + shift) / 2)
    return [part for pair in zip(even, odd) for part in pair]


def inverse_butterflies(parts, shift):
    if len(parts) == 1:
        return parts
    turn_re, turn_im = math.cos(math.pi * shift), math.sin(math.pi * shift)
    even = inverse_butterflies(parts[0::2], shift / 2)
    odd = inverse_butterflies(parts[1::2], (1 + shift) / 2)
    first, second = [], []
    for (a_re, a_im), (b_re, b_im) in zip(even, odd):
        d_re, d_im = a_re - b_re, a_im - b_im
        first.append((a_re + b_re, a_im + b_im))
        second.append((d_re * turn_re - d_im * turn_im, d_re * turn_im + d_im * turn_re))
    return first + second


def split(value):
    high = value.astype(jnp.bfloat16)
    return high, (value - high.astype(jnp.float32)).astype(jnp.bfloat16)


def product(left, right, contract=((1,), (0,))):
    def dot(a, b):
        return lax.dot_general(a, b, (contract, ((), ())), preferred_element_type=jnp.float32)

    return dot(left[0], right[0]) + (dot(left[0], right[1]) + dot(left[1], right[0]))


def tiles(rows, lanes):
    step = min(8, rows)
    for row in range(0, rows, step):
        for lane in range(0, lanes, LANES):
            yield slice(row, row + step), lane


def slice_kernel(chunk, noise_ref, *refs):
    here = lax.axis_index("tm")
    outs, sem = refs[:-1], refs[-1]
    copies = [
        pltpu.make_async_copy(noise_ref.at[here ^ step, chunk], out, sem.at[step]) for step, out in enumerate(outs)
    ]
    for copy in copies:
        copy.start()
    for copy in copies:
        copy.wait()


def hold_kernel(*refs):
    count = len(refs) // 2
    sem = refs[-1]
    copies = [pltpu.make_async_copy(refs[at], refs[count + at], sem.at[at]) for at in range(count)]
    for copy in copies:
        copy.start()
    for copy in copies:
        copy.wait()


def forward_kernel(n1, n2, chunk, planes, *refs):
    here = lax.axis_index("tm")
    blocks, (turn_ref, high_ref, low_ref) = refs[:planes], refs[planes : planes + 3]
    out_ref, x_ref, mid_ref, stage_ref, sem = refs[-5:]
    _, dets, span = x_ref.shape
    _, groups, pieces, _, width = stage_ref.shape
    per = span // n2
    for step, block in enumerate(blocks):
        x_ref[here ^ step] = block[...]
    for rows, lane in tiles(dets, n2):

        def load(index):
            start = (index % per) * n2 + lane
            return x_ref[index // per, rows, start : start + LANES]

        parts = [(load(t1), -load(t1 + n1)) for t1 in range(n1)]
        for k1, (re, im) in enumerate(forward_butterflies(parts, 0.25)):
            cosine = turn_ref[0, k1 : k1 + 1, lane : lane + LANES]
            sine = turn_ref[1, k1 : k1 + 1, lane : lane + LANES]
            place = slice(k1 * dets + rows.start, k1 * dets + rows.stop)
            mid_ref[place, lane : lane + LANES] = re * cosine + im * sine
            mid_ref[place, n2 + lane : n2 + lane + LANES] = im * cosine - re * sine
    copies = []
    share = groups // 2
    for part in range(2):
        count = share * pieces * dets
        spectrum = product(split(mid_ref[part * count : (part + 1) * count]), (high_ref[...], low_ref[...]))
        these = pl.ds(part * share, share)
        for plane in range(planes):
            value = spectrum[:, plane * width : (plane + 1) * width]
            stage_ref[plane, these] = value.reshape(share, pieces, dets, width)
        copies.append(pltpu.make_async_copy(stage_ref.at[:, these], out_ref.at[:, these, chunk], sem.at[part]))
        copies[-1].start()
    for copy in copies:
        copy.wait()


def inverse_kernel(n1, n2, chunk, y_ref, turn_ref, high_ref, low_ref, *refs):
    here = lax.axis_index("tm")
    outs, (x_ref, mid_ref) = refs[:-2], refs[-2:]
    _, dets, span = x_ref.shape
    planes, _, _, _, _, width = y_ref.shape
    per = span // n2
    scale = 1.0 / (n1 * n2)
    bins = jnp.concatenate([y_ref[plane, :, chunk].reshape(n1 * dets, width) for plane in range(planes)], axis=1)
    mid_ref[...] = product(split(bins), (high_ref[...], low_ref[...]), ((1,), (1,)))
    for rows, lane in tiles(dets, n2):
        parts = []
        for k1 in range(n1):
            cosine = turn_ref[0, k1 : k1 + 1, lane : lane + LANES] * scale
            sine = turn_ref[1, k1 : k1 + 1, lane : lane + LANES] * scale
            place = slice(k1 * dets + rows.start, k1 * dets + rows.stop)
            re = mid_ref[place, lane : lane + LANES]
            im = mid_ref[place, n2 + lane : n2 + lane + LANES]
            parts.append((re * cosine - im * sine, im * cosine + re * sine))
        for t1, (re, im) in enumerate(inverse_butterflies(parts, 0.25)):
            for index, value in ((t1, re), (t1 + n1, -im)):
                start = (index % per) * n2 + lane
                x_ref[index // per, rows, start : start + LANES] = value
    for step, out in enumerate(outs):
        out[...] = x_ref[here ^ step]


def place_kernel(chunk, *refs):
    here = lax.axis_index("tm")
    out_ref, sem = refs[-2:]
    copies = [
        pltpu.make_async_copy(refs[step], out_ref.at[here ^ step, chunk], sem.at[step])
        for step in range(out_ref.shape[0])
    ]
    for copy in copies:
        copy.start()
    for copy in copies:
        copy.wait()


def factor_kernel(masks, factor_ref, high_ref, low_ref):
    here = lax.axis_index("det")
    shares, rows, _ = factor_ref.shape
    for share in range(shares):
        source = here
        for bit, mask in enumerate(masks):
            source = source ^ (mask if share >> bit & 1 else 0)
        place = pl.ds(pl.multiple_of(source * rows, rows), rows)
        high_ref[place], low_ref[place] = split(factor_ref[share])


def mix_kernel(x_ref, f_high, f_low, out_ref, x_mid, stage_ref, sem):
    planes, groups, chunks, pieces, dets, width = x_ref.shape

    def rows_of(group, plane, chunk):
        start = ((group * planes + plane) * chunks + chunk) * dets
        return slice(start, start + dets)

    places = [
        (plane, group, chunk, piece)
        for group in range(groups) for plane in range(planes) for chunk in range(chunks) for piece in range(pieces)
    ]
    for plane, group, chunk, piece in places:
        x_mid[rows_of(group, plane, chunk), piece * width : (piece + 1) * width] = x_ref[plane, group, chunk, piece]
    x_high, x_low = split(x_mid[...])
    steps = 4
    count, share = f_high.shape[0] // steps, groups // steps
    copies = []
    for step in range(steps):
        rows, reach = slice(step * count, (step + 1) * count), (step + 1) * count
        value = product((f_high[rows, :reach], f_low[rows, :reach]), (x_high[:reach], x_low[:reach]))
        for plane, group, chunk, piece in places:
            if group // share == step:
                own = rows_of(group - step * share, plane, chunk)
                stage_ref[plane, group, chunk, piece] = value[own, piece * width : (piece + 1) * width]
        these = pl.ds(step * share, share)
        copies.append(pltpu.make_async_copy(stage_ref.at[:, these], out_ref.at[:, these], sem.at[step]))
        copies[-1].start()
    for copy in copies:
        copy.wait()


def call(kernel, outs, scratch, flops, *args, spaces=None, out_space=pltpu.VMEM, aliases=None):
    spaces = spaces or [pltpu.VMEM] * len(args)
    count = sum(math.prod(arg.shape) * arg.dtype.itemsize for arg in (*args, *outs))
    return pl.pallas_call(
        kernel,
        out_shape=outs,
        in_specs=[pl.BlockSpec(memory_space=space) for space in spaces],
        out_specs=[pl.BlockSpec(memory_space=out_space)] * len(outs),
        scratch_shapes=[pltpu.VMEM(item, jnp.float32) if isinstance(item, tuple) else item for item in scratch],
        compiler_params=pltpu.CompilerParams(vmem_limit_bytes=VMEM_LIMIT),
        cost_estimate=pl.CostEstimate(flops=flops, bytes_accessed=count, transcendentals=0),
        input_output_aliases=aliases or {},
    )(*args)


def array(*shape, dtype=jnp.float32):
    return jax.ShapeDtypeStruct(shape, dtype)


def dma(count):
    return pltpu.SemaphoreType.DMA((count,))


def swap(value, axis, mask):
    return lax.ppermute(value, axis, [(place, place ^ mask) for place in range(lax.axis_size(axis))])


def band_factor(factor, planes, groups):
    half = factor.shape[1] // 2
    upper = lax.axis_index("det") >= groups // 2
    mine = lax.dynamic_slice_in_dim(factor[0], jnp.where(upper, half, 0), half, 0)
    pairs = []
    for plane in range(planes):
        for group in range(groups):
            target = min(group, groups - 1 - group)
            pairs.append((plane * groups + group, target * groups + 2 * plane + (group >= groups // 2)))
    share = lax.ppermute(mine, ("tm", "det"), pairs)[None]
    masks = [2**bit for bit in range(1, groups.bit_length() - 1)] + [1]
    for mask in masks:
        share = jnp.concatenate([share, swap(share, "det", mask)])
    whole = array(groups * half, factor.shape[2], dtype=jnp.bfloat16)
    return call(lambda *refs: factor_kernel(masks, *refs), [whole, whole], [], 0, share)


def bind(kernel, *static):
    return lambda *refs: kernel(*static, *refs)


def local(noise, factor):
    planes = lax.axis_size("tm")
    groups = lax.axis_size("det")
    rows, span = noise.shape
    n2 = LANES // 2 * planes
    n1 = span * planes // 2 // n2
    pieces = n1 // groups
    chunks = CHUNKS if rows // planes % (8 * CHUNKS) == 0 else 1
    dets = rows // planes // chunks
    flops = 3 * 2 * n1 * dets * (2 * n2) ** 2
    block, series, middle = array(dets, span), (planes, dets, span), (n1 * dets, 2 * n2)
    layout = (planes, groups, chunks, pieces, dets, LANES)
    tables = (twiddles(n1, n2), *fourier_matrix(n2, planes))

    noise = noise.reshape(planes, chunks, dets, span)
    arrived = []
    for chunk in range(chunks):
        parts = call(bind(slice_kernel, chunk), [block] * planes, [dma(planes)], 0, noise, spaces=[pl.ANY])
        arrived.append([swap(part, "tm", step) if step else part for step, part in enumerate(parts)])
    f_high, f_low = band_factor(factor, planes, groups)
    tables = call(
        hold_kernel, [array(*table.shape, dtype=table.dtype) for table in tables], [dma(len(tables))], 0, *tables,
        spaces=[pl.ANY] * len(tables),
    )
    arrived, f_high, f_low = lax.optimization_barrier((arrived, f_high, f_low))
    buffer = []
    for chunk in range(chunks):
        buffer = call(
            bind(forward_kernel, n1, n2, chunk, planes), [array(*layout)],
            [series, middle, (planes, groups, pieces, dets, LANES), dma(2)], flops,
            *arrived[chunk], *tables, *buffer,
            spaces=[pltpu.VMEM] * (planes + len(tables)) + [pl.ANY] * len(buffer),
            out_space=pl.ANY, aliases={planes + len(tables): 0} if buffer else None,
        )

    def exchange(value):
        value = value.reshape(planes * groups, chunks * pieces * dets, LANES)
        return lax.all_to_all(value, ("tm", "det"), split_axis=0, concat_axis=0, tiled=True).reshape(layout)

    count = f_high.shape[0]
    (mixed,) = call(
        mix_kernel, [array(*layout)], [(count, pieces * LANES), layout, dma(4)],
        2 * 3 * count * count * pieces * LANES,
        exchange(buffer[0]), f_high, f_low, out_space=pl.ANY,
    )
    back = exchange(mixed)
    result = []
    for chunk in range(chunks):
        parts = call(
            bind(inverse_kernel, n1, n2, chunk), [block] * planes, [series, middle], flops, back, *tables
        )
        parts = [swap(part, "tm", step) if step else part for step, part in enumerate(parts)]
        result = call(
            bind(place_kernel, chunk), [array(planes, chunks, dets, span)], [dma(planes)], 0, *parts, *result,
            spaces=[pl.ANY] * (planes + len(result)), out_space=pl.ANY, aliases={planes: 0} if result else None,
        )
    return result[0].reshape(rows, span)


def solution(mesh):
    in_specs = (P("det", "tm"), P("det", "tm", None))
    return jax.shard_map(local, mesh=mesh, in_specs=in_specs, out_specs=P("det", "tm"), check_vma=False)
```

time: 145 us -> 144 us (level)
  blocking collectives: 0 us -> 63.8 us
  waiting for transfers between devices: 78.4 us -> 43.9 us
  starting transfers between devices: 52.8 us -> 26.8 us
  local copies, waits for them, and re-layouts: 5.19 us -> 0.98 us
  Pallas kernels: 4.37 us -> 6.38 us
  other arithmetic: 1.67 us -> 0.12 us
    all_to_all x0 -> x2, blocking collectives: none -> 63.8 us  [exchange(): lax.all_to_all(value, ('tm', 'det'), split_axis=0, concat_axis=0, tiled=T...]
    all_to_all x2 -> x0, waiting for transfers between devices: 26.2 us -> none  [the longest x1 26.2 us: local(): lax.all_to_all(mixed.reshape(planes * groups, pieces * dets, LANES), ('tm...]
    ppermute x9, starting transfers between devices: 43.6 us -> 26.2 us  [swap(): lax.ppermute(value, axis, [(place, place ^ mask) for place in range(lax.a...]
    all_to_all x2 -> x0, starting transfers between devices: 8.51 us -> none  [the longest x1 4.72 us: local(): lax.all_to_all(spectrum.reshape(planes * groups, pieces * dets, LANES), (...]
    ppermute x9, waiting for transfers between devices: 52.1 us -> 43.9 us  [swap(): lax.ppermute(value, axis, [(place, place ^ mask) for place in range(lax.a...]
    unnamed x18 -> x10, local copies, waits for them, and re-layouts: 3.75 us -> 0.97 us
    pallas_call x3 -> x7, Pallas kernels: 4.37 us -> 6.38 us  [call(): pl.pallas_call(kernel, out_shape=outs, in_specs=[pl.BlockSpec(memory_spac...]
    pallas_call x1 -> x0, other arithmetic: 1.55 us -> none  [call(): pl.pallas_call(kernel, out_shape=outs, in_specs=[whole] * len(args), out_...]
  transfers between devices with their start and end apart: 12 -> 10, of which waited for: 8 -> 6; matrix products, arithmetic and copies ran while one was open for 0% -> 0% of each run, Pallas kernels for 0% -> 0%
where the time goes in v3:
time: 144 us; the launch traced here: 142 us
  blocking collectives  63.8 us (44%)
  waiting for transfers between devices  43.9 us (30%)
  starting transfers between devices  26.8 us (19%)
  Pallas kernels  6.38 us (4%)
    all_to_all x2, blocking collectives, exchange(): lax.all_to_all(value, ('tm', 'det'), split_axis=0, concat_axis=0, tiled=T...  63.8 us
    ppermute x9, waiting for transfers between devices, swap(): lax.ppermute(value, axis, [(place, place ^ mask) for place in range(lax.a...  43.9 us
    ppermute x9, starting transfers between devices, swap(): lax.ppermute(value, axis, [(place, place ^ mask) for place in range(lax.a...  26.2 us
    pallas_call x7, Pallas kernels, call(): pl.pallas_call(kernel, out_shape=outs, in_specs=[pl.BlockSpec(memory_spac...  6.38 us
  transfers between devices with their start and end apart: 10, of which 6 were waited for; matrix products, arithmetic and copies ran while one was open for 0% of the time, Pallas kernels for 0%

profile of v3, /device:TPU:0, one launch (start us, length us, event | category | flops | bytes accessed | tf_op | source)
XLA Modules:
  0.0 142.1 jit_solution(11161299884066268399)
XLA Ops:
  0.0 0.9 copy-done
  1.0 0.7 collective-permute-start.3
  1.7 10.6 %collective-permute-start.4 = (f32[1,64,512]{2,1,0:T(8,128)S(1)}, f32[1,64,512]{2,1,0:T(8,128)S(1)}, u32[]{:S(2)}, u32[]{:S(2)}) collective-permute-start(f32[1,64,512]{2,1,0:T(8,128)S(1)} %bitcast.14), channel_id=1, source_target_pairs={{0,2},{1,3},{2,0},{3,1},{4,6},{5,7},{6,4},{7,5},{8,10},{9,11},{10,... | collective-permute-start | bytes 393224 | tf_op jit(solution)/shard_map/ppermute | solution.py:253
  12.2 3.9 %collective-permute-done.4 = f32[1,64,512]{2,1,0:T(8,128)S(1)} collective-permute-done((f32[1,64,512]{2,1,0:T(8,128)S(1)}, f32[1,64,512]{2,1,0:T(8,128)S(1)}, u32[]{:S(2)}, u32[]{:S(2)}) %collective-permute-start.4) | collective-permute-done | bytes 131104 | tf_op jit(solution)/shard_map/ppermute | solution.py:253
  16.2 5.2 %collective-permute-start.5 = (f32[2,64,512]{2,1,0:T(8,128)S(1)}, f32[2,64,512]{2,1,0:T(8,128)S(1)}, u32[]{:S(2)}, u32[]{:S(2)}) collective-permute-start(f32[2,64,512]{2,1,0:T(8,128)S(1)} %pad_maximum_fusion.2), channel_id=1, source_target_pairs={{0,4},{1,5},{2,6},{3,7},{4,0},{5,1},{6,2},{7,3},{8,12},{9,13},{10,... | collective-permute-start | bytes 786440 | tf_op jit(solution)/shard_map/ppermute | solution.py:253
  21.4 4.4 %collective-permute-done.5 = f32[2,64,512]{2,1,0:T(8,128)S(1)} collective-permute-done((f32[2,64,512]{2,1,0:T(8,128)S(1)}, f32[2,64,512]{2,1,0:T(8,128)S(1)}, u32[]{:S(2)}, u32[]{:S(2)}) %collective-permute-start.5) | collective-permute-done | bytes 262176 | tf_op jit(solution)/shard_map/ppermute | solution.py:253
  25.9 0.1 shard_map.55
  26.0 1.9 %collective-permute-start = (f32[16,4096]{1,0:T(8,128)S(1)}, f32[16,4096]{1,0:T(8,128)S(1)}, u32[]{:S(2)}, u32[]{:S(2)}) collective-permute-start(f32[16,4096]{1,0:T(8,128)S(1)} %get-tuple-element.25), channel_id=1, source_target_pairs={{0,8},{8,0},{16,24},{24,16},{1,9},{9,1},{17,25},{25,17},{2,10},{10... | collective-permute-start | bytes 786440 | tf_op jit(solution)/shard_map/ppermute | solution.py:253
  28.0 3.9 %collective-permute-start.1 = (f32[16,4096]{1,0:T(8,128)S(1)}, f32[16,4096]{1,0:T(8,128)S(1)}, u32[]{:S(2)}, u32[]{:S(2)}) collective-permute-start(f32[16,4096]{1,0:T(8,128)S(1)} %get-tuple-element.26), channel_id=1, source_target_pairs={{0,16},{8,24},{16,0},{24,8},{1,17},{9,25},{17,1},{25,9},{2,18},{10... | collective-permute-start | bytes 786440 | tf_op jit(solution)/shard_map/ppermute | solution.py:253
  31.9 0.2 shard_map.57
  32.2 0.1 shard_map.56
  32.3 7.9 %collective-permute-done.refs_1_ = f32[16,4096]{1,0:T(8,128)S(1)} collective-permute-done((f32[16,4096]{1,0:T(8,128)S(1)}, f32[16,4096]{1,0:T(8,128)S(1)}, u32[]{:S(2)}, u32[]{:S(2)}) %collective-permute-start) | collective-permute-done | bytes 262176 | tf_op jit(solution)/shard_map/ppermute | solution.py:253
  40.2 10.0 %collective-permute-done.1.refs_2_ = f32[16,4096]{1,0:T(8,128)S(1)} collective-permute-done((f32[16,4096]{1,0:T(8,128)S(1)}, f32[16,4096]{1,0:T(8,128)S(1)}, u32[]{:S(2)}, u32[]{:S(2)}) %collective-permute-start.1) | collective-permute-done | bytes 262176 | tf_op jit(solution)/shard_map/ppermute | solution.py:253
  50.3 1.8 %shard_map.58 = f32[4,8,1,4,16,128]{5,4,3,2,1,0:T(8,128)S(1)} custom-call(f32[16,4096]{1,0:T(8,128)S(1)} %get-tuple-element.30.refs_0_, f32[16,4096]{1,0:T(8,128)S(1)} %collective-permute-done.refs_1_, f32[16,4096]{1,0:T(8,128)S(1)} %collective-permute-done.1.refs_2_, f32[16,4096]{1,0:T(8,128)S(1)} %collective-permute-done.2.refs_3_, ...), custom_call_target="tpu_custom_call" | custom-call | flops 805306368 | bytes 3211264 | tf_op jit(solution)/shard_map/pallas_call | solution.py:232
  52.1 34.1 %all_to_all.10 = f32[32,64,128]{2,1,0:T(8,128)S(1)} all-to-all(f32[32,64,128]{2,1,0:T(8,128)S(1)} %bitcast.9), channel_id=1, replica_groups=mesh['tm'=4,'det'=8] {'tm','det'}, dimensions={0} | all-to-all | bytes 2097152 | tf_op jit(solution)/shard_map/all_to_all | solution.py:314
  86.2 1.6 %shard_map.59 = f32[4,8,1,4,16,128]{5,4,3,2,1,0:T(8,128)S(1)} custom-call(f32[4,8,1,4,16,128]{5,4,3,2,1,0:T(8,128)S(1)} %bitcast.10, bf16[512,512]{1,0:T(8,128)(2,1)S(1)} %get-tuple-element.37.f_high, bf16[512,512]{1,0:T(8,128)(2,1)S(1)} %get-tuple-element.38.f_low), custom_call_target="tpu_custom_call" | custom-call | flops 805306368 | bytes 3145728 | tf_op jit(solution)/shard_map/pallas_call | solution.py:232
  87.8 29.7 %all_to_all.11 = f32[32,64,128]{2,1,0:T(8,128)S(1)} all-to-all(f32[32,64,128]{2,1,0:T(8,128)S(1)} %bitcast.11), channel_id=1, replica_groups=mesh['tm'=4,'det'=8] {'tm','det'}, dimensions={0} | all-to-all | bytes 2097152 | tf_op jit(solution)/shard_map/all_to_all | solution.py:314
  117.4 1.5 %shard_map.60 = (f32[16,4096]{1,0:T(8,128)S(1)}, f32[16,4096]{1,0:T(8,128)S(1)}, f32[16,4096]{1,0:T(8,128)S(1)}, f32[16,4096]{1,0:T(8,128)S(1)}) custom-call(f32[4,8,1,4,16,128]{5,4,3,2,1,0:T(8,128)S(1)} %bitcast.13, f32[2,32,256]{2,1,0:T(8,128)S(1)} %get-tuple-element.34.refs_4_.refs_1_, bf16[512,512]{1,0:T(8,128)(2,1)S(1)} %get-tuple-element.35.refs_5_.refs_2_, ...), custom_call_target="tpu_custom_call" | custom-call | flops 805306368 | bytes 3211264 | tf_op jit(solution)/shard_map/pallas_call | solution.py:232
  119.0 0.8 collective-permute-start.7
  119.8 1.1 collective-permute-start.8
  120.9 2.5 %collective-permute-start.9 = (f32[16,4096]{1,0:T(8,128)S(1)}, f32[16,4096]{1,0:T(8,128)S(1)}, u32[]{:S(2)}, u32[]{:S(2)}) collective-permute-start(f32[16,4096]{1,0:T(8,128)S(1)} %get-tuple-element.42), channel_id=1, source_target_pairs={{0,24},{8,16},{16,8},{24,0},{1,25},{9,17},{17,9},{25,1},{2,26},{10... | collective-permute-start | bytes 786440 | tf_op jit(solution)/shard_map/ppermute | solution.py:253
  123.4 8.0 %collective-permute-done.7.refs_1_ = f32[16,4096]{1,0:T(8,128)S(1)} collective-permute-done((f32[16,4096]{1,0:T(8,128)S(1)}, f32[16,4096]{1,0:T(8,128)S(1)}, u32[]{:S(2)}, u32[]{:S(2)}) %collective-permute-start.7) | collective-permute-done | bytes 262176 | tf_op jit(solution)/shard_map/ppermute | solution.py:253
  131.4 9.7 %collective-permute-done.8.refs_2_ = f32[16,4096]{1,0:T(8,128)S(1)} collective-permute-done((f32[16,4096]{1,0:T(8,128)S(1)}, f32[16,4096]{1,0:T(8,128)S(1)}, u32[]{:S(2)}, u32[]{:S(2)}) %collective-permute-start.8) | collective-permute-done | bytes 262176 | tf_op jit(solution)/shard_map/ppermute | solution.py:253
  141.1 1.0 shard_map.61
  (19 shorter events, 0.2 us)
Async XLA Ops:
  0.0 1.0 copy-start
  0.0 25.9 %copy-start.1 = (f32[64,4096]{1,0:T(8,128)S(1)}, f32[64,4096]{1,0:T(8,128)}, u32[]{:S(2)}) copy-start(f32[64,4096]{1,0:T(8,128)} %param.5) | copy-start | bytes 3145732
  1.0 0.7 collective-permute-start.3
  1.7 14.5 %collective-permute-start.4 = (f32[1,64,512]{2,1,0:T(8,128)S(1)}, f32[1,64,512]{2,1,0:T(8,128)S(1)}, u32[]{:S(2)}, u32[]{:S(2)}) collective-permute-start(f32[1,64,512]{2,1,0:T(8,128)S(1)} %bitcast.14), channel_id=1, source_target_pairs={{0,2},{1,3},{2,0},{3,1},{4,6},{5,7},{6,4},{7,5},{8,10},{9,11},{10,... | collective-permute-start | bytes 393224 | tf_op jit(solution)/shard_map/ppermute | solution.py:253
  16.2 9.6 %collective-permute-start.5 = (f32[2,64,512]{2,1,0:T(8,128)S(1)}, f32[2,64,512]{2,1,0:T(8,128)S(1)}, u32[]{:S(2)}, u32[]{:S(2)}) collective-permute-start(f32[2,64,512]{2,1,0:T(8,128)S(1)} %pad_maximum_fusion.2), channel_id=1, source_target_pairs={{0,4},{1,5},{2,6},{3,7},{4,0},{5,1},{6,2},{7,3},{8,12},{9,13},{10,... | collective-permute-start | bytes 786440 | tf_op jit(solution)/shard_map/ppermute | solution.py:253
  25.8 6.1 %copy-start.4 = (f32[2,32,256]{2,1,0:T(8,128)S(1)}, f32[2,32,256]{2,1,0:T(8,128)}, u32[]{:S(2)}) copy-start(f32[2,32,256]{2,1,0:T(8,128)} %constant.19.clone.refs_0_) | copy-start | bytes 196612
  25.8 6.3 %collective-permute-start.6 = (f32[4,64,512]{2,1,0:T(8,128)S(1)}, f32[4,64,512]{2,1,0:T(8,128)S(1)}, u32[]{:S(2)}, u32[]{:S(2)}) collective-permute-start(f32[4,64,512]{2,1,0:T(8,128)S(1)} %pad_maximum_fusion.1), channel_id=1, source_target_pairs={{0,1},{1,0},{2,3},{3,2},{4,5},{5,4},{6,7},{7,6},{8,9},{9,8},{10,11... | collective-permute-start | bytes 1572872 | tf_op jit(solution)/shard_map/ppermute | solution.py:253
  25.9 6.0 %copy-start.2 = (bf16[512,512]{1,0:T(8,128)(2,1)S(1)}, bf16[512,512]{1,0:T(8,128)(2,1)}, u32[]{:S(2)}) copy-start(bf16[512,512]{1,0:T(8,128)(2,1)} %constant.21.clone.refs_2_) | copy-start | bytes 1572868
  25.9 6.0 %copy-start.3 = (bf16[512,512]{1,0:T(8,128)(2,1)S(1)}, bf16[512,512]{1,0:T(8,128)(2,1)}, u32[]{:S(2)}) copy-start(bf16[512,512]{1,0:T(8,128)(2,1)} %constant.20.clone.refs_1_) | copy-start | bytes 1572868
  26.0 14.2 %collective-permute-start = (f32[16,4096]{1,0:T(8,128)S(1)}, f32[16,4096]{1,0:T(8,128)S(1)}, u32[]{:S(2)}, u32[]{:S(2)}) collective-permute-start(f32[16,4096]{1,0:T(8,128)S(1)} %get-tuple-element.25), channel_id=1, source_target_pairs={{0,8},{8,0},{16,24},{24,16},{1,9},{9,1},{17,25},{25,17},{2,10},{10... | collective-permute-start | bytes 786440 | tf_op jit(solution)/shard_map/ppermute | solution.py:253
  28.0 22.3 %collective-permute-start.1 = (f32[16,4096]{1,0:T(8,128)S(1)}, f32[16,4096]{1,0:T(8,128)S(1)}, u32[]{:S(2)}, u32[]{:S(2)}) collective-permute-start(f32[16,4096]{1,0:T(8,128)S(1)} %get-tuple-element.26), channel_id=1, source_target_pairs={{0,16},{8,24},{16,0},{24,8},{1,17},{9,25},{17,1},{25,9},{2,18},{10... | collective-permute-start | bytes 786440 | tf_op jit(solution)/shard_map/ppermute | solution.py:253
  31.9 18.4 %collective-permute-start.2 = (f32[16,4096]{1,0:T(8,128)S(1)}, f32[16,4096]{1,0:T(8,128)S(1)}, u32[]{:S(2)}, u32[]{:S(2)}) collective-permute-start(f32[16,4096]{1,0:T(8,128)S(1)} %get-tuple-element.27), channel_id=1, source_target_pairs={{0,24},{8,16},{16,8},{24,0},{1,25},{9,17},{17,9},{25,1},{2,26},{10... | collective-permute-start | bytes 786440 | tf_op jit(solution)/shard_map/ppermute | solution.py:253
  119.0 12.4 %collective-permute-start.7 = (f32[16,4096]{1,0:T(8,128)S(1)}, f32[16,4096]{1,0:T(8,128)S(1)}, u32[]{:S(2)}, u32[]{:S(2)}) collective-permute-start(f32[16,4096]{1,0:T(8,128)S(1)} %get-tuple-element.40), channel_id=1, source_target_pairs={{0,8},{8,0},{16,24},{24,16},{1,9},{9,1},{17,25},{25,17},{2,10},{10... | collective-permute-start | bytes 786440 | tf_op jit(solution)/shard_map/ppermute | solution.py:253
  119.8 21.3 %collective-permute-start.8 = (f32[16,4096]{1,0:T(8,128)S(1)}, f32[16,4096]{1,0:T(8,128)S(1)}, u32[]{:S(2)}, u32[]{:S(2)}) collective-permute-start(f32[16,4096]{1,0:T(8,128)S(1)} %get-tuple-element.41), channel_id=1, source_target_pairs={{0,16},{8,24},{16,0},{24,8},{1,17},{9,25},{17,1},{25,9},{2,18},{10... | collective-permute-start | bytes 786440 | tf_op jit(solution)/shard_map/ppermute | solution.py:253
  120.9 20.2 %collective-permute-start.9 = (f32[16,4096]{1,0:T(8,128)S(1)}, f32[16,4096]{1,0:T(8,128)S(1)}, u32[]{:S(2)}, u32[]{:S(2)}) collective-permute-start(f32[16,4096]{1,0:T(8,128)S(1)} %get-tuple-element.42), channel_id=1, source_target_pairs={{0,24},{8,16},{16,8},{24,0},{1,25},{9,17},{17,9},{25,1},{2,26},{10... | collective-permute-start | bytes 786440 | tf_op jit(solution)/shard_map/ppermute | solution.py:253

commit v4 on v3

--- a/solution.py
+++ b/solution.py
@@ -253,7 +253,7 @@
     return lax.ppermute(value, axis, [(place, place ^ mask) for place in range(lax.axis_size(axis))])
 
 
-def band_factor(factor, planes, groups):
+def plane_factor(factor, planes, groups):
     half = factor.shape[1] // 2
     upper = lax.axis_index("det") >= groups // 2
     mine = lax.dynamic_slice_in_dim(factor[0], jnp.where(upper, half, 0), half, 0)
@@ -262,11 +262,16 @@
         for group in range(groups):
             target = min(group, groups - 1 - group)
             pairs.append((plane * groups + group, target * groups + 2 * plane + (group >= groups // 2)))
-    share = lax.ppermute(mine, ("tm", "det"), pairs)[None]
+    return lax.ppermute(mine, ("tm", "det"), pairs)
+
+
+def band_factor(share, groups):
+    rows, columns = share.shape
+    share = share[None]
     masks = [2**bit for bit in range(1, groups.bit_length() - 1)] + [1]
     for mask in masks:
         share = jnp.concatenate([share, swap(share, "det", mask)])
-    whole = array(groups * half, factor.shape[2], dtype=jnp.bfloat16)
+    whole = array(groups * rows, columns, dtype=jnp.bfloat16)
     return call(lambda *refs: factor_kernel(masks, *refs), [whole, whole], [], 0, share)
 
 
@@ -293,12 +298,13 @@
     for chunk in range(chunks):
         parts = call(bind(slice_kernel, chunk), [block] * planes, [dma(planes)], 0, noise, spaces=[pl.ANY])
         arrived.append([swap(part, "tm", step) if step else part for step, part in enumerate(parts)])
-    f_high, f_low = band_factor(factor, planes, groups)
+    share = plane_factor(factor, planes, groups)
     tables = call(
         hold_kernel, [array(*table.shape, dtype=table.dtype) for table in tables], [dma(len(tables))], 0, *tables,
         spaces=[pl.ANY] * len(tables),
     )
-    arrived, f_high, f_low = lax.optimization_barrier((arrived, f_high, f_low))
+    arrived, share = lax.optimization_barrier((arrived, share))
+    f_high, f_low = band_factor(share, groups)
     buffer = []
     for chunk in range(chunks):
         buffer = call(

time: 144 us -> 129 us (0.90)
  blocking collectives: 63.8 us -> 31.2 us
  waiting for transfers between devices: 43.9 us -> 60.7 us
    all_to_all x2 -> x1, blocking collectives: 63.8 us -> 31.2 us  [exchange(): lax.all_to_all(value, ('tm', 'det'), split_axis=0, concat_axis=0, tiled=T...]
    ppermute x9, waiting for transfers between devices: 43.9 us -> 60 us  [swap(): lax.ppermute(value, axis, [(place, place ^ mask) for place in range(lax.a...]
    ppermute x9, starting transfers between devices: 26.2 us -> 13.8 us  [swap(): lax.ppermute(value, axis, [(place, place ^ mask) for place in range(lax.a...]
    all_to_all x0 -> x1, starting transfers between devices: none -> 11.2 us  [exchange(): lax.all_to_all(value, ('tm', 'det'), split_axis=0, concat_axis=0, tiled=T...]
  transfers between devices with their start and end apart: 10 -> 11, of which waited for: 6 -> 8; matrix products, arithmetic and copies ran while one was open for 0% -> 0% of each run, Pallas kernels for 0% -> 0%
where the time goes in v4:
time: 129 us; the launch traced here: 127 us
  waiting for transfers between devices  60.7 us (47%)
  blocking collectives  31.2 us (24%)
  starting transfers between devices  25.7 us (20%)
  Pallas kernels  7.68 us (6%)
  local copies, waits for them, and re-layouts  1.42 us (1%)
    ppermute x9, waiting for transfers between devices, swap(): lax.ppermute(value, axis, [(place, place ^ mask) for place in range(lax.a...  60 us
    all_to_all x1, blocking collectives, exchange(): lax.all_to_all(value, ('tm', 'det'), split_axis=0, concat_axis=0, tiled=T...  31.2 us
    ppermute x9, starting transfers between devices, swap(): lax.ppermute(value, axis, [(place, place ^ mask) for place in range(lax.a...  13.8 us
    all_to_all x1, starting transfers between devices, exchange(): lax.all_to_all(value, ('tm', 'det'), split_axis=0, concat_axis=0, tiled=T...  11.2 us
    pallas_call x7, Pallas kernels, call(): pl.pallas_call(kernel, out_shape=outs, in_specs=[pl.BlockSpec(memory_spac...  7.68 us
  transfers between devices with their start and end apart: 11, of which 8 were waited for; matrix products, arithmetic and copies ran while one was open for 0% of the time, Pallas kernels for 0%

profile of v4, /device:TPU:0, one launch (start us, length us, event | category | flops | bytes accessed | tf_op | source)
XLA Modules:
  0.0 127.0 jit_solution(3697312764138297233)
XLA Ops:
  0.0 1.3 copy-done.1
  1.3 1.0 shard_map.55
  2.3 3.1 %collective-permute-start = (f32[16,4096]{1,0:T(8,128)}, f32[16,4096]{1,0:T(8,128)S(1)}, u32[]{:S(2)}, u32[]{:S(2)}) collective-permute-start(f32[16,4096]{1,0:T(8,128)} %get-tuple-element.24), channel_id=1, source_target_pairs={{0,8},{8,0},{16,24},{24,16},{1,9},{9,1},{17,25},{25,17},{2,10},{10... | collective-permute-start | bytes 786440 | tf_op jit(solution)/shard_map/ppermute | solution.py:253
  5.4 2.6 %collective-permute-start.1 = (f32[16,4096]{1,0:T(8,128)}, f32[16,4096]{1,0:T(8,128)S(1)}, u32[]{:S(2)}, u32[]{:S(2)}) collective-permute-start(f32[16,4096]{1,0:T(8,128)} %get-tuple-element.25), channel_id=1, source_target_pairs={{0,16},{8,24},{16,0},{24,8},{1,17},{9,25},{17,1},{25,9},{2,18},{10... | collective-permute-start | bytes 786440 | tf_op jit(solution)/shard_map/ppermute | solution.py:253
  8.0 0.7 collective-permute-start.3
  9.0 7.7 %collective-permute-done.refs_1_ = f32[16,4096]{1,0:T(8,128)S(1)} collective-permute-done((f32[16,4096]{1,0:T(8,128)}, f32[16,4096]{1,0:T(8,128)S(1)}, u32[]{:S(2)}, u32[]{:S(2)}) %collective-permute-start) | collective-permute-done | bytes 262176 | tf_op jit(solution)/shard_map/ppermute | solution.py:253
  16.7 13.0 %collective-permute-done.1.refs_2_ = f32[16,4096]{1,0:T(8,128)S(1)} collective-permute-done((f32[16,4096]{1,0:T(8,128)}, f32[16,4096]{1,0:T(8,128)S(1)}, u32[]{:S(2)}, u32[]{:S(2)}) %collective-permute-start.1) | collective-permute-done | bytes 262176 | tf_op jit(solution)/shard_map/ppermute | solution.py:253
  29.8 2.3 %shard_map.57 = f32[4,8,1,4,16,128]{5,4,3,2,1,0:T(8,128)} custom-call(f32[16,4096]{1,0:T(8,128)S(1)} %get-tuple-element.27.refs_0_, f32[16,4096]{1,0:T(8,128)S(1)} %collective-permute-done.refs_1_, f32[16,4096]{1,0:T(8,128)S(1)} %collective-permute-done.1.refs_2_, f32[16,4096]{1,0:T(8,128)S(1)} %collective-permute-done.2.refs_3_, ...), custom_call_target="tpu_custom_call" | custom-call | flops 805306368 | bytes 3211264 | tf_op jit(solution)/shard_map/pallas_call | solution.py:232
  32.1 11.2 %all-to-all-start = ((f32[32,64,128]{2,1,0:T(8,128)}), f32[32,64,128]{2,1,0:T(8,128)S(1)}, u32[]{:S(2)}, u32[]{:S(2)}) async-start(f32[32,64,128]{2,1,0:T(8,128)} %bitcast.2), calls=%async_computation | async-start | bytes 2097152 | tf_op jit(solution)/shard_map/all_to_all | solution.py:320
  43.3 1.8 %collective-permute-start.4 = (f32[1,64,512]{2,1,0:T(8,128)S(1)}, f32[1,64,512]{2,1,0:T(8,128)S(1)}, u32[]{:S(2)}, u32[]{:S(2)}) collective-permute-start(f32[1,64,512]{2,1,0:T(8,128)S(1)} %bitcast.13), channel_id=1, source_target_pairs={{0,2},{1,3},{2,0},{3,1},{4,6},{5,7},{6,4},{7,5},{8,10},{9,11},{10,... | collective-permute-start | bytes 393224 | tf_op jit(solution)/shard_map/ppermute | solution.py:253
  45.1 11.7 %collective-permute-done.4 = f32[1,64,512]{2,1,0:T(8,128)S(1)} collective-permute-done((f32[1,64,512]{2,1,0:T(8,128)S(1)}, f32[1,64,512]{2,1,0:T(8,128)S(1)}, u32[]{:S(2)}, u32[]{:S(2)}) %collective-permute-start.4) | collective-permute-done | bytes 131104 | tf_op jit(solution)/shard_map/ppermute | solution.py:253
  56.8 1.8 %collective-permute-start.5 = (f32[2,64,512]{2,1,0:T(8,128)S(1)}, f32[2,64,512]{2,1,0:T(8,128)S(1)}, u32[]{:S(2)}, u32[]{:S(2)}) collective-permute-start(f32[2,64,512]{2,1,0:T(8,128)S(1)} %pad_maximum_fusion.2), channel_id=1, source_target_pairs={{0,4},{1,5},{2,6},{3,7},{4,0},{5,1},{6,2},{7,3},{8,12},{9,13},{10,... | collective-permute-start | bytes 786440 | tf_op jit(solution)/shard_map/ppermute | solution.py:253
  58.6 8.0 %collective-permute-done.5 = f32[2,64,512]{2,1,0:T(8,128)S(1)} collective-permute-done((f32[2,64,512]{2,1,0:T(8,128)S(1)}, f32[2,64,512]{2,1,0:T(8,128)S(1)}, u32[]{:S(2)}, u32[]{:S(2)}) %collective-permute-start.5) | collective-permute-done | bytes 262176 | tf_op jit(solution)/shard_map/ppermute | solution.py:253
  66.7 1.9 %collective-permute-done.6 = f32[4,64,512]{2,1,0:T(8,128)S(1)} collective-permute-done((f32[4,64,512]{2,1,0:T(8,128)S(1)}, f32[4,64,512]{2,1,0:T(8,128)S(1)}, u32[]{:S(2)}, u32[]{:S(2)}) %collective-permute-start.6) | collective-permute-done | bytes 524320 | tf_op jit(solution)/shard_map/ppermute | solution.py:253
  68.8 0.8 all-to-all-done
  69.5 1.6 %shard_map.59 = f32[4,8,1,4,16,128]{5,4,3,2,1,0:T(8,128)S(1)} custom-call(f32[4,8,1,4,16,128]{5,4,3,2,1,0:T(8,128)S(1)} %bitcast.9, bf16[512,512]{1,0:T(8,128)(2,1)S(1)} %get-tuple-element.35.f_high, bf16[512,512]{1,0:T(8,128)(2,1)S(1)} %get-tuple-element.36.f_low), custom_call_target="tpu_custom_call" | custom-call | flops 805306368 | bytes 3145728 | tf_op jit(solution)/shard_map/pallas_call | solution.py:232
  71.1 31.2 %all_to_all.10 = f32[32,64,128]{2,1,0:T(8,128)S(1)} all-to-all(f32[32,64,128]{2,1,0:T(8,128)S(1)} %bitcast.10), channel_id=1, replica_groups=mesh['tm'=4,'det'=8] {'tm','det'}, dimensions={0} | all-to-all | bytes 2097152 | tf_op jit(solution)/shard_map/all_to_all | solution.py:320
  102.3 1.5 %shard_map.60 = (f32[16,4096]{1,0:T(8,128)S(1)}, f32[16,4096]{1,0:T(8,128)S(1)}, f32[16,4096]{1,0:T(8,128)S(1)}, f32[16,4096]{1,0:T(8,128)S(1)}) custom-call(f32[4,8,1,4,16,128]{5,4,3,2,1,0:T(8,128)S(1)} %bitcast.12, f32[2,32,256]{2,1,0:T(8,128)S(1)} %get-tuple-element.31.refs_4_.refs_1_, bf16[512,512]{1,0:T(8,128)(2,1)S(1)} %get-tuple-element.32.refs_5_.refs_2_, ...), custom_call_target="tpu_custom_call" | custom-call | flops 805306368 | bytes 3211264 | tf_op jit(solution)/shard_map/pallas_call | solution.py:232
  103.9 0.8 collective-permute-start.7
  104.7 1.1 collective-permute-start.8
  105.8 2.5 %collective-permute-start.9 = (f32[16,4096]{1,0:T(8,128)S(1)}, f32[16,4096]{1,0:T(8,128)S(1)}, u32[]{:S(2)}, u32[]{:S(2)}) collective-permute-start(f32[16,4096]{1,0:T(8,128)S(1)} %get-tuple-element.40), channel_id=1, source_target_pairs={{0,24},{8,16},{16,8},{24,0},{1,25},{9,17},{17,9},{25,1},{2,26},{10... | collective-permute-start | bytes 786440 | tf_op jit(solution)/shard_map/ppermute | solution.py:253
  108.3 8.0 %collective-permute-done.7.refs_1_ = f32[16,4096]{1,0:T(8,128)S(1)} collective-permute-done((f32[16,4096]{1,0:T(8,128)S(1)}, f32[16,4096]{1,0:T(8,128)S(1)}, u32[]{:S(2)}, u32[]{:S(2)}) %collective-permute-start.7) | collective-permute-done | bytes 262176 | tf_op jit(solution)/shard_map/ppermute | solution.py:253
  116.3 9.7 %collective-permute-done.8.refs_2_ = f32[16,4096]{1,0:T(8,128)S(1)} collective-permute-done((f32[16,4096]{1,0:T(8,128)S(1)}, f32[16,4096]{1,0:T(8,128)S(1)}, u32[]{:S(2)}, u32[]{:S(2)}) %collective-permute-start.8) | collective-permute-done | bytes 262176 | tf_op jit(solution)/shard_map/ppermute | solution.py:253
  126.0 1.0 shard_map.61
  (24 shorter events, 0.6 us)
Async XLA Ops:
  0.0 8.0 %copy-start = (f32[1,128,512]{2,1,0:T(8,128)S(1)}, f32[1,128,512]{2,1,0:T(8,128)}, u32[]{:S(2)}) copy-start(f32[1,128,512]{2,1,0:T(8,128)} %param.6) | copy-start | bytes 786436
  0.0 1.3 copy-start.1
  1.3 7.4 %copy-start.2 = (bf16[512,512]{1,0:T(8,128)(2,1)S(1)}, bf16[512,512]{1,0:T(8,128)(2,1)}, u32[]{:S(2)}) copy-start(bf16[512,512]{1,0:T(8,128)(2,1)} %constant.20.clone.refs_1_) | copy-start | bytes 1572868
  1.3 7.4 %copy-start.3 = (bf16[512,512]{1,0:T(8,128)(2,1)S(1)}, bf16[512,512]{1,0:T(8,128)(2,1)}, u32[]{:S(2)}) copy-start(bf16[512,512]{1,0:T(8,128)(2,1)} %constant.21.clone.refs_2_) | copy-start | bytes 1572868
  2.3 14.5 %collective-permute-start = (f32[16,4096]{1,0:T(8,128)}, f32[16,4096]{1,0:T(8,128)S(1)}, u32[]{:S(2)}, u32[]{:S(2)}) collective-permute-start(f32[16,4096]{1,0:T(8,128)} %get-tuple-element.24), channel_id=1, source_target_pairs={{0,8},{8,0},{16,24},{24,16},{1,9},{9,1},{17,25},{25,17},{2,10},{10... | collective-permute-start | bytes 786440 | tf_op jit(solution)/shard_map/ppermute | solution.py:253
  5.4 24.4 %collective-permute-start.1 = (f32[16,4096]{1,0:T(8,128)}, f32[16,4096]{1,0:T(8,128)S(1)}, u32[]{:S(2)}, u32[]{:S(2)}) collective-permute-start(f32[16,4096]{1,0:T(8,128)} %get-tuple-element.25), channel_id=1, source_target_pairs={{0,16},{8,24},{16,0},{24,8},{1,17},{9,25},{17,1},{25,9},{2,18},{10... | collective-permute-start | bytes 786440 | tf_op jit(solution)/shard_map/ppermute | solution.py:253
  8.0 21.8 %collective-permute-start.2 = (f32[16,4096]{1,0:T(8,128)}, f32[16,4096]{1,0:T(8,128)S(1)}, u32[]{:S(2)}, u32[]{:S(2)}) collective-permute-start(f32[16,4096]{1,0:T(8,128)} %get-tuple-element.26), channel_id=1, source_target_pairs={{0,24},{8,16},{16,8},{24,0},{1,25},{9,17},{17,9},{25,1},{2,26},{10... | collective-permute-start | bytes 786440 | tf_op jit(solution)/shard_map/ppermute | solution.py:253
  8.0 0.8 copy-start.4
  8.0 1.0 collective-permute-start.3
  9.0 23.1 %copy-start.5 = (f32[64,512]{1,0:T(8,128)}, f32[64,512]{1,0:T(8,128)S(1)}, u32[]{:S(2)}) copy-start(f32[64,512]{1,0:T(8,128)S(1)} %collective-permute-done.3) | copy-start | bytes 393220
  32.1 11.2 %copy-start.6 = (f32[64,512]{1,0:T(8,128)S(1)}, f32[64,512]{1,0:T(8,128)}, u32[]{:S(2)}) copy-start(f32[64,512]{1,0:T(8,128)} %copy-done.5) | copy-start | bytes 393220
  32.1 37.4 %all-to-all-start = ((f32[32,64,128]{2,1,0:T(8,128)}), f32[32,64,128]{2,1,0:T(8,128)S(1)}, u32[]{:S(2)}, u32[]{:S(2)}) async-start(f32[32,64,128]{2,1,0:T(8,128)} %bitcast.2), calls=%async_computation | async-start | bytes 2097152 | tf_op jit(solution)/shard_map/all_to_all | solution.py:320
  43.3 13.5 %collective-permute-start.4 = (f32[1,64,512]{2,1,0:T(8,128)S(1)}, f32[1,64,512]{2,1,0:T(8,128)S(1)}, u32[]{:S(2)}, u32[]{:S(2)}) collective-permute-start(f32[1,64,512]{2,1,0:T(8,128)S(1)} %bitcast.13), channel_id=1, source_target_pairs={{0,2},{1,3},{2,0},{3,1},{4,6},{5,7},{6,4},{7,5},{8,10},{9,11},{10,... | collective-permute-start | bytes 393224 | tf_op jit(solution)/shard_map/ppermute | solution.py:253
  56.8 9.7 %collective-permute-start.5 = (f32[2,64,512]{2,1,0:T(8,128)S(1)}, f32[2,64,512]{2,1,0:T(8,128)S(1)}, u32[]{:S(2)}, u32[]{:S(2)}) collective-permute-start(f32[2,64,512]{2,1,0:T(8,128)S(1)} %pad_maximum_fusion.2), channel_id=1, source_target_pairs={{0,4},{1,5},{2,6},{3,7},{4,0},{5,1},{6,2},{7,3},{8,12},{9,13},{10,... | collective-permute-start | bytes 786440 | tf_op jit(solution)/shard_map/ppermute | solution.py:253
  66.6 2.0 %collective-permute-start.6 = (f32[4,64,512]{2,1,0:T(8,128)S(1)}, f32[4,64,512]{2,1,0:T(8,128)S(1)}, u32[]{:S(2)}, u32[]{:S(2)}) collective-permute-start(f32[4,64,512]{2,1,0:T(8,128)S(1)} %pad_maximum_fusion.1), channel_id=1, source_target_pairs={{0,1},{1,0},{2,3},{3,2},{4,5},{5,4},{6,7},{7,6},{8,9},{9,8},{10,11... | collective-permute-start | bytes 1572872 | tf_op jit(solution)/shard_map/ppermute | solution.py:253
  103.9 12.4 %collective-permute-start.7 = (f32[16,4096]{1,0:T(8,128)S(1)}, f32[16,4096]{1,0:T(8,128)S(1)}, u32[]{:S(2)}, u32[]{:S(2)}) collective-permute-start(f32[16,4096]{1,0:T(8,128)S(1)} %get-tuple-element.38), channel_id=1, source_target_pairs={{0,8},{8,0},{16,24},{24,16},{1,9},{9,1},{17,25},{25,17},{2,10},{10... | collective-permute-start | bytes 786440 | tf_op jit(solution)/shard_map/ppermute | solution.py:253
  104.7 21.3 %collective-permute-start.8 = (f32[16,4096]{1,0:T(8,128)S(1)}, f32[16,4096]{1,0:T(8,128)S(1)}, u32[]{:S(2)}, u32[]{:S(2)}) collective-permute-start(f32[16,4096]{1,0:T(8,128)S(1)} %get-tuple-element.39), channel_id=1, source_target_pairs={{0,16},{8,24},{16,0},{24,8},{1,17},{9,25},{17,1},{25,9},{2,18},{10... | collective-permute-start | bytes 786440 | tf_op jit(solution)/shard_map/ppermute | solution.py:253
  105.8 20.2 %collective-permute-start.9 = (f32[16,4096]{1,0:T(8,128)S(1)}, f32[16,4096]{1,0:T(8,128)S(1)}, u32[]{:S(2)}, u32[]{:S(2)}) collective-permute-start(f32[16,4096]{1,0:T(8,128)S(1)} %get-tuple-element.40), channel_id=1, source_target_pairs={{0,24},{8,16},{16,8},{24,0},{1,25},{9,17},{17,9},{25,1},{2,26},{10... | collective-permute-start | bytes 786440 | tf_op jit(solution)/shard_map/ppermute | solution.py:253

commit v5 on v4

--- a/solution.py
+++ b/solution.py
@@ -15,11 +15,15 @@
 CHUNKS = 1
 
 
+def band_of(plane, planes):
+    return 2 * plane if 2 * plane < planes else 2 * (planes - 1 - plane) + 1
+
+
 def fourier_matrix(n2, planes):
     share = n2 // (2 * planes)
     order = []
     for plane in range(planes):
-        low = np.arange(plane * share, (plane + 1) * share)
+        low = band_of(plane, planes) * share + np.arange(share)
         order.append(np.concatenate([low, n2 - 1 - low[::-1]]))
     order = np.stack(order)
     angle = 2.0 * np.pi / n2 * (np.arange(n2)[:, None, None] * order[None] % n2)
@@ -184,13 +188,11 @@
         copy.wait()
 
 
-def factor_kernel(masks, factor_ref, high_ref, low_ref):
+def factor_kernel(factor_ref, high_ref, low_ref):
     here = lax.axis_index("det")
     shares, rows, _ = factor_ref.shape
     for share in range(shares):
-        source = here
-        for bit, mask in enumerate(masks):
-            source = source ^ (mask if share >> bit & 1 else 0)
+        source = here ^ (2 * share if 2 * share < shares else 2 * share - shares + 1)
         place = pl.ds(pl.multiple_of(source * rows, rows), rows)
         high_ref[place], low_ref[place] = split(factor_ref[share])
 
@@ -253,26 +255,29 @@
     return lax.ppermute(value, axis, [(place, place ^ mask) for place in range(lax.axis_size(axis))])
 
 
+def spread_out(parts):
+    return [swap(part, "tm", step) if step else part for step, part in reversed(list(enumerate(parts)))][::-1]
+
+
 def plane_factor(factor, planes, groups):
     half = factor.shape[1] // 2
     upper = lax.axis_index("det") >= groups // 2
     mine = lax.dynamic_slice_in_dim(factor[0], jnp.where(upper, half, 0), half, 0)
+    plane_of = {band_of(plane, planes): plane for plane in range(planes)}
     pairs = []
     for plane in range(planes):
         for group in range(groups):
-            target = min(group, groups - 1 - group)
+            target = plane_of[min(group, groups - 1 - group)]
             pairs.append((plane * groups + group, target * groups + 2 * plane + (group >= groups // 2)))
     return lax.ppermute(mine, ("tm", "det"), pairs)
 
 
 def band_factor(share, groups):
     rows, columns = share.shape
-    share = share[None]
-    masks = [2**bit for bit in range(1, groups.bit_length() - 1)] + [1]
-    for mask in masks:
-        share = jnp.concatenate([share, swap(share, "det", mask)])
+    share = jnp.stack([share] + [swap(share, "det", mask) for mask in range(2, groups, 2)])
+    share = jnp.concatenate([share, swap(share, "det", 1)])
     whole = array(groups * rows, columns, dtype=jnp.bfloat16)
-    return call(lambda *refs: factor_kernel(masks, *refs), [whole, whole], [], 0, share)
+    return call(factor_kernel, [whole, whole], [], 0, share)
 
 
 def bind(kernel, *static):
@@ -297,14 +302,13 @@
     arrived = []
     for chunk in range(chunks):
         parts = call(bind(slice_kernel, chunk), [block] * planes, [dma(planes)], 0, noise, spaces=[pl.ANY])
-        arrived.append([swap(part, "tm", step) if step else part for step, part in enumerate(parts)])
-    share = plane_factor(factor, planes, groups)
+        arrived.append(spread_out(parts))
     tables = call(
         hold_kernel, [array(*table.shape, dtype=table.dtype) for table in tables], [dma(len(tables))], 0, *tables,
         spaces=[pl.ANY] * len(tables),
     )
-    arrived, share = lax.optimization_barrier((arrived, share))
-    f_high, f_low = band_factor(share, groups)
+    arrived, factor = lax.optimization_barrier((arrived, factor))
+    f_high, f_low = band_factor(plane_factor(factor, planes, groups), groups)
     buffer = []
     for chunk in range(chunks):
         buffer = call(
@@ -331,7 +335,7 @@
         parts = call(
             bind(inverse_kernel, n1, n2, chunk), [block] * planes, [series, middle], flops, back, *tables
         )
-        parts = [swap(part, "tm", step) if step else part for step, part in enumerate(parts)]
+        parts = spread_out(parts)
         result = call(
             bind(place_kernel, chunk), [array(planes, chunks, dets, span)], [dma(planes)], 0, *parts, *result,
             spaces=[pl.ANY] * (planes + len(result)), out_space=pl.ANY, aliases={planes: 0} if result else None,

time: 129 us -> 135 us (1.047)
  starting transfers between devices: 25.7 us -> 50.1 us
  waiting for transfers between devices: 60.7 us -> 44.3 us
  blocking collectives: 31.2 us -> 28.7 us
    ppermute x9 -> x10, starting transfers between devices: 13.8 us -> 41.4 us  [swap(): lax.ppermute(value, axis, [(place, place ^ mask) for place in range(lax.a...]
    ppermute x9 -> x10, waiting for transfers between devices: 60 us -> 44.3 us  [swap(): lax.ppermute(value, axis, [(place, place ^ mask) for place in range(lax.a...]
    all_to_all x1, starting transfers between devices: 11.2 us -> 8.02 us  [exchange(): lax.all_to_all(value, ('tm', 'det'), split_axis=0, concat_axis=0, tiled=T...]
    all_to_all x1, blocking collectives: 31.2 us -> 28.7 us  [exchange(): lax.all_to_all(value, ('tm', 'det'), split_axis=0, concat_axis=0, tiled=T...]
  transfers between devices with their start and end apart: 11 -> 12, of which waited for: 8 -> 7; matrix products, arithmetic and copies ran while one was open for 0% -> 0% of each run, Pallas kernels for 0% -> 0%
where the time goes in v5:
time: 135 us; the launch traced here: 132 us
  starting transfers between devices  50.1 us (37%)
  waiting for transfers between devices  44.3 us (33%)
  blocking collectives  28.7 us (21%)
  Pallas kernels  6.81 us (5%)
  local copies, waits for them, and re-layouts  2.21 us (2%)
    ppermute x10, waiting for transfers between devices, swap(): lax.ppermute(value, axis, [(place, place ^ mask) for place in range(lax.a...  44.3 us
    ppermute x10, starting transfers between devices, swap(): lax.ppermute(value, axis, [(place, place ^ mask) for place in range(lax.a...  41.4 us
    all_to_all x1, blocking collectives, exchange(): lax.all_to_all(value, ('tm', 'det'), split_axis=0, concat_axis=0, tiled=T...  28.7 us
    all_to_all x1, starting transfers between devices, exchange(): lax.all_to_all(value, ('tm', 'det'), split_axis=0, concat_axis=0, tiled=T...  8.02 us
    pallas_call x7, Pallas kernels, call(): pl.pallas_call(kernel, out_shape=outs, in_specs=[pl.BlockSpec(memory_spac...  6.81 us
  transfers between devices with their start and end apart: 12, of which 7 were waited for; matrix products, arithmetic and copies ran while one was open for 0% of the time, Pallas kernels for 0%

profile of v5, /device:TPU:0, one launch (start us, length us, event | category | flops | bytes accessed | tf_op | source)
XLA Modules:
  0.0 132.4 jit_solution(10469325567666907131)
XLA Ops:
  0.0 1.3 copy-done.1
  1.4 3.1 %collective-permute-start = (f32[16,4096]{1,0:T(8,128)S(1)}, f32[16,4096]{1,0:T(8,128)S(1)}, u32[]{:S(2)}, u32[]{:S(2)}) collective-permute-start(f32[16,4096]{1,0:T(8,128)S(1)} %get-tuple-element.24), channel_id=1, source_target_pairs={{0,8},{8,0},{16,24},{24,16},{1,9},{9,1},{17,25},{25,17},{2,10},{10... | collective-permute-start | bytes 786440 | tf_op jit(solution)/shard_map/ppermute | solution.py:255
  4.5 2.6 %collective-permute-start.1 = (f32[16,4096]{1,0:T(8,128)S(1)}, f32[16,4096]{1,0:T(8,128)S(1)}, u32[]{:S(2)}, u32[]{:S(2)}) collective-permute-start(f32[16,4096]{1,0:T(8,128)S(1)} %get-tuple-element.25), channel_id=1, source_target_pairs={{0,16},{8,24},{16,0},{24,8},{1,17},{9,25},{17,1},{25,9},{2,18},{10... | collective-permute-start | bytes 786440 | tf_op jit(solution)/shard_map/ppermute | solution.py:255
  7.1 0.8 copy-done.4
  8.1 7.5 %collective-permute-done.refs_1_ = f32[16,4096]{1,0:T(8,128)S(1)} collective-permute-done((f32[16,4096]{1,0:T(8,128)S(1)}, f32[16,4096]{1,0:T(8,128)S(1)}, u32[]{:S(2)}, u32[]{:S(2)}) %collective-permute-start) | collective-permute-done | bytes 262176 | tf_op jit(solution)/shard_map/ppermute | solution.py:255
  15.6 10.2 %collective-permute-done.1.refs_2_ = f32[16,4096]{1,0:T(8,128)S(1)} collective-permute-done((f32[16,4096]{1,0:T(8,128)S(1)}, f32[16,4096]{1,0:T(8,128)S(1)}, u32[]{:S(2)}, u32[]{:S(2)}) %collective-permute-start.1) | collective-permute-done | bytes 262176 | tf_op jit(solution)/shard_map/ppermute | solution.py:255
  25.9 2.3 %shard_map.57 = f32[4,8,1,4,16,128]{5,4,3,2,1,0:T(8,128)} custom-call(f32[16,4096]{1,0:T(8,128)S(1)} %get-tuple-element.27.refs_0_, f32[16,4096]{1,0:T(8,128)S(1)} %collective-permute-done.refs_1_, f32[16,4096]{1,0:T(8,128)S(1)} %collective-permute-done.1.refs_2_, f32[16,4096]{1,0:T(8,128)S(1)} %collective-permute-done.2.refs_3_, ...), custom_call_target="tpu_custom_call" | custom-call | flops 805306368 | bytes 3211264 | tf_op jit(solution)/shard_map/pallas_call | solution.py:234
  28.2 8.0 %all-to-all-start = ((f32[32,64,128]{2,1,0:T(8,128)}), f32[32,64,128]{2,1,0:T(8,128)S(1)}, u32[]{:S(2)}, u32[]{:S(2)}) async-start(f32[32,64,128]{2,1,0:T(8,128)} %bitcast.1), calls=%async_computation | async-start | bytes 2097152 | tf_op jit(solution)/shard_map/all_to_all | solution.py:324
  36.2 0.7 collective-permute-start.3
  36.9 24.6 %collective-permute-start.6 = (f32[64,512]{1,0:T(8,128)S(1)}, f32[64,512]{1,0:T(8,128)S(1)}, u32[]{:S(2)}, u32[]{:S(2)}) collective-permute-start(f32[64,512]{1,0:T(8,128)S(1)} %collective-permute-done.3), channel_id=1, source_target_pairs={{0,6},{1,7},{2,4},{3,5},{4,2},{5,3},{6,0},{7,1},{8,14},{9,15},{10,... | collective-permute-start | bytes 393224 | tf_op jit(solution)/shard_map/ppermute | solution.py:255
  61.5 5.2 %collective-permute-start.5 = (f32[64,512]{1,0:T(8,128)S(1)}, f32[64,512]{1,0:T(8,128)S(1)}, u32[]{:S(2)}, u32[]{:S(2)}) collective-permute-start(f32[64,512]{1,0:T(8,128)S(1)} %collective-permute-done.3), channel_id=1, source_target_pairs={{0,4},{1,5},{2,6},{3,7},{4,0},{5,1},{6,2},{7,3},{8,12},{9,13},{10,... | collective-permute-start | bytes 393224 | tf_op jit(solution)/shard_map/ppermute | solution.py:255
  66.7 1.5 %collective-permute-start.4 = (f32[64,512]{1,0:T(8,128)S(1)}, f32[64,512]{1,0:T(8,128)S(1)}, u32[]{:S(2)}, u32[]{:S(2)}) collective-permute-start(f32[64,512]{1,0:T(8,128)S(1)} %collective-permute-done.3), channel_id=1, source_target_pairs={{0,2},{1,3},{2,0},{3,1},{4,6},{5,7},{6,4},{7,5},{8,10},{9,11},{10,... | collective-permute-start | bytes 393224 | tf_op jit(solution)/shard_map/ppermute | solution.py:255
  68.2 5.0 %collective-permute-done.5 = f32[64,512]{1,0:T(8,128)S(1)} collective-permute-done((f32[64,512]{1,0:T(8,128)S(1)}, f32[64,512]{1,0:T(8,128)S(1)}, u32[]{:S(2)}, u32[]{:S(2)}) %collective-permute-start.5) | collective-permute-done | bytes 131104 | tf_op jit(solution)/shard_map/ppermute | solution.py:255
  73.3 2.0 %collective-permute-done.4 = f32[64,512]{1,0:T(8,128)S(1)} collective-permute-done((f32[64,512]{1,0:T(8,128)S(1)}, f32[64,512]{1,0:T(8,128)S(1)}, u32[]{:S(2)}, u32[]{:S(2)}) %collective-permute-start.4) | collective-permute-done | bytes 131104 | tf_op jit(solution)/shard_map/ppermute | solution.py:255
  75.4 1.8 %collective-permute-done.7 = f32[4,64,512]{2,1,0:T(8,128)S(1)} collective-permute-done((f32[4,64,512]{2,1,0:T(8,128)S(1)}, f32[4,64,512]{2,1,0:T(8,128)S(1)}, u32[]{:S(2)}, u32[]{:S(2)}) %collective-permute-start.7) | collective-permute-done | bytes 524320 | tf_op jit(solution)/shard_map/ppermute | solution.py:255
  77.4 1.6 %shard_map.59 = f32[4,8,1,4,16,128]{5,4,3,2,1,0:T(8,128)S(1)} custom-call(f32[4,8,1,4,16,128]{5,4,3,2,1,0:T(8,128)S(1)} %bitcast.16, bf16[512,512]{1,0:T(8,128)(2,1)S(1)} %get-tuple-element.35.f_high, bf16[512,512]{1,0:T(8,128)(2,1)S(1)} %get-tuple-element.36.f_low), custom_call_target="tpu_custom_call" | custom-call | flops 805306368 | bytes 3145728 | tf_op jit(solution)/shard_map/pallas_call | solution.py:234
  79.0 28.7 %all_to_all.10 = f32[32,64,128]{2,1,0:T(8,128)S(1)} all-to-all(f32[32,64,128]{2,1,0:T(8,128)S(1)} %bitcast.17), channel_id=1, replica_groups=mesh['tm'=4,'det'=8] {'tm','det'}, dimensions={0} | all-to-all | bytes 2097152 | tf_op jit(solution)/shard_map/all_to_all | solution.py:324
  107.7 1.5 %shard_map.60 = (f32[16,4096]{1,0:T(8,128)S(1)}, f32[16,4096]{1,0:T(8,128)S(1)}, f32[16,4096]{1,0:T(8,128)S(1)}, f32[16,4096]{1,0:T(8,128)S(1)}) custom-call(f32[4,8,1,4,16,128]{5,4,3,2,1,0:T(8,128)S(1)} %bitcast.19, f32[2,32,256]{2,1,0:T(8,128)S(1)} %get-tuple-element.31.refs_4_.refs_1_, bf16[512,512]{1,0:T(8,128)(2,1)S(1)} %get-tuple-element.32.refs_5_.refs_2_, ...), custom_call_target="tpu_custom_call" | custom-call | flops 805306368 | bytes 3211264 | tf_op jit(solution)/shard_map/pallas_call | solution.py:234
  109.2 0.8 collective-permute-start.8
  110.0 1.1 collective-permute-start.9
  111.1 2.5 %collective-permute-start.10 = (f32[16,4096]{1,0:T(8,128)S(1)}, f32[16,4096]{1,0:T(8,128)S(1)}, u32[]{:S(2)}, u32[]{:S(2)}) collective-permute-start(f32[16,4096]{1,0:T(8,128)S(1)} %get-tuple-element.40), channel_id=1, source_target_pairs={{0,24},{8,16},{16,8},{24,0},{1,25},{9,17},{17,9},{25,1},{2,26},{10... | collective-permute-start | bytes 786440 | tf_op jit(solution)/shard_map/ppermute | solution.py:255
  113.7 8.0 %collective-permute-done.8.refs_1_ = f32[16,4096]{1,0:T(8,128)S(1)} collective-permute-done((f32[16,4096]{1,0:T(8,128)S(1)}, f32[16,4096]{1,0:T(8,128)S(1)}, u32[]{:S(2)}, u32[]{:S(2)}) %collective-permute-start.8) | collective-permute-done | bytes 262176 | tf_op jit(solution)/shard_map/ppermute | solution.py:255
  121.7 9.7 %collective-permute-done.9.refs_2_ = f32[16,4096]{1,0:T(8,128)S(1)} collective-permute-done((f32[16,4096]{1,0:T(8,128)S(1)}, f32[16,4096]{1,0:T(8,128)S(1)}, u32[]{:S(2)}, u32[]{:S(2)}) %collective-permute-start.9) | collective-permute-done | bytes 262176 | tf_op jit(solution)/shard_map/ppermute | solution.py:255
  131.4 1.0 shard_map.61
  (25 shorter events, 0.6 us)
Async XLA Ops:
  0.0 36.2 %copy-start = (f32[1,128,512]{2,1,0:T(8,128)S(1)}, f32[1,128,512]{2,1,0:T(8,128)}, u32[]{:S(2)}) copy-start(f32[1,128,512]{2,1,0:T(8,128)} %param.6) | copy-start | bytes 786436
  0.0 1.3 copy-start.1
  1.3 5.8 %copy-start.2 = (bf16[512,512]{1,0:T(8,128)(2,1)S(1)}, bf16[512,512]{1,0:T(8,128)(2,1)}, u32[]{:S(2)}) copy-start(bf16[512,512]{1,0:T(8,128)(2,1)} %constant.21.clone.refs_2_) | copy-start | bytes 1572868
  1.3 5.8 %copy-start.3 = (bf16[512,512]{1,0:T(8,128)(2,1)S(1)}, bf16[512,512]{1,0:T(8,128)(2,1)}, u32[]{:S(2)}) copy-start(bf16[512,512]{1,0:T(8,128)(2,1)} %constant.20.clone.refs_1_) | copy-start | bytes 1572868
  1.4 14.2 %collective-permute-start = (f32[16,4096]{1,0:T(8,128)S(1)}, f32[16,4096]{1,0:T(8,128)S(1)}, u32[]{:S(2)}, u32[]{:S(2)}) collective-permute-start(f32[16,4096]{1,0:T(8,128)S(1)} %get-tuple-element.24), channel_id=1, source_target_pairs={{0,8},{8,0},{16,24},{24,16},{1,9},{9,1},{17,25},{25,17},{2,10},{10... | collective-permute-start | bytes 786440 | tf_op jit(solution)/shard_map/ppermute | solution.py:255
  4.5 21.4 %collective-permute-start.1 = (f32[16,4096]{1,0:T(8,128)S(1)}, f32[16,4096]{1,0:T(8,128)S(1)}, u32[]{:S(2)}, u32[]{:S(2)}) collective-permute-start(f32[16,4096]{1,0:T(8,128)S(1)} %get-tuple-element.25), channel_id=1, source_target_pairs={{0,16},{8,24},{16,0},{24,8},{1,17},{9,25},{17,1},{25,9},{2,18},{10... | collective-permute-start | bytes 786440 | tf_op jit(solution)/shard_map/ppermute | solution.py:255
  7.1 18.8 %collective-permute-start.2 = (f32[16,4096]{1,0:T(8,128)S(1)}, f32[16,4096]{1,0:T(8,128)S(1)}, u32[]{:S(2)}, u32[]{:S(2)}) collective-permute-start(f32[16,4096]{1,0:T(8,128)S(1)} %get-tuple-element.26), channel_id=1, source_target_pairs={{0,24},{8,16},{16,8},{24,0},{1,25},{9,17},{17,9},{25,1},{2,26},{10... | collective-permute-start | bytes 786440 | tf_op jit(solution)/shard_map/ppermute | solution.py:255
  7.1 0.8 copy-start.4
  28.2 49.2 %all-to-all-start = ((f32[32,64,128]{2,1,0:T(8,128)}), f32[32,64,128]{2,1,0:T(8,128)S(1)}, u32[]{:S(2)}, u32[]{:S(2)}) async-start(f32[32,64,128]{2,1,0:T(8,128)} %bitcast.1), calls=%async_computation | async-start | bytes 2097152 | tf_op jit(solution)/shard_map/all_to_all | solution.py:324
  36.2 0.7 collective-permute-start.3
  36.9 31.3 %collective-permute-start.6 = (f32[64,512]{1,0:T(8,128)S(1)}, f32[64,512]{1,0:T(8,128)S(1)}, u32[]{:S(2)}, u32[]{:S(2)}) collective-permute-start(f32[64,512]{1,0:T(8,128)S(1)} %collective-permute-done.3), channel_id=1, source_target_pairs={{0,6},{1,7},{2,4},{3,5},{4,2},{5,3},{6,0},{7,1},{8,14},{9,15},{10,... | collective-permute-start | bytes 393224 | tf_op jit(solution)/shard_map/ppermute | solution.py:255
  61.5 11.7 %collective-permute-start.5 = (f32[64,512]{1,0:T(8,128)S(1)}, f32[64,512]{1,0:T(8,128)S(1)}, u32[]{:S(2)}, u32[]{:S(2)}) collective-permute-start(f32[64,512]{1,0:T(8,128)S(1)} %collective-permute-done.3), channel_id=1, source_target_pairs={{0,4},{1,5},{2,6},{3,7},{4,0},{5,1},{6,2},{7,3},{8,12},{9,13},{10,... | collective-permute-start | bytes 393224 | tf_op jit(solution)/shard_map/ppermute | solution.py:255
  66.7 8.5 %collective-permute-start.4 = (f32[64,512]{1,0:T(8,128)S(1)}, f32[64,512]{1,0:T(8,128)S(1)}, u32[]{:S(2)}, u32[]{:S(2)}) collective-permute-start(f32[64,512]{1,0:T(8,128)S(1)} %collective-permute-done.3), channel_id=1, source_target_pairs={{0,2},{1,3},{2,0},{3,1},{4,6},{5,7},{6,4},{7,5},{8,10},{9,11},{10,... | collective-permute-start | bytes 393224 | tf_op jit(solution)/shard_map/ppermute | solution.py:255
  75.3 2.0 %collective-permute-start.7 = (f32[4,64,512]{2,1,0:T(8,128)S(1)}, f32[4,64,512]{2,1,0:T(8,128)S(1)}, u32[]{:S(2)}, u32[]{:S(2)}) collective-permute-start(f32[4,64,512]{2,1,0:T(8,128)S(1)} %pad_maximum_fusion), channel_id=1, source_target_pairs={{0,1},{1,0},{2,3},{3,2},{4,5},{5,4},{6,7},{7,6},{8,9},{9,8},{10,11... | collective-permute-start | bytes 1572872 | tf_op jit(solution)/shard_map/ppermute | solution.py:255
  109.2 12.4 %collective-permute-start.8 = (f32[16,4096]{1,0:T(8,128)S(1)}, f32[16,4096]{1,0:T(8,128)S(1)}, u32[]{:S(2)}, u32[]{:S(2)}) collective-permute-start(f32[16,4096]{1,0:T(8,128)S(1)} %get-tuple-element.38), channel_id=1, source_target_pairs={{0,8},{8,0},{16,24},{24,16},{1,9},{9,1},{17,25},{25,17},{2,10},{10... | collective-permute-start | bytes 786440 | tf_op jit(solution)/shard_map/ppermute | solution.py:255
  110.0 21.3 %collective-permute-start.9 = (f32[16,4096]{1,0:T(8,128)S(1)}, f32[16,4096]{1,0:T(8,128)S(1)}, u32[]{:S(2)}, u32[]{:S(2)}) collective-permute-start(f32[16,4096]{1,0:T(8,128)S(1)} %get-tuple-element.39), channel_id=1, source_target_pairs={{0,16},{8,24},{16,0},{24,8},{1,17},{9,25},{17,1},{25,9},{2,18},{10... | collective-permute-start | bytes 786440 | tf_op jit(solution)/shard_map/ppermute | solution.py:255
  111.1 20.2 %collective-permute-start.10 = (f32[16,4096]{1,0:T(8,128)S(1)}, f32[16,4096]{1,0:T(8,128)S(1)}, u32[]{:S(2)}, u32[]{:S(2)}) collective-permute-start(f32[16,4096]{1,0:T(8,128)S(1)} %get-tuple-element.40), channel_id=1, source_target_pairs={{0,24},{8,16},{16,8},{24,0},{1,25},{9,17},{17,9},{25,1},{2,26},{10... | collective-permute-start | bytes 786440 | tf_op jit(solution)/shard_map/ppermute | solution.py:255

commit v6 on v5

--- a/solution.py
+++ b/solution.py
@@ -94,7 +94,8 @@
     here = lax.axis_index("tm")
     outs, sem = refs[:-1], refs[-1]
     copies = [
-        pltpu.make_async_copy(noise_ref.at[here ^ step, chunk], out, sem.at[step]) for step, out in enumerate(outs)
+        pltpu.make_async_copy(noise_ref.at[lax.rem(here + step, noise_ref.shape[0]), chunk], out, sem.at[step])
+        for step, out in enumerate(outs)
     ]
     for copy in copies:
         copy.start()
@@ -120,7 +121,7 @@
     _, groups, pieces, _, width = stage_ref.shape
     per = span // n2
     for step, block in enumerate(blocks):
-        x_ref[here ^ step] = block[...]
+        x_ref[lax.rem(here + planes - step, planes)] = block[...]
     for rows, lane in tiles(dets, n2):
 
         def load(index):
@@ -172,15 +173,16 @@
                 start = (index % per) * n2 + lane
                 x_ref[index // per, rows, start : start + LANES] = value
     for step, out in enumerate(outs):
-        out[...] = x_ref[here ^ step]
+        out[...] = x_ref[lax.rem(here + step, planes)]
 
 
 def place_kernel(chunk, *refs):
     here = lax.axis_index("tm")
     out_ref, sem = refs[-2:]
+    planes = out_ref.shape[0]
     copies = [
-        pltpu.make_async_copy(refs[step], out_ref.at[here ^ step, chunk], sem.at[step])
-        for step in range(out_ref.shape[0])
+        pltpu.make_async_copy(refs[step], out_ref.at[lax.rem(here + planes - step, planes), chunk], sem.at[step])
+        for step in range(planes)
     ]
     for copy in copies:
         copy.start()
@@ -197,35 +199,21 @@
         high_ref[place], low_ref[place] = split(factor_ref[share])
 
 
-def mix_kernel(x_ref, f_high, f_low, out_ref, x_mid, stage_ref, sem):
+def mix_kernel(x_ref, f_high, f_low, out_ref, x_mid, y_mid):
     planes, groups, chunks, pieces, dets, width = x_ref.shape
-
-    def rows_of(group, plane, chunk):
+    places = []
+    for plane, group, chunk, piece in np.ndindex(planes, groups, chunks, pieces):
         start = ((group * planes + plane) * chunks + chunk) * dets
-        return slice(start, start + dets)
-
-    places = [
-        (plane, group, chunk, piece)
-        for group in range(groups) for plane in range(planes) for chunk in range(chunks) for piece in range(pieces)
-    ]
-    for plane, group, chunk, piece in places:
-        x_mid[rows_of(group, plane, chunk), piece * width : (piece + 1) * width] = x_ref[plane, group, chunk, piece]
+        rows, lanes = slice(start, start + dets), slice(piece * width, (piece + 1) * width)
+        places.append(((plane, group, chunk, piece), (rows, lanes)))
+    for source, target in places:
+        x_mid[target] = x_ref[source]
     x_high, x_low = split(x_mid[...])
-    steps = 4
-    count, share = f_high.shape[0] // steps, groups // steps
-    copies = []
-    for step in range(steps):
-        rows, reach = slice(step * count, (step + 1) * count), (step + 1) * count
-        value = product((f_high[rows, :reach], f_low[rows, :reach]), (x_high[:reach], x_low[:reach]))
-        for plane, group, chunk, piece in places:
-            if group // share == step:
-                own = rows_of(group - step * share, plane, chunk)
-                stage_ref[plane, group, chunk, piece] = value[own, piece * width : (piece + 1) * width]
-        these = pl.ds(step * share, share)
-        copies.append(pltpu.make_async_copy(stage_ref.at[:, these], out_ref.at[:, these], sem.at[step]))
-        copies[-1].start()
-    for copy in copies:
-        copy.wait()
+    half = f_high.shape[0] // 2
+    y_mid[:half] = product((f_high[:half, :half], f_low[:half, :half]), (x_high[:half], x_low[:half]))
+    y_mid[half:] = product((f_high[half:, :], f_low[half:, :]), (x_high, x_low))
+    for target, source in places:
+        out_ref[target] = y_mid[source]
 
 
 def call(kernel, outs, scratch, flops, *args, spaces=None, out_space=pltpu.VMEM, aliases=None):
@@ -255,8 +243,12 @@
     return lax.ppermute(value, axis, [(place, place ^ mask) for place in range(lax.axis_size(axis))])
 
 
-def spread_out(parts):
-    return [swap(part, "tm", step) if step else part for step, part in reversed(list(enumerate(parts)))][::-1]
+def rotate(parts):
+    planes = len(parts)
+    return [parts[0]] + [
+        lax.ppermute(parts[step], "tm", [(place, (place + step) % planes) for place in range(planes)])
+        for step in range(1, planes)
+    ]
 
 
 def plane_factor(factor, planes, groups):
@@ -301,14 +293,15 @@
     noise = noise.reshape(planes, chunks, dets, span)
     arrived = []
     for chunk in range(chunks):
-        parts = call(bind(slice_kernel, chunk), [block] * planes, [dma(planes)], 0, noise, spaces=[pl.ANY])
-        arrived.append(spread_out(parts))
+        parts = call(bind(slice_kernel, chunk), [block] * planes, [dma(planes)], 0, noise, spaces=[pltpu.HBM])
+        arrived.append(rotate(parts))
+    share = plane_factor(factor, planes, groups)
     tables = call(
         hold_kernel, [array(*table.shape, dtype=table.dtype) for table in tables], [dma(len(tables))], 0, *tables,
         spaces=[pl.ANY] * len(tables),
     )
-    arrived, factor = lax.optimization_barrier((arrived, factor))
-    f_high, f_low = band_factor(plane_factor(factor, planes, groups), groups)
+    arrived, share = lax.optimization_barrier((arrived, share))
+    f_high, f_low = band_factor(share, groups)
     buffer = []
     for chunk in range(chunks):
         buffer = call(
@@ -325,9 +318,9 @@
 
     count = f_high.shape[0]
     (mixed,) = call(
-        mix_kernel, [array(*layout)], [(count, pieces * LANES), layout, dma(4)],
+        mix_kernel, [array(*layout)], [(count, pieces * LANES)] * 2,
         2 * 3 * count * count * pieces * LANES,
-        exchange(buffer[0]), f_high, f_low, out_space=pl.ANY,
+        exchange(buffer[0]), f_high, f_low,
     )
     back = exchange(mixed)
     result = []
@@ -335,7 +328,7 @@
         parts = call(
             bind(inverse_kernel, n1, n2, chunk), [block] * planes, [series, middle], flops, back, *tables
         )
-        parts = spread_out(parts)
+        parts = rotate(parts)
         result = call(
             bind(place_kernel, chunk), [array(planes, chunks, dets, span)], [dma(planes)], 0, *parts, *result,
             spaces=[pl.ANY] * (planes + len(result)), out_space=pl.ANY, aliases={planes: 0} if result else None,

time: 135 us -> 123 us (0.911)
  the two profiles are of different devices: /device:TPU:0 before, /device:TPU:11 now
where the time goes in v6:
time: 123 us
  waiting for transfers between devices  65.2 us (53%)
  blocking collectives  29.7 us (24%)
  starting transfers between devices  19.6 us (16%)
  Pallas kernels  6.98 us (6%)
  local copies, waits for them, and re-layouts  1.38 us (1%)
    all_to_all x1, blocking collectives, exchange(): lax.all_to_all(value, ('tm', 'det'), split_axis=0, concat_axis=0, tiled=T...  29.7 us
    ppermute x6, waiting for transfers between devices, rotate(): lax.ppermute(parts[step], 'tm', [(place, (place + step) % planes) for pla...  24 us
    ppermute x1, waiting for transfers between devices, plane_factor(): return lax.ppermute(mine, ('tm', 'det'), pairs)  19.9 us
    ppermute x4, waiting for transfers between devices, swap(): lax.ppermute(value, axis, [(place, place ^ mask) for place in range(lax.a...  15.3 us
    pallas_call x7, Pallas kernels, call(): pl.pallas_call(kernel, out_shape=outs, in_specs=[pl.BlockSpec(memory_spac...  6.98 us
    ppermute x6, starting transfers between devices, rotate(): lax.ppermute(parts[step], 'tm', [(place, (place + step) % planes) for pla...  6.54 us
    all_to_all x1, starting transfers between devices, exchange(): lax.all_to_all(value, ('tm', 'det'), split_axis=0, concat_axis=0, tiled=T...  6.01 us
    all_to_all x1, waiting for transfers between devices, exchange(): lax.all_to_all(value, ('tm', 'det'), split_axis=0, concat_axis=0, tiled=T...  6 us
  transfers between devices with their start and end apart: 12, of which 10 were waited for; matrix products, arithmetic and copies ran while one was open for 0% of the time, Pallas kernels for 0%

profile of v6, /device:TPU:11, one launch (start us, length us, event | category | flops | bytes accessed | tf_op | source)
XLA Modules:
  0.0 123.0 jit_solution(15151111208606600777)
XLA Ops:
  0.0 1.3 %copy-done.1 = f32[64,4096]{1,0:T(8,128)S(1)} copy-done((f32[64,4096]{1,0:T(8,128)S(1)}, f32[64,4096]{1,0:T(8,128)}, u32[]{:S(2)}) %copy-start.1) | copy-done | bytes 1048600
  1.3 1.0 shard_map.55
  2.3 1.3 %collective-permute-start = (f32[16,4096]{1,0:T(8,128)}, f32[16,4096]{1,0:T(8,128)S(1)}, u32[]{:S(2)}, u32[]{:S(2)}) collective-permute-start(f32[16,4096]{1,0:T(8,128)} %get-tuple-element.24), channel_id=1, source_target_pairs={{0,8},{8,16},{16,24},{24,0},{1,9},{9,17},{17,25},{25,1},{2,10},{10... | collective-permute-start | bytes 786440 | tf_op jit(solution)/shard_map/ppermute | solution.py:249
  3.6 1.1 collective-permute-start.1
  4.7 1.4 %collective-permute-start.2 = (f32[16,4096]{1,0:T(8,128)}, f32[16,4096]{1,0:T(8,128)S(1)}, u32[]{:S(2)}, u32[]{:S(2)}) collective-permute-start(f32[16,4096]{1,0:T(8,128)} %get-tuple-element.26), channel_id=1, source_target_pairs={{0,24},{8,0},{16,8},{24,16},{1,25},{9,1},{17,9},{25,17},{2,26},{10... | collective-permute-start | bytes 786440 | tf_op jit(solution)/shard_map/ppermute | solution.py:249
  6.1 3.4 %collective-permute-start.3 = (f32[64,512]{1,0:T(8,128)S(1)}, f32[64,512]{1,0:T(8,128)S(1)}, u32[]{:S(2)}, u32[]{:S(2)}) collective-permute-start(f32[64,512]{1,0:T(8,128)S(1)} %dynamic-slice_bitcast_fusion), channel_id=1, source_target_pairs={{0,0},{1,24},{2,8},{3,16},{4,17},{5,9},{6,25},{7,1},{8,2},{9,26},{... | collective-permute-start | bytes 393224 | tf_op jit(solution)/shard_map/ppermute | solution.py:264
  9.7 19.9 %collective-permute-done.3 = f32[64,512]{1,0:T(8,128)S(1)} collective-permute-done((f32[64,512]{1,0:T(8,128)S(1)}, f32[64,512]{1,0:T(8,128)S(1)}, u32[]{:S(2)}, u32[]{:S(2)}) %collective-permute-start.3) | collective-permute-done | bytes 131104 | tf_op jit(solution)/shard_map/ppermute | solution.py:264
  29.9 2.3 %shard_map.57 = f32[4,8,1,4,16,128]{5,4,3,2,1,0:T(8,128)} custom-call(f32[16,4096]{1,0:T(8,128)S(1)} %get-tuple-element.27.refs_0_, f32[16,4096]{1,0:T(8,128)S(1)} %collective-permute-done.refs_1_, f32[16,4096]{1,0:T(8,128)S(1)} %collective-permute-done.1.refs_2_, f32[16,4096]{1,0:T(8,128)S(1)} %collective-permute-done.2.refs_3_, ...), custom_call_target="tpu_custom_call" | custom-call | flops 805306368 | bytes 3211264 | tf_op jit(solution)/shard_map/pallas_call | solution.py:222
  32.3 6.0 %all-to-all-start = ((f32[32,64,128]{2,1,0:T(8,128)}), f32[32,64,128]{2,1,0:T(8,128)S(1)}, u32[]{:S(2)}, u32[]{:S(2)}) async-start(f32[32,64,128]{2,1,0:T(8,128)} %bitcast.2), calls=%async_computation | async-start | bytes 2097152 | tf_op jit(solution)/shard_map/all_to_all | solution.py:317
  38.3 1.2 %collective-permute-start.6 = (f32[64,512]{1,0:T(8,128)S(1)}, f32[64,512]{1,0:T(8,128)S(1)}, u32[]{:S(2)}, u32[]{:S(2)}) collective-permute-start(f32[64,512]{1,0:T(8,128)S(1)} %copy-done.6), channel_id=1, source_target_pairs={{0,6},{1,7},{2,4},{3,5},{4,2},{5,3},{6,0},{7,1},{8,14},{9,15},{10,... | collective-permute-start | bytes 393224 | tf_op jit(solution)/shard_map/ppermute | solution.py:243
  39.8 1.2 collective-permute-start.4
  41.0 8.7 %collective-permute-done.6 = f32[64,512]{1,0:T(8,128)S(1)} collective-permute-done((f32[64,512]{1,0:T(8,128)S(1)}, f32[64,512]{1,0:T(8,128)S(1)}, u32[]{:S(2)}, u32[]{:S(2)}) %collective-permute-start.6) | collective-permute-done | bytes 131104 | tf_op jit(solution)/shard_map/ppermute | solution.py:243
  49.7 4.9 %collective-permute-done.5 = f32[64,512]{1,0:T(8,128)S(1)} collective-permute-done((f32[64,512]{1,0:T(8,128)S(1)}, f32[64,512]{1,0:T(8,128)S(1)}, u32[]{:S(2)}, u32[]{:S(2)}) %collective-permute-start.5) | collective-permute-done | bytes 131104 | tf_op jit(solution)/shard_map/ppermute | solution.py:243
  54.9 0.9 collective-permute-start.7
  55.9 1.5 %collective-permute-done.7 = f32[4,64,512]{2,1,0:T(8,128)S(1)} collective-permute-done((f32[4,64,512]{2,1,0:T(8,128)S(1)}, f32[4,64,512]{2,1,0:T(8,128)S(1)}, u32[]{:S(2)}, u32[]{:S(2)}) %collective-permute-start.7) | collective-permute-done | bytes 524320 | tf_op jit(solution)/shard_map/ppermute | solution.py:243
  57.6 6.0 %all-to-all-done = f32[32,64,128]{2,1,0:T(8,128)S(1)} async-done(((f32[32,64,128]{2,1,0:T(8,128)}), f32[32,64,128]{2,1,0:T(8,128)S(1)}, u32[]{:S(2)}, u32[]{:S(2)}) %all-to-all-start) | async-done | bytes 1048608 | tf_op jit(solution)/shard_map/all_to_all | solution.py:317
  63.6 0.8 shard_map.59
  64.4 29.7 %all_to_all.10 = f32[32,64,128]{2,1,0:T(8,128)S(1)} all-to-all(f32[32,64,128]{2,1,0:T(8,128)S(1)} %bitcast.17), channel_id=1, replica_groups=mesh['tm'=4,'det'=8] {'tm','det'}, dimensions={0} | all-to-all | bytes 2097152 | tf_op jit(solution)/shard_map/all_to_all | solution.py:317
  94.0 1.6 %shard_map.60 = (f32[16,4096]{1,0:T(8,128)S(1)}, f32[16,4096]{1,0:T(8,128)S(1)}, f32[16,4096]{1,0:T(8,128)S(1)}, f32[16,4096]{1,0:T(8,128)S(1)}) custom-call(f32[4,8,1,4,16,128]{5,4,3,2,1,0:T(8,128)S(1)} %bitcast.19, f32[2,32,256]{2,1,0:T(8,128)S(1)} %get-tuple-element.31.refs_4_.refs_1_, bf16[512,512]{1,0:T(8,128)(2,1)S(1)} %get-tuple-element.32.refs_5_.refs_2_, ...), custom_call_target="tpu_custom_call" | custom-call | flops 805306368 | bytes 3211264 | tf_op jit(solution)/shard_map/pallas_call | solution.py:222
  95.7 2.7 %collective-permute-start.9 = (f32[16,4096]{1,0:T(8,128)S(1)}, f32[16,4096]{1,0:T(8,128)S(1)}, u32[]{:S(2)}, u32[]{:S(2)}) collective-permute-start(f32[16,4096]{1,0:T(8,128)S(1)} %get-tuple-element.39), channel_id=1, source_target_pairs={{0,16},{8,24},{16,0},{24,8},{1,17},{9,25},{17,1},{25,9},{2,18},{10... | collective-permute-start | bytes 786440 | tf_op jit(solution)/shard_map/ppermute | solution.py:249
  98.3 5.4 %collective-permute-done.8.refs_1_ = f32[16,4096]{1,0:T(8,128)S(1)} collective-permute-done((f32[16,4096]{1,0:T(8,128)S(1)}, f32[16,4096]{1,0:T(8,128)S(1)}, u32[]{:S(2)}, u32[]{:S(2)}) %collective-permute-start.8) | collective-permute-done | bytes 262176 | tf_op jit(solution)/shard_map/ppermute | solution.py:249
  103.7 14.0 %collective-permute-done.9.refs_2_ = f32[16,4096]{1,0:T(8,128)S(1)} collective-permute-done((f32[16,4096]{1,0:T(8,128)S(1)}, f32[16,4096]{1,0:T(8,128)S(1)}, u32[]{:S(2)}, u32[]{:S(2)}) %collective-permute-start.9) | collective-permute-done | bytes 262176 | tf_op jit(solution)/shard_map/ppermute | solution.py:249
  117.7 4.4 %collective-permute-done.10.refs_3_ = f32[16,4096]{1,0:T(8,128)S(1)} collective-permute-done((f32[16,4096]{1,0:T(8,128)S(1)}, f32[16,4096]{1,0:T(8,128)S(1)}, u32[]{:S(2)}, u32[]{:S(2)}) %collective-permute-start.10) | collective-permute-done | bytes 262176 | tf_op jit(solution)/shard_map/ppermute | solution.py:249
  122.0 1.0 shard_map.61
  (29 shorter events, 1.3 us)
Async XLA Ops:
  0.0 6.1 %copy-start = (f32[1,128,512]{2,1,0:T(8,128)S(1)}, f32[1,128,512]{2,1,0:T(8,128)}, u32[]{:S(2)}) copy-start(f32[1,128,512]{2,1,0:T(8,128)} %param.6) | copy-start | bytes 786436
  0.0 1.3 %copy-start.1 = (f32[64,4096]{1,0:T(8,128)S(1)}, f32[64,4096]{1,0:T(8,128)}, u32[]{:S(2)}) copy-start(f32[64,4096]{1,0:T(8,128)} %param.5) | copy-start | bytes 3145732
  1.3 8.2 %copy-start.2 = (bf16[512,512]{1,0:T(8,128)(2,1)S(1)}, bf16[512,512]{1,0:T(8,128)(2,1)}, u32[]{:S(2)}) copy-start(bf16[512,512]{1,0:T(8,128)(2,1)} %constant.21.clone.refs_2_) | copy-start | bytes 1572868
  1.3 8.2 %copy-start.3 = (bf16[512,512]{1,0:T(8,128)(2,1)S(1)}, bf16[512,512]{1,0:T(8,128)(2,1)}, u32[]{:S(2)}) copy-start(bf16[512,512]{1,0:T(8,128)(2,1)} %constant.20.clone.refs_1_) | copy-start | bytes 1572868
  2.3 27.4 %collective-permute-start = (f32[16,4096]{1,0:T(8,128)}, f32[16,4096]{1,0:T(8,128)S(1)}, u32[]{:S(2)}, u32[]{:S(2)}) collective-permute-start(f32[16,4096]{1,0:T(8,128)} %get-tuple-element.24), channel_id=1, source_target_pairs={{0,8},{8,16},{16,24},{24,0},{1,9},{9,17},{17,25},{25,1},{2,10},{10... | collective-permute-start | bytes 786440 | tf_op jit(solution)/shard_map/ppermute | solution.py:249
  3.6 26.0 %collective-permute-start.1 = (f32[16,4096]{1,0:T(8,128)}, f32[16,4096]{1,0:T(8,128)S(1)}, u32[]{:S(2)}, u32[]{:S(2)}) collective-permute-start(f32[16,4096]{1,0:T(8,128)} %get-tuple-element.25), channel_id=1, source_target_pairs={{0,16},{8,24},{16,0},{24,8},{1,17},{9,25},{17,1},{25,9},{2,18},{10... | collective-permute-start | bytes 786440 | tf_op jit(solution)/shard_map/ppermute | solution.py:249
  4.7 25.2 %collective-permute-start.2 = (f32[16,4096]{1,0:T(8,128)}, f32[16,4096]{1,0:T(8,128)S(1)}, u32[]{:S(2)}, u32[]{:S(2)}) collective-permute-start(f32[16,4096]{1,0:T(8,128)} %get-tuple-element.26), channel_id=1, source_target_pairs={{0,24},{8,0},{16,8},{24,16},{1,25},{9,1},{17,9},{25,17},{2,26},{10... | collective-permute-start | bytes 786440 | tf_op jit(solution)/shard_map/ppermute | solution.py:249
  6.1 3.4 %copy-start.4 = (f32[2,32,256]{2,1,0:T(8,128)S(1)}, f32[2,32,256]{2,1,0:T(8,128)}, u32[]{:S(2)}) copy-start(f32[2,32,256]{2,1,0:T(8,128)} %constant.19.clone.refs_0_) | copy-start | bytes 196612
  6.1 23.5 %collective-permute-start.3 = (f32[64,512]{1,0:T(8,128)S(1)}, f32[64,512]{1,0:T(8,128)S(1)}, u32[]{:S(2)}, u32[]{:S(2)}) collective-permute-start(f32[64,512]{1,0:T(8,128)S(1)} %dynamic-slice_bitcast_fusion), channel_id=1, source_target_pairs={{0,0},{1,24},{2,8},{3,16},{4,17},{5,9},{6,25},{7,1},{8,2},{9,26},{... | collective-permute-start | bytes 393224 | tf_op jit(solution)/shard_map/ppermute | solution.py:264
  29.6 2.6 %copy-start.5 = (f32[64,512]{1,0:T(8,128)}, f32[64,512]{1,0:T(8,128)S(1)}, u32[]{:S(2)}) copy-start(f32[64,512]{1,0:T(8,128)S(1)} %collective-permute-done.3) | copy-start | bytes 393220
  32.3 6.0 %copy-start.6 = (f32[64,512]{1,0:T(8,128)S(1)}, f32[64,512]{1,0:T(8,128)}, u32[]{:S(2)}) copy-start(f32[64,512]{1,0:T(8,128)} %copy-done.5) | copy-start | bytes 393220
  32.3 31.3 %all-to-all-start = ((f32[32,64,128]{2,1,0:T(8,128)}), f32[32,64,128]{2,1,0:T(8,128)S(1)}, u32[]{:S(2)}, u32[]{:S(2)}) async-start(f32[32,64,128]{2,1,0:T(8,128)} %bitcast.2), calls=%async_computation | async-start | bytes 2097152 | tf_op jit(solution)/shard_map/all_to_all | solution.py:317
  38.3 11.4 %collective-permute-start.6 = (f32[64,512]{1,0:T(8,128)S(1)}, f32[64,512]{1,0:T(8,128)S(1)}, u32[]{:S(2)}, u32[]{:S(2)}) collective-permute-start(f32[64,512]{1,0:T(8,128)S(1)} %copy-done.6), channel_id=1, source_target_pairs={{0,6},{1,7},{2,4},{3,5},{4,2},{5,3},{6,0},{7,1},{8,14},{9,15},{10,... | collective-permute-start | bytes 393224 | tf_op jit(solution)/shard_map/ppermute | solution.py:243
  39.6 15.1 %collective-permute-start.5 = (f32[64,512]{1,0:T(8,128)S(1)}, f32[64,512]{1,0:T(8,128)S(1)}, u32[]{:S(2)}, u32[]{:S(2)}) collective-permute-start(f32[64,512]{1,0:T(8,128)S(1)} %copy-done.6), channel_id=1, source_target_pairs={{0,4},{1,5},{2,6},{3,7},{4,0},{5,1},{6,2},{7,3},{8,12},{9,13},{10,... | collective-permute-start | bytes 393224 | tf_op jit(solution)/shard_map/ppermute | solution.py:243
  39.8 15.1 %collective-permute-start.4 = (f32[64,512]{1,0:T(8,128)S(1)}, f32[64,512]{1,0:T(8,128)S(1)}, u32[]{:S(2)}, u32[]{:S(2)}) collective-permute-start(f32[64,512]{1,0:T(8,128)S(1)} %copy-done.6), channel_id=1, source_target_pairs={{0,2},{1,3},{2,0},{3,1},{4,6},{5,7},{6,4},{7,5},{8,10},{9,11},{10,... | collective-permute-start | bytes 393224 | tf_op jit(solution)/shard_map/ppermute | solution.py:243
  54.9 2.5 %collective-permute-start.7 = (f32[4,64,512]{2,1,0:T(8,128)S(1)}, f32[4,64,512]{2,1,0:T(8,128)S(1)}, u32[]{:S(2)}, u32[]{:S(2)}) collective-permute-start(f32[4,64,512]{2,1,0:T(8,128)S(1)} %pad_maximum_fusion), channel_id=1, source_target_pairs={{0,1},{1,0},{2,3},{3,2},{4,5},{5,4},{6,7},{7,6},{8,9},{9,8},{10,11... | collective-permute-start | bytes 1572872 | tf_op jit(solution)/shard_map/ppermute | solution.py:243
  95.6 8.1 %collective-permute-start.8 = (f32[16,4096]{1,0:T(8,128)S(1)}, f32[16,4096]{1,0:T(8,128)S(1)}, u32[]{:S(2)}, u32[]{:S(2)}) collective-permute-start(f32[16,4096]{1,0:T(8,128)S(1)} %get-tuple-element.38), channel_id=1, source_target_pairs={{0,8},{8,16},{16,24},{24,0},{1,9},{9,17},{17,25},{25,1},{2,10},{10... | collective-permute-start | bytes 786440 | tf_op jit(solution)/shard_map/ppermute | solution.py:249
  95.7 22.0 %collective-permute-start.9 = (f32[16,4096]{1,0:T(8,128)S(1)}, f32[16,4096]{1,0:T(8,128)S(1)}, u32[]{:S(2)}, u32[]{:S(2)}) collective-permute-start(f32[16,4096]{1,0:T(8,128)S(1)} %get-tuple-element.39), channel_id=1, source_target_pairs={{0,16},{8,24},{16,0},{24,8},{1,17},{9,25},{17,1},{25,9},{2,18},{10... | collective-permute-start | bytes 786440 | tf_op jit(solution)/shard_map/ppermute | solution.py:249
  98.3 23.7 %collective-permute-start.10 = (f32[16,4096]{1,0:T(8,128)S(1)}, f32[16,4096]{1,0:T(8,128)S(1)}, u32[]{:S(2)}, u32[]{:S(2)}) collective-permute-start(f32[16,4096]{1,0:T(8,128)S(1)} %get-tuple-element.40), channel_id=1, source_target_pairs={{0,24},{8,0},{16,8},{24,16},{1,25},{9,1},{17,9},{25,17},{2,26},{10... | collective-permute-start | bytes 786440 | tf_op jit(solution)/shard_map/ppermute | solution.py:249

commit v7 on v6

--- a/solution.py
+++ b/solution.py
@@ -90,19 +90,6 @@
             yield slice(row, row + step), lane
 
 
-def slice_kernel(chunk, noise_ref, *refs):
-    here = lax.axis_index("tm")
-    outs, sem = refs[:-1], refs[-1]
-    copies = [
-        pltpu.make_async_copy(noise_ref.at[lax.rem(here + step, noise_ref.shape[0]), chunk], out, sem.at[step])
-        for step, out in enumerate(outs)
-    ]
-    for copy in copies:
-        copy.start()
-    for copy in copies:
-        copy.wait()
-
-
 def hold_kernel(*refs):
     count = len(refs) // 2
     sem = refs[-1]
@@ -120,7 +107,7 @@
     _, dets, span = x_ref.shape
     _, groups, pieces, _, width = stage_ref.shape
     per = span // n2
-    for step, block in enumerate(blocks):
+    for step, block in enumerate(reversed(blocks)):
         x_ref[lax.rem(here + planes - step, planes)] = block[...]
     for rows, lane in tiles(dets, n2):
 
@@ -181,7 +168,7 @@
     out_ref, sem = refs[-2:]
     planes = out_ref.shape[0]
     copies = [
-        pltpu.make_async_copy(refs[step], out_ref.at[lax.rem(here + planes - step, planes), chunk], sem.at[step])
+        pltpu.make_async_copy(refs[planes - 1 - step], out_ref.at[lax.rem(here + planes - step, planes), chunk], sem.at[step])
         for step in range(planes)
     ]
     for copy in copies:
@@ -251,6 +238,17 @@
     ]
 
 
+def blocks_of(noise, chunk):
+    here, planes = lax.axis_index("tm"), lax.axis_size("tm")
+    parts = []
+    for step in [*range(1, planes), 0]:
+        place = (lax.rem(here + step, planes), chunk, 0, 0)
+        part = lax.dynamic_slice(noise, place, (1, 1, *noise.shape[2:]))[0, 0]
+        noise, part = lax.optimization_barrier((noise, part))
+        parts.append(part)
+    return parts[-1:] + parts[:-1]
+
+
 def plane_factor(factor, planes, groups):
     half = factor.shape[1] // 2
     upper = lax.axis_index("det") >= groups // 2
@@ -290,17 +288,16 @@
     layout = (planes, groups, chunks, pieces, dets, LANES)
     tables = (twiddles(n1, n2), *fourier_matrix(n2, planes))
 
+    share = plane_factor(factor, planes, groups)
     noise = noise.reshape(planes, chunks, dets, span)
     arrived = []
     for chunk in range(chunks):
-        parts = call(bind(slice_kernel, chunk), [block] * planes, [dma(planes)], 0, noise, spaces=[pltpu.HBM])
-        arrived.append(rotate(parts))
-    share = plane_factor(factor, planes, groups)
+        arrived.append(rotate(blocks_of(noise, chunk)))
     tables = call(
         hold_kernel, [array(*table.shape, dtype=table.dtype) for table in tables], [dma(len(tables))], 0, *tables,
         spaces=[pl.ANY] * len(tables),
     )
-    arrived, share = lax.optimization_barrier((arrived, share))
+    share, arrived = lax.optimization_barrier((share, [blocks[::-1] for blocks in arrived]))
     f_high, f_low = band_factor(share, groups)
     buffer = []
     for chunk in range(chunks):
@@ -330,7 +327,7 @@
         )
         parts = rotate(parts)
         result = call(
-            bind(place_kernel, chunk), [array(planes, chunks, dets, span)], [dma(planes)], 0, *parts, *result,
+            bind(place_kernel, chunk), [array(planes, chunks, dets, span)], [dma(planes)], 0, *parts[::-1], *result,
             spaces=[pl.ANY] * (planes + len(result)), out_space=pl.ANY, aliases={planes: 0} if result else None,
         )
     return result[0].reshape(rows, span)

time: 123 us -> 129 us (1.049)
  the two profiles are of different devices: /device:TPU:11 before, /device:TPU:0 now
where the time goes in v7:
time: 129 us; the launch traced here: 128 us
  waiting for transfers between devices  65.8 us (51%)
  blocking collectives  29.7 us (23%)
  starting transfers between devices  20.9 us (16%)
  Pallas kernels  6 us (5%)
  local copies, waits for them, and re-layouts  5.8 us (4%)
    ppermute x6, waiting for transfers between devices, rotate(): lax.ppermute(parts[step], 'tm', [(place, (place + step) % planes) for pla...  43.4 us
    all_to_all x1, blocking collectives, exchange(): lax.all_to_all(value, ('tm', 'det'), split_axis=0, concat_axis=0, tiled=T...  29.7 us
    ppermute x4, waiting for transfers between devices, swap(): lax.ppermute(value, axis, [(place, place ^ mask) for place in range(lax.a...  16.6 us
    ppermute x6, starting transfers between devices, rotate(): lax.ppermute(parts[step], 'tm', [(place, (place + step) % planes) for pla...  10.9 us
    pallas_call x6, Pallas kernels, call(): pl.pallas_call(kernel, out_shape=outs, in_specs=[pl.BlockSpec(memory_spac...  6 us
    all_to_all x1, waiting for transfers between devices, exchange(): lax.all_to_all(value, ('tm', 'det'), split_axis=0, concat_axis=0, tiled=T...  5.69 us
    all_to_all x1, starting transfers between devices, exchange(): lax.all_to_all(value, ('tm', 'det'), split_axis=0, concat_axis=0, tiled=T...  4.8 us
    squeeze x4, local copies, waits for them, and re-layouts, blocks_of(): part = lax.dynamic_slice(noise, place, (1, 1, *noise.shape[2:]))[0, 0]  4.1 us
  transfers between devices with their start and end apart: 12, of which 9 were waited for; matrix products, arithmetic and copies ran while one was open for 3% of the time, Pallas kernels for 0%

profile of v7, /device:TPU:0, one launch (start us, length us, event | category | flops | bytes accessed | tf_op | source)
XLA Modules:
  0.0 128.3 jit_solution(14172067987152472644)
XLA Ops:
  0.0 0.9 copy-done
  1.6 1.6 %collective-permute-start = (f32[64,512]{1,0:T(8,128)}, f32[64,512]{1,0:T(8,128)S(1)}, u32[]{:S(2)}, u32[]{:S(2)}) collective-permute-start(f32[64,512]{1,0:T(8,128)} %dynamic-slice_bitcast_fusion.4), channel_id=1, source_target_pairs={{0,0},{1,24},{2,8},{3,16},{4,17},{5,9},{6,25},{7,1},{8,2},{9,26},{... | collective-permute-start | bytes 393224 | tf_op jit(solution)/shard_map/ppermute | solution.py:262
  3.2 1.7 %dynamic-slice_bitcast_fusion.3 = f32[16,4096]{1,0:T(8,128)} fusion(f32[4,1,16,4096]{3,2,1,0:T(8,128)} %bitcast.32, s32[]{:T(128)S(6)} %select_n.18), kind=kLoop, calls=%fused_computation.4 | loop fusion | bytes 524292 | tf_op jit(solution)/shard_map/squeeze | solution.py:246
  4.8 1.7 %dynamic-slice_bitcast_fusion.2 = f32[16,4096]{1,0:T(8,128)} fusion(f32[4,1,16,4096]{3,2,1,0:T(8,128)} %bitcast.33, s32[]{:T(128)S(6)} %select_n.19), kind=kLoop, calls=%fused_computation.3 | loop fusion | bytes 524292 | tf_op jit(solution)/shard_map/squeeze | solution.py:246
  6.5 0.7 dynamic-slice_bitcast_fusion.1
  7.2 7.5 %collective-permute-start.1 = (f32[16,4096]{1,0:T(8,128)}, f32[16,4096]{1,0:T(8,128)S(1)}, u32[]{:S(2)}, u32[]{:S(2)}) collective-permute-start(f32[16,4096]{1,0:T(8,128)} %dynamic-slice_bitcast_fusion.1), channel_id=1, source_target_pairs={{0,24},{8,0},{16,8},{24,16},{1,25},{9,1},{17,9},{25,17},{2,26},{10... | collective-permute-start | bytes 786440 | tf_op jit(solution)/shard_map/ppermute | solution.py:236
  15.6 6.2 %collective-permute-done.1.refs_0_ = f32[16,4096]{1,0:T(8,128)S(1)} collective-permute-done((f32[16,4096]{1,0:T(8,128)}, f32[16,4096]{1,0:T(8,128)S(1)}, u32[]{:S(2)}, u32[]{:S(2)}) %collective-permute-start.1) | collective-permute-done | bytes 262176 | tf_op jit(solution)/shard_map/ppermute | solution.py:236
  21.8 14.6 %collective-permute-done.2.refs_1_ = f32[16,4096]{1,0:T(8,128)S(1)} collective-permute-done((f32[16,4096]{1,0:T(8,128)}, f32[16,4096]{1,0:T(8,128)S(1)}, u32[]{:S(2)}, u32[]{:S(2)}) %collective-permute-start.2) | collective-permute-done | bytes 262176 | tf_op jit(solution)/shard_map/ppermute | solution.py:236
  36.4 2.3 %shard_map.56 = f32[4,8,1,4,16,128]{5,4,3,2,1,0:T(8,128)} custom-call(f32[16,4096]{1,0:T(8,128)S(1)} %collective-permute-done.1.refs_0_, f32[16,4096]{1,0:T(8,128)S(1)} %collective-permute-done.2.refs_1_, f32[16,4096]{1,0:T(8,128)S(1)} %collective-permute-done.3.refs_2_, f32[16,4096]{1,0:T(8,128)S(1)} %dynamic-slice_bitcast_fusion.refs_3_, ...), custom_call_target="tpu_custom_call" | custom-call | flops 805306368 | bytes 3211264 | tf_op jit(solution)/shard_map/pallas_call | solution.py:209
  38.7 4.8 %all-to-all-start = ((f32[32,64,128]{2,1,0:T(8,128)}), f32[32,64,128]{2,1,0:T(8,128)S(1)}, u32[]{:S(2)}, u32[]{:S(2)}) async-start(f32[32,64,128]{2,1,0:T(8,128)} %bitcast.10), calls=%async_computation | async-start | bytes 2097152 | tf_op jit(solution)/shard_map/all_to_all | solution.py:314
  43.5 2.7 %collective-permute-start.6 = (f32[64,512]{1,0:T(8,128)S(1)}, f32[64,512]{1,0:T(8,128)S(1)}, u32[]{:S(2)}, u32[]{:S(2)}) collective-permute-start(f32[64,512]{1,0:T(8,128)S(1)} %collective-permute-done), channel_id=1, source_target_pairs={{0,6},{1,7},{2,4},{3,5},{4,2},{5,3},{6,0},{7,1},{8,14},{9,15},{10,... | collective-permute-start | bytes 393224 | tf_op jit(solution)/shard_map/ppermute | solution.py:230
  47.1 12.5 %collective-permute-done.6 = f32[64,512]{1,0:T(8,128)S(1)} collective-permute-done((f32[64,512]{1,0:T(8,128)S(1)}, f32[64,512]{1,0:T(8,128)S(1)}, u32[]{:S(2)}, u32[]{:S(2)}) %collective-permute-start.6) | collective-permute-done | bytes 131104 | tf_op jit(solution)/shard_map/ppermute | solution.py:230
  59.6 1.3 %collective-permute-done.5 = f32[64,512]{1,0:T(8,128)S(1)} collective-permute-done((f32[64,512]{1,0:T(8,128)S(1)}, f32[64,512]{1,0:T(8,128)S(1)}, u32[]{:S(2)}, u32[]{:S(2)}) %collective-permute-start.5) | collective-permute-done | bytes 131104 | tf_op jit(solution)/shard_map/ppermute | solution.py:230
  60.9 1.0 collective-permute-done.4
  62.1 1.8 %collective-permute-done.7 = f32[4,64,512]{2,1,0:T(8,128)S(1)} collective-permute-done((f32[4,64,512]{2,1,0:T(8,128)S(1)}, f32[4,64,512]{2,1,0:T(8,128)S(1)}, u32[]{:S(2)}, u32[]{:S(2)}) %collective-permute-start.7) | collective-permute-done | bytes 524320 | tf_op jit(solution)/shard_map/ppermute | solution.py:230
  64.1 5.7 %all-to-all-done = f32[32,64,128]{2,1,0:T(8,128)S(1)} async-done(((f32[32,64,128]{2,1,0:T(8,128)}), f32[32,64,128]{2,1,0:T(8,128)S(1)}, u32[]{:S(2)}, u32[]{:S(2)}) %all-to-all-start) | async-done | bytes 1048608 | tf_op jit(solution)/shard_map/all_to_all | solution.py:314
  69.8 0.8 shard_map.58
  70.6 29.7 %all_to_all.10 = f32[32,64,128]{2,1,0:T(8,128)S(1)} all-to-all(f32[32,64,128]{2,1,0:T(8,128)S(1)} %bitcast.30), channel_id=1, replica_groups=mesh['tm'=4,'det'=8] {'tm','det'}, dimensions={0} | all-to-all | bytes 2097152 | tf_op jit(solution)/shard_map/all_to_all | solution.py:314
  100.3 1.5 %shard_map.59 = (f32[16,4096]{1,0:T(8,128)S(1)}, f32[16,4096]{1,0:T(8,128)S(1)}, f32[16,4096]{1,0:T(8,128)S(1)}, f32[16,4096]{1,0:T(8,128)S(1)}) custom-call(f32[4,8,1,4,16,128]{5,4,3,2,1,0:T(8,128)S(1)} %bitcast.31, f32[2,32,256]{2,1,0:T(8,128)S(1)} %get-tuple-element.37.refs_4_.refs_1_, bf16[512,512]{1,0:T(8,128)(2,1)S(1)} %get-tuple-element.38.refs_5_.refs_2_, ...), custom_call_target="tpu_custom_call" | custom-call | flops 805306368 | bytes 3211264 | tf_op jit(solution)/shard_map/pallas_call | solution.py:209
  101.8 1.4 %collective-permute-start.8 = (f32[16,4096]{1,0:T(8,128)S(1)}, f32[16,4096]{1,0:T(8,128)S(1)}, u32[]{:S(2)}, u32[]{:S(2)}) collective-permute-start(f32[16,4096]{1,0:T(8,128)S(1)} %get-tuple-element.43), channel_id=1, source_target_pairs={{0,24},{8,0},{16,8},{24,16},{1,25},{9,1},{17,9},{25,17},{2,26},{10... | collective-permute-start | bytes 786440 | tf_op jit(solution)/shard_map/ppermute | solution.py:236
  103.2 0.9 collective-permute-start.9
  104.6 5.3 %collective-permute-done.8.refs_0_ = f32[16,4096]{1,0:T(8,128)S(1)} collective-permute-done((f32[16,4096]{1,0:T(8,128)S(1)}, f32[16,4096]{1,0:T(8,128)S(1)}, u32[]{:S(2)}, u32[]{:S(2)}) %collective-permute-start.8) | collective-permute-done | bytes 262176 | tf_op jit(solution)/shard_map/ppermute | solution.py:236
  110.0 17.3 %collective-permute-done.9.refs_1_ = f32[16,4096]{1,0:T(8,128)S(1)} collective-permute-done((f32[16,4096]{1,0:T(8,128)S(1)}, f32[16,4096]{1,0:T(8,128)S(1)}, u32[]{:S(2)}, u32[]{:S(2)}) %collective-permute-start.9) | collective-permute-done | bytes 262176 | tf_op jit(solution)/shard_map/ppermute | solution.py:236
  127.3 1.0 shard_map.60
  (28 shorter events, 3.1 us)
Async XLA Ops:
  0.0 1.0 copy-start
  0.0 6.5 %copy-start.4 = (f32[64,4096]{1,0:T(8,128)S(1)}, f32[64,4096]{1,0:T(8,128)}, u32[]{:S(2)}) copy-start(f32[64,4096]{1,0:T(8,128)} %param.5) | copy-start | bytes 3145732
  1.6 14.0 %collective-permute-start = (f32[64,512]{1,0:T(8,128)}, f32[64,512]{1,0:T(8,128)S(1)}, u32[]{:S(2)}, u32[]{:S(2)}) collective-permute-start(f32[64,512]{1,0:T(8,128)} %dynamic-slice_bitcast_fusion.4), channel_id=1, source_target_pairs={{0,0},{1,24},{2,8},{3,16},{4,17},{5,9},{6,25},{7,1},{8,2},{9,26},{... | collective-permute-start | bytes 393224 | tf_op jit(solution)/shard_map/ppermute | solution.py:262
  4.8 10.5 %copy-start.3 = (f32[2,32,256]{2,1,0:T(8,128)S(1)}, f32[2,32,256]{2,1,0:T(8,128)}, u32[]{:S(2)}) copy-start(f32[2,32,256]{2,1,0:T(8,128)} %constant.37.clone.refs_0_) | copy-start | bytes 196612
  6.5 8.9 %copy-start.1 = (bf16[512,512]{1,0:T(8,128)(2,1)S(1)}, bf16[512,512]{1,0:T(8,128)(2,1)}, u32[]{:S(2)}) copy-start(bf16[512,512]{1,0:T(8,128)(2,1)} %constant.39.clone.refs_2_) | copy-start | bytes 1572868
  6.5 8.9 %copy-start.2 = (bf16[512,512]{1,0:T(8,128)(2,1)S(1)}, bf16[512,512]{1,0:T(8,128)(2,1)}, u32[]{:S(2)}) copy-start(bf16[512,512]{1,0:T(8,128)(2,1)} %constant.38.clone.refs_1_) | copy-start | bytes 1572868
  7.2 14.6 %collective-permute-start.1 = (f32[16,4096]{1,0:T(8,128)}, f32[16,4096]{1,0:T(8,128)S(1)}, u32[]{:S(2)}, u32[]{:S(2)}) collective-permute-start(f32[16,4096]{1,0:T(8,128)} %dynamic-slice_bitcast_fusion.1), channel_id=1, source_target_pairs={{0,24},{8,0},{16,8},{24,16},{1,25},{9,1},{17,9},{25,17},{2,26},{10... | collective-permute-start | bytes 786440 | tf_op jit(solution)/shard_map/ppermute | solution.py:236
  14.8 21.6 %collective-permute-start.2 = (f32[16,4096]{1,0:T(8,128)}, f32[16,4096]{1,0:T(8,128)S(1)}, u32[]{:S(2)}, u32[]{:S(2)}) collective-permute-start(f32[16,4096]{1,0:T(8,128)} %dynamic-slice_bitcast_fusion.2), channel_id=1, source_target_pairs={{0,16},{8,24},{16,0},{24,8},{1,17},{9,25},{17,1},{25,9},{2,18},{10... | collective-permute-start | bytes 786440 | tf_op jit(solution)/shard_map/ppermute | solution.py:236
  14.8 21.6 %collective-permute-start.3 = (f32[16,4096]{1,0:T(8,128)}, f32[16,4096]{1,0:T(8,128)S(1)}, u32[]{:S(2)}, u32[]{:S(2)}) collective-permute-start(f32[16,4096]{1,0:T(8,128)} %dynamic-slice_bitcast_fusion.3), channel_id=1, source_target_pairs={{0,8},{8,16},{16,24},{24,0},{1,9},{9,17},{17,25},{25,1},{2,10},{10... | collective-permute-start | bytes 786440 | tf_op jit(solution)/shard_map/ppermute | solution.py:236
  38.7 31.0 %all-to-all-start = ((f32[32,64,128]{2,1,0:T(8,128)}), f32[32,64,128]{2,1,0:T(8,128)S(1)}, u32[]{:S(2)}, u32[]{:S(2)}) async-start(f32[32,64,128]{2,1,0:T(8,128)} %bitcast.10), calls=%async_computation | async-start | bytes 2097152 | tf_op jit(solution)/shard_map/all_to_all | solution.py:314
  43.5 16.0 %collective-permute-start.6 = (f32[64,512]{1,0:T(8,128)S(1)}, f32[64,512]{1,0:T(8,128)S(1)}, u32[]{:S(2)}, u32[]{:S(2)}) collective-permute-start(f32[64,512]{1,0:T(8,128)S(1)} %collective-permute-done), channel_id=1, source_target_pairs={{0,6},{1,7},{2,4},{3,5},{4,2},{5,3},{6,0},{7,1},{8,14},{9,15},{10,... | collective-permute-start | bytes 393224 | tf_op jit(solution)/shard_map/ppermute | solution.py:230
  46.3 14.6 %collective-permute-start.5 = (f32[64,512]{1,0:T(8,128)S(1)}, f32[64,512]{1,0:T(8,128)S(1)}, u32[]{:S(2)}, u32[]{:S(2)}) collective-permute-start(f32[64,512]{1,0:T(8,128)S(1)} %collective-permute-done), channel_id=1, source_target_pairs={{0,4},{1,5},{2,6},{3,7},{4,0},{5,1},{6,2},{7,3},{8,12},{9,13},{10,... | collective-permute-start | bytes 393224 | tf_op jit(solution)/shard_map/ppermute | solution.py:230
  46.8 15.1 %collective-permute-start.4 = (f32[64,512]{1,0:T(8,128)S(1)}, f32[64,512]{1,0:T(8,128)S(1)}, u32[]{:S(2)}, u32[]{:S(2)}) collective-permute-start(f32[64,512]{1,0:T(8,128)S(1)} %collective-permute-done), channel_id=1, source_target_pairs={{0,2},{1,3},{2,0},{3,1},{4,6},{5,7},{6,4},{7,5},{8,10},{9,11},{10,... | collective-permute-start | bytes 393224 | tf_op jit(solution)/shard_map/ppermute | solution.py:230
  61.9 2.0 %collective-permute-start.7 = (f32[4,64,512]{2,1,0:T(8,128)S(1)}, f32[4,64,512]{2,1,0:T(8,128)S(1)}, u32[]{:S(2)}, u32[]{:S(2)}) collective-permute-start(f32[4,64,512]{2,1,0:T(8,128)S(1)} %pad_maximum_fusion), channel_id=1, source_target_pairs={{0,1},{1,0},{2,3},{3,2},{4,5},{5,4},{6,7},{7,6},{8,9},{9,8},{10,11... | collective-permute-start | bytes 1572872 | tf_op jit(solution)/shard_map/ppermute | solution.py:230
  101.8 8.2 %collective-permute-start.8 = (f32[16,4096]{1,0:T(8,128)S(1)}, f32[16,4096]{1,0:T(8,128)S(1)}, u32[]{:S(2)}, u32[]{:S(2)}) collective-permute-start(f32[16,4096]{1,0:T(8,128)S(1)} %get-tuple-element.43), channel_id=1, source_target_pairs={{0,24},{8,0},{16,8},{24,16},{1,25},{9,1},{17,9},{25,17},{2,26},{10... | collective-permute-start | bytes 786440 | tf_op jit(solution)/shard_map/ppermute | solution.py:236
  103.2 24.1 %collective-permute-start.9 = (f32[16,4096]{1,0:T(8,128)S(1)}, f32[16,4096]{1,0:T(8,128)S(1)}, u32[]{:S(2)}, u32[]{:S(2)}) collective-permute-start(f32[16,4096]{1,0:T(8,128)S(1)} %get-tuple-element.44), channel_id=1, source_target_pairs={{0,16},{8,24},{16,0},{24,8},{1,17},{9,25},{17,1},{25,9},{2,18},{10... | collective-permute-start | bytes 786440 | tf_op jit(solution)/shard_map/ppermute | solution.py:236
  104.1 23.2 %collective-permute-start.10 = (f32[16,4096]{1,0:T(8,128)S(1)}, f32[16,4096]{1,0:T(8,128)S(1)}, u32[]{:S(2)}, u32[]{:S(2)}) collective-permute-start(f32[16,4096]{1,0:T(8,128)S(1)} %get-tuple-element.45), channel_id=1, source_target_pairs={{0,8},{8,16},{16,24},{24,0},{1,9},{9,17},{17,25},{25,1},{2,10},{10... | collective-permute-start | bytes 786440 | tf_op jit(solution)/shard_map/ppermute | solution.py:236

commit v8 on v6

--- a/solution.py
+++ b/solution.py
@@ -94,7 +94,7 @@
     here = lax.axis_index("tm")
     outs, sem = refs[:-1], refs[-1]
     copies = [
-        pltpu.make_async_copy(noise_ref.at[lax.rem(here + step, noise_ref.shape[0]), chunk], out, sem.at[step])
+        pltpu.make_async_copy(noise_ref.at[lax.rem(here + step, len(outs)), chunk], out, sem.at[step])
         for step, out in enumerate(outs)
     ]
     for copy in copies:
@@ -243,12 +243,13 @@
     return lax.ppermute(value, axis, [(place, place ^ mask) for place in range(lax.axis_size(axis))])
 
 
-def rotate(parts):
-    planes = len(parts)
-    return [parts[0]] + [
-        lax.ppermute(parts[step], "tm", [(place, (place + step) % planes) for place in range(planes)])
-        for step in range(1, planes)
-    ]
+def far_first(planes):
+    return sorted(range(1, planes), key=lambda step: abs(2 * step - planes))
+
+
+def rotate(part, step):
+    planes = lax.axis_size("tm")
+    return lax.ppermute(part, "tm", [(place, (place + step) % planes) for place in range(planes)])
 
 
 def plane_factor(factor, planes, groups):
@@ -293,14 +294,18 @@
     noise = noise.reshape(planes, chunks, dets, span)
     arrived = []
     for chunk in range(chunks):
-        parts = call(bind(slice_kernel, chunk), [block] * planes, [dma(planes)], 0, noise, spaces=[pltpu.HBM])
-        arrived.append(rotate(parts))
-    share = plane_factor(factor, planes, groups)
+        parts = call(bind(slice_kernel, chunk), [block] * planes, [dma(planes)], 0, noise, spaces=[pl.ANY])
+        parts = list(parts)
+        for at, step in enumerate(far_first(planes)):
+            parts[step] = rotate(parts[step], step)
+            if chunk == 0 and at == 0:
+                share = plane_factor(factor, planes, groups)
+        arrived.append(parts)
     tables = call(
         hold_kernel, [array(*table.shape, dtype=table.dtype) for table in tables], [dma(len(tables))], 0, *tables,
         spaces=[pl.ANY] * len(tables),
     )
-    arrived, share = lax.optimization_barrier((arrived, share))
+    share, arrived = lax.optimization_barrier((share, arrived))
     f_high, f_low = band_factor(share, groups)
     buffer = []
     for chunk in range(chunks):
@@ -328,7 +333,9 @@
         parts = call(
             bind(inverse_kernel, n1, n2, chunk), [block] * planes, [series, middle], flops, back, *tables
         )
-        parts = rotate(parts)
+        parts = list(parts)
+        for step in far_first(planes):
+            parts[step] = rotate(parts[step], step)
         result = call(
             bind(place_kernel, chunk), [array(planes, chunks, dets, span)], [dma(planes)], 0, *parts, *result,
             spaces=[pl.ANY] * (planes + len(result)), out_space=pl.ANY, aliases={planes: 0} if result else None,

time: 123 us -> 123 us (level)
  no operation moved by 1% of the time
where the time goes in v8:
time: 123 us
  waiting for transfers between devices  65.2 us (53%)
  blocking collectives  29.7 us (24%)
  starting transfers between devices  19.6 us (16%)
  Pallas kernels  6.98 us (6%)
  local copies, waits for them, and re-layouts  1.38 us (1%)
    all_to_all x1, blocking collectives, exchange(): lax.all_to_all(value, ('tm', 'det'), split_axis=0, concat_axis=0, tiled=T...  29.7 us
    ppermute x6, waiting for transfers between devices, rotate(): lax.ppermute(part, 'tm', [(place, (place + step) % planes) for place in r...  24 us
    ppermute x1, waiting for transfers between devices, plane_factor(): return lax.ppermute(mine, ('tm', 'det'), pairs)  19.9 us
    ppermute x4, waiting for transfers between devices, swap(): lax.ppermute(value, axis, [(place, place ^ mask) for place in range(lax.a...  15.3 us
    pallas_call x7, Pallas kernels, call(): pl.pallas_call(kernel, out_shape=outs, in_specs=[pl.BlockSpec(memory_spac...  6.98 us
    ppermute x6, starting transfers between devices, rotate(): lax.ppermute(part, 'tm', [(place, (place + step) % planes) for place in r...  6.54 us
    all_to_all x1, starting transfers between devices, exchange(): lax.all_to_all(value, ('tm', 'det'), split_axis=0, concat_axis=0, tiled=T...  6.01 us
    all_to_all x1, waiting for transfers between devices, exchange(): lax.all_to_all(value, ('tm', 'det'), split_axis=0, concat_axis=0, tiled=T...  6 us
  transfers between devices with their start and end apart: 12, of which 10 were waited for; matrix products, arithmetic and copies ran while one was open for 0% of the time, Pallas kernels for 0%

profile of v8, /device:TPU:11, one launch (start us, length us, event | category | flops | bytes accessed | tf_op | source)
XLA Modules:
  0.0 123.0 jit_solution(15151111208606600777)
XLA Ops:
  0.0 1.3 %copy-done.1 = f32[64,4096]{1,0:T(8,128)S(1)} copy-done((f32[64,4096]{1,0:T(8,128)S(1)}, f32[64,4096]{1,0:T(8,128)}, u32[]{:S(2)}) %copy-start.1) | copy-done | bytes 1048600
  1.3 1.0 shard_map.55
  2.3 1.3 %collective-permute-start.1 = (f32[16,4096]{1,0:T(8,128)}, f32[16,4096]{1,0:T(8,128)S(1)}, u32[]{:S(2)}, u32[]{:S(2)}) collective-permute-start(f32[16,4096]{1,0:T(8,128)} %get-tuple-element.24), channel_id=1, source_target_pairs={{0,8},{8,16},{16,24},{24,0},{1,9},{9,17},{17,25},{25,1},{2,10},{10... | collective-permute-start | bytes 786440 | tf_op jit(solution)/shard_map/ppermute | solution.py:252
  3.6 1.1 collective-permute-start.2
  4.7 1.4 %collective-permute-start.3 = (f32[16,4096]{1,0:T(8,128)}, f32[16,4096]{1,0:T(8,128)S(1)}, u32[]{:S(2)}, u32[]{:S(2)}) collective-permute-start(f32[16,4096]{1,0:T(8,128)} %get-tuple-element.26), channel_id=1, source_target_pairs={{0,24},{8,0},{16,8},{24,16},{1,25},{9,1},{17,9},{25,17},{2,26},{10... | collective-permute-start | bytes 786440 | tf_op jit(solution)/shard_map/ppermute | solution.py:252
  6.1 3.4 %collective-permute-start = (f32[64,512]{1,0:T(8,128)S(1)}, f32[64,512]{1,0:T(8,128)S(1)}, u32[]{:S(2)}, u32[]{:S(2)}) collective-permute-start(f32[64,512]{1,0:T(8,128)S(1)} %dynamic-slice_bitcast_fusion), channel_id=1, source_target_pairs={{0,0},{1,24},{2,8},{3,16},{4,17},{5,9},{6,25},{7,1},{8,2},{9,26},{... | collective-permute-start | bytes 393224 | tf_op jit(solution)/shard_map/ppermute | solution.py:265
  9.7 19.9 %collective-permute-done = f32[64,512]{1,0:T(8,128)S(1)} collective-permute-done((f32[64,512]{1,0:T(8,128)S(1)}, f32[64,512]{1,0:T(8,128)S(1)}, u32[]{:S(2)}, u32[]{:S(2)}) %collective-permute-start) | collective-permute-done | bytes 131104 | tf_op jit(solution)/shard_map/ppermute | solution.py:265
  29.9 2.3 %shard_map.57 = f32[4,8,1,4,16,128]{5,4,3,2,1,0:T(8,128)} custom-call(f32[16,4096]{1,0:T(8,128)S(1)} %get-tuple-element.27.refs_0_, f32[16,4096]{1,0:T(8,128)S(1)} %collective-permute-done.1.refs_1_, f32[16,4096]{1,0:T(8,128)S(1)} %collective-permute-done.2.refs_2_, f32[16,4096]{1,0:T(8,128)S(1)} %collective-permute-done.3.refs_3_, ...), custom_call_target="tpu_custom_call" | custom-call | flops 805306368 | bytes 3211264 | tf_op jit(solution)/shard_map/pallas_call | solution.py:222
  32.3 6.0 %all-to-all-start = ((f32[32,64,128]{2,1,0:T(8,128)}), f32[32,64,128]{2,1,0:T(8,128)S(1)}, u32[]{:S(2)}, u32[]{:S(2)}) async-start(f32[32,64,128]{2,1,0:T(8,128)} %bitcast.2), calls=%async_computation | async-start | bytes 2097152 | tf_op jit(solution)/shard_map/all_to_all | solution.py:322
  38.3 1.2 %collective-permute-start.6 = (f32[64,512]{1,0:T(8,128)S(1)}, f32[64,512]{1,0:T(8,128)S(1)}, u32[]{:S(2)}, u32[]{:S(2)}) collective-permute-start(f32[64,512]{1,0:T(8,128)S(1)} %copy-done.6), channel_id=1, source_target_pairs={{0,6},{1,7},{2,4},{3,5},{4,2},{5,3},{6,0},{7,1},{8,14},{9,15},{10,... | collective-permute-start | bytes 393224 | tf_op jit(solution)/shard_map/ppermute | solution.py:243
  39.8 1.2 collective-permute-start.4
  41.0 8.7 %collective-permute-done.6 = f32[64,512]{1,0:T(8,128)S(1)} collective-permute-done((f32[64,512]{1,0:T(8,128)S(1)}, f32[64,512]{1,0:T(8,128)S(1)}, u32[]{:S(2)}, u32[]{:S(2)}) %collective-permute-start.6) | collective-permute-done | bytes 131104 | tf_op jit(solution)/shard_map/ppermute | solution.py:243
  49.7 4.9 %collective-permute-done.5 = f32[64,512]{1,0:T(8,128)S(1)} collective-permute-done((f32[64,512]{1,0:T(8,128)S(1)}, f32[64,512]{1,0:T(8,128)S(1)}, u32[]{:S(2)}, u32[]{:S(2)}) %collective-permute-start.5) | collective-permute-done | bytes 131104 | tf_op jit(solution)/shard_map/ppermute | solution.py:243
  54.9 0.9 collective-permute-start.7
  55.9 1.5 %collective-permute-done.7 = f32[4,64,512]{2,1,0:T(8,128)S(1)} collective-permute-done((f32[4,64,512]{2,1,0:T(8,128)S(1)}, f32[4,64,512]{2,1,0:T(8,128)S(1)}, u32[]{:S(2)}, u32[]{:S(2)}) %collective-permute-start.7) | collective-permute-done | bytes 524320 | tf_op jit(solution)/shard_map/ppermute | solution.py:243
  57.6 6.0 %all-to-all-done = f32[32,64,128]{2,1,0:T(8,128)S(1)} async-done(((f32[32,64,128]{2,1,0:T(8,128)}), f32[32,64,128]{2,1,0:T(8,128)S(1)}, u32[]{:S(2)}, u32[]{:S(2)}) %all-to-all-start) | async-done | bytes 1048608 | tf_op jit(solution)/shard_map/all_to_all | solution.py:322
  63.6 0.8 shard_map.59
  64.4 29.7 %all_to_all.10 = f32[32,64,128]{2,1,0:T(8,128)S(1)} all-to-all(f32[32,64,128]{2,1,0:T(8,128)S(1)} %bitcast.17), channel_id=1, replica_groups=mesh['tm'=4,'det'=8] {'tm','det'}, dimensions={0} | all-to-all | bytes 2097152 | tf_op jit(solution)/shard_map/all_to_all | solution.py:322
  94.0 1.6 %shard_map.60 = (f32[16,4096]{1,0:T(8,128)S(1)}, f32[16,4096]{1,0:T(8,128)S(1)}, f32[16,4096]{1,0:T(8,128)S(1)}, f32[16,4096]{1,0:T(8,128)S(1)}) custom-call(f32[4,8,1,4,16,128]{5,4,3,2,1,0:T(8,128)S(1)} %bitcast.19, f32[2,32,256]{2,1,0:T(8,128)S(1)} %get-tuple-element.31.refs_4_.refs_1_, bf16[512,512]{1,0:T(8,128)(2,1)S(1)} %get-tuple-element.32.refs_5_.refs_2_, ...), custom_call_target="tpu_custom_call" | custom-call | flops 805306368 | bytes 3211264 | tf_op jit(solution)/shard_map/pallas_call | solution.py:222
  95.7 2.7 %collective-permute-start.9 = (f32[16,4096]{1,0:T(8,128)S(1)}, f32[16,4096]{1,0:T(8,128)S(1)}, u32[]{:S(2)}, u32[]{:S(2)}) collective-permute-start(f32[16,4096]{1,0:T(8,128)S(1)} %get-tuple-element.39), channel_id=1, source_target_pairs={{0,16},{8,24},{16,0},{24,8},{1,17},{9,25},{17,1},{25,9},{2,18},{10... | collective-permute-start | bytes 786440 | tf_op jit(solution)/shard_map/ppermute | solution.py:252
  98.3 5.4 %collective-permute-done.8.refs_1_ = f32[16,4096]{1,0:T(8,128)S(1)} collective-permute-done((f32[16,4096]{1,0:T(8,128)S(1)}, f32[16,4096]{1,0:T(8,128)S(1)}, u32[]{:S(2)}, u32[]{:S(2)}) %collective-permute-start.8) | collective-permute-done | bytes 262176 | tf_op jit(solution)/shard_map/ppermute | solution.py:252
  103.7 14.0 %collective-permute-done.9.refs_2_ = f32[16,4096]{1,0:T(8,128)S(1)} collective-permute-done((f32[16,4096]{1,0:T(8,128)S(1)}, f32[16,4096]{1,0:T(8,128)S(1)}, u32[]{:S(2)}, u32[]{:S(2)}) %collective-permute-start.9) | collective-permute-done | bytes 262176 | tf_op jit(solution)/shard_map/ppermute | solution.py:252
  117.7 4.4 %collective-permute-done.10.refs_3_ = f32[16,4096]{1,0:T(8,128)S(1)} collective-permute-done((f32[16,4096]{1,0:T(8,128)S(1)}, f32[16,4096]{1,0:T(8,128)S(1)}, u32[]{:S(2)}, u32[]{:S(2)}) %collective-permute-start.10) | collective-permute-done | bytes 262176 | tf_op jit(solution)/shard_map/ppermute | solution.py:252
  122.0 1.0 shard_map.61
  (29 shorter events, 1.3 us)
Async XLA Ops:
  0.0 6.1 %copy-start = (f32[1,128,512]{2,1,0:T(8,128)S(1)}, f32[1,128,512]{2,1,0:T(8,128)}, u32[]{:S(2)}) copy-start(f32[1,128,512]{2,1,0:T(8,128)} %param.6) | copy-start | bytes 786436
  0.0 1.3 %copy-start.1 = (f32[64,4096]{1,0:T(8,128)S(1)}, f32[64,4096]{1,0:T(8,128)}, u32[]{:S(2)}) copy-start(f32[64,4096]{1,0:T(8,128)} %param.5) | copy-start | bytes 3145732
  1.3 8.2 %copy-start.2 = (bf16[512,512]{1,0:T(8,128)(2,1)S(1)}, bf16[512,512]{1,0:T(8,128)(2,1)}, u32[]{:S(2)}) copy-start(bf16[512,512]{1,0:T(8,128)(2,1)} %constant.21.clone.refs_2_) | copy-start | bytes 1572868
  1.3 8.2 %copy-start.3 = (bf16[512,512]{1,0:T(8,128)(2,1)S(1)}, bf16[512,512]{1,0:T(8,128)(2,1)}, u32[]{:S(2)}) copy-start(bf16[512,512]{1,0:T(8,128)(2,1)} %constant.20.clone.refs_1_) | copy-start | bytes 1572868
  2.3 27.4 %collective-permute-start.1 = (f32[16,4096]{1,0:T(8,128)}, f32[16,4096]{1,0:T(8,128)S(1)}, u32[]{:S(2)}, u32[]{:S(2)}) collective-permute-start(f32[16,4096]{1,0:T(8,128)} %get-tuple-element.24), channel_id=1, source_target_pairs={{0,8},{8,16},{16,24},{24,0},{1,9},{9,17},{17,25},{25,1},{2,10},{10... | collective-permute-start | bytes 786440 | tf_op jit(solution)/shard_map/ppermute | solution.py:252
  3.6 26.0 %collective-permute-start.2 = (f32[16,4096]{1,0:T(8,128)}, f32[16,4096]{1,0:T(8,128)S(1)}, u32[]{:S(2)}, u32[]{:S(2)}) collective-permute-start(f32[16,4096]{1,0:T(8,128)} %get-tuple-element.25), channel_id=1, source_target_pairs={{0,16},{8,24},{16,0},{24,8},{1,17},{9,25},{17,1},{25,9},{2,18},{10... | collective-permute-start | bytes 786440 | tf_op jit(solution)/shard_map/ppermute | solution.py:252
  4.7 25.2 %collective-permute-start.3 = (f32[16,4096]{1,0:T(8,128)}, f32[16,4096]{1,0:T(8,128)S(1)}, u32[]{:S(2)}, u32[]{:S(2)}) collective-permute-start(f32[16,4096]{1,0:T(8,128)} %get-tuple-element.26), channel_id=1, source_target_pairs={{0,24},{8,0},{16,8},{24,16},{1,25},{9,1},{17,9},{25,17},{2,26},{10... | collective-permute-start | bytes 786440 | tf_op jit(solution)/shard_map/ppermute | solution.py:252
  6.1 3.4 %copy-start.4 = (f32[2,32,256]{2,1,0:T(8,128)S(1)}, f32[2,32,256]{2,1,0:T(8,128)}, u32[]{:S(2)}) copy-start(f32[2,32,256]{2,1,0:T(8,128)} %constant.19.clone.refs_0_) | copy-start | bytes 196612
  6.1 23.5 %collective-permute-start = (f32[64,512]{1,0:T(8,128)S(1)}, f32[64,512]{1,0:T(8,128)S(1)}, u32[]{:S(2)}, u32[]{:S(2)}) collective-permute-start(f32[64,512]{1,0:T(8,128)S(1)} %dynamic-slice_bitcast_fusion), channel_id=1, source_target_pairs={{0,0},{1,24},{2,8},{3,16},{4,17},{5,9},{6,25},{7,1},{8,2},{9,26},{... | collective-permute-start | bytes 393224 | tf_op jit(solution)/shard_map/ppermute | solution.py:265
  29.6 2.6 %copy-start.5 = (f32[64,512]{1,0:T(8,128)}, f32[64,512]{1,0:T(8,128)S(1)}, u32[]{:S(2)}) copy-start(f32[64,512]{1,0:T(8,128)S(1)} %collective-permute-done) | copy-start | bytes 393220
  32.3 6.0 %copy-start.6 = (f32[64,512]{1,0:T(8,128)S(1)}, f32[64,512]{1,0:T(8,128)}, u32[]{:S(2)}) copy-start(f32[64,512]{1,0:T(8,128)} %copy-done.5) | copy-start | bytes 393220
  32.3 31.3 %all-to-all-start = ((f32[32,64,128]{2,1,0:T(8,128)}), f32[32,64,128]{2,1,0:T(8,128)S(1)}, u32[]{:S(2)}, u32[]{:S(2)}) async-start(f32[32,64,128]{2,1,0:T(8,128)} %bitcast.2), calls=%async_computation | async-start | bytes 2097152 | tf_op jit(solution)/shard_map/all_to_all | solution.py:322
  38.3 11.4 %collective-permute-start.6 = (f32[64,512]{1,0:T(8,128)S(1)}, f32[64,512]{1,0:T(8,128)S(1)}, u32[]{:S(2)}, u32[]{:S(2)}) collective-permute-start(f32[64,512]{1,0:T(8,128)S(1)} %copy-done.6), channel_id=1, source_target_pairs={{0,6},{1,7},{2,4},{3,5},{4,2},{5,3},{6,0},{7,1},{8,14},{9,15},{10,... | collective-permute-start | bytes 393224 | tf_op jit(solution)/shard_map/ppermute | solution.py:243
  39.6 15.1 %collective-permute-start.5 = (f32[64,512]{1,0:T(8,128)S(1)}, f32[64,512]{1,0:T(8,128)S(1)}, u32[]{:S(2)}, u32[]{:S(2)}) collective-permute-start(f32[64,512]{1,0:T(8,128)S(1)} %copy-done.6), channel_id=1, source_target_pairs={{0,4},{1,5},{2,6},{3,7},{4,0},{5,1},{6,2},{7,3},{8,12},{9,13},{10,... | collective-permute-start | bytes 393224 | tf_op jit(solution)/shard_map/ppermute | solution.py:243
  39.8 15.1 %collective-permute-start.4 = (f32[64,512]{1,0:T(8,128)S(1)}, f32[64,512]{1,0:T(8,128)S(1)}, u32[]{:S(2)}, u32[]{:S(2)}) collective-permute-start(f32[64,512]{1,0:T(8,128)S(1)} %copy-done.6), channel_id=1, source_target_pairs={{0,2},{1,3},{2,0},{3,1},{4,6},{5,7},{6,4},{7,5},{8,10},{9,11},{10,... | collective-permute-start | bytes 393224 | tf_op jit(solution)/shard_map/ppermute | solution.py:243
  54.9 2.5 %collective-permute-start.7 = (f32[4,64,512]{2,1,0:T(8,128)S(1)}, f32[4,64,512]{2,1,0:T(8,128)S(1)}, u32[]{:S(2)}, u32[]{:S(2)}) collective-permute-start(f32[4,64,512]{2,1,0:T(8,128)S(1)} %pad_maximum_fusion), channel_id=1, source_target_pairs={{0,1},{1,0},{2,3},{3,2},{4,5},{5,4},{6,7},{7,6},{8,9},{9,8},{10,11... | collective-permute-start | bytes 1572872 | tf_op jit(solution)/shard_map/ppermute | solution.py:243
  95.6 8.1 %collective-permute-start.8 = (f32[16,4096]{1,0:T(8,128)S(1)}, f32[16,4096]{1,0:T(8,128)S(1)}, u32[]{:S(2)}, u32[]{:S(2)}) collective-permute-start(f32[16,4096]{1,0:T(8,128)S(1)} %get-tuple-element.38), channel_id=1, source_target_pairs={{0,8},{8,16},{16,24},{24,0},{1,9},{9,17},{17,25},{25,1},{2,10},{10... | collective-permute-start | bytes 786440 | tf_op jit(solution)/shard_map/ppermute | solution.py:252
  95.7 22.0 %collective-permute-start.9 = (f32[16,4096]{1,0:T(8,128)S(1)}, f32[16,4096]{1,0:T(8,128)S(1)}, u32[]{:S(2)}, u32[]{:S(2)}) collective-permute-start(f32[16,4096]{1,0:T(8,128)S(1)} %get-tuple-element.39), channel_id=1, source_target_pairs={{0,16},{8,24},{16,0},{24,8},{1,17},{9,25},{17,1},{25,9},{2,18},{10... | collective-permute-start | bytes 786440 | tf_op jit(solution)/shard_map/ppermute | solution.py:252
  98.3 23.7 %collective-permute-start.10 = (f32[16,4096]{1,0:T(8,128)S(1)}, f32[16,4096]{1,0:T(8,128)S(1)}, u32[]{:S(2)}, u32[]{:S(2)}) collective-permute-start(f32[16,4096]{1,0:T(8,128)S(1)} %get-tuple-element.40), channel_id=1, source_target_pairs={{0,24},{8,0},{16,8},{24,16},{1,25},{9,1},{17,9},{25,17},{2,26},{10... | collective-permute-start | bytes 786440 | tf_op jit(solution)/shard_map/ppermute | solution.py:252

commit v9 on v6

--- a/solution.py
+++ b/solution.py
@@ -12,7 +12,7 @@
 
 LANES = 128
 VMEM_LIMIT = 48 * 1024 * 1024
-CHUNKS = 1
+CHUNKS = 2
 
 
 def band_of(plane, planes):
@@ -94,7 +94,7 @@
     here = lax.axis_index("tm")
     outs, sem = refs[:-1], refs[-1]
     copies = [
-        pltpu.make_async_copy(noise_ref.at[lax.rem(here + step, noise_ref.shape[0]), chunk], out, sem.at[step])
+        pltpu.make_async_copy(noise_ref.at[lax.rem(here + step, len(outs)), chunk], out, sem.at[step])
         for step, out in enumerate(outs)
     ]
     for copy in copies:
@@ -120,7 +120,7 @@
     _, dets, span = x_ref.shape
     _, groups, pieces, _, width = stage_ref.shape
     per = span // n2
-    for step, block in enumerate(blocks):
+    for step, block in zip([*far_first(planes), 0], blocks):
         x_ref[lax.rem(here + planes - step, planes)] = block[...]
     for rows, lane in tiles(dets, n2):
 
@@ -181,8 +181,8 @@
     out_ref, sem = refs[-2:]
     planes = out_ref.shape[0]
     copies = [
-        pltpu.make_async_copy(refs[step], out_ref.at[lax.rem(here + planes - step, planes), chunk], sem.at[step])
-        for step in range(planes)
+        pltpu.make_async_copy(block, out_ref.at[lax.rem(here + planes - step, planes), chunk], sem.at[step])
+        for step, block in zip([*far_first(planes), 0], refs)
     ]
     for copy in copies:
         copy.start()
@@ -243,12 +243,16 @@
     return lax.ppermute(value, axis, [(place, place ^ mask) for place in range(lax.axis_size(axis))])
 
 
+def far_first(planes):
+    return sorted(range(1, planes), key=lambda step: abs(2 * step - planes))
+
+
 def rotate(parts):
     planes = len(parts)
-    return [parts[0]] + [
+    return [
         lax.ppermute(parts[step], "tm", [(place, (place + step) % planes) for place in range(planes)])
-        for step in range(1, planes)
-    ]
+        for step in far_first(planes)
+    ] + [parts[0]]
 
 
 def plane_factor(factor, planes, groups):
@@ -293,14 +297,13 @@
     noise = noise.reshape(planes, chunks, dets, span)
     arrived = []
     for chunk in range(chunks):
-        parts = call(bind(slice_kernel, chunk), [block] * planes, [dma(planes)], 0, noise, spaces=[pltpu.HBM])
+        parts = call(bind(slice_kernel, chunk), [block] * planes, [dma(planes)], 0, noise, spaces=[pl.ANY])
         arrived.append(rotate(parts))
-    share = plane_factor(factor, planes, groups)
     tables = call(
         hold_kernel, [array(*table.shape, dtype=table.dtype) for table in tables], [dma(len(tables))], 0, *tables,
         spaces=[pl.ANY] * len(tables),
     )
-    arrived, share = lax.optimization_barrier((arrived, share))
+    arrived[-1], share = lax.optimization_barrier((arrived[-1], plane_factor(factor, planes, groups)))
     f_high, f_low = band_factor(share, groups)
     buffer = []
     for chunk in range(chunks):

time: 123 us -> 125 us (1.016)
  the two profiles are of different devices: /device:TPU:11 before, /device:TPU:0 now
where the time goes in v9:
time: 125 us; the launch traced here: 124 us
  waiting for transfers between devices  55 us (44%)
  blocking collectives  29.7 us (24%)
  starting transfers between devices  27.8 us (22%)
  Pallas kernels  9.42 us (8%)
  local copies, waits for them, and re-layouts  2.28 us (2%)
    ppermute x12, waiting for transfers between devices, rotate(): lax.ppermute(parts[step], 'tm', [(place, (place + step) % planes) for pla...  32.7 us
    all_to_all x1, blocking collectives, exchange(): lax.all_to_all(value, ('tm', 'det'), split_axis=0, concat_axis=0, tiled=T...  29.7 us
    ppermute x12, starting transfers between devices, rotate(): lax.ppermute(parts[step], 'tm', [(place, (place + step) % planes) for pla...  18.1 us
    ppermute x4, waiting for transfers between devices, swap(): lax.ppermute(value, axis, [(place, place ^ mask) for place in range(lax.a...  16.6 us
    pallas_call x11, Pallas kernels, call(): pl.pallas_call(kernel, out_shape=outs, in_specs=[pl.BlockSpec(memory_spac...  9.42 us
    all_to_all x1, waiting for transfers between devices, exchange(): lax.all_to_all(value, ('tm', 'det'), split_axis=0, concat_axis=0, tiled=T...  5.68 us
    all_to_all x1, starting transfers between devices, exchange(): lax.all_to_all(value, ('tm', 'det'), split_axis=0, concat_axis=0, tiled=T...  5.34 us
    ppermute x4, starting transfers between devices, swap(): lax.ppermute(value, axis, [(place, place ^ mask) for place in range(lax.a...  3.62 us
  transfers between devices with their start and end apart: 18, of which 11 were waited for; matrix products, arithmetic and copies ran while one was open for 0% of the time, Pallas kernels for 3%

profile of v9, /device:TPU:0, one launch (start us, length us, event | category | flops | bytes accessed | tf_op | source)
XLA Modules:
  0.0 124.4 jit_solution(14768277005010197200)
XLA Ops:
  0.0 0.9 copy-done
  1.7 1.2 copy-done.1
  3.6 6.6 %collective-permute-start = (f32[8,4096]{1,0:T(8,128)S(1)}, f32[8,4096]{1,0:T(8,128)S(1)}, u32[]{:S(2)}, u32[]{:S(2)}) collective-permute-start(f32[8,4096]{1,0:T(8,128)S(1)} %get-tuple-element.31), channel_id=1, source_target_pairs={{0,16},{8,24},{16,0},{24,8},{1,17},{9,25},{17,1},{25,9},{2,18},{10... | collective-permute-start | bytes 393224 | tf_op jit(solution)/shard_map/ppermute | solution.py:253
  11.1 2.4 %collective-permute-start.1 = (f32[8,4096]{1,0:T(8,128)S(1)}, f32[8,4096]{1,0:T(8,128)S(1)}, u32[]{:S(2)}, u32[]{:S(2)}) collective-permute-start(f32[8,4096]{1,0:T(8,128)S(1)} %get-tuple-element.32), channel_id=1, source_target_pairs={{0,8},{8,16},{16,24},{24,0},{1,9},{9,17},{17,25},{25,1},{2,10},{10... | collective-permute-start | bytes 393224 | tf_op jit(solution)/shard_map/ppermute | solution.py:253
  13.4 2.3 %collective-permute-start.2 = (f32[8,4096]{1,0:T(8,128)S(1)}, f32[8,4096]{1,0:T(8,128)S(1)}, u32[]{:S(2)}, u32[]{:S(2)}) collective-permute-start(f32[8,4096]{1,0:T(8,128)S(1)} %get-tuple-element.33), channel_id=1, source_target_pairs={{0,24},{8,0},{16,8},{24,16},{1,25},{9,1},{17,9},{25,17},{2,26},{10... | collective-permute-start | bytes 393224 | tf_op jit(solution)/shard_map/ppermute | solution.py:253
  15.7 7.9 %collective-permute-done.refs_0_ = f32[8,4096]{1,0:T(8,128)S(1)} collective-permute-done((f32[8,4096]{1,0:T(8,128)S(1)}, f32[8,4096]{1,0:T(8,128)S(1)}, u32[]{:S(2)}, u32[]{:S(2)}) %collective-permute-start) | collective-permute-done | bytes 131104 | tf_op jit(solution)/shard_map/ppermute | solution.py:253
  24.7 5.4 %collective-permute-done.2.refs_2_ = f32[8,4096]{1,0:T(8,128)S(1)} collective-permute-done((f32[8,4096]{1,0:T(8,128)S(1)}, f32[8,4096]{1,0:T(8,128)S(1)}, u32[]{:S(2)}, u32[]{:S(2)}) %collective-permute-start.2) | collective-permute-done | bytes 131104 | tf_op jit(solution)/shard_map/ppermute | solution.py:253
  30.1 3.0 %collective-permute-done.6.refs_2_ = f32[8,4096]{1,0:T(8,128)S(1)} collective-permute-done((f32[8,4096]{1,0:T(8,128)S(1)}, f32[8,4096]{1,0:T(8,128)S(1)}, u32[]{:S(2)}, u32[]{:S(2)}) %collective-permute-start.6) | collective-permute-done | bytes 131104 | tf_op jit(solution)/shard_map/ppermute | solution.py:253
  33.1 1.8 %shard_map.58.refs_7_ = f32[4,8,2,4,8,128]{5,4,3,2,1,0:T(8,128)} custom-call(f32[8,4096]{1,0:T(8,128)S(1)} %collective-permute-done.4.refs_0_, f32[8,4096]{1,0:T(8,128)S(1)} %collective-permute-done.5.refs_1_, f32[8,4096]{1,0:T(8,128)S(1)} %collective-permute-done.6.refs_2_, f32[8,4096]{1,0:T(8,128)S(1)} %get-tuple-element.45.refs_3_, ...), custom_call_target="tpu_custom_call" | custom-call | flops 402653184 | bytes 2686976 | tf_op jit(solution)/shard_map/pallas_call | solution.py:222
  34.9 1.8 %shard_map.59 = f32[4,8,2,4,8,128]{5,4,3,2,1,0:T(8,128)} custom-call(f32[8,4096]{1,0:T(8,128)S(1)} %collective-permute-done.refs_0_, f32[8,4096]{1,0:T(8,128)S(1)} %collective-permute-done.1.refs_1_, f32[8,4096]{1,0:T(8,128)S(1)} %collective-permute-done.2.refs_2_, f32[8,4096]{1,0:T(8,128)S(1)} %get-tuple-element.38.refs_3_, ...), custom_call_target="tpu_custom_call", output_to_operand_aliasing={{}: (7, {})} | custom-call | flops 402653184 | bytes 3735552 | tf_op jit(solution)/shard_map/pallas_call | solution.py:222
  36.6 5.3 %all-to-all-start = ((f32[32,64,128]{2,1,0:T(8,128)}), f32[32,64,128]{2,1,0:T(8,128)S(1)}, u32[]{:S(2)}, u32[]{:S(2)}) async-start(f32[32,64,128]{2,1,0:T(8,128)} %bitcast.2), calls=%async_computation | async-start | bytes 2097152 | tf_op jit(solution)/shard_map/all_to_all | solution.py:320
  42.0 2.7 %collective-permute-start.9 = (f32[64,512]{1,0:T(8,128)S(1)}, f32[64,512]{1,0:T(8,128)S(1)}, u32[]{:S(2)}, u32[]{:S(2)}) collective-permute-start(f32[64,512]{1,0:T(8,128)S(1)} %collective-permute-done.3), channel_id=1, source_target_pairs={{0,6},{1,7},{2,4},{3,5},{4,2},{5,3},{6,0},{7,1},{8,14},{9,15},{10,... | collective-permute-start | bytes 393224 | tf_op jit(solution)/shard_map/ppermute | solution.py:243
  45.5 12.5 %collective-permute-done.9 = f32[64,512]{1,0:T(8,128)S(1)} collective-permute-done((f32[64,512]{1,0:T(8,128)S(1)}, f32[64,512]{1,0:T(8,128)S(1)}, u32[]{:S(2)}, u32[]{:S(2)}) %collective-permute-start.9) | collective-permute-done | bytes 131104 | tf_op jit(solution)/shard_map/ppermute | solution.py:243
  58.0 1.3 %collective-permute-done.8 = f32[64,512]{1,0:T(8,128)S(1)} collective-permute-done((f32[64,512]{1,0:T(8,128)S(1)}, f32[64,512]{1,0:T(8,128)S(1)}, u32[]{:S(2)}, u32[]{:S(2)}) %collective-permute-start.8) | collective-permute-done | bytes 131104 | tf_op jit(solution)/shard_map/ppermute | solution.py:243
  59.3 1.0 collective-permute-done.7
  60.5 1.8 %collective-permute-done.10 = f32[4,64,512]{2,1,0:T(8,128)S(1)} collective-permute-done((f32[4,64,512]{2,1,0:T(8,128)S(1)}, f32[4,64,512]{2,1,0:T(8,128)S(1)}, u32[]{:S(2)}, u32[]{:S(2)}) %collective-permute-start.10) | collective-permute-done | bytes 524320 | tf_op jit(solution)/shard_map/ppermute | solution.py:243
  62.5 5.7 %all-to-all-done = f32[32,64,128]{2,1,0:T(8,128)S(1)} async-done(((f32[32,64,128]{2,1,0:T(8,128)}), f32[32,64,128]{2,1,0:T(8,128)S(1)}, u32[]{:S(2)}, u32[]{:S(2)}) %all-to-all-start) | async-done | bytes 1048608 | tf_op jit(solution)/shard_map/all_to_all | solution.py:320
  69.0 29.7 %all_to_all.10 = f32[32,64,128]{2,1,0:T(8,128)S(1)} all-to-all(f32[32,64,128]{2,1,0:T(8,128)S(1)} %bitcast.19), channel_id=1, replica_groups=mesh['tm'=4,'det'=8] {'tm','det'}, dimensions={0} | all-to-all | bytes 2097152 | tf_op jit(solution)/shard_map/all_to_all | solution.py:320
  98.7 0.9 shard_map.63
  100.4 1.1 collective-permute-start.15
  101.5 2.7 %collective-permute-start.16 = (f32[8,4096]{1,0:T(8,128)S(1)}, f32[8,4096]{1,0:T(8,128)S(1)}, u32[]{:S(2)}, u32[]{:S(2)}) collective-permute-start(f32[8,4096]{1,0:T(8,128)S(1)} %get-tuple-element.55), channel_id=1, source_target_pairs={{0,24},{8,0},{16,8},{24,16},{1,25},{9,1},{17,9},{25,17},{2,26},{10... | collective-permute-start | bytes 393224 | tf_op jit(solution)/shard_map/ppermute | solution.py:253
  104.2 0.9 shard_map.62
  106.3 10.7 %collective-permute-done.14.refs_0_ = f32[8,4096]{1,0:T(8,128)S(1)} collective-permute-done((f32[8,4096]{1,0:T(8,128)S(1)}, f32[8,4096]{1,0:T(8,128)S(1)}, u32[]{:S(2)}, u32[]{:S(2)}) %collective-permute-start.14) | collective-permute-done | bytes 131104 | tf_op jit(solution)/shard_map/ppermute | solution.py:253
  117.9 5.4 %collective-permute-done.11.refs_0_ = f32[8,4096]{1,0:T(8,128)S(1)} collective-permute-done((f32[8,4096]{1,0:T(8,128)S(1)}, f32[8,4096]{1,0:T(8,128)S(1)}, u32[]{:S(2)}, u32[]{:S(2)}) %collective-permute-start.11) | collective-permute-done | bytes 131104 | tf_op jit(solution)/shard_map/ppermute | solution.py:253
  (41 shorter events, 9.1 us)
Async XLA Ops:
  0.0 1.0 copy-start
  1.0 14.8 %collective-permute-start.3 = (f32[64,512]{1,0:T(8,128)S(1)}, f32[64,512]{1,0:T(8,128)S(1)}, u32[]{:S(2)}, u32[]{:S(2)}) collective-permute-start(f32[64,512]{1,0:T(8,128)S(1)} %dynamic-slice_bitcast_fusion), channel_id=1, source_target_pairs={{0,0},{1,24},{2,8},{3,16},{4,17},{5,9},{6,25},{7,1},{8,2},{9,26},{... | collective-permute-start | bytes 393224 | tf_op jit(solution)/shard_map/ppermute | solution.py:268
  1.6 1.2 copy-start.1
  2.9 21.6 %copy-start.4 = (f32[2,32,256]{2,1,0:T(8,128)S(1)}, f32[2,32,256]{2,1,0:T(8,128)}, u32[]{:S(2)}) copy-start(f32[2,32,256]{2,1,0:T(8,128)} %constant.19.clone.refs_0_) | copy-start | bytes 196612
  3.6 20.9 %copy-start.2 = (bf16[512,512]{1,0:T(8,128)(2,1)S(1)}, bf16[512,512]{1,0:T(8,128)(2,1)}, u32[]{:S(2)}) copy-start(bf16[512,512]{1,0:T(8,128)(2,1)} %constant.21.clone.refs_2_) | copy-start | bytes 1572868
  3.6 20.9 %copy-start.3 = (bf16[512,512]{1,0:T(8,128)(2,1)S(1)}, bf16[512,512]{1,0:T(8,128)(2,1)}, u32[]{:S(2)}) copy-start(bf16[512,512]{1,0:T(8,128)(2,1)} %constant.20.clone.refs_1_) | copy-start | bytes 1572868
  3.6 20.0 %collective-permute-start = (f32[8,4096]{1,0:T(8,128)S(1)}, f32[8,4096]{1,0:T(8,128)S(1)}, u32[]{:S(2)}, u32[]{:S(2)}) collective-permute-start(f32[8,4096]{1,0:T(8,128)S(1)} %get-tuple-element.31), channel_id=1, source_target_pairs={{0,16},{8,24},{16,0},{24,8},{1,17},{9,25},{17,1},{25,9},{2,18},{10... | collective-permute-start | bytes 393224 | tf_op jit(solution)/shard_map/ppermute | solution.py:253
  10.9 19.2 %collective-permute-start.4 = (f32[8,4096]{1,0:T(8,128)S(1)}, f32[8,4096]{1,0:T(8,128)S(1)}, u32[]{:S(2)}, u32[]{:S(2)}) collective-permute-start(f32[8,4096]{1,0:T(8,128)S(1)} %get-tuple-element.42), channel_id=1, source_target_pairs={{0,16},{8,24},{16,0},{24,8},{1,17},{9,25},{17,1},{25,9},{2,18},{10... | collective-permute-start | bytes 393224 | tf_op jit(solution)/shard_map/ppermute | solution.py:253
  11.1 13.6 %collective-permute-start.1 = (f32[8,4096]{1,0:T(8,128)S(1)}, f32[8,4096]{1,0:T(8,128)S(1)}, u32[]{:S(2)}, u32[]{:S(2)}) collective-permute-start(f32[8,4096]{1,0:T(8,128)S(1)} %get-tuple-element.32), channel_id=1, source_target_pairs={{0,8},{8,16},{16,24},{24,0},{1,9},{9,17},{17,25},{25,1},{2,10},{10... | collective-permute-start | bytes 393224 | tf_op jit(solution)/shard_map/ppermute | solution.py:253
  13.4 16.6 %collective-permute-start.2 = (f32[8,4096]{1,0:T(8,128)S(1)}, f32[8,4096]{1,0:T(8,128)S(1)}, u32[]{:S(2)}, u32[]{:S(2)}) collective-permute-start(f32[8,4096]{1,0:T(8,128)S(1)} %get-tuple-element.33), channel_id=1, source_target_pairs={{0,24},{8,0},{16,8},{24,16},{1,25},{9,1},{17,9},{25,17},{2,26},{10... | collective-permute-start | bytes 393224 | tf_op jit(solution)/shard_map/ppermute | solution.py:253
  15.7 14.3 %collective-permute-start.5 = (f32[8,4096]{1,0:T(8,128)S(1)}, f32[8,4096]{1,0:T(8,128)S(1)}, u32[]{:S(2)}, u32[]{:S(2)}) collective-permute-start(f32[8,4096]{1,0:T(8,128)S(1)} %get-tuple-element.43), channel_id=1, source_target_pairs={{0,8},{8,16},{16,24},{24,0},{1,9},{9,17},{17,25},{25,1},{2,10},{10... | collective-permute-start | bytes 393224 | tf_op jit(solution)/shard_map/ppermute | solution.py:253
  23.6 9.5 %collective-permute-start.6 = (f32[8,4096]{1,0:T(8,128)S(1)}, f32[8,4096]{1,0:T(8,128)S(1)}, u32[]{:S(2)}, u32[]{:S(2)}) collective-permute-start(f32[8,4096]{1,0:T(8,128)S(1)} %get-tuple-element.44), channel_id=1, source_target_pairs={{0,24},{8,0},{16,8},{24,16},{1,25},{9,1},{17,9},{25,17},{2,26},{10... | collective-permute-start | bytes 393224 | tf_op jit(solution)/shard_map/ppermute | solution.py:253
  36.6 31.6 %all-to-all-start = ((f32[32,64,128]{2,1,0:T(8,128)}), f32[32,64,128]{2,1,0:T(8,128)S(1)}, u32[]{:S(2)}, u32[]{:S(2)}) async-start(f32[32,64,128]{2,1,0:T(8,128)} %bitcast.2), calls=%async_computation | async-start | bytes 2097152 | tf_op jit(solution)/shard_map/all_to_all | solution.py:320
  42.0 16.0 %collective-permute-start.9 = (f32[64,512]{1,0:T(8,128)S(1)}, f32[64,512]{1,0:T(8,128)S(1)}, u32[]{:S(2)}, u32[]{:S(2)}) collective-permute-start(f32[64,512]{1,0:T(8,128)S(1)} %collective-permute-done.3), channel_id=1, source_target_pairs={{0,6},{1,7},{2,4},{3,5},{4,2},{5,3},{6,0},{7,1},{8,14},{9,15},{10,... | collective-permute-start | bytes 393224 | tf_op jit(solution)/shard_map/ppermute | solution.py:243
  44.7 14.6 %collective-permute-start.8 = (f32[64,512]{1,0:T(8,128)S(1)}, f32[64,512]{1,0:T(8,128)S(1)}, u32[]{:S(2)}, u32[]{:S(2)}) collective-permute-start(f32[64,512]{1,0:T(8,128)S(1)} %collective-permute-done.3), channel_id=1, source_target_pairs={{0,4},{1,5},{2,6},{3,7},{4,0},{5,1},{6,2},{7,3},{8,12},{9,13},{10,... | collective-permute-start | bytes 393224 | tf_op jit(solution)/shard_map/ppermute | solution.py:243
  45.3 15.1 %collective-permute-start.7 = (f32[64,512]{1,0:T(8,128)S(1)}, f32[64,512]{1,0:T(8,128)S(1)}, u32[]{:S(2)}, u32[]{:S(2)}) collective-permute-start(f32[64,512]{1,0:T(8,128)S(1)} %collective-permute-done.3), channel_id=1, source_target_pairs={{0,2},{1,3},{2,0},{3,1},{4,6},{5,7},{6,4},{7,5},{8,10},{9,11},{10,... | collective-permute-start | bytes 393224 | tf_op jit(solution)/shard_map/ppermute | solution.py:243
  60.4 2.0 %collective-permute-start.10 = (f32[4,64,512]{2,1,0:T(8,128)S(1)}, f32[4,64,512]{2,1,0:T(8,128)S(1)}, u32[]{:S(2)}, u32[]{:S(2)}) collective-permute-start(f32[4,64,512]{2,1,0:T(8,128)S(1)} %pad_maximum_fusion), channel_id=1, source_target_pairs={{0,1},{1,0},{2,3},{3,2},{4,5},{5,4},{6,7},{7,6},{8,9},{9,8},{10,11... | collective-permute-start | bytes 1572872 | tf_op jit(solution)/shard_map/ppermute | solution.py:243
  99.6 17.5 %collective-permute-start.14 = (f32[8,4096]{1,0:T(8,128)S(1)}, f32[8,4096]{1,0:T(8,128)S(1)}, u32[]{:S(2)}, u32[]{:S(2)}) collective-permute-start(f32[8,4096]{1,0:T(8,128)S(1)} %get-tuple-element.53), channel_id=1, source_target_pairs={{0,16},{8,24},{16,0},{24,8},{1,17},{9,25},{17,1},{25,9},{2,18},{10... | collective-permute-start | bytes 393224 | tf_op jit(solution)/shard_map/ppermute | solution.py:253
  100.4 16.7 %collective-permute-start.15 = (f32[8,4096]{1,0:T(8,128)S(1)}, f32[8,4096]{1,0:T(8,128)S(1)}, u32[]{:S(2)}, u32[]{:S(2)}) collective-permute-start(f32[8,4096]{1,0:T(8,128)S(1)} %get-tuple-element.54), channel_id=1, source_target_pairs={{0,8},{8,16},{16,24},{24,0},{1,9},{9,17},{17,25},{25,1},{2,10},{10... | collective-permute-start | bytes 393224 | tf_op jit(solution)/shard_map/ppermute | solution.py:253
  101.5 15.5 %collective-permute-start.16 = (f32[8,4096]{1,0:T(8,128)S(1)}, f32[8,4096]{1,0:T(8,128)S(1)}, u32[]{:S(2)}, u32[]{:S(2)}) collective-permute-start(f32[8,4096]{1,0:T(8,128)S(1)} %get-tuple-element.55), channel_id=1, source_target_pairs={{0,24},{8,0},{16,8},{24,16},{1,25},{9,1},{17,9},{25,17},{2,26},{10... | collective-permute-start | bytes 393224 | tf_op jit(solution)/shard_map/ppermute | solution.py:253
  105.1 18.2 %collective-permute-start.11 = (f32[8,4096]{1,0:T(8,128)S(1)}, f32[8,4096]{1,0:T(8,128)S(1)}, u32[]{:S(2)}, u32[]{:S(2)}) collective-permute-start(f32[8,4096]{1,0:T(8,128)S(1)} %get-tuple-element.49), channel_id=1, source_target_pairs={{0,16},{8,24},{16,0},{24,8},{1,17},{9,25},{17,1},{25,9},{2,18},{10... | collective-permute-start | bytes 393224 | tf_op jit(solution)/shard_map/ppermute | solution.py:253
  105.5 17.8 %collective-permute-start.12 = (f32[8,4096]{1,0:T(8,128)S(1)}, f32[8,4096]{1,0:T(8,128)S(1)}, u32[]{:S(2)}, u32[]{:S(2)}) collective-permute-start(f32[8,4096]{1,0:T(8,128)S(1)} %get-tuple-element.50), channel_id=1, source_target_pairs={{0,8},{8,16},{16,24},{24,0},{1,9},{9,17},{17,25},{25,1},{2,10},{10... | collective-permute-start | bytes 393224 | tf_op jit(solution)/shard_map/ppermute | solution.py:253
  117.0 6.5 %collective-permute-start.13 = (f32[8,4096]{1,0:T(8,128)S(1)}, f32[8,4096]{1,0:T(8,128)S(1)}, u32[]{:S(2)}, u32[]{:S(2)}) collective-permute-start(f32[8,4096]{1,0:T(8,128)S(1)} %get-tuple-element.51), channel_id=1, source_target_pairs={{0,24},{8,0},{16,8},{24,16},{1,25},{9,1},{17,9},{25,17},{2,26},{10... | collective-permute-start | bytes 393224 | tf_op jit(solution)/shard_map/ppermute | solution.py:253

commit v10 on v9

--- a/solution.py
+++ b/solution.py
@@ -12,6 +12,7 @@
 
 LANES = 128
 VMEM_LIMIT = 48 * 1024 * 1024
+VMEM_ALL = 63 * 1024 * 1024
 CHUNKS = 2
 
 
@@ -80,7 +81,9 @@
     def dot(a, b):
         return lax.dot_general(a, b, (contract, ((), ())), preferred_element_type=jnp.float32)
 
-    return dot(left[0], right[0]) + (dot(left[0], right[1]) + dot(left[1], right[0]))
+    rows = left[0].shape[0]
+    both = dot(jnp.concatenate(left), right[0])
+    return both[:rows] + (both[rows:] + dot(left[0], right[1]))
 
 
 def tiles(rows, lanes):
@@ -135,16 +138,17 @@
             place = slice(k1 * dets + rows.start, k1 * dets + rows.stop)
             mid_ref[place, lane : lane + LANES] = re * cosine + im * sine
             mid_ref[place, n2 + lane : n2 + lane + LANES] = im * cosine - re * sine
+    halves = split(mid_ref[...])
     copies = []
-    share = groups // 2
+    share = planes // 2
     for part in range(2):
-        count = share * pieces * dets
-        spectrum = product(split(mid_ref[part * count : (part + 1) * count]), (high_ref[...], low_ref[...]))
+        columns = slice(part * share * width, (part + 1) * share * width)
+        spectrum = product(halves, (high_ref[:, columns], low_ref[:, columns]))
         these = pl.ds(part * share, share)
-        for plane in range(planes):
+        for plane in range(share):
             value = spectrum[:, plane * width : (plane + 1) * width]
-            stage_ref[plane, these] = value.reshape(share, pieces, dets, width)
-        copies.append(pltpu.make_async_copy(stage_ref.at[:, these], out_ref.at[:, these, chunk], sem.at[part]))
+            stage_ref[part * share + plane] = value.reshape(groups, pieces, dets, width)
+        copies.append(pltpu.make_async_copy(stage_ref.at[these], out_ref.at[these, :, chunk], sem.at[part]))
         copies[-1].start()
     for copy in copies:
         copy.wait()
@@ -176,13 +180,13 @@
         out[...] = x_ref[lax.rem(here + step, planes)]
 
 
-def place_kernel(chunk, *refs):
+def place_kernel(chunk, steps, *refs):
     here = lax.axis_index("tm")
     out_ref, sem = refs[-2:]
     planes = out_ref.shape[0]
     copies = [
-        pltpu.make_async_copy(block, out_ref.at[lax.rem(here + planes - step, planes), chunk], sem.at[step])
-        for step, block in zip([*far_first(planes), 0], refs)
+        pltpu.make_async_copy(block, out_ref.at[lax.rem(here + planes - step, planes), chunk], sem.at[at])
+        for at, (step, block) in enumerate(zip(steps, refs))
     ]
     for copy in copies:
         copy.start()
@@ -199,7 +203,7 @@
         high_ref[place], low_ref[place] = split(factor_ref[share])
 
 
-def mix_kernel(x_ref, f_high, f_low, out_ref, x_mid, y_mid):
+def mix_kernel(x_ref, f_high, f_low, out_ref, x_mid, y_mid, stage_ref, sem):
     planes, groups, chunks, pieces, dets, width = x_ref.shape
     places = []
     for plane, group, chunk, piece in np.ndindex(planes, groups, chunks, pieces):
@@ -209,14 +213,22 @@
     for source, target in places:
         x_mid[target] = x_ref[source]
     x_high, x_low = split(x_mid[...])
-    half = f_high.shape[0] // 2
-    y_mid[:half] = product((f_high[:half, :half], f_low[:half, :half]), (x_high[:half], x_low[:half]))
-    y_mid[half:] = product((f_high[half:, :], f_low[half:, :]), (x_high, x_low))
-    for target, source in places:
-        out_ref[target] = y_mid[source]
-
-
-def call(kernel, outs, scratch, flops, *args, spaces=None, out_space=pltpu.VMEM, aliases=None):
+    half, share = f_high.shape[0] // 2, groups // 2
+    copies = []
+    for part in range(2):
+        rows, reach = slice(part * half, (part + 1) * half), (part + 1) * half
+        y_mid[rows] = product((f_high[rows, :reach], f_low[rows, :reach]), (x_high[:reach], x_low[:reach]))
+        for target, source in places:
+            if target[1] // share == part:
+                stage_ref[target] = y_mid[source]
+        these = pl.ds(part * share, share)
+        copies.append(pltpu.make_async_copy(stage_ref.at[:, these], out_ref.at[:, these], sem.at[part]))
+        copies[-1].start()
+    for copy in copies:
+        copy.wait()
+
+
+def call(kernel, outs, scratch, flops, *args, spaces=None, out_space=pltpu.VMEM, aliases=None, limit=VMEM_LIMIT):
     spaces = spaces or [pltpu.VMEM] * len(args)
     count = sum(math.prod(arg.shape) * arg.dtype.itemsize for arg in (*args, *outs))
     return pl.pallas_call(
@@ -225,7 +237,7 @@
         in_specs=[pl.BlockSpec(memory_space=space) for space in spaces],
         out_specs=[pl.BlockSpec(memory_space=out_space)] * len(outs),
         scratch_shapes=[pltpu.VMEM(item, jnp.float32) if isinstance(item, tuple) else item for item in scratch],
-        compiler_params=pltpu.CompilerParams(vmem_limit_bytes=VMEM_LIMIT),
+        compiler_params=pltpu.CompilerParams(vmem_limit_bytes=limit),
         cost_estimate=pl.CostEstimate(flops=flops, bytes_accessed=count, transcendentals=0),
         input_output_aliases=aliases or {},
     )(*args)
@@ -274,6 +286,11 @@
     share = jnp.concatenate([share, swap(share, "det", 1)])
     whole = array(groups * rows, columns, dtype=jnp.bfloat16)
     return call(factor_kernel, [whole, whole], [], 0, share)
+
+
+def hold(tables):
+    outs = [array(*table.shape, dtype=table.dtype) for table in tables]
+    return call(hold_kernel, outs, [dma(len(tables))], 0, *tables, spaces=[pl.ANY] * len(tables))
 
 
 def bind(kernel, *static):
@@ -297,12 +314,13 @@
     noise = noise.reshape(planes, chunks, dets, span)
     arrived = []
     for chunk in range(chunks):
-        parts = call(bind(slice_kernel, chunk), [block] * planes, [dma(planes)], 0, noise, spaces=[pl.ANY])
+        parts = call(
+            bind(slice_kernel, chunk), [block] * planes, [dma(planes)], 0, noise, spaces=[pl.ANY], out_space=pl.ANY,
+            limit=VMEM_ALL,
+        )
         arrived.append(rotate(parts))
-    tables = call(
-        hold_kernel, [array(*table.shape, dtype=table.dtype) for table in tables], [dma(len(tables))], 0, *tables,
-        spaces=[pl.ANY] * len(tables),
-    )
+    tables = hold(tables)
+    arrived[0][0], factor = lax.optimization_barrier((arrived[0][0], factor))
     arrived[-1], share = lax.optimization_barrier((arrived[-1], plane_factor(factor, planes, groups)))
     f_high, f_low = band_factor(share, groups)
     buffer = []
@@ -321,10 +339,12 @@
 
     count = f_high.shape[0]
     (mixed,) = call(
-        mix_kernel, [array(*layout)], [(count, pieces * LANES)] * 2,
+        mix_kernel, [array(*layout)], [(count, pieces * LANES)] * 2 + [layout, dma(2)],
         2 * 3 * count * count * pieces * LANES,
-        exchange(buffer[0]), f_high, f_low,
+        exchange(buffer[0]), f_high, f_low, out_space=pl.ANY,
     )
+    mixed, tables = lax.optimization_barrier((mixed, tables))
+    tables = hold(tables)
     back = exchange(mixed)
     result = []
     for chunk in range(chunks):
@@ -332,10 +352,15 @@
             bind(inverse_kernel, n1, n2, chunk), [block] * planes, [series, middle], flops, back, *tables
         )
         parts = rotate(parts)
-        result = call(
-            bind(place_kernel, chunk), [array(planes, chunks, dets, span)], [dma(planes)], 0, *parts, *result,
-            spaces=[pl.ANY] * (planes + len(result)), out_space=pl.ANY, aliases={planes: 0} if result else None,
-        )
+        pairs = list(zip([*far_first(planes), 0], parts))
+        pairs = [pairs[-1], *pairs[:-1]]
+        for group in [pairs] if chunk < chunks - 1 else [pairs[:-1], pairs[-1:]]:
+            steps, blocks = zip(*group)
+            result = call(
+                bind(place_kernel, chunk, steps), [array(planes, chunks, dets, span)], [dma(len(steps))], 0,
+                *blocks, *result, spaces=[pl.ANY] * (len(steps) + len(result)), out_space=pl.ANY,
+                aliases={len(steps): 0} if result else None,
+            )
     return result[0].reshape(rows, span)
 
 

time: 125 us -> 147 us (1.18)
  Pallas kernels: 9.42 us -> 44.4 us
  blocking collectives: 29.7 us -> 0 us
  waiting for transfers between devices: 55 us -> 66.6 us
  starting transfers between devices: 27.8 us -> 33.1 us
    pallas_call x11 -> x13, Pallas kernels: 9.42 us -> 44.4 us  [call(): pl.pallas_call(kernel, out_shape=outs, in_specs=[pl.BlockSpec(memory_spac...]
    all_to_all x1 -> x0, blocking collectives: 29.7 us -> none  [exchange(): lax.all_to_all(value, ('tm', 'det'), split_axis=0, concat_axis=0, tiled=T...]
    all_to_all x1 -> x2, waiting for transfers between devices: 5.68 us -> 31.7 us  [exchange(): lax.all_to_all(value, ('tm', 'det'), split_axis=0, concat_axis=0, tiled=T...]
    ppermute x12, waiting for transfers between devices: 32.7 us -> 18.3 us  [rotate(): lax.ppermute(parts[step], 'tm', [(place, (place + step) % planes) for pla...]
    all_to_all x1 -> x2, starting transfers between devices: 5.34 us -> 10.9 us  [exchange(): lax.all_to_all(value, ('tm', 'det'), split_axis=0, concat_axis=0, tiled=T...]
  transfers between devices with their start and end apart: 18 -> 19, of which waited for: 11 -> 10; matrix products, arithmetic and copies ran while one was open for 0% -> 0% of each run, Pallas kernels for 3% -> 15%
where the time goes in v10:
time: 147 us; the launch traced here: 146 us
  waiting for transfers between devices  66.6 us (45%)
  Pallas kernels  44.4 us (30%)
  starting transfers between devices  33.1 us (23%)
  local copies, waits for them, and re-layouts  1.86 us (1%)
    pallas_call x13, Pallas kernels, call(): pl.pallas_call(kernel, out_shape=outs, in_specs=[pl.BlockSpec(memory_spac...  44.4 us
    all_to_all x2, waiting for transfers between devices, exchange(): lax.all_to_all(value, ('tm', 'det'), split_axis=0, concat_axis=0, tiled=T...  31.7 us
    ppermute x12, waiting for transfers between devices, rotate(): lax.ppermute(parts[step], 'tm', [(place, (place + step) % planes) for pla...  18.3 us
    ppermute x12, starting transfers between devices, rotate(): lax.ppermute(parts[step], 'tm', [(place, (place + step) % planes) for pla...  17.7 us
    ppermute x4, waiting for transfers between devices, swap(): lax.ppermute(value, axis, [(place, place ^ mask) for place in range(lax.a...  16.6 us
    all_to_all x2, starting transfers between devices, exchange(): lax.all_to_all(value, ('tm', 'det'), split_axis=0, concat_axis=0, tiled=T...  10.9 us
    ppermute x4, starting transfers between devices, swap(): lax.ppermute(value, axis, [(place, place ^ mask) for place in range(lax.a...  3.62 us
  transfers between devices with their start and end apart: 19, of which 10 were waited for; matrix products, arithmetic and copies ran while one was open for 0% of the time, Pallas kernels for 15%

profile of v10, /device:TPU:0, one launch (start us, length us, event | category | flops | bytes accessed | tf_op | source)
XLA Modules:
  0.0 146.3 jit_solution(2495585176315601609)
XLA Ops:
  0.0 17.0 %shard_map.56 = (f32[8,4096]{1,0:T(8,128)}, f32[8,4096]{1,0:T(8,128)}, f32[8,4096]{1,0:T(8,128)}, f32[8,4096]{1,0:T(8,128)}) custom-call(f32[4,2,8,4096]{3,2,1,0:T(8,128)} %bitcast.19), custom_call_target="tpu_custom_call" | custom-call | bytes 1572864 | tf_op jit(solution)/shard_map/pallas_call | solution.py:234
  17.0 4.1 %collective-permute-start.3 = (f32[8,4096]{1,0:T(8,128)}, f32[8,4096]{1,0:T(8,128)S(1)}, u32[]{:S(2)}, u32[]{:S(2)}) collective-permute-start(f32[8,4096]{1,0:T(8,128)} %get-tuple-element.44), channel_id=1, source_target_pairs={{0,16},{8,24},{16,0},{24,8},{1,17},{9,25},{17,1},{25,9},{2,18},{10... | collective-permute-start | bytes 393224 | tf_op jit(solution)/shard_map/ppermute | solution.py:265
  21.1 1.6 %collective-permute-start.5 = (f32[8,4096]{1,0:T(8,128)}, f32[8,4096]{1,0:T(8,128)}, u32[]{:S(2)}, u32[]{:S(2)}) collective-permute-start(f32[8,4096]{1,0:T(8,128)} %get-tuple-element.54), channel_id=1, source_target_pairs={{0,8},{8,16},{16,24},{24,0},{1,9},{9,17},{17,25},{25,1},{2,10},{10... | collective-permute-start | bytes 393224 | tf_op jit(solution)/shard_map/ppermute | solution.py:265
  22.7 2.2 %collective-permute-start.6 = (f32[8,4096]{1,0:T(8,128)}, f32[8,4096]{1,0:T(8,128)}, u32[]{:S(2)}, u32[]{:S(2)}) collective-permute-start(f32[8,4096]{1,0:T(8,128)} %get-tuple-element.55), channel_id=1, source_target_pairs={{0,24},{8,0},{16,8},{24,16},{1,25},{9,1},{17,9},{25,17},{2,26},{10... | collective-permute-start | bytes 393224 | tf_op jit(solution)/shard_map/ppermute | solution.py:265
  25.0 17.0 %shard_map.55 = (f32[8,4096]{1,0:T(8,128)}, f32[8,4096]{1,0:T(8,128)}, f32[8,4096]{1,0:T(8,128)}, f32[8,4096]{1,0:T(8,128)}) custom-call(f32[4,2,8,4096]{3,2,1,0:T(8,128)} %bitcast.20), custom_call_target="tpu_custom_call" | custom-call | bytes 1572864 | tf_op jit(solution)/shard_map/pallas_call | solution.py:234
  42.6 3.3 %collective-permute-start.2 = (f32[8,4096]{1,0:T(8,128)}, f32[8,4096]{1,0:T(8,128)S(1)}, u32[]{:S(2)}, u32[]{:S(2)}) collective-permute-start(f32[8,4096]{1,0:T(8,128)} %get-tuple-element.42), channel_id=1, source_target_pairs={{0,24},{8,0},{16,8},{24,16},{1,25},{9,1},{17,9},{25,17},{2,26},{10... | collective-permute-start | bytes 393224 | tf_op jit(solution)/shard_map/ppermute | solution.py:265
  46.8 1.0 copy-done.2
  48.8 2.6 %shard_map.58.refs_7_ = f32[4,8,2,4,8,128]{5,4,3,2,1,0:T(8,128)} custom-call(f32[8,4096]{1,0:T(8,128)S(1)} %copy-done.6, f32[8,4096]{1,0:T(8,128)} %collective-permute-done.5.refs_1_, f32[8,4096]{1,0:T(8,128)} %collective-permute-done.6.refs_2_, f32[8,4096]{1,0:T(8,128)S(1)} %copy-done.4, f32[2,32,256]{2,1,0:T(8,128)S(1)} %get-tuple-element.61.refs_4_.refs_0_, ...), custom_call_target="tpu_custom_call" | custom-call | flops 402653184 | bytes 2686976 | tf_op jit(solution)/shard_map/pallas_call | solution.py:234
  51.4 1.3 collective-permute-done.refs_0_
  53.4 1.6 %shard_map.59 = f32[4,8,2,4,8,128]{5,4,3,2,1,0:T(8,128)} custom-call(f32[8,4096]{1,0:T(8,128)S(1)} %collective-permute-done.refs_0_, f32[8,4096]{1,0:T(8,128)S(1)} %collective-permute-done.1.refs_1_, f32[8,4096]{1,0:T(8,128)S(1)} %collective-permute-done.2.refs_2_, f32[8,4096]{1,0:T(8,128)S(1)} %copy-done.3, ...), custom_call_target="tpu_custom_call", output_to_operand_aliasing={{}: (7, {})} | custom-call | flops 402653184 | bytes 3735552 | tf_op jit(solution)/shard_map/pallas_call | solution.py:234
  55.1 7.3 %all-to-all-start = ((f32[32,64,128]{2,1,0:T(8,128)}), f32[32,64,128]{2,1,0:T(8,128)S(1)}, u32[]{:S(2)}, u32[]{:S(2)}) async-start(f32[32,64,128]{2,1,0:T(8,128)} %bitcast.2), calls=%async_computation | async-start | bytes 2097152 | tf_op jit(solution)/shard_map/all_to_all | solution.py:338
  62.4 2.7 %collective-permute-start.9 = (f32[64,512]{1,0:T(8,128)S(1)}, f32[64,512]{1,0:T(8,128)S(1)}, u32[]{:S(2)}, u32[]{:S(2)}) collective-permute-start(f32[64,512]{1,0:T(8,128)S(1)} %collective-permute-done.4), channel_id=1, source_target_pairs={{0,6},{1,7},{2,4},{3,5},{4,2},{5,3},{6,0},{7,1},{8,14},{9,15},{10,... | collective-permute-start | bytes 393224 | tf_op jit(solution)/shard_map/ppermute | solution.py:255
  66.0 12.5 %collective-permute-done.9 = f32[64,512]{1,0:T(8,128)S(1)} collective-permute-done((f32[64,512]{1,0:T(8,128)S(1)}, f32[64,512]{1,0:T(8,128)S(1)}, u32[]{:S(2)}, u32[]{:S(2)}) %collective-permute-start.9) | collective-permute-done | bytes 131104 | tf_op jit(solution)/shard_map/ppermute | solution.py:255
  78.5 1.3 collective-permute-done.8
  79.8 1.0 collective-permute-done.7
  81.0 1.8 %collective-permute-done.10 = f32[4,64,512]{2,1,0:T(8,128)S(1)} collective-permute-done((f32[4,64,512]{2,1,0:T(8,128)S(1)}, f32[4,64,512]{2,1,0:T(8,128)S(1)}, u32[]{:S(2)}, u32[]{:S(2)}) %collective-permute-start.10) | collective-permute-done | bytes 524320 | tf_op jit(solution)/shard_map/ppermute | solution.py:255
  83.0 5.7 %all-to-all-done = f32[32,64,128]{2,1,0:T(8,128)S(1)} async-done(((f32[32,64,128]{2,1,0:T(8,128)}), f32[32,64,128]{2,1,0:T(8,128)S(1)}, u32[]{:S(2)}, u32[]{:S(2)}) %all-to-all-start) | async-done | bytes 1048608 | tf_op jit(solution)/shard_map/all_to_all | solution.py:338
  88.7 1.6 %shard_map.61 = f32[4,8,2,4,8,128]{5,4,3,2,1,0:T(8,128)} custom-call(f32[4,8,2,4,8,128]{5,4,3,2,1,0:T(8,128)S(1)} %bitcast.18, bf16[512,512]{1,0:T(8,128)(2,1)S(1)} %get-tuple-element.58.f_high, bf16[512,512]{1,0:T(8,128)(2,1)S(1)} %get-tuple-element.59.f_low), custom_call_target="tpu_custom_call" | custom-call | flops 805306368 | bytes 3145728 | tf_op jit(solution)/shard_map/pallas_call | solution.py:234
  90.3 3.6 %all-to-all-start.1 = ((f32[32,64,128]{2,1,0:T(8,128)}), f32[32,64,128]{2,1,0:T(8,128)S(1)}, u32[]{:S(2)}, u32[]{:S(2)}) async-start(f32[32,64,128]{2,1,0:T(8,128)} %bitcast.8), calls=%async_computation.1 | async-start | bytes 2097152 | tf_op jit(solution)/shard_map/all_to_all | solution.py:338
  94.1 26.0 %all-to-all-done.1 = f32[32,64,128]{2,1,0:T(8,128)S(1)} async-done(((f32[32,64,128]{2,1,0:T(8,128)}), f32[32,64,128]{2,1,0:T(8,128)S(1)}, u32[]{:S(2)}, u32[]{:S(2)}) %all-to-all-start.1) | async-done | bytes 1048608 | tf_op jit(solution)/shard_map/all_to_all | solution.py:338
  121.8 1.1 collective-permute-start.15
  123.8 2.8 %collective-permute-start.16 = (f32[8,4096]{1,0:T(8,128)S(1)}, f32[8,4096]{1,0:T(8,128)S(1)}, u32[]{:S(2)}, u32[]{:S(2)}) collective-permute-start(f32[8,4096]{1,0:T(8,128)S(1)} %get-tuple-element.74), channel_id=1, source_target_pairs={{0,24},{8,0},{16,8},{24,16},{1,25},{9,1},{17,9},{25,17},{2,26},{10... | collective-permute-start | bytes 393224 | tf_op jit(solution)/shard_map/ppermute | solution.py:265
  127.7 10.8 %collective-permute-done.14.refs_1_ = f32[8,4096]{1,0:T(8,128)S(1)} collective-permute-done((f32[8,4096]{1,0:T(8,128)S(1)}, f32[8,4096]{1,0:T(8,128)S(1)}, u32[]{:S(2)}, u32[]{:S(2)}) %collective-permute-start.14) | collective-permute-done | bytes 131104 | tf_op jit(solution)/shard_map/ppermute | solution.py:265
  139.4 5.4 %collective-permute-done.12.refs_1_ = f32[8,4096]{1,0:T(8,128)S(1)} collective-permute-done((f32[8,4096]{1,0:T(8,128)S(1)}, f32[8,4096]{1,0:T(8,128)S(1)}, u32[]{:S(2)}, u32[]{:S(2)}) %collective-permute-start.12) | collective-permute-done | bytes 131104 | tf_op jit(solution)/shard_map/ppermute | solution.py:265
  (50 shorter events, 10.4 us)
Async XLA Ops:
  0.0 45.9 %copy-start = (f32[1,128,512]{2,1,0:T(8,128)S(1)}, f32[1,128,512]{2,1,0:T(8,128)}, u32[]{:S(2)}) copy-start(f32[1,128,512]{2,1,0:T(8,128)} %param.6) | copy-start | bytes 786436
  17.0 25.6 %collective-permute-start.3 = (f32[8,4096]{1,0:T(8,128)}, f32[8,4096]{1,0:T(8,128)S(1)}, u32[]{:S(2)}, u32[]{:S(2)}) collective-permute-start(f32[8,4096]{1,0:T(8,128)} %get-tuple-element.44), channel_id=1, source_target_pairs={{0,16},{8,24},{16,0},{24,8},{1,17},{9,25},{17,1},{25,9},{2,18},{10... | collective-permute-start | bytes 393224 | tf_op jit(solution)/shard_map/ppermute | solution.py:265
  21.1 24.8 %collective-permute-start.5 = (f32[8,4096]{1,0:T(8,128)}, f32[8,4096]{1,0:T(8,128)}, u32[]{:S(2)}, u32[]{:S(2)}) collective-permute-start(f32[8,4096]{1,0:T(8,128)} %get-tuple-element.54), channel_id=1, source_target_pairs={{0,8},{8,16},{16,24},{24,0},{1,9},{9,17},{17,25},{25,1},{2,10},{10... | collective-permute-start | bytes 393224 | tf_op jit(solution)/shard_map/ppermute | solution.py:265
  22.7 24.1 %copy-start.1 = (bf16[512,512]{1,0:T(8,128)(2,1)S(1)}, bf16[512,512]{1,0:T(8,128)(2,1)}, u32[]{:S(2)}) copy-start(bf16[512,512]{1,0:T(8,128)(2,1)} %constant.21.clone.refs_2_) | copy-start | bytes 1572868
  22.7 25.3 %collective-permute-start.6 = (f32[8,4096]{1,0:T(8,128)}, f32[8,4096]{1,0:T(8,128)}, u32[]{:S(2)}, u32[]{:S(2)}) collective-permute-start(f32[8,4096]{1,0:T(8,128)} %get-tuple-element.55), channel_id=1, source_target_pairs={{0,24},{8,0},{16,8},{24,16},{1,25},{9,1},{17,9},{25,17},{2,26},{10... | collective-permute-start | bytes 393224 | tf_op jit(solution)/shard_map/ppermute | solution.py:265
  42.0 10.7 %collective-permute-start = (f32[8,4096]{1,0:T(8,128)}, f32[8,4096]{1,0:T(8,128)S(1)}, u32[]{:S(2)}, u32[]{:S(2)}) collective-permute-start(f32[8,4096]{1,0:T(8,128)} %get-tuple-element.40), channel_id=1, source_target_pairs={{0,16},{8,24},{16,0},{24,8},{1,17},{9,25},{17,1},{25,9},{2,18},{10... | collective-permute-start | bytes 393224 | tf_op jit(solution)/shard_map/ppermute | solution.py:265
  42.1 10.7 %collective-permute-start.1 = (f32[8,4096]{1,0:T(8,128)}, f32[8,4096]{1,0:T(8,128)S(1)}, u32[]{:S(2)}, u32[]{:S(2)}) collective-permute-start(f32[8,4096]{1,0:T(8,128)} %get-tuple-element.41), channel_id=1, source_target_pairs={{0,8},{8,16},{16,24},{24,0},{1,9},{9,17},{17,25},{25,1},{2,10},{10... | collective-permute-start | bytes 393224 | tf_op jit(solution)/shard_map/ppermute | solution.py:265
  42.6 3.3 %copy-start.5 = (f32[8,4096]{1,0:T(8,128)}, f32[8,4096]{1,0:T(8,128)S(1)}, u32[]{:S(2)}) copy-start(f32[8,4096]{1,0:T(8,128)S(1)} %collective-permute-done.3.refs_0_) | copy-start | bytes 393220
  42.6 4.2 %copy-start.7 = (f32[2,32,256]{2,1,0:T(8,128)S(1)}, f32[2,32,256]{2,1,0:T(8,128)}, u32[]{:S(2)}) copy-start(f32[2,32,256]{2,1,0:T(8,128)} %constant.19.clone.refs_0_) | copy-start | bytes 196612
  42.6 10.8 %collective-permute-start.2 = (f32[8,4096]{1,0:T(8,128)}, f32[8,4096]{1,0:T(8,128)S(1)}, u32[]{:S(2)}, u32[]{:S(2)}) collective-permute-start(f32[8,4096]{1,0:T(8,128)} %get-tuple-element.42), channel_id=1, source_target_pairs={{0,24},{8,0},{16,8},{24,16},{1,25},{9,1},{17,9},{25,17},{2,26},{10... | collective-permute-start | bytes 393224 | tf_op jit(solution)/shard_map/ppermute | solution.py:265
  46.0 7.5 %collective-permute-start.4 = (f32[64,512]{1,0:T(8,128)S(1)}, f32[64,512]{1,0:T(8,128)S(1)}, u32[]{:S(2)}, u32[]{:S(2)}) collective-permute-start(f32[64,512]{1,0:T(8,128)S(1)} %dynamic-slice_bitcast_fusion), channel_id=1, source_target_pairs={{0,0},{1,24},{2,8},{3,16},{4,17},{5,9},{6,25},{7,1},{8,2},{9,26},{... | collective-permute-start | bytes 393224 | tf_op jit(solution)/shard_map/ppermute | solution.py:280
  48.8 4.7 %copy-start.3 = (f32[8,4096]{1,0:T(8,128)S(1)}, f32[8,4096]{1,0:T(8,128)}, u32[]{:S(2)}) copy-start(f32[8,4096]{1,0:T(8,128)} %get-tuple-element.49.refs_3_) | copy-start | bytes 393220
  55.1 33.6 %all-to-all-start = ((f32[32,64,128]{2,1,0:T(8,128)}), f32[32,64,128]{2,1,0:T(8,128)S(1)}, u32[]{:S(2)}, u32[]{:S(2)}) async-start(f32[32,64,128]{2,1,0:T(8,128)} %bitcast.2), calls=%async_computation | async-start | bytes 2097152 | tf_op jit(solution)/shard_map/all_to_all | solution.py:338
  62.4 16.0 %collective-permute-start.9 = (f32[64,512]{1,0:T(8,128)S(1)}, f32[64,512]{1,0:T(8,128)S(1)}, u32[]{:S(2)}, u32[]{:S(2)}) collective-permute-start(f32[64,512]{1,0:T(8,128)S(1)} %collective-permute-done.4), channel_id=1, source_target_pairs={{0,6},{1,7},{2,4},{3,5},{4,2},{5,3},{6,0},{7,1},{8,14},{9,15},{10,... | collective-permute-start | bytes 393224 | tf_op jit(solution)/shard_map/ppermute | solution.py:255
  65.2 14.6 %collective-permute-start.8 = (f32[64,512]{1,0:T(8,128)S(1)}, f32[64,512]{1,0:T(8,128)S(1)}, u32[]{:S(2)}, u32[]{:S(2)}) collective-permute-start(f32[64,512]{1,0:T(8,128)S(1)} %collective-permute-done.4), channel_id=1, source_target_pairs={{0,4},{1,5},{2,6},{3,7},{4,0},{5,1},{6,2},{7,3},{8,12},{9,13},{10,... | collective-permute-start | bytes 393224 | tf_op jit(solution)/shard_map/ppermute | solution.py:255
  65.7 15.1 %collective-permute-start.7 = (f32[64,512]{1,0:T(8,128)S(1)}, f32[64,512]{1,0:T(8,128)S(1)}, u32[]{:S(2)}, u32[]{:S(2)}) collective-permute-start(f32[64,512]{1,0:T(8,128)S(1)} %collective-permute-done.4), channel_id=1, source_target_pairs={{0,2},{1,3},{2,0},{3,1},{4,6},{5,7},{6,4},{7,5},{8,10},{9,11},{10,... | collective-permute-start | bytes 393224 | tf_op jit(solution)/shard_map/ppermute | solution.py:255
  80.8 2.0 %collective-permute-start.10 = (f32[4,64,512]{2,1,0:T(8,128)S(1)}, f32[4,64,512]{2,1,0:T(8,128)S(1)}, u32[]{:S(2)}, u32[]{:S(2)}) collective-permute-start(f32[4,64,512]{2,1,0:T(8,128)S(1)} %pad_maximum_fusion), channel_id=1, source_target_pairs={{0,1},{1,0},{2,3},{3,2},{4,5},{5,4},{6,7},{7,6},{8,9},{9,8},{10,11... | collective-permute-start | bytes 1572872 | tf_op jit(solution)/shard_map/ppermute | solution.py:255
  90.3 29.9 %all-to-all-start.1 = ((f32[32,64,128]{2,1,0:T(8,128)}), f32[32,64,128]{2,1,0:T(8,128)S(1)}, u32[]{:S(2)}, u32[]{:S(2)}) async-start(f32[32,64,128]{2,1,0:T(8,128)} %bitcast.8), calls=%async_computation.1 | async-start | bytes 2097152 | tf_op jit(solution)/shard_map/all_to_all | solution.py:338
  121.0 17.6 %collective-permute-start.14 = (f32[8,4096]{1,0:T(8,128)S(1)}, f32[8,4096]{1,0:T(8,128)S(1)}, u32[]{:S(2)}, u32[]{:S(2)}) collective-permute-start(f32[8,4096]{1,0:T(8,128)S(1)} %get-tuple-element.72), channel_id=1, source_target_pairs={{0,16},{8,24},{16,0},{24,8},{1,17},{9,25},{17,1},{25,9},{2,18},{10... | collective-permute-start | bytes 393224 | tf_op jit(solution)/shard_map/ppermute | solution.py:265
  121.8 16.7 %collective-permute-start.15 = (f32[8,4096]{1,0:T(8,128)S(1)}, f32[8,4096]{1,0:T(8,128)S(1)}, u32[]{:S(2)}, u32[]{:S(2)}) collective-permute-start(f32[8,4096]{1,0:T(8,128)S(1)} %get-tuple-element.73), channel_id=1, source_target_pairs={{0,8},{8,16},{16,24},{24,0},{1,9},{9,17},{17,25},{25,1},{2,10},{10... | collective-permute-start | bytes 393224 | tf_op jit(solution)/shard_map/ppermute | solution.py:265
  123.8 14.7 %collective-permute-start.16 = (f32[8,4096]{1,0:T(8,128)S(1)}, f32[8,4096]{1,0:T(8,128)S(1)}, u32[]{:S(2)}, u32[]{:S(2)}) collective-permute-start(f32[8,4096]{1,0:T(8,128)S(1)} %get-tuple-element.74), channel_id=1, source_target_pairs={{0,24},{8,0},{16,8},{24,16},{1,25},{9,1},{17,9},{25,17},{2,26},{10... | collective-permute-start | bytes 393224 | tf_op jit(solution)/shard_map/ppermute | solution.py:265
  126.6 18.2 %collective-permute-start.12 = (f32[8,4096]{1,0:T(8,128)S(1)}, f32[8,4096]{1,0:T(8,128)S(1)}, u32[]{:S(2)}, u32[]{:S(2)}) collective-permute-start(f32[8,4096]{1,0:T(8,128)S(1)} %get-tuple-element.69), channel_id=1, source_target_pairs={{0,16},{8,24},{16,0},{24,8},{1,17},{9,25},{17,1},{25,9},{2,18},{10... | collective-permute-start | bytes 393224 | tf_op jit(solution)/shard_map/ppermute | solution.py:265
  127.0 17.9 %collective-permute-start.13 = (f32[8,4096]{1,0:T(8,128)S(1)}, f32[8,4096]{1,0:T(8,128)S(1)}, u32[]{:S(2)}, u32[]{:S(2)}) collective-permute-start(f32[8,4096]{1,0:T(8,128)S(1)} %get-tuple-element.70), channel_id=1, source_target_pairs={{0,8},{8,16},{16,24},{24,0},{1,9},{9,17},{17,25},{25,1},{2,10},{10... | collective-permute-start | bytes 393224 | tf_op jit(solution)/shard_map/ppermute | solution.py:265
  138.6 7.0 %collective-permute-start.11 = (f32[8,4096]{1,0:T(8,128)S(1)}, f32[8,4096]{1,0:T(8,128)S(1)}, u32[]{:S(2)}, u32[]{:S(2)}) collective-permute-start(f32[8,4096]{1,0:T(8,128)S(1)} %get-tuple-element.67), channel_id=1, source_target_pairs={{0,24},{8,0},{16,8},{24,16},{1,25},{9,1},{17,9},{25,17},{2,26},{10... | collective-permute-start | bytes 393224 | tf_op jit(solution)/shard_map/ppermute | solution.py:265
  (3 other events, 4.0 us)

commit v11 on v6

--- a/solution.py
+++ b/solution.py
@@ -12,7 +12,7 @@
 
 LANES = 128
 VMEM_LIMIT = 48 * 1024 * 1024
-CHUNKS = 1
+CHUNKS = 2
 
 
 def band_of(plane, planes):
@@ -80,7 +80,9 @@
     def dot(a, b):
         return lax.dot_general(a, b, (contract, ((), ())), preferred_element_type=jnp.float32)
 
-    return dot(left[0], right[0]) + (dot(left[0], right[1]) + dot(left[1], right[0]))
+    rows = left[0].shape[0]
+    both = dot(jnp.concatenate(left), right[0])
+    return both[:rows] + (both[rows:] + dot(left[0], right[1]))
 
 
 def tiles(rows, lanes):
@@ -90,12 +92,11 @@
             yield slice(row, row + step), lane
 
 
-def slice_kernel(chunk, noise_ref, *refs):
+def slice_kernel(noise_ref, *refs):
     here = lax.axis_index("tm")
     outs, sem = refs[:-1], refs[-1]
     copies = [
-        pltpu.make_async_copy(noise_ref.at[lax.rem(here + step, noise_ref.shape[0]), chunk], out, sem.at[step])
-        for step, out in enumerate(outs)
+        pltpu.make_async_copy(noise_ref.at[here ^ step], out, sem.at[step]) for step, out in enumerate(outs)
     ]
     for copy in copies:
         copy.start()
@@ -113,15 +114,15 @@
         copy.wait()
 
 
-def forward_kernel(n1, n2, chunk, planes, *refs):
+def forward_kernel(n1, n2, planes, *refs):
     here = lax.axis_index("tm")
     blocks, (turn_ref, high_ref, low_ref) = refs[:planes], refs[planes : planes + 3]
     out_ref, x_ref, mid_ref, stage_ref, sem = refs[-5:]
     _, dets, span = x_ref.shape
     _, groups, pieces, _, width = stage_ref.shape
     per = span // n2
-    for step, block in enumerate(blocks):
-        x_ref[lax.rem(here + planes - step, planes)] = block[...]
+    for step, block in enumerate(reversed(blocks)):
+        x_ref[here ^ step] = block[...]
     for rows, lane in tiles(dets, n2):
 
         def load(index):
@@ -135,16 +136,17 @@
             place = slice(k1 * dets + rows.start, k1 * dets + rows.stop)
             mid_ref[place, lane : lane + LANES] = re * cosine + im * sine
             mid_ref[place, n2 + lane : n2 + lane + LANES] = im * cosine - re * sine
+    halves = split(mid_ref[...])
     copies = []
-    share = groups // 2
+    share = planes // 2
     for part in range(2):
-        count = share * pieces * dets
-        spectrum = product(split(mid_ref[part * count : (part + 1) * count]), (high_ref[...], low_ref[...]))
+        columns = slice(part * share * width, (part + 1) * share * width)
+        spectrum = product(halves, (high_ref[:, columns], low_ref[:, columns]))
         these = pl.ds(part * share, share)
-        for plane in range(planes):
+        for plane in range(share):
             value = spectrum[:, plane * width : (plane + 1) * width]
-            stage_ref[plane, these] = value.reshape(share, pieces, dets, width)
-        copies.append(pltpu.make_async_copy(stage_ref.at[:, these], out_ref.at[:, these, chunk], sem.at[part]))
+            stage_ref[part * share + plane] = value.reshape(groups, pieces, dets, width)
+        copies.append(pltpu.make_async_copy(stage_ref.at[these], out_ref.at[these], sem.at[part]))
         copies[-1].start()
     for copy in copies:
         copy.wait()
@@ -173,7 +175,7 @@
                 start = (index % per) * n2 + lane
                 x_ref[index // per, rows, start : start + LANES] = value
     for step, out in enumerate(outs):
-        out[...] = x_ref[lax.rem(here + step, planes)]
+        out[...] = x_ref[here ^ step]
 
 
 def place_kernel(chunk, *refs):
@@ -181,7 +183,7 @@
     out_ref, sem = refs[-2:]
     planes = out_ref.shape[0]
     copies = [
-        pltpu.make_async_copy(refs[step], out_ref.at[lax.rem(here + planes - step, planes), chunk], sem.at[step])
+        pltpu.make_async_copy(refs[planes - 1 - step], out_ref.at[here ^ step, chunk], sem.at[step])
         for step in range(planes)
     ]
     for copy in copies:
@@ -200,20 +202,19 @@
 
 
 def mix_kernel(x_ref, f_high, f_low, out_ref, x_mid, y_mid):
-    planes, groups, chunks, pieces, dets, width = x_ref.shape
-    places = []
-    for plane, group, chunk, piece in np.ndindex(planes, groups, chunks, pieces):
-        start = ((group * planes + plane) * chunks + chunk) * dets
-        rows, lanes = slice(start, start + dets), slice(piece * width, (piece + 1) * width)
-        places.append(((plane, group, chunk, piece), (rows, lanes)))
-    for source, target in places:
-        x_mid[target] = x_ref[source]
+    planes, groups, chunks, pieces, dets, width = out_ref.shape
+    own = chunks * dets
+    for plane, group, piece in np.ndindex(planes, groups, pieces):
+        start = (group * planes + plane) * own
+        x_mid[start : start + own, piece * width : (piece + 1) * width] = x_ref[plane, group, piece]
     x_high, x_low = split(x_mid[...])
     half = f_high.shape[0] // 2
-    y_mid[:half] = product((f_high[:half, :half], f_low[:half, :half]), (x_high[:half], x_low[:half]))
-    y_mid[half:] = product((f_high[half:, :], f_low[half:, :]), (x_high, x_low))
-    for target, source in places:
-        out_ref[target] = y_mid[source]
+    for part in range(2):
+        rows, reach = slice(part * half, (part + 1) * half), (part + 1) * half
+        y_mid[rows] = product((f_high[rows, :reach], f_low[rows, :reach]), (x_high[:reach], x_low[:reach]))
+    for plane, group, chunk, piece in np.ndindex(planes, groups, chunks, pieces):
+        start = (group * planes + plane) * own + chunk * dets
+        out_ref[plane, group, chunk, piece] = y_mid[start : start + dets, piece * width : (piece + 1) * width]
 
 
 def call(kernel, outs, scratch, flops, *args, spaces=None, out_space=pltpu.VMEM, aliases=None):
@@ -243,12 +244,8 @@
     return lax.ppermute(value, axis, [(place, place ^ mask) for place in range(lax.axis_size(axis))])
 
 
-def rotate(parts):
-    planes = len(parts)
-    return [parts[0]] + [
-        lax.ppermute(parts[step], "tm", [(place, (place + step) % planes) for place in range(planes)])
-        for step in range(1, planes)
-    ]
+def trade(parts):
+    return [swap(parts[step], "tm", step) for step in reversed(range(1, len(parts)))] + [parts[0]]
 
 
 def plane_factor(factor, planes, groups):
@@ -272,6 +269,11 @@
     return call(factor_kernel, [whole, whole], [], 0, share)
 
 
+def hold(tables):
+    outs = [array(*table.shape, dtype=table.dtype) for table in tables]
+    return call(hold_kernel, outs, [dma(len(tables))], 0, *tables, spaces=[pl.ANY] * len(tables))
+
+
 def bind(kernel, *static):
     return lambda *refs: kernel(*static, *refs)
 
@@ -280,57 +282,44 @@
     planes = lax.axis_size("tm")
     groups = lax.axis_size("det")
     rows, span = noise.shape
+    own = rows // planes
     n2 = LANES // 2 * planes
     n1 = span * planes // 2 // n2
     pieces = n1 // groups
-    chunks = CHUNKS if rows // planes % (8 * CHUNKS) == 0 else 1
-    dets = rows // planes // chunks
-    flops = 3 * 2 * n1 * dets * (2 * n2) ** 2
-    block, series, middle = array(dets, span), (planes, dets, span), (n1 * dets, 2 * n2)
-    layout = (planes, groups, chunks, pieces, dets, LANES)
-    tables = (twiddles(n1, n2), *fourier_matrix(n2, planes))
-
-    noise = noise.reshape(planes, chunks, dets, span)
-    arrived = []
-    for chunk in range(chunks):
-        parts = call(bind(slice_kernel, chunk), [block] * planes, [dma(planes)], 0, noise, spaces=[pltpu.HBM])
-        arrived.append(rotate(parts))
-    share = plane_factor(factor, planes, groups)
-    tables = call(
-        hold_kernel, [array(*table.shape, dtype=table.dtype) for table in tables], [dma(len(tables))], 0, *tables,
-        spaces=[pl.ANY] * len(tables),
+    chunks = CHUNKS if own % (8 * CHUNKS) == 0 else 1
+    dets = own // chunks
+    flops = 3 * 2 * n1 * own * (2 * n2) ** 2
+    tables = hold((twiddles(n1, n2), *fourier_matrix(n2, planes)))
+
+    def exchange(value, shape):
+        value = value.reshape(planes * groups, pieces * own, LANES)
+        return lax.all_to_all(value, ("tm", "det"), split_axis=0, concat_axis=0, tiled=True).reshape(shape)
+
+    parts = call(
+        slice_kernel, [array(own, span)] * planes, [dma(planes)], 0, noise.reshape(planes, own, span), spaces=[pl.ANY]
     )
-    arrived, share = lax.optimization_barrier((arrived, share))
+    layout = (planes, groups, pieces, own, LANES)
+    (spectrum,) = call(
+        bind(forward_kernel, n1, n2, planes), [array(*layout)],
+        [(planes, own, span), (n1 * own, 2 * n2), layout, dma(2)], flops, *trade(parts), *tables, out_space=pl.ANY,
+    )
+    spectrum, share = lax.optimization_barrier((spectrum, plane_factor(factor, planes, groups)))
     f_high, f_low = band_factor(share, groups)
-    buffer = []
-    for chunk in range(chunks):
-        buffer = call(
-            bind(forward_kernel, n1, n2, chunk, planes), [array(*layout)],
-            [series, middle, (planes, groups, pieces, dets, LANES), dma(2)], flops,
-            *arrived[chunk], *tables, *buffer,
-            spaces=[pltpu.VMEM] * (planes + len(tables)) + [pl.ANY] * len(buffer),
-            out_space=pl.ANY, aliases={planes + len(tables): 0} if buffer else None,
-        )
-
-    def exchange(value):
-        value = value.reshape(planes * groups, chunks * pieces * dets, LANES)
-        return lax.all_to_all(value, ("tm", "det"), split_axis=0, concat_axis=0, tiled=True).reshape(layout)
 
     count = f_high.shape[0]
     (mixed,) = call(
-        mix_kernel, [array(*layout)], [(count, pieces * LANES)] * 2,
-        2 * 3 * count * count * pieces * LANES,
-        exchange(buffer[0]), f_high, f_low,
+        mix_kernel, [array(planes, groups, chunks, pieces, dets, LANES)], [(count, pieces * LANES)] * 2,
+        2 * 3 * count * count * pieces * LANES, exchange(spectrum, layout), f_high, f_low,
     )
-    back = exchange(mixed)
+    back = exchange(mixed, mixed.shape)
     result = []
     for chunk in range(chunks):
         parts = call(
-            bind(inverse_kernel, n1, n2, chunk), [block] * planes, [series, middle], flops, back, *tables
+            bind(inverse_kernel, n1, n2, chunk), [array(dets, span)] * planes,
+            [(planes, dets, span), (n1 * dets, 2 * n2)], flops // chunks, back, *tables,
         )
-        parts = rotate(parts)
         result = call(
-            bind(place_kernel, chunk), [array(planes, chunks, dets, span)], [dma(planes)], 0, *parts, *result,
+            bind(place_kernel, chunk), [array(planes, chunks, dets, span)], [dma(planes)], 0, *trade(parts), *result,
             spaces=[pl.ANY] * (planes + len(result)), out_space=pl.ANY, aliases={planes: 0} if result else None,
         )
     return result[0].reshape(rows, span)

time: 123 us -> 123 us (level)
  the two profiles are of different devices: /device:TPU:11 before, /device:TPU:0 now
where the time goes in v11:
time: 123 us
  waiting for transfers between devices  50.6 us (41%)
  starting transfers between devices  31 us (25%)
  blocking collectives  29.7 us (24%)
  Pallas kernels  7.95 us (6%)
  local copies, waits for them, and re-layouts  2.31 us (2%)
    ppermute x13, waiting for transfers between devices, swap(): lax.ppermute(value, axis, [(place, place ^ mask) for place in range(lax.a...  46.7 us
    all_to_all x1, blocking collectives, exchange(): lax.all_to_all(value, ('tm', 'det'), split_axis=0, concat_axis=0, tiled=T...  29.7 us
    ppermute x13, starting transfers between devices, swap(): lax.ppermute(value, axis, [(place, place ^ mask) for place in range(lax.a...  24.7 us
    pallas_call x9, Pallas kernels, call(): pl.pallas_call(kernel, out_shape=outs, in_specs=[pl.BlockSpec(memory_spac...  7.95 us
    all_to_all x1, starting transfers between devices, exchange(): lax.all_to_all(value, ('tm', 'det'), split_axis=0, concat_axis=0, tiled=T...  4.92 us
    all_to_all x1, waiting for transfers between devices, exchange(): lax.all_to_all(value, ('tm', 'det'), split_axis=0, concat_axis=0, tiled=T...  3.87 us
  transfers between devices with their start and end apart: 15, of which 8 were waited for; matrix products, arithmetic and copies ran while one was open for 2% of the time, Pallas kernels for 4%

profile of v11, /device:TPU:0, one launch (start us, length us, event | category | flops | bytes accessed | tf_op | source)
XLA Modules:
  0.0 122.7 jit_solution(79636328078231255)
XLA Ops:
  0.0 1.3 %copy-done.1 = f32[64,4096]{1,0:T(8,128)S(1)} copy-done((f32[64,4096]{1,0:T(8,128)S(1)}, f32[64,4096]{1,0:T(8,128)}, u32[]{:S(2)}) %copy-start.1) | copy-done | bytes 1048600
  1.3 1.0 shard_map.55
  2.3 5.1 %collective-permute-start = (f32[16,4096]{1,0:T(8,128)}, f32[16,4096]{1,0:T(8,128)S(1)}, u32[]{:S(2)}, u32[]{:S(2)}) collective-permute-start(f32[16,4096]{1,0:T(8,128)} %get-tuple-element.24), channel_id=1, source_target_pairs={{0,24},{8,16},{16,8},{24,0},{1,25},{9,17},{17,9},{25,1},{2,26},{10... | collective-permute-start | bytes 786440 | tf_op jit(solution)/shard_map/ppermute | solution.py:244
  8.1 1.4 %collective-permute-start.3 = (f32[64,512]{1,0:T(8,128)S(1)}, f32[64,512]{1,0:T(8,128)}, u32[]{:S(2)}, u32[]{:S(2)}) collective-permute-start(f32[64,512]{1,0:T(8,128)S(1)} %dynamic-slice_bitcast_fusion), channel_id=1, source_target_pairs={{0,0},{1,24},{2,8},{3,16},{4,17},{5,9},{6,25},{7,1},{8,2},{9,26},{... | collective-permute-start | bytes 393224 | tf_op jit(solution)/shard_map/ppermute | solution.py:261
  9.7 5.2 %collective-permute-done.refs_0_ = f32[16,4096]{1,0:T(8,128)S(1)} collective-permute-done((f32[16,4096]{1,0:T(8,128)}, f32[16,4096]{1,0:T(8,128)S(1)}, u32[]{:S(2)}, u32[]{:S(2)}) %collective-permute-start) | collective-permute-done | bytes 262176 | tf_op jit(solution)/shard_map/ppermute | solution.py:244
  14.9 16.4 %collective-permute-done.1.refs_1_ = f32[16,4096]{1,0:T(8,128)S(1)} collective-permute-done((f32[16,4096]{1,0:T(8,128)}, f32[16,4096]{1,0:T(8,128)S(1)}, u32[]{:S(2)}, u32[]{:S(2)}) %collective-permute-start.1) | collective-permute-done | bytes 262176 | tf_op jit(solution)/shard_map/ppermute | solution.py:244
  31.3 2.5 %shard_map.57 = f32[4,8,4,16,128]{4,3,2,1,0:T(8,128)} custom-call(f32[16,4096]{1,0:T(8,128)S(1)} %collective-permute-done.refs_0_, f32[16,4096]{1,0:T(8,128)S(1)} %collective-permute-done.1.refs_1_, f32[16,4096]{1,0:T(8,128)S(1)} %collective-permute-done.2.refs_2_, f32[16,4096]{1,0:T(8,128)S(1)} %get-tuple-element.27.refs_3_, ...), custom_call_target="tpu_custom_call" | custom-call | flops 805306368 | bytes 3211264 | tf_op jit(solution)/shard_map/pallas_call | solution.py:223
  33.8 4.9 %all-to-all-start = ((f32[32,64,128]{2,1,0:T(8,128)}), f32[32,64,128]{2,1,0:T(8,128)S(1)}, u32[]{:S(2)}, u32[]{:S(2)}) async-start(f32[32,64,128]{2,1,0:T(8,128)} %bitcast.2), calls=%async_computation | async-start | bytes 2097152 | tf_op jit(solution)/shard_map/all_to_all | solution.py:296
  38.7 1.8 %collective-permute-start.4 = (f32[64,512]{1,0:T(8,128)}, f32[64,512]{1,0:T(8,128)S(1)}, u32[]{:S(2)}, u32[]{:S(2)}) collective-permute-start(f32[64,512]{1,0:T(8,128)} %collective-permute-done.3), channel_id=1, source_target_pairs={{0,2},{1,3},{2,0},{3,1},{4,6},{5,7},{6,4},{7,5},{8,10},{9,11},{10,... | collective-permute-start | bytes 393224 | tf_op jit(solution)/shard_map/ppermute | solution.py:244
  40.6 1.5 %collective-permute-start.5 = (f32[64,512]{1,0:T(8,128)}, f32[64,512]{1,0:T(8,128)S(1)}, u32[]{:S(2)}, u32[]{:S(2)}) collective-permute-start(f32[64,512]{1,0:T(8,128)} %collective-permute-done.3), channel_id=1, source_target_pairs={{0,4},{1,5},{2,6},{3,7},{4,0},{5,1},{6,2},{7,3},{8,12},{9,13},{10,... | collective-permute-start | bytes 393224 | tf_op jit(solution)/shard_map/ppermute | solution.py:244
  42.3 0.9 constant_dynamic-update-slice_fusion.4
  43.2 10.1 %collective-permute-done.4 = f32[64,512]{1,0:T(8,128)S(1)} collective-permute-done((f32[64,512]{1,0:T(8,128)}, f32[64,512]{1,0:T(8,128)S(1)}, u32[]{:S(2)}, u32[]{:S(2)}) %collective-permute-start.4) | collective-permute-done | bytes 131104 | tf_op jit(solution)/shard_map/ppermute | solution.py:244
  53.3 4.7 %collective-permute-done.6 = f32[64,512]{1,0:T(8,128)S(1)} collective-permute-done((f32[64,512]{1,0:T(8,128)}, f32[64,512]{1,0:T(8,128)S(1)}, u32[]{:S(2)}, u32[]{:S(2)}) %collective-permute-start.6) | collective-permute-done | bytes 131104 | tf_op jit(solution)/shard_map/ppermute | solution.py:244
  58.0 0.9 pad_maximum_fusion
  59.1 1.8 %collective-permute-done.7 = f32[4,64,512]{2,1,0:T(8,128)S(1)} collective-permute-done((f32[4,64,512]{2,1,0:T(8,128)S(1)}, f32[4,64,512]{2,1,0:T(8,128)S(1)}, u32[]{:S(2)}, u32[]{:S(2)}) %collective-permute-start.7) | collective-permute-done | bytes 524320 | tf_op jit(solution)/shard_map/ppermute | solution.py:244
  61.1 3.9 %all-to-all-done = f32[32,64,128]{2,1,0:T(8,128)S(1)} async-done(((f32[32,64,128]{2,1,0:T(8,128)}), f32[32,64,128]{2,1,0:T(8,128)S(1)}, u32[]{:S(2)}, u32[]{:S(2)}) %all-to-all-start) | async-done | bytes 1048608 | tf_op jit(solution)/shard_map/all_to_all | solution.py:296
  65.8 29.7 %all_to_all.10 = f32[32,64,128]{2,1,0:T(8,128)S(1)} all-to-all(f32[32,64,128]{2,1,0:T(8,128)S(1)} %bitcast.19), channel_id=1, replica_groups=mesh['tm'=4,'det'=8] {'tm','det'}, dimensions={0} | all-to-all | bytes 2097152 | tf_op jit(solution)/shard_map/all_to_all | solution.py:296
  96.3 1.4 %collective-permute-start.11 = (f32[8,4096]{1,0:T(8,128)S(1)}, f32[8,4096]{1,0:T(8,128)S(1)}, u32[]{:S(2)}, u32[]{:S(2)}) collective-permute-start(f32[8,4096]{1,0:T(8,128)S(1)} %get-tuple-element.39), channel_id=1, source_target_pairs={{0,24},{8,16},{16,8},{24,0},{1,25},{9,17},{17,9},{25,1},{2,26},{10... | collective-permute-start | bytes 393224 | tf_op jit(solution)/shard_map/ppermute | solution.py:244
  98.6 2.6 %collective-permute-start.8 = (f32[8,4096]{1,0:T(8,128)S(1)}, f32[8,4096]{1,0:T(8,128)S(1)}, u32[]{:S(2)}, u32[]{:S(2)}) collective-permute-start(f32[8,4096]{1,0:T(8,128)S(1)} %get-tuple-element.35), channel_id=1, source_target_pairs={{0,24},{8,16},{16,8},{24,0},{1,25},{9,17},{17,9},{25,1},{2,26},{10... | collective-permute-start | bytes 393224 | tf_op jit(solution)/shard_map/ppermute | solution.py:244
  101.2 1.9 %collective-permute-start.13 = (f32[8,4096]{1,0:T(8,128)S(1)}, f32[8,4096]{1,0:T(8,128)S(1)}, u32[]{:S(2)}, u32[]{:S(2)}) collective-permute-start(f32[8,4096]{1,0:T(8,128)S(1)} %get-tuple-element.41), channel_id=1, source_target_pairs={{0,8},{8,0},{16,24},{24,16},{1,9},{9,1},{17,25},{25,17},{2,10},{10... | collective-permute-start | bytes 393224 | tf_op jit(solution)/shard_map/ppermute | solution.py:244
  103.0 1.1 collective-permute-start.9
  104.1 8.4 %collective-permute-start.10 = (f32[8,4096]{1,0:T(8,128)S(1)}, f32[8,4096]{1,0:T(8,128)S(1)}, u32[]{:S(2)}, u32[]{:S(2)}) collective-permute-start(f32[8,4096]{1,0:T(8,128)S(1)} %get-tuple-element.37), channel_id=1, source_target_pairs={{0,8},{8,0},{16,24},{24,16},{1,9},{9,1},{17,25},{25,17},{2,10},{10... | collective-permute-start | bytes 393224 | tf_op jit(solution)/shard_map/ppermute | solution.py:244
  112.5 7.2 %collective-permute-done.12.refs_1_ = f32[8,4096]{1,0:T(8,128)S(1)} collective-permute-done((f32[8,4096]{1,0:T(8,128)S(1)}, f32[8,4096]{1,0:T(8,128)S(1)}, u32[]{:S(2)}, u32[]{:S(2)}) %collective-permute-start.12) | collective-permute-done | bytes 131104 | tf_op jit(solution)/shard_map/ppermute | solution.py:244
  120.6 1.2 %collective-permute-done.9.refs_1_ = f32[8,4096]{1,0:T(8,128)S(1)} collective-permute-done((f32[8,4096]{1,0:T(8,128)S(1)}, f32[8,4096]{1,0:T(8,128)S(1)}, u32[]{:S(2)}, u32[]{:S(2)}) %collective-permute-start.9) | collective-permute-done | bytes 131104 | tf_op jit(solution)/shard_map/ppermute | solution.py:244
  (33 shorter events, 5.6 us)
Async XLA Ops:
  0.0 8.0 %copy-start = (f32[1,128,512]{2,1,0:T(8,128)S(1)}, f32[1,128,512]{2,1,0:T(8,128)}, u32[]{:S(2)}) copy-start(f32[1,128,512]{2,1,0:T(8,128)} %param.6) | copy-start | bytes 786436
  0.0 1.3 %copy-start.1 = (f32[64,4096]{1,0:T(8,128)S(1)}, f32[64,4096]{1,0:T(8,128)}, u32[]{:S(2)}) copy-start(f32[64,4096]{1,0:T(8,128)} %param.5) | copy-start | bytes 3145732
  1.3 8.2 %copy-start.2 = (bf16[512,512]{1,0:T(8,128)(2,1)S(1)}, bf16[512,512]{1,0:T(8,128)(2,1)}, u32[]{:S(2)}) copy-start(bf16[512,512]{1,0:T(8,128)(2,1)} %constant.20.clone.refs_1_) | copy-start | bytes 1572868
  1.3 8.2 %copy-start.3 = (bf16[512,512]{1,0:T(8,128)(2,1)S(1)}, bf16[512,512]{1,0:T(8,128)(2,1)}, u32[]{:S(2)}) copy-start(bf16[512,512]{1,0:T(8,128)(2,1)} %constant.21.clone.refs_2_) | copy-start | bytes 1572868
  2.3 12.6 %collective-permute-start = (f32[16,4096]{1,0:T(8,128)}, f32[16,4096]{1,0:T(8,128)S(1)}, u32[]{:S(2)}, u32[]{:S(2)}) collective-permute-start(f32[16,4096]{1,0:T(8,128)} %get-tuple-element.24), channel_id=1, source_target_pairs={{0,24},{8,16},{16,8},{24,0},{1,25},{9,17},{17,9},{25,1},{2,26},{10... | collective-permute-start | bytes 786440 | tf_op jit(solution)/shard_map/ppermute | solution.py:244
  7.4 23.9 %collective-permute-start.1 = (f32[16,4096]{1,0:T(8,128)}, f32[16,4096]{1,0:T(8,128)S(1)}, u32[]{:S(2)}, u32[]{:S(2)}) collective-permute-start(f32[16,4096]{1,0:T(8,128)} %get-tuple-element.25), channel_id=1, source_target_pairs={{0,16},{8,24},{16,0},{24,8},{1,17},{9,25},{17,1},{25,9},{2,18},{10... | collective-permute-start | bytes 786440 | tf_op jit(solution)/shard_map/ppermute | solution.py:244
  7.4 23.9 %collective-permute-start.2 = (f32[16,4096]{1,0:T(8,128)}, f32[16,4096]{1,0:T(8,128)S(1)}, u32[]{:S(2)}, u32[]{:S(2)}) collective-permute-start(f32[16,4096]{1,0:T(8,128)} %get-tuple-element.26), channel_id=1, source_target_pairs={{0,8},{8,0},{16,24},{24,16},{1,9},{9,1},{17,25},{25,17},{2,10},{10... | collective-permute-start | bytes 786440 | tf_op jit(solution)/shard_map/ppermute | solution.py:244
  8.0 1.5 %copy-start.4 = (f32[2,32,256]{2,1,0:T(8,128)S(1)}, f32[2,32,256]{2,1,0:T(8,128)}, u32[]{:S(2)}) copy-start(f32[2,32,256]{2,1,0:T(8,128)} %constant.19.clone.refs_0_) | copy-start | bytes 196612
  8.1 25.8 %collective-permute-start.3 = (f32[64,512]{1,0:T(8,128)S(1)}, f32[64,512]{1,0:T(8,128)}, u32[]{:S(2)}, u32[]{:S(2)}) collective-permute-start(f32[64,512]{1,0:T(8,128)S(1)} %dynamic-slice_bitcast_fusion), channel_id=1, source_target_pairs={{0,0},{1,24},{2,8},{3,16},{4,17},{5,9},{6,25},{7,1},{8,2},{9,26},{... | collective-permute-start | bytes 393224 | tf_op jit(solution)/shard_map/ppermute | solution.py:261
  33.8 31.2 %all-to-all-start = ((f32[32,64,128]{2,1,0:T(8,128)}), f32[32,64,128]{2,1,0:T(8,128)S(1)}, u32[]{:S(2)}, u32[]{:S(2)}) async-start(f32[32,64,128]{2,1,0:T(8,128)} %bitcast.2), calls=%async_computation | async-start | bytes 2097152 | tf_op jit(solution)/shard_map/all_to_all | solution.py:296
  38.7 14.6 %collective-permute-start.4 = (f32[64,512]{1,0:T(8,128)}, f32[64,512]{1,0:T(8,128)S(1)}, u32[]{:S(2)}, u32[]{:S(2)}) collective-permute-start(f32[64,512]{1,0:T(8,128)} %collective-permute-done.3), channel_id=1, source_target_pairs={{0,2},{1,3},{2,0},{3,1},{4,6},{5,7},{6,4},{7,5},{8,10},{9,11},{10,... | collective-permute-start | bytes 393224 | tf_op jit(solution)/shard_map/ppermute | solution.py:244
  40.6 12.8 %collective-permute-start.5 = (f32[64,512]{1,0:T(8,128)}, f32[64,512]{1,0:T(8,128)S(1)}, u32[]{:S(2)}, u32[]{:S(2)}) collective-permute-start(f32[64,512]{1,0:T(8,128)} %collective-permute-done.3), channel_id=1, source_target_pairs={{0,4},{1,5},{2,6},{3,7},{4,0},{5,1},{6,2},{7,3},{8,12},{9,13},{10,... | collective-permute-start | bytes 393224 | tf_op jit(solution)/shard_map/ppermute | solution.py:244
  42.0 16.0 %collective-permute-start.6 = (f32[64,512]{1,0:T(8,128)}, f32[64,512]{1,0:T(8,128)S(1)}, u32[]{:S(2)}, u32[]{:S(2)}) collective-permute-start(f32[64,512]{1,0:T(8,128)} %collective-permute-done.3), channel_id=1, source_target_pairs={{0,6},{1,7},{2,4},{3,5},{4,2},{5,3},{6,0},{7,1},{8,14},{9,15},{10,... | collective-permute-start | bytes 393224 | tf_op jit(solution)/shard_map/ppermute | solution.py:244
  59.0 2.0 %collective-permute-start.7 = (f32[4,64,512]{2,1,0:T(8,128)S(1)}, f32[4,64,512]{2,1,0:T(8,128)S(1)}, u32[]{:S(2)}, u32[]{:S(2)}) collective-permute-start(f32[4,64,512]{2,1,0:T(8,128)S(1)} %pad_maximum_fusion), channel_id=1, source_target_pairs={{0,1},{1,0},{2,3},{3,2},{4,5},{5,4},{6,7},{7,6},{8,9},{9,8},{10,11... | collective-permute-start | bytes 1572872 | tf_op jit(solution)/shard_map/ppermute | solution.py:244
  96.3 7.8 %collective-permute-start.11 = (f32[8,4096]{1,0:T(8,128)S(1)}, f32[8,4096]{1,0:T(8,128)S(1)}, u32[]{:S(2)}, u32[]{:S(2)}) collective-permute-start(f32[8,4096]{1,0:T(8,128)S(1)} %get-tuple-element.39), channel_id=1, source_target_pairs={{0,24},{8,16},{16,8},{24,0},{1,25},{9,17},{17,9},{25,1},{2,26},{10... | collective-permute-start | bytes 393224 | tf_op jit(solution)/shard_map/ppermute | solution.py:244
  98.6 22.0 %collective-permute-start.8 = (f32[8,4096]{1,0:T(8,128)S(1)}, f32[8,4096]{1,0:T(8,128)S(1)}, u32[]{:S(2)}, u32[]{:S(2)}) collective-permute-start(f32[8,4096]{1,0:T(8,128)S(1)} %get-tuple-element.35), channel_id=1, source_target_pairs={{0,24},{8,16},{16,8},{24,0},{1,25},{9,17},{17,9},{25,1},{2,26},{10... | collective-permute-start | bytes 393224 | tf_op jit(solution)/shard_map/ppermute | solution.py:244
  101.2 18.6 %collective-permute-start.12 = (f32[8,4096]{1,0:T(8,128)S(1)}, f32[8,4096]{1,0:T(8,128)S(1)}, u32[]{:S(2)}, u32[]{:S(2)}) collective-permute-start(f32[8,4096]{1,0:T(8,128)S(1)} %get-tuple-element.40), channel_id=1, source_target_pairs={{0,16},{8,24},{16,0},{24,8},{1,17},{9,25},{17,1},{25,9},{2,18},{10... | collective-permute-start | bytes 393224 | tf_op jit(solution)/shard_map/ppermute | solution.py:244
  101.2 18.6 %collective-permute-start.13 = (f32[8,4096]{1,0:T(8,128)S(1)}, f32[8,4096]{1,0:T(8,128)S(1)}, u32[]{:S(2)}, u32[]{:S(2)}) collective-permute-start(f32[8,4096]{1,0:T(8,128)S(1)} %get-tuple-element.41), channel_id=1, source_target_pairs={{0,8},{8,0},{16,24},{24,16},{1,9},{9,1},{17,25},{25,17},{2,10},{10... | collective-permute-start | bytes 393224 | tf_op jit(solution)/shard_map/ppermute | solution.py:244
  103.0 18.8 %collective-permute-start.9 = (f32[8,4096]{1,0:T(8,128)S(1)}, f32[8,4096]{1,0:T(8,128)S(1)}, u32[]{:S(2)}, u32[]{:S(2)}) collective-permute-start(f32[8,4096]{1,0:T(8,128)S(1)} %get-tuple-element.36), channel_id=1, source_target_pairs={{0,16},{8,24},{16,0},{24,8},{1,17},{9,25},{17,1},{25,9},{2,18},{10... | collective-permute-start | bytes 393224 | tf_op jit(solution)/shard_map/ppermute | solution.py:244
  104.1 17.7 %collective-permute-start.10 = (f32[8,4096]{1,0:T(8,128)S(1)}, f32[8,4096]{1,0:T(8,128)S(1)}, u32[]{:S(2)}, u32[]{:S(2)}) collective-permute-start(f32[8,4096]{1,0:T(8,128)S(1)} %get-tuple-element.37), channel_id=1, source_target_pairs={{0,8},{8,0},{16,24},{24,16},{1,9},{9,1},{17,25},{25,17},{2,10},{10... | collective-permute-start | bytes 393224 | tf_op jit(solution)/shard_map/ppermute | solution.py:244

commit v12 on v11

--- a/solution.py
+++ b/solution.py
@@ -98,16 +98,6 @@
     copies = [
         pltpu.make_async_copy(noise_ref.at[here ^ step], out, sem.at[step]) for step, out in enumerate(outs)
     ]
-    for copy in copies:
-        copy.start()
-    for copy in copies:
-        copy.wait()
-
-
-def hold_kernel(*refs):
-    count = len(refs) // 2
-    sem = refs[-1]
-    copies = [pltpu.make_async_copy(refs[at], refs[count + at], sem.at[at]) for at in range(count)]
     for copy in copies:
         copy.start()
     for copy in copies:
@@ -269,11 +259,6 @@
     return call(factor_kernel, [whole, whole], [], 0, share)
 
 
-def hold(tables):
-    outs = [array(*table.shape, dtype=table.dtype) for table in tables]
-    return call(hold_kernel, outs, [dma(len(tables))], 0, *tables, spaces=[pl.ANY] * len(tables))
-
-
 def bind(kernel, *static):
     return lambda *refs: kernel(*static, *refs)
 
@@ -289,14 +274,15 @@
     chunks = CHUNKS if own % (8 * CHUNKS) == 0 else 1
     dets = own // chunks
     flops = 3 * 2 * n1 * own * (2 * n2) ** 2
-    tables = hold((twiddles(n1, n2), *fourier_matrix(n2, planes)))
+    tables = (twiddles(n1, n2), *fourier_matrix(n2, planes))
 
     def exchange(value, shape):
         value = value.reshape(planes * groups, pieces * own, LANES)
         return lax.all_to_all(value, ("tm", "det"), split_axis=0, concat_axis=0, tiled=True).reshape(shape)
 
     parts = call(
-        slice_kernel, [array(own, span)] * planes, [dma(planes)], 0, noise.reshape(planes, own, span), spaces=[pl.ANY]
+        slice_kernel, [array(own, span)] * planes, [dma(planes)], 0, noise.reshape(planes, own, span), spaces=[pl.ANY],
+        out_space=pl.ANY,
     )
     layout = (planes, groups, pieces, own, LANES)
     (spectrum,) = call(

time: 123 us -> 122 us (level)
  waiting for transfers between devices: 50.6 us -> 53.1 us
    ppermute x13, waiting for transfers between devices: 46.7 us -> 48.3 us  [swap(): lax.ppermute(value, axis, [(place, place ^ mask) for place in range(lax.a...]
    pallas_call x9 -> x8, Pallas kernels: 7.95 us -> 6.9 us  [call(): pl.pallas_call(kernel, out_shape=outs, in_specs=[pl.BlockSpec(memory_spac...]
  transfers between devices with their start and end apart: 15 -> 15, of which waited for: 8 -> 8; matrix products, arithmetic and copies ran while one was open for 2% -> 0% of each run, Pallas kernels for 4% -> 4%
where the time goes in v12:
time: 122 us
  waiting for transfers between devices  53.1 us (44%)
  starting transfers between devices  30.4 us (25%)
  blocking collectives  29.7 us (24%)
  Pallas kernels  6.9 us (6%)
  local copies, waits for them, and re-layouts  1.37 us (1%)
    ppermute x13, waiting for transfers between devices, swap(): lax.ppermute(value, axis, [(place, place ^ mask) for place in range(lax.a...  48.3 us
    all_to_all x1, blocking collectives, exchange(): lax.all_to_all(value, ('tm', 'det'), split_axis=0, concat_axis=0, tiled=T...  29.7 us
    ppermute x13, starting transfers between devices, swap(): lax.ppermute(value, axis, [(place, place ^ mask) for place in range(lax.a...  24.7 us
    pallas_call x8, Pallas kernels, call(): pl.pallas_call(kernel, out_shape=outs, in_specs=[pl.BlockSpec(memory_spac...  6.9 us
    all_to_all x1, starting transfers between devices, exchange(): lax.all_to_all(value, ('tm', 'det'), split_axis=0, concat_axis=0, tiled=T...  4.92 us
    all_to_all x1, waiting for transfers between devices, exchange(): lax.all_to_all(value, ('tm', 'det'), split_axis=0, concat_axis=0, tiled=T...  4.78 us
  transfers between devices with their start and end apart: 15, of which 8 were waited for; matrix products, arithmetic and copies ran while one was open for 0% of the time, Pallas kernels for 4%

profile of v12, /device:TPU:0, one launch (start us, length us, event | category | flops | bytes accessed | tf_op | source)
XLA Modules:
  0.0 121.6 jit_solution(6246901656066497608)
XLA Ops:
  0.0 1.3 %copy-done.3 = f32[64,4096]{1,0:T(8,128)S(1)} copy-done((f32[64,4096]{1,0:T(8,128)S(1)}, f32[64,4096]{1,0:T(8,128)}, u32[]{:S(2)}) %copy-start.3) | copy-done | bytes 1048600
  1.4 5.1 %collective-permute-start = (f32[16,4096]{1,0:T(8,128)S(1)}, f32[16,4096]{1,0:T(8,128)S(1)}, u32[]{:S(2)}, u32[]{:S(2)}) collective-permute-start(f32[16,4096]{1,0:T(8,128)S(1)} %get-tuple-element.21), channel_id=1, source_target_pairs={{0,24},{8,16},{16,8},{24,0},{1,25},{9,17},{17,9},{25,1},{2,26},{10... | collective-permute-start | bytes 786440 | tf_op jit(solution)/shard_map/ppermute | solution.py:234
  8.0 5.8 %collective-permute-done.refs_0_ = f32[16,4096]{1,0:T(8,128)S(1)} collective-permute-done((f32[16,4096]{1,0:T(8,128)S(1)}, f32[16,4096]{1,0:T(8,128)S(1)}, u32[]{:S(2)}, u32[]{:S(2)}) %collective-permute-start) | collective-permute-done | bytes 262176 | tf_op jit(solution)/shard_map/ppermute | solution.py:234
  13.8 16.4 %collective-permute-done.1.refs_1_ = f32[16,4096]{1,0:T(8,128)S(1)} collective-permute-done((f32[16,4096]{1,0:T(8,128)S(1)}, f32[16,4096]{1,0:T(8,128)S(1)}, u32[]{:S(2)}, u32[]{:S(2)}) %collective-permute-start.1) | collective-permute-done | bytes 262176 | tf_op jit(solution)/shard_map/ppermute | solution.py:234
  30.2 2.5 %shard_map.56 = f32[4,8,4,16,128]{4,3,2,1,0:T(8,128)} custom-call(f32[16,4096]{1,0:T(8,128)S(1)} %collective-permute-done.refs_0_, f32[16,4096]{1,0:T(8,128)S(1)} %collective-permute-done.1.refs_1_, f32[16,4096]{1,0:T(8,128)S(1)} %collective-permute-done.2.refs_2_, f32[16,4096]{1,0:T(8,128)S(1)} %get-tuple-element.24.refs_3_, f32[2,32,256]{2,1,0:T(8,128)S(1)} %copy-done.4, ...), custom_call_target="tpu_custom_call" | custom-call | flops 805306368 | bytes 3211264 | tf_op jit(solution)/shard_map/pallas_call | solution.py:213
  32.7 4.9 %all-to-all-start = ((f32[32,64,128]{2,1,0:T(8,128)}), f32[32,64,128]{2,1,0:T(8,128)S(1)}, u32[]{:S(2)}, u32[]{:S(2)}) async-start(f32[32,64,128]{2,1,0:T(8,128)} %bitcast.2), calls=%async_computation | async-start | bytes 2097152 | tf_op jit(solution)/shard_map/all_to_all | solution.py:281
  37.7 1.8 %collective-permute-start.4 = (f32[64,512]{1,0:T(8,128)S(1)}, f32[64,512]{1,0:T(8,128)S(1)}, u32[]{:S(2)}, u32[]{:S(2)}) collective-permute-start(f32[64,512]{1,0:T(8,128)S(1)} %collective-permute-done.3), channel_id=1, source_target_pairs={{0,2},{1,3},{2,0},{3,1},{4,6},{5,7},{6,4},{7,5},{8,10},{9,11},{10,... | collective-permute-start | bytes 393224 | tf_op jit(solution)/shard_map/ppermute | solution.py:234
  39.5 1.5 %collective-permute-start.5 = (f32[64,512]{1,0:T(8,128)S(1)}, f32[64,512]{1,0:T(8,128)S(1)}, u32[]{:S(2)}, u32[]{:S(2)}) collective-permute-start(f32[64,512]{1,0:T(8,128)S(1)} %collective-permute-done.3), channel_id=1, source_target_pairs={{0,4},{1,5},{2,6},{3,7},{4,0},{5,1},{6,2},{7,3},{8,12},{9,13},{10,... | collective-permute-start | bytes 393224 | tf_op jit(solution)/shard_map/ppermute | solution.py:234
  41.2 11.0 %collective-permute-done.4 = f32[64,512]{1,0:T(8,128)S(1)} collective-permute-done((f32[64,512]{1,0:T(8,128)S(1)}, f32[64,512]{1,0:T(8,128)S(1)}, u32[]{:S(2)}, u32[]{:S(2)}) %collective-permute-start.4) | collective-permute-done | bytes 131104 | tf_op jit(solution)/shard_map/ppermute | solution.py:234
  52.3 4.7 %collective-permute-done.6 = f32[64,512]{1,0:T(8,128)S(1)} collective-permute-done((f32[64,512]{1,0:T(8,128)S(1)}, f32[64,512]{1,0:T(8,128)S(1)}, u32[]{:S(2)}, u32[]{:S(2)}) %collective-permute-start.6) | collective-permute-done | bytes 131104 | tf_op jit(solution)/shard_map/ppermute | solution.py:234
  57.1 1.8 %collective-permute-done.7 = f32[4,64,512]{2,1,0:T(8,128)S(1)} collective-permute-done((f32[4,64,512]{2,1,0:T(8,128)S(1)}, f32[4,64,512]{2,1,0:T(8,128)S(1)}, u32[]{:S(2)}, u32[]{:S(2)}) %collective-permute-start.7) | collective-permute-done | bytes 524320 | tf_op jit(solution)/shard_map/ppermute | solution.py:234
  59.1 4.8 %all-to-all-done = f32[32,64,128]{2,1,0:T(8,128)S(1)} async-done(((f32[32,64,128]{2,1,0:T(8,128)}), f32[32,64,128]{2,1,0:T(8,128)S(1)}, u32[]{:S(2)}, u32[]{:S(2)}) %all-to-all-start) | async-done | bytes 1048608 | tf_op jit(solution)/shard_map/all_to_all | solution.py:281
  64.7 29.7 %all_to_all.10 = f32[32,64,128]{2,1,0:T(8,128)S(1)} all-to-all(f32[32,64,128]{2,1,0:T(8,128)S(1)} %bitcast.19), channel_id=1, replica_groups=mesh['tm'=4,'det'=8] {'tm','det'}, dimensions={0} | all-to-all | bytes 2097152 | tf_op jit(solution)/shard_map/all_to_all | solution.py:281
  94.4 0.9 shard_map.60
  95.2 1.4 %collective-permute-start.11 = (f32[8,4096]{1,0:T(8,128)S(1)}, f32[8,4096]{1,0:T(8,128)S(1)}, u32[]{:S(2)}, u32[]{:S(2)}) collective-permute-start(f32[8,4096]{1,0:T(8,128)S(1)} %get-tuple-element.33), channel_id=1, source_target_pairs={{0,24},{8,16},{16,8},{24,0},{1,25},{9,17},{17,9},{25,1},{2,26},{10... | collective-permute-start | bytes 393224 | tf_op jit(solution)/shard_map/ppermute | solution.py:234
  96.6 0.9 shard_map.59
  97.5 2.6 %collective-permute-start.8 = (f32[8,4096]{1,0:T(8,128)S(1)}, f32[8,4096]{1,0:T(8,128)S(1)}, u32[]{:S(2)}, u32[]{:S(2)}) collective-permute-start(f32[8,4096]{1,0:T(8,128)S(1)} %get-tuple-element.29), channel_id=1, source_target_pairs={{0,24},{8,16},{16,8},{24,0},{1,25},{9,17},{17,9},{25,1},{2,26},{10... | collective-permute-start | bytes 393224 | tf_op jit(solution)/shard_map/ppermute | solution.py:234
  100.1 1.9 %collective-permute-start.13 = (f32[8,4096]{1,0:T(8,128)S(1)}, f32[8,4096]{1,0:T(8,128)S(1)}, u32[]{:S(2)}, u32[]{:S(2)}) collective-permute-start(f32[8,4096]{1,0:T(8,128)S(1)} %get-tuple-element.35), channel_id=1, source_target_pairs={{0,8},{8,0},{16,24},{24,16},{1,9},{9,1},{17,25},{25,17},{2,10},{10... | collective-permute-start | bytes 393224 | tf_op jit(solution)/shard_map/ppermute | solution.py:234
  102.0 1.1 collective-permute-start.9
  103.0 8.4 %collective-permute-start.10 = (f32[8,4096]{1,0:T(8,128)S(1)}, f32[8,4096]{1,0:T(8,128)S(1)}, u32[]{:S(2)}, u32[]{:S(2)}) collective-permute-start(f32[8,4096]{1,0:T(8,128)S(1)} %get-tuple-element.31), channel_id=1, source_target_pairs={{0,8},{8,0},{16,24},{24,16},{1,9},{9,1},{17,25},{25,17},{2,10},{10... | collective-permute-start | bytes 393224 | tf_op jit(solution)/shard_map/ppermute | solution.py:234
  111.4 7.2 %collective-permute-done.12.refs_1_ = f32[8,4096]{1,0:T(8,128)S(1)} collective-permute-done((f32[8,4096]{1,0:T(8,128)S(1)}, f32[8,4096]{1,0:T(8,128)S(1)}, u32[]{:S(2)}, u32[]{:S(2)}) %collective-permute-start.12) | collective-permute-done | bytes 131104 | tf_op jit(solution)/shard_map/ppermute | solution.py:234
  118.7 0.8 shard_map.61.refs_4_
  119.5 1.2 %collective-permute-done.9.refs_1_ = f32[8,4096]{1,0:T(8,128)S(1)} collective-permute-done((f32[8,4096]{1,0:T(8,128)S(1)}, f32[8,4096]{1,0:T(8,128)S(1)}, u32[]{:S(2)}, u32[]{:S(2)}) %collective-permute-start.9) | collective-permute-done | bytes 131104 | tf_op jit(solution)/shard_map/ppermute | solution.py:234
  120.8 0.8 shard_map.62
  (32 shorter events, 2.9 us)
Async XLA Ops:
  0.0 7.2 %copy-start = (f32[1,128,512]{2,1,0:T(8,128)S(1)}, f32[1,128,512]{2,1,0:T(8,128)}, u32[]{:S(2)}) copy-start(f32[1,128,512]{2,1,0:T(8,128)} %param.6) | copy-start | bytes 786436
  0.0 1.3 %copy-start.3 = (f32[64,4096]{1,0:T(8,128)S(1)}, f32[64,4096]{1,0:T(8,128)}, u32[]{:S(2)}) copy-start(f32[64,4096]{1,0:T(8,128)} %param.5) | copy-start | bytes 3145732
  1.3 29.0 %copy-start.1 = (bf16[512,512]{1,0:T(8,128)(2,1)S(1)}, bf16[512,512]{1,0:T(8,128)(2,1)}, u32[]{:S(2)}) copy-start(bf16[512,512]{1,0:T(8,128)(2,1)} %constant.20.clone.refs_5_.refs_2_) | copy-start | bytes 1572868
  1.3 29.0 %copy-start.2 = (bf16[512,512]{1,0:T(8,128)(2,1)S(1)}, bf16[512,512]{1,0:T(8,128)(2,1)}, u32[]{:S(2)}) copy-start(bf16[512,512]{1,0:T(8,128)(2,1)} %constant.21.clone.refs_6_.refs_3_) | copy-start | bytes 1572868
  1.4 12.4 %collective-permute-start = (f32[16,4096]{1,0:T(8,128)S(1)}, f32[16,4096]{1,0:T(8,128)S(1)}, u32[]{:S(2)}, u32[]{:S(2)}) collective-permute-start(f32[16,4096]{1,0:T(8,128)S(1)} %get-tuple-element.21), channel_id=1, source_target_pairs={{0,24},{8,16},{16,8},{24,0},{1,25},{9,17},{17,9},{25,1},{2,26},{10... | collective-permute-start | bytes 786440 | tf_op jit(solution)/shard_map/ppermute | solution.py:234
  6.5 23.7 %collective-permute-start.1 = (f32[16,4096]{1,0:T(8,128)S(1)}, f32[16,4096]{1,0:T(8,128)S(1)}, u32[]{:S(2)}, u32[]{:S(2)}) collective-permute-start(f32[16,4096]{1,0:T(8,128)S(1)} %get-tuple-element.22), channel_id=1, source_target_pairs={{0,16},{8,24},{16,0},{24,8},{1,17},{9,25},{17,1},{25,9},{2,18},{10... | collective-permute-start | bytes 786440 | tf_op jit(solution)/shard_map/ppermute | solution.py:234
  6.5 23.7 %collective-permute-start.2 = (f32[16,4096]{1,0:T(8,128)S(1)}, f32[16,4096]{1,0:T(8,128)S(1)}, u32[]{:S(2)}, u32[]{:S(2)}) collective-permute-start(f32[16,4096]{1,0:T(8,128)S(1)} %get-tuple-element.23), channel_id=1, source_target_pairs={{0,8},{8,0},{16,24},{24,16},{1,9},{9,1},{17,25},{25,17},{2,10},{10... | collective-permute-start | bytes 786440 | tf_op jit(solution)/shard_map/ppermute | solution.py:234
  7.2 23.1 %copy-start.4 = (f32[2,32,256]{2,1,0:T(8,128)S(1)}, f32[2,32,256]{2,1,0:T(8,128)}, u32[]{:S(2)}) copy-start(f32[2,32,256]{2,1,0:T(8,128)} %constant.19.clone.refs_4_.refs_1_) | copy-start | bytes 196612
  7.2 25.6 %collective-permute-start.3 = (f32[64,512]{1,0:T(8,128)S(1)}, f32[64,512]{1,0:T(8,128)S(1)}, u32[]{:S(2)}, u32[]{:S(2)}) collective-permute-start(f32[64,512]{1,0:T(8,128)S(1)} %dynamic-slice_bitcast_fusion), channel_id=1, source_target_pairs={{0,0},{1,24},{2,8},{3,16},{4,17},{5,9},{6,25},{7,1},{8,2},{9,26},{... | collective-permute-start | bytes 393224 | tf_op jit(solution)/shard_map/ppermute | solution.py:251
  32.7 31.2 %all-to-all-start = ((f32[32,64,128]{2,1,0:T(8,128)}), f32[32,64,128]{2,1,0:T(8,128)S(1)}, u32[]{:S(2)}, u32[]{:S(2)}) async-start(f32[32,64,128]{2,1,0:T(8,128)} %bitcast.2), calls=%async_computation | async-start | bytes 2097152 | tf_op jit(solution)/shard_map/all_to_all | solution.py:281
  37.7 14.6 %collective-permute-start.4 = (f32[64,512]{1,0:T(8,128)S(1)}, f32[64,512]{1,0:T(8,128)S(1)}, u32[]{:S(2)}, u32[]{:S(2)}) collective-permute-start(f32[64,512]{1,0:T(8,128)S(1)} %collective-permute-done.3), channel_id=1, source_target_pairs={{0,2},{1,3},{2,0},{3,1},{4,6},{5,7},{6,4},{7,5},{8,10},{9,11},{10,... | collective-permute-start | bytes 393224 | tf_op jit(solution)/shard_map/ppermute | solution.py:234
  39.5 12.8 %collective-permute-start.5 = (f32[64,512]{1,0:T(8,128)S(1)}, f32[64,512]{1,0:T(8,128)S(1)}, u32[]{:S(2)}, u32[]{:S(2)}) collective-permute-start(f32[64,512]{1,0:T(8,128)S(1)} %collective-permute-done.3), channel_id=1, source_target_pairs={{0,4},{1,5},{2,6},{3,7},{4,0},{5,1},{6,2},{7,3},{8,12},{9,13},{10,... | collective-permute-start | bytes 393224 | tf_op jit(solution)/shard_map/ppermute | solution.py:234
  41.0 16.0 %collective-permute-start.6 = (f32[64,512]{1,0:T(8,128)S(1)}, f32[64,512]{1,0:T(8,128)S(1)}, u32[]{:S(2)}, u32[]{:S(2)}) collective-permute-start(f32[64,512]{1,0:T(8,128)S(1)} %collective-permute-done.3), channel_id=1, source_target_pairs={{0,6},{1,7},{2,4},{3,5},{4,2},{5,3},{6,0},{7,1},{8,14},{9,15},{10,... | collective-permute-start | bytes 393224 | tf_op jit(solution)/shard_map/ppermute | solution.py:234
  57.0 2.0 %collective-permute-start.7 = (f32[4,64,512]{2,1,0:T(8,128)S(1)}, f32[4,64,512]{2,1,0:T(8,128)S(1)}, u32[]{:S(2)}, u32[]{:S(2)}) collective-permute-start(f32[4,64,512]{2,1,0:T(8,128)S(1)} %pad_maximum_fusion), channel_id=1, source_target_pairs={{0,1},{1,0},{2,3},{3,2},{4,5},{5,4},{6,7},{7,6},{8,9},{9,8},{10,11... | collective-permute-start | bytes 1572872 | tf_op jit(solution)/shard_map/ppermute | solution.py:234
  95.2 7.8 %collective-permute-start.11 = (f32[8,4096]{1,0:T(8,128)S(1)}, f32[8,4096]{1,0:T(8,128)S(1)}, u32[]{:S(2)}, u32[]{:S(2)}) collective-permute-start(f32[8,4096]{1,0:T(8,128)S(1)} %get-tuple-element.33), channel_id=1, source_target_pairs={{0,24},{8,16},{16,8},{24,0},{1,25},{9,17},{17,9},{25,1},{2,26},{10... | collective-permute-start | bytes 393224 | tf_op jit(solution)/shard_map/ppermute | solution.py:234
  97.5 22.0 %collective-permute-start.8 = (f32[8,4096]{1,0:T(8,128)S(1)}, f32[8,4096]{1,0:T(8,128)S(1)}, u32[]{:S(2)}, u32[]{:S(2)}) collective-permute-start(f32[8,4096]{1,0:T(8,128)S(1)} %get-tuple-element.29), channel_id=1, source_target_pairs={{0,24},{8,16},{16,8},{24,0},{1,25},{9,17},{17,9},{25,1},{2,26},{10... | collective-permute-start | bytes 393224 | tf_op jit(solution)/shard_map/ppermute | solution.py:234
  100.1 18.6 %collective-permute-start.12 = (f32[8,4096]{1,0:T(8,128)S(1)}, f32[8,4096]{1,0:T(8,128)S(1)}, u32[]{:S(2)}, u32[]{:S(2)}) collective-permute-start(f32[8,4096]{1,0:T(8,128)S(1)} %get-tuple-element.34), channel_id=1, source_target_pairs={{0,16},{8,24},{16,0},{24,8},{1,17},{9,25},{17,1},{25,9},{2,18},{10... | collective-permute-start | bytes 393224 | tf_op jit(solution)/shard_map/ppermute | solution.py:234
  100.1 18.6 %collective-permute-start.13 = (f32[8,4096]{1,0:T(8,128)S(1)}, f32[8,4096]{1,0:T(8,128)S(1)}, u32[]{:S(2)}, u32[]{:S(2)}) collective-permute-start(f32[8,4096]{1,0:T(8,128)S(1)} %get-tuple-element.35), channel_id=1, source_target_pairs={{0,8},{8,0},{16,24},{24,16},{1,9},{9,1},{17,25},{25,17},{2,10},{10... | collective-permute-start | bytes 393224 | tf_op jit(solution)/shard_map/ppermute | solution.py:234
  102.0 18.8 %collective-permute-start.9 = (f32[8,4096]{1,0:T(8,128)S(1)}, f32[8,4096]{1,0:T(8,128)S(1)}, u32[]{:S(2)}, u32[]{:S(2)}) collective-permute-start(f32[8,4096]{1,0:T(8,128)S(1)} %get-tuple-element.30), channel_id=1, source_target_pairs={{0,16},{8,24},{16,0},{24,8},{1,17},{9,25},{17,1},{25,9},{2,18},{10... | collective-permute-start | bytes 393224 | tf_op jit(solution)/shard_map/ppermute | solution.py:234
  103.0 17.7 %collective-permute-start.10 = (f32[8,4096]{1,0:T(8,128)S(1)}, f32[8,4096]{1,0:T(8,128)S(1)}, u32[]{:S(2)}, u32[]{:S(2)}) collective-permute-start(f32[8,4096]{1,0:T(8,128)S(1)} %get-tuple-element.31), channel_id=1, source_target_pairs={{0,8},{8,0},{16,24},{24,16},{1,9},{9,1},{17,25},{25,17},{2,10},{10... | collective-permute-start | bytes 393224 | tf_op jit(solution)/shard_map/ppermute | solution.py:234

commit v13 on v12

--- a/solution.py
+++ b/solution.py
@@ -108,35 +108,32 @@
     here = lax.axis_index("tm")
     blocks, (turn_ref, high_ref, low_ref) = refs[:planes], refs[planes : planes + 3]
     out_ref, x_ref, mid_ref, stage_ref, sem = refs[-5:]
-    _, dets, span = x_ref.shape
-    _, groups, pieces, _, width = stage_ref.shape
+    span = x_ref.shape[-1]
+    _, groups, chunks, pieces, dets, width = stage_ref.shape
     per = span // n2
     for step, block in enumerate(reversed(blocks)):
         x_ref[here ^ step] = block[...]
-    for rows, lane in tiles(dets, n2):
-
-        def load(index):
-            start = (index % per) * n2 + lane
-            return x_ref[index // per, rows, start : start + LANES]
-
-        parts = [(load(t1), -load(t1 + n1)) for t1 in range(n1)]
-        for k1, (re, im) in enumerate(forward_butterflies(parts, 0.25)):
-            cosine = turn_ref[0, k1 : k1 + 1, lane : lane + LANES]
-            sine = turn_ref[1, k1 : k1 + 1, lane : lane + LANES]
-            place = slice(k1 * dets + rows.start, k1 * dets + rows.stop)
-            mid_ref[place, lane : lane + LANES] = re * cosine + im * sine
-            mid_ref[place, n2 + lane : n2 + lane + LANES] = im * cosine - re * sine
-    halves = split(mid_ref[...])
     copies = []
-    share = planes // 2
-    for part in range(2):
-        columns = slice(part * share * width, (part + 1) * share * width)
-        spectrum = product(halves, (high_ref[:, columns], low_ref[:, columns]))
-        these = pl.ds(part * share, share)
-        for plane in range(share):
+    for chunk in range(chunks):
+        for tile, lane in tiles(dets, n2):
+            rows = slice(chunk * dets + tile.start, chunk * dets + tile.stop)
+
+            def load(index):
+                start = (index % per) * n2 + lane
+                return x_ref[index // per, rows, start : start + LANES]
+
+            parts = [(load(t1), -load(t1 + n1)) for t1 in range(n1)]
+            for k1, (re, im) in enumerate(forward_butterflies(parts, 0.25)):
+                cosine = turn_ref[0, k1 : k1 + 1, lane : lane + LANES]
+                sine = turn_ref[1, k1 : k1 + 1, lane : lane + LANES]
+                place = slice(k1 * dets + tile.start, k1 * dets + tile.stop)
+                mid_ref[chunk, place, lane : lane + LANES] = re * cosine + im * sine
+                mid_ref[chunk, place, n2 + lane : n2 + lane + LANES] = im * cosine - re * sine
+        spectrum = product(split(mid_ref[chunk]), (high_ref[...], low_ref[...]))
+        for plane in range(planes):
             value = spectrum[:, plane * width : (plane + 1) * width]
-            stage_ref[part * share + plane] = value.reshape(groups, pieces, dets, width)
-        copies.append(pltpu.make_async_copy(stage_ref.at[these], out_ref.at[these], sem.at[part]))
+            stage_ref[plane, :, chunk] = value.reshape(groups, pieces, dets, width)
+        copies.append(pltpu.make_async_copy(stage_ref.at[:, :, chunk], out_ref.at[:, :, chunk], sem.at[chunk]))
         copies[-1].start()
     for copy in copies:
         copy.wait()
@@ -193,18 +190,20 @@
 
 def mix_kernel(x_ref, f_high, f_low, out_ref, x_mid, y_mid):
     planes, groups, chunks, pieces, dets, width = out_ref.shape
-    own = chunks * dets
-    for plane, group, piece in np.ndindex(planes, groups, pieces):
-        start = (group * planes + plane) * own
-        x_mid[start : start + own, piece * width : (piece + 1) * width] = x_ref[plane, group, piece]
+    places = []
+    for plane, group, chunk, piece in np.ndindex(planes, groups, chunks, pieces):
+        start = ((group * planes + plane) * chunks + chunk) * dets
+        rows, lanes = slice(start, start + dets), slice(piece * width, (piece + 1) * width)
+        places.append(((plane, group, chunk, piece), (rows, lanes)))
+    for source, target in places:
+        x_mid[target] = x_ref[source]
     x_high, x_low = split(x_mid[...])
     half = f_high.shape[0] // 2
     for part in range(2):
         rows, reach = slice(part * half, (part + 1) * half), (part + 1) * half
         y_mid[rows] = product((f_high[rows, :reach], f_low[rows, :reach]), (x_high[:reach], x_low[:reach]))
-    for plane, group, chunk, piece in np.ndindex(planes, groups, chunks, pieces):
-        start = (group * planes + plane) * own + chunk * dets
-        out_ref[plane, group, chunk, piece] = y_mid[start : start + dets, piece * width : (piece + 1) * width]
+    for target, source in places:
+        out_ref[target] = y_mid[source]
 
 
 def call(kernel, outs, scratch, flops, *args, spaces=None, out_space=pltpu.VMEM, aliases=None):
@@ -248,10 +247,14 @@
         for group in range(groups):
             target = plane_of[min(group, groups - 1 - group)]
             pairs.append((plane * groups + group, target * groups + 2 * plane + (group >= groups // 2)))
-    return lax.ppermute(mine, ("tm", "det"), pairs)
-
-
-def band_factor(share, groups):
+    middle = factor.shape[2] // 2
+    low = lax.ppermute(mine[:, :middle], ("tm", "det"), pairs)
+    high = lax.ppermute(mine[:, middle:], ("tm", "det"), [pair for pair in pairs if 2 * (pair[0] // groups) >= planes])
+    return low, high
+
+
+def band_factor(sides, groups):
+    share = jnp.concatenate(sides, axis=1)
     rows, columns = share.shape
     share = jnp.stack([share] + [swap(share, "det", mask) for mask in range(2, groups, 2)])
     share = jnp.concatenate([share, swap(share, "det", 1)])
@@ -276,28 +279,29 @@
     flops = 3 * 2 * n1 * own * (2 * n2) ** 2
     tables = (twiddles(n1, n2), *fourier_matrix(n2, planes))
 
-    def exchange(value, shape):
-        value = value.reshape(planes * groups, pieces * own, LANES)
-        return lax.all_to_all(value, ("tm", "det"), split_axis=0, concat_axis=0, tiled=True).reshape(shape)
-
     parts = call(
         slice_kernel, [array(own, span)] * planes, [dma(planes)], 0, noise.reshape(planes, own, span), spaces=[pl.ANY],
         out_space=pl.ANY,
     )
-    layout = (planes, groups, pieces, own, LANES)
+    layout = (planes, groups, chunks, pieces, dets, LANES)
+
+    def exchange(value):
+        value = value.reshape(planes * groups, pieces * own, LANES)
+        return lax.all_to_all(value, ("tm", "det"), split_axis=0, concat_axis=0, tiled=True).reshape(layout)
+
     (spectrum,) = call(
         bind(forward_kernel, n1, n2, planes), [array(*layout)],
-        [(planes, own, span), (n1 * own, 2 * n2), layout, dma(2)], flops, *trade(parts), *tables, out_space=pl.ANY,
+        [(planes, own, span), (chunks, n1 * dets, 2 * n2), layout, dma(chunks)], flops, *trade(parts), *tables, out_space=pl.ANY,
     )
-    spectrum, share = lax.optimization_barrier((spectrum, plane_factor(factor, planes, groups)))
-    f_high, f_low = band_factor(share, groups)
+    spectrum, sides = lax.optimization_barrier((spectrum, plane_factor(factor, planes, groups)))
+    f_high, f_low = band_factor(sides, groups)
 
     count = f_high.shape[0]
     (mixed,) = call(
-        mix_kernel, [array(planes, groups, chunks, pieces, dets, LANES)], [(count, pieces * LANES)] * 2,
-        2 * 3 * count * count * pieces * LANES, exchange(spectrum, layout), f_high, f_low,
+        mix_kernel, [array(*layout)], [(count, pieces * LANES)] * 2,
+        2 * 3 * count * count * pieces * LANES, exchange(spectrum), f_high, f_low,
     )
-    back = exchange(mixed, mixed.shape)
+    back = exchange(mixed)
     result = []
     for chunk in range(chunks):
         parts = call(

time: 122 us -> 121 us (level)
  transfers between devices with their start and end apart: 15 -> 16, of which waited for: 8 -> 8; matrix products, arithmetic and copies ran while one was open for 0% -> 0% of each run, Pallas kernels for 4% -> 3%
where the time goes in v13:
time: 121 us; the launch traced here: 120 us
  waiting for transfers between devices  52.5 us (43%)
  starting transfers between devices  30 us (25%)
  blocking collectives  29.7 us (25%)
  Pallas kernels  6.68 us (6%)
  local copies, waits for them, and re-layouts  1.4 us (1%)
    ppermute x13, waiting for transfers between devices, swap(): lax.ppermute(value, axis, [(place, place ^ mask) for place in range(lax.a...  47.7 us
    all_to_all x1, blocking collectives, exchange(): lax.all_to_all(value, ('tm', 'det'), split_axis=0, concat_axis=0, tiled=T...  29.7 us
    ppermute x13, starting transfers between devices, swap(): lax.ppermute(value, axis, [(place, place ^ mask) for place in range(lax.a...  24.7 us
    pallas_call x8, Pallas kernels, call(): pl.pallas_call(kernel, out_shape=outs, in_specs=[pl.BlockSpec(memory_spac...  6.68 us
    all_to_all x1, waiting for transfers between devices, exchange(): lax.all_to_all(value, ('tm', 'det'), split_axis=0, concat_axis=0, tiled=T...  4.78 us
    all_to_all x1, starting transfers between devices, exchange(): lax.all_to_all(value, ('tm', 'det'), split_axis=0, concat_axis=0, tiled=T...  4.03 us
  transfers between devices with their start and end apart: 16, of which 8 were waited for; matrix products, arithmetic and copies ran while one was open for 0% of the time, Pallas kernels for 3%

profile of v13, /device:TPU:0, one launch (start us, length us, event | category | flops | bytes accessed | tf_op | source)
XLA Modules:
  0.0 120.5 jit_solution(6615802276765739629)
XLA Ops:
  0.0 1.3 %copy-done.3 = f32[64,4096]{1,0:T(8,128)S(1)} copy-done((f32[64,4096]{1,0:T(8,128)S(1)}, f32[64,4096]{1,0:T(8,128)}, u32[]{:S(2)}) %copy-start.3) | copy-done | bytes 1048600
  1.4 5.1 %collective-permute-start = (f32[16,4096]{1,0:T(8,128)S(1)}, f32[16,4096]{1,0:T(8,128)S(1)}, u32[]{:S(2)}, u32[]{:S(2)}) collective-permute-start(f32[16,4096]{1,0:T(8,128)S(1)} %get-tuple-element.22), channel_id=1, source_target_pairs={{0,24},{8,16},{16,8},{24,0},{1,25},{9,17},{17,9},{25,1},{2,26},{10... | collective-permute-start | bytes 786440 | tf_op jit(solution)/shard_map/ppermute | solution.py:233
  8.5 5.3 %collective-permute-done.refs_0_ = f32[16,4096]{1,0:T(8,128)S(1)} collective-permute-done((f32[16,4096]{1,0:T(8,128)S(1)}, f32[16,4096]{1,0:T(8,128)S(1)}, u32[]{:S(2)}, u32[]{:S(2)}) %collective-permute-start) | collective-permute-done | bytes 262176 | tf_op jit(solution)/shard_map/ppermute | solution.py:233
  13.8 16.4 %collective-permute-done.1.refs_1_ = f32[16,4096]{1,0:T(8,128)S(1)} collective-permute-done((f32[16,4096]{1,0:T(8,128)S(1)}, f32[16,4096]{1,0:T(8,128)S(1)}, u32[]{:S(2)}, u32[]{:S(2)}) %collective-permute-start.1) | collective-permute-done | bytes 262176 | tf_op jit(solution)/shard_map/ppermute | solution.py:233
  30.3 2.3 %shard_map.56 = f32[4,8,2,4,8,128]{5,4,3,2,1,0:T(8,128)} custom-call(f32[16,4096]{1,0:T(8,128)S(1)} %collective-permute-done.refs_0_, f32[16,4096]{1,0:T(8,128)S(1)} %collective-permute-done.1.refs_1_, f32[16,4096]{1,0:T(8,128)S(1)} %collective-permute-done.2.refs_2_, f32[16,4096]{1,0:T(8,128)S(1)} %get-tuple-element.25.refs_3_, ...), custom_call_target="tpu_custom_call" | custom-call | flops 805306368 | bytes 3211264 | tf_op jit(solution)/shard_map/pallas_call | solution.py:212
  32.5 4.0 %all-to-all-start = ((f32[32,64,128]{2,1,0:T(8,128)}), f32[32,64,128]{2,1,0:T(8,128)S(1)}, u32[]{:S(2)}, u32[]{:S(2)}) async-start(f32[32,64,128]{2,1,0:T(8,128)} %bitcast.2), calls=%async_computation | async-start | bytes 2097152 | tf_op jit(solution)/shard_map/all_to_all | solution.py:290
  36.6 1.8 %collective-permute-start.5 = (f32[64,512]{1,0:T(8,128)S(1)}, f32[64,512]{1,0:T(8,128)S(1)}, u32[]{:S(2)}, u32[]{:S(2)}) collective-permute-start(f32[64,512]{1,0:T(8,128)S(1)} %constant_dynamic-update-slice_fusion), channel_id=1, source_target_pairs={{0,2},{1,3},{2,0},{3,1},{4,6},{5,7},{6,4},{7,5},{8,10},{9,11},{10,... | collective-permute-start | bytes 393224 | tf_op jit(solution)/shard_map/ppermute | solution.py:233
  38.4 1.5 %collective-permute-start.6 = (f32[64,512]{1,0:T(8,128)S(1)}, f32[64,512]{1,0:T(8,128)S(1)}, u32[]{:S(2)}, u32[]{:S(2)}) collective-permute-start(f32[64,512]{1,0:T(8,128)S(1)} %constant_dynamic-update-slice_fusion), channel_id=1, source_target_pairs={{0,4},{1,5},{2,6},{3,7},{4,0},{5,1},{6,2},{7,3},{8,12},{9,13},{10,... | collective-permute-start | bytes 393224 | tf_op jit(solution)/shard_map/ppermute | solution.py:233
  40.2 11.0 %collective-permute-done.5 = f32[64,512]{1,0:T(8,128)S(1)} collective-permute-done((f32[64,512]{1,0:T(8,128)S(1)}, f32[64,512]{1,0:T(8,128)S(1)}, u32[]{:S(2)}, u32[]{:S(2)}) %collective-permute-start.5) | collective-permute-done | bytes 131104 | tf_op jit(solution)/shard_map/ppermute | solution.py:233
  51.2 4.7 %collective-permute-done.7 = f32[64,512]{1,0:T(8,128)S(1)} collective-permute-done((f32[64,512]{1,0:T(8,128)S(1)}, f32[64,512]{1,0:T(8,128)S(1)}, u32[]{:S(2)}, u32[]{:S(2)}) %collective-permute-start.7) | collective-permute-done | bytes 131104 | tf_op jit(solution)/shard_map/ppermute | solution.py:233
  56.0 1.8 %collective-permute-done.8 = f32[4,64,512]{2,1,0:T(8,128)S(1)} collective-permute-done((f32[4,64,512]{2,1,0:T(8,128)S(1)}, f32[4,64,512]{2,1,0:T(8,128)S(1)}, u32[]{:S(2)}, u32[]{:S(2)}) %collective-permute-start.8) | collective-permute-done | bytes 524320 | tf_op jit(solution)/shard_map/ppermute | solution.py:233
  58.0 4.8 %all-to-all-done = f32[32,64,128]{2,1,0:T(8,128)S(1)} async-done(((f32[32,64,128]{2,1,0:T(8,128)}), f32[32,64,128]{2,1,0:T(8,128)S(1)}, u32[]{:S(2)}, u32[]{:S(2)}) %all-to-all-start) | async-done | bytes 1048608 | tf_op jit(solution)/shard_map/all_to_all | solution.py:290
  63.6 29.7 %all_to_all.10 = f32[32,64,128]{2,1,0:T(8,128)S(1)} all-to-all(f32[32,64,128]{2,1,0:T(8,128)S(1)} %bitcast.19), channel_id=1, replica_groups=mesh['tm'=4,'det'=8] {'tm','det'}, dimensions={0} | all-to-all | bytes 2097152 | tf_op jit(solution)/shard_map/all_to_all | solution.py:290
  93.3 0.9 shard_map.60
  94.2 1.4 %collective-permute-start.12 = (f32[8,4096]{1,0:T(8,128)S(1)}, f32[8,4096]{1,0:T(8,128)S(1)}, u32[]{:S(2)}, u32[]{:S(2)}) collective-permute-start(f32[8,4096]{1,0:T(8,128)S(1)} %get-tuple-element.35), channel_id=1, source_target_pairs={{0,24},{8,16},{16,8},{24,0},{1,25},{9,17},{17,9},{25,1},{2,26},{10... | collective-permute-start | bytes 393224 | tf_op jit(solution)/shard_map/ppermute | solution.py:233
  95.5 0.9 shard_map.59
  96.4 2.6 %collective-permute-start.9 = (f32[8,4096]{1,0:T(8,128)S(1)}, f32[8,4096]{1,0:T(8,128)S(1)}, u32[]{:S(2)}, u32[]{:S(2)}) collective-permute-start(f32[8,4096]{1,0:T(8,128)S(1)} %get-tuple-element.31), channel_id=1, source_target_pairs={{0,24},{8,16},{16,8},{24,0},{1,25},{9,17},{17,9},{25,1},{2,26},{10... | collective-permute-start | bytes 393224 | tf_op jit(solution)/shard_map/ppermute | solution.py:233
  99.0 1.9 %collective-permute-start.14 = (f32[8,4096]{1,0:T(8,128)S(1)}, f32[8,4096]{1,0:T(8,128)S(1)}, u32[]{:S(2)}, u32[]{:S(2)}) collective-permute-start(f32[8,4096]{1,0:T(8,128)S(1)} %get-tuple-element.37), channel_id=1, source_target_pairs={{0,8},{8,0},{16,24},{24,16},{1,9},{9,1},{17,25},{25,17},{2,10},{10... | collective-permute-start | bytes 393224 | tf_op jit(solution)/shard_map/ppermute | solution.py:233
  100.9 1.1 collective-permute-start.10
  101.9 8.4 %collective-permute-start.11 = (f32[8,4096]{1,0:T(8,128)S(1)}, f32[8,4096]{1,0:T(8,128)S(1)}, u32[]{:S(2)}, u32[]{:S(2)}) collective-permute-start(f32[8,4096]{1,0:T(8,128)S(1)} %get-tuple-element.33), channel_id=1, source_target_pairs={{0,8},{8,0},{16,24},{24,16},{1,9},{9,1},{17,25},{25,17},{2,10},{10... | collective-permute-start | bytes 393224 | tf_op jit(solution)/shard_map/ppermute | solution.py:233
  110.4 7.3 %collective-permute-done.13.refs_1_ = f32[8,4096]{1,0:T(8,128)S(1)} collective-permute-done((f32[8,4096]{1,0:T(8,128)S(1)}, f32[8,4096]{1,0:T(8,128)S(1)}, u32[]{:S(2)}, u32[]{:S(2)}) %collective-permute-start.13) | collective-permute-done | bytes 131104 | tf_op jit(solution)/shard_map/ppermute | solution.py:233
  117.6 0.8 shard_map.61.refs_4_
  118.4 1.2 %collective-permute-done.10.refs_1_ = f32[8,4096]{1,0:T(8,128)S(1)} collective-permute-done((f32[8,4096]{1,0:T(8,128)S(1)}, f32[8,4096]{1,0:T(8,128)S(1)}, u32[]{:S(2)}, u32[]{:S(2)}) %collective-permute-start.10) | collective-permute-done | bytes 131104 | tf_op jit(solution)/shard_map/ppermute | solution.py:233
  119.7 0.8 shard_map.62
  (37 shorter events, 3.5 us)
Async XLA Ops:
  0.0 7.2 %copy-start = (f32[1,128,512]{2,1,0:T(8,128)S(1)}, f32[1,128,512]{2,1,0:T(8,128)}, u32[]{:S(2)}) copy-start(f32[1,128,512]{2,1,0:T(8,128)} %param.6) | copy-start | bytes 786436
  0.0 1.3 %copy-start.3 = (f32[64,4096]{1,0:T(8,128)S(1)}, f32[64,4096]{1,0:T(8,128)}, u32[]{:S(2)}) copy-start(f32[64,4096]{1,0:T(8,128)} %param.5) | copy-start | bytes 3145732
  1.3 29.0 %copy-start.2 = (bf16[512,512]{1,0:T(8,128)(2,1)S(1)}, bf16[512,512]{1,0:T(8,128)(2,1)}, u32[]{:S(2)}) copy-start(bf16[512,512]{1,0:T(8,128)(2,1)} %constant.21.clone.refs_6_.refs_3_) | copy-start | bytes 1572868
  1.3 29.0 %copy-start.4 = (f32[2,32,256]{2,1,0:T(8,128)S(1)}, f32[2,32,256]{2,1,0:T(8,128)}, u32[]{:S(2)}) copy-start(f32[2,32,256]{2,1,0:T(8,128)} %constant.19.clone.refs_4_.refs_1_) | copy-start | bytes 196612
  1.4 28.9 %copy-start.1 = (bf16[512,512]{1,0:T(8,128)(2,1)S(1)}, bf16[512,512]{1,0:T(8,128)(2,1)}, u32[]{:S(2)}) copy-start(bf16[512,512]{1,0:T(8,128)(2,1)} %constant.20.clone.refs_5_.refs_2_) | copy-start | bytes 1572868
  1.4 12.4 %collective-permute-start = (f32[16,4096]{1,0:T(8,128)S(1)}, f32[16,4096]{1,0:T(8,128)S(1)}, u32[]{:S(2)}, u32[]{:S(2)}) collective-permute-start(f32[16,4096]{1,0:T(8,128)S(1)} %get-tuple-element.22), channel_id=1, source_target_pairs={{0,24},{8,16},{16,8},{24,0},{1,25},{9,17},{17,9},{25,1},{2,26},{10... | collective-permute-start | bytes 786440 | tf_op jit(solution)/shard_map/ppermute | solution.py:233
  6.5 23.7 %collective-permute-start.1 = (f32[16,4096]{1,0:T(8,128)S(1)}, f32[16,4096]{1,0:T(8,128)S(1)}, u32[]{:S(2)}, u32[]{:S(2)}) collective-permute-start(f32[16,4096]{1,0:T(8,128)S(1)} %get-tuple-element.23), channel_id=1, source_target_pairs={{0,16},{8,24},{16,0},{24,8},{1,17},{9,25},{17,1},{25,9},{2,18},{10... | collective-permute-start | bytes 786440 | tf_op jit(solution)/shard_map/ppermute | solution.py:233
  6.5 23.7 %collective-permute-start.2 = (f32[16,4096]{1,0:T(8,128)S(1)}, f32[16,4096]{1,0:T(8,128)S(1)}, u32[]{:S(2)}, u32[]{:S(2)}) collective-permute-start(f32[16,4096]{1,0:T(8,128)S(1)} %get-tuple-element.24), channel_id=1, source_target_pairs={{0,8},{8,0},{16,24},{24,16},{1,9},{9,1},{17,25},{25,17},{2,10},{10... | collective-permute-start | bytes 786440 | tf_op jit(solution)/shard_map/ppermute | solution.py:233
  7.2 25.3 %collective-permute-start.3 = (f32[64,256]{1,0:T(8,128)S(1)}, f32[64,256]{1,0:T(8,128)S(1)}, u32[]{:S(2)}, u32[]{:S(2)}) collective-permute-start(f32[64,256]{1,0:T(8,128)S(1)} %get-tuple-element.40), channel_id=1, source_target_pairs={{0,0},{1,24},{2,8},{3,16},{4,17},{5,9},{6,25},{7,1},{8,2},{9,26},{... | collective-permute-start | bytes 196616 | tf_op jit(solution)/shard_map/ppermute | solution.py:251
  7.9 24.7 %collective-permute-start.4 = (f32[64,256]{1,0:T(8,128)S(1)}, f32[64,256]{1,0:T(8,128)S(1)}, u32[]{:S(2)}, u32[]{:S(2)}) collective-permute-start(f32[64,256]{1,0:T(8,128)S(1)} %get-tuple-element.39), channel_id=1, source_target_pairs={{16,4},{17,28},{18,12},{19,20},{20,21},{21,13},{22,29},{23,5},{24,... | collective-permute-start | bytes 196616 | tf_op jit(solution)/shard_map/ppermute | solution.py:252
  32.5 30.3 %all-to-all-start = ((f32[32,64,128]{2,1,0:T(8,128)}), f32[32,64,128]{2,1,0:T(8,128)S(1)}, u32[]{:S(2)}, u32[]{:S(2)}) async-start(f32[32,64,128]{2,1,0:T(8,128)} %bitcast.2), calls=%async_computation | async-start | bytes 2097152 | tf_op jit(solution)/shard_map/all_to_all | solution.py:290
  36.6 14.6 %collective-permute-start.5 = (f32[64,512]{1,0:T(8,128)S(1)}, f32[64,512]{1,0:T(8,128)S(1)}, u32[]{:S(2)}, u32[]{:S(2)}) collective-permute-start(f32[64,512]{1,0:T(8,128)S(1)} %constant_dynamic-update-slice_fusion), channel_id=1, source_target_pairs={{0,2},{1,3},{2,0},{3,1},{4,6},{5,7},{6,4},{7,5},{8,10},{9,11},{10,... | collective-permute-start | bytes 393224 | tf_op jit(solution)/shard_map/ppermute | solution.py:233
  38.4 12.7 %collective-permute-start.6 = (f32[64,512]{1,0:T(8,128)S(1)}, f32[64,512]{1,0:T(8,128)S(1)}, u32[]{:S(2)}, u32[]{:S(2)}) collective-permute-start(f32[64,512]{1,0:T(8,128)S(1)} %constant_dynamic-update-slice_fusion), channel_id=1, source_target_pairs={{0,4},{1,5},{2,6},{3,7},{4,0},{5,1},{6,2},{7,3},{8,12},{9,13},{10,... | collective-permute-start | bytes 393224 | tf_op jit(solution)/shard_map/ppermute | solution.py:233
  39.9 15.9 %collective-permute-start.7 = (f32[64,512]{1,0:T(8,128)S(1)}, f32[64,512]{1,0:T(8,128)S(1)}, u32[]{:S(2)}, u32[]{:S(2)}) collective-permute-start(f32[64,512]{1,0:T(8,128)S(1)} %constant_dynamic-update-slice_fusion), channel_id=1, source_target_pairs={{0,6},{1,7},{2,4},{3,5},{4,2},{5,3},{6,0},{7,1},{8,14},{9,15},{10,... | collective-permute-start | bytes 393224 | tf_op jit(solution)/shard_map/ppermute | solution.py:233
  55.9 2.0 %collective-permute-start.8 = (f32[4,64,512]{2,1,0:T(8,128)S(1)}, f32[4,64,512]{2,1,0:T(8,128)S(1)}, u32[]{:S(2)}, u32[]{:S(2)}) collective-permute-start(f32[4,64,512]{2,1,0:T(8,128)S(1)} %pad_maximum_fusion), channel_id=1, source_target_pairs={{0,1},{1,0},{2,3},{3,2},{4,5},{5,4},{6,7},{7,6},{8,9},{9,8},{10,11... | collective-permute-start | bytes 1572872 | tf_op jit(solution)/shard_map/ppermute | solution.py:233
  94.2 7.8 %collective-permute-start.12 = (f32[8,4096]{1,0:T(8,128)S(1)}, f32[8,4096]{1,0:T(8,128)S(1)}, u32[]{:S(2)}, u32[]{:S(2)}) collective-permute-start(f32[8,4096]{1,0:T(8,128)S(1)} %get-tuple-element.35), channel_id=1, source_target_pairs={{0,24},{8,16},{16,8},{24,0},{1,25},{9,17},{17,9},{25,1},{2,26},{10... | collective-permute-start | bytes 393224 | tf_op jit(solution)/shard_map/ppermute | solution.py:233
  96.4 22.0 %collective-permute-start.9 = (f32[8,4096]{1,0:T(8,128)S(1)}, f32[8,4096]{1,0:T(8,128)S(1)}, u32[]{:S(2)}, u32[]{:S(2)}) collective-permute-start(f32[8,4096]{1,0:T(8,128)S(1)} %get-tuple-element.31), channel_id=1, source_target_pairs={{0,24},{8,16},{16,8},{24,0},{1,25},{9,17},{17,9},{25,1},{2,26},{10... | collective-permute-start | bytes 393224 | tf_op jit(solution)/shard_map/ppermute | solution.py:233
  99.0 18.6 %collective-permute-start.13 = (f32[8,4096]{1,0:T(8,128)S(1)}, f32[8,4096]{1,0:T(8,128)S(1)}, u32[]{:S(2)}, u32[]{:S(2)}) collective-permute-start(f32[8,4096]{1,0:T(8,128)S(1)} %get-tuple-element.36), channel_id=1, source_target_pairs={{0,16},{8,24},{16,0},{24,8},{1,17},{9,25},{17,1},{25,9},{2,18},{10... | collective-permute-start | bytes 393224 | tf_op jit(solution)/shard_map/ppermute | solution.py:233
  99.0 18.6 %collective-permute-start.14 = (f32[8,4096]{1,0:T(8,128)S(1)}, f32[8,4096]{1,0:T(8,128)S(1)}, u32[]{:S(2)}, u32[]{:S(2)}) collective-permute-start(f32[8,4096]{1,0:T(8,128)S(1)} %get-tuple-element.37), channel_id=1, source_target_pairs={{0,8},{8,0},{16,24},{24,16},{1,9},{9,1},{17,25},{25,17},{2,10},{10... | collective-permute-start | bytes 393224 | tf_op jit(solution)/shard_map/ppermute | solution.py:233
  100.9 18.8 %collective-permute-start.10 = (f32[8,4096]{1,0:T(8,128)S(1)}, f32[8,4096]{1,0:T(8,128)S(1)}, u32[]{:S(2)}, u32[]{:S(2)}) collective-permute-start(f32[8,4096]{1,0:T(8,128)S(1)} %get-tuple-element.32), channel_id=1, source_target_pairs={{0,16},{8,24},{16,0},{24,8},{1,17},{9,25},{17,1},{25,9},{2,18},{10... | collective-permute-start | bytes 393224 | tf_op jit(solution)/shard_map/ppermute | solution.py:233
  101.9 17.7 %collective-permute-start.11 = (f32[8,4096]{1,0:T(8,128)S(1)}, f32[8,4096]{1,0:T(8,128)S(1)}, u32[]{:S(2)}, u32[]{:S(2)}) collective-permute-start(f32[8,4096]{1,0:T(8,128)S(1)} %get-tuple-element.33), channel_id=1, source_target_pairs={{0,8},{8,0},{16,24},{24,16},{1,9},{9,1},{17,25},{25,17},{2,10},{10... | collective-permute-start | bytes 393224 | tf_op jit(solution)/shard_map/ppermute | solution.py:233

commit v14 on v13

--- a/solution.py
+++ b/solution.py
@@ -13,6 +13,7 @@
 LANES = 128
 VMEM_LIMIT = 48 * 1024 * 1024
 CHUNKS = 2
+FACTOR_WORK = 7 * 10**9
 
 
 def band_of(plane, planes):
@@ -259,7 +260,7 @@
     share = jnp.stack([share] + [swap(share, "det", mask) for mask in range(2, groups, 2)])
     share = jnp.concatenate([share, swap(share, "det", 1)])
     whole = array(groups * rows, columns, dtype=jnp.bfloat16)
-    return call(factor_kernel, [whole, whole], [], 0, share)
+    return call(factor_kernel, [whole, whole], [], FACTOR_WORK, share)
 
 
 def bind(kernel, *static):
@@ -293,7 +294,7 @@
         bind(forward_kernel, n1, n2, planes), [array(*layout)],
         [(planes, own, span), (chunks, n1 * dets, 2 * n2), layout, dma(chunks)], flops, *trade(parts), *tables, out_space=pl.ANY,
     )
-    spectrum, sides = lax.optimization_barrier((spectrum, plane_factor(factor, planes, groups)))
+    sides = plane_factor(factor, planes, groups)
     f_high, f_low = band_factor(sides, groups)
 
     count = f_high.shape[0]

time: 121 us -> 121 us (level)
  waiting for transfers between devices: 52.5 us -> 55.7 us
  starting transfers between devices: 30 us -> 26.8 us
    ppermute x13, starting transfers between devices: 24.7 us -> 21.4 us  [swap(): lax.ppermute(value, axis, [(place, place ^ mask) for place in range(lax.a...]
    ppermute x13, waiting for transfers between devices: 47.7 us -> 50 us  [swap(): lax.ppermute(value, axis, [(place, place ^ mask) for place in range(lax.a...]
  transfers between devices with their start and end apart: 16 -> 16, of which waited for: 8 -> 10; matrix products, arithmetic and copies ran while one was open for 0% -> 0% of each run, Pallas kernels for 3% -> 3%
where the time goes in v14:
time: 121 us; the launch traced here: 120 us
  waiting for transfers between devices  55.7 us (46%)
  blocking collectives  29.7 us (25%)
  starting transfers between devices  26.8 us (22%)
  Pallas kernels  6.7 us (6%)
  local copies, waits for them, and re-layouts  1.4 us (1%)
    ppermute x13, waiting for transfers between devices, swap(): lax.ppermute(value, axis, [(place, place ^ mask) for place in range(lax.a...  50 us
    all_to_all x1, blocking collectives, exchange(): lax.all_to_all(value, ('tm', 'det'), split_axis=0, concat_axis=0, tiled=T...  29.7 us
    ppermute x13, starting transfers between devices, swap(): lax.ppermute(value, axis, [(place, place ^ mask) for place in range(lax.a...  21.4 us
    pallas_call x8, Pallas kernels, call(): pl.pallas_call(kernel, out_shape=outs, in_specs=[pl.BlockSpec(memory_spac...  6.7 us
    all_to_all x1, waiting for transfers between devices, exchange(): lax.all_to_all(value, ('tm', 'det'), split_axis=0, concat_axis=0, tiled=T...  5.69 us
    all_to_all x1, starting transfers between devices, exchange(): lax.all_to_all(value, ('tm', 'det'), split_axis=0, concat_axis=0, tiled=T...  4.03 us
  transfers between devices with their start and end apart: 16, of which 10 were waited for; matrix products, arithmetic and copies ran while one was open for 0% of the time, Pallas kernels for 3%

profile of v14, /device:TPU:0, one launch (start us, length us, event | category | flops | bytes accessed | tf_op | source)
XLA Modules:
  0.0 120.5 jit_solution(6411054114580648215)
XLA Ops:
  0.0 1.3 %copy-done.3 = f32[64,4096]{1,0:T(8,128)S(1)} copy-done((f32[64,4096]{1,0:T(8,128)S(1)}, f32[64,4096]{1,0:T(8,128)}, u32[]{:S(2)}) %copy-start.3) | copy-done | bytes 1048600
  1.4 5.1 %collective-permute-start = (f32[16,4096]{1,0:T(8,128)S(1)}, f32[16,4096]{1,0:T(8,128)S(1)}, u32[]{:S(2)}, u32[]{:S(2)}) collective-permute-start(f32[16,4096]{1,0:T(8,128)S(1)} %get-tuple-element.19), channel_id=1, source_target_pairs={{0,24},{8,16},{16,8},{24,0},{1,25},{9,17},{17,9},{25,1},{2,26},{10... | collective-permute-start | bytes 786440 | tf_op jit(solution)/shard_map/ppermute | solution.py:234
  8.5 5.3 %collective-permute-done.refs_0_ = f32[16,4096]{1,0:T(8,128)S(1)} collective-permute-done((f32[16,4096]{1,0:T(8,128)S(1)}, f32[16,4096]{1,0:T(8,128)S(1)}, u32[]{:S(2)}, u32[]{:S(2)}) %collective-permute-start) | collective-permute-done | bytes 262176 | tf_op jit(solution)/shard_map/ppermute | solution.py:234
  13.8 16.4 %collective-permute-done.1.refs_1_ = f32[16,4096]{1,0:T(8,128)S(1)} collective-permute-done((f32[16,4096]{1,0:T(8,128)S(1)}, f32[16,4096]{1,0:T(8,128)S(1)}, u32[]{:S(2)}, u32[]{:S(2)}) %collective-permute-start.1) | collective-permute-done | bytes 262176 | tf_op jit(solution)/shard_map/ppermute | solution.py:234
  30.3 2.3 %shard_map.56 = f32[4,8,2,4,8,128]{5,4,3,2,1,0:T(8,128)} custom-call(f32[16,4096]{1,0:T(8,128)S(1)} %collective-permute-done.refs_0_, f32[16,4096]{1,0:T(8,128)S(1)} %collective-permute-done.1.refs_1_, f32[16,4096]{1,0:T(8,128)S(1)} %collective-permute-done.2.refs_2_, f32[16,4096]{1,0:T(8,128)S(1)} %get-tuple-element.22.refs_3_, ...), custom_call_target="tpu_custom_call" | custom-call | flops 805306368 | bytes 3211264 | tf_op jit(solution)/shard_map/pallas_call | solution.py:213
  32.5 4.0 %all-to-all-start = ((f32[32,64,128]{2,1,0:T(8,128)}), f32[32,64,128]{2,1,0:T(8,128)S(1)}, u32[]{:S(2)}, u32[]{:S(2)}) async-start(f32[32,64,128]{2,1,0:T(8,128)} %bitcast.1), calls=%async_computation | async-start | bytes 2097152 | tf_op jit(solution)/shard_map/all_to_all | solution.py:291
  36.6 2.7 %collective-permute-start.7 = (f32[64,512]{1,0:T(8,128)S(1)}, f32[64,512]{1,0:T(8,128)S(1)}, u32[]{:S(2)}, u32[]{:S(2)}) collective-permute-start(f32[64,512]{1,0:T(8,128)S(1)} %constant_dynamic-update-slice_fusion), channel_id=1, source_target_pairs={{0,6},{1,7},{2,4},{3,5},{4,2},{5,3},{6,0},{7,1},{8,14},{9,15},{10,... | collective-permute-start | bytes 393224 | tf_op jit(solution)/shard_map/ppermute | solution.py:234
  40.2 12.4 %collective-permute-done.7 = f32[64,512]{1,0:T(8,128)S(1)} collective-permute-done((f32[64,512]{1,0:T(8,128)S(1)}, f32[64,512]{1,0:T(8,128)S(1)}, u32[]{:S(2)}, u32[]{:S(2)}) %collective-permute-start.7) | collective-permute-done | bytes 131104 | tf_op jit(solution)/shard_map/ppermute | solution.py:234
  52.6 1.3 %collective-permute-done.6 = f32[64,512]{1,0:T(8,128)S(1)} collective-permute-done((f32[64,512]{1,0:T(8,128)S(1)}, f32[64,512]{1,0:T(8,128)S(1)}, u32[]{:S(2)}, u32[]{:S(2)}) %collective-permute-start.6) | collective-permute-done | bytes 131104 | tf_op jit(solution)/shard_map/ppermute | solution.py:234
  53.9 1.0 collective-permute-done.5
  55.1 1.8 %collective-permute-done.8 = f32[4,64,512]{2,1,0:T(8,128)S(1)} collective-permute-done((f32[4,64,512]{2,1,0:T(8,128)S(1)}, f32[4,64,512]{2,1,0:T(8,128)S(1)}, u32[]{:S(2)}, u32[]{:S(2)}) %collective-permute-start.8) | collective-permute-done | bytes 524320 | tf_op jit(solution)/shard_map/ppermute | solution.py:234
  57.1 5.7 %all-to-all-done = f32[32,64,128]{2,1,0:T(8,128)S(1)} async-done(((f32[32,64,128]{2,1,0:T(8,128)}), f32[32,64,128]{2,1,0:T(8,128)S(1)}, u32[]{:S(2)}, u32[]{:S(2)}) %all-to-all-start) | async-done | bytes 1048608 | tf_op jit(solution)/shard_map/all_to_all | solution.py:291
  63.6 29.7 %all_to_all.10 = f32[32,64,128]{2,1,0:T(8,128)S(1)} all-to-all(f32[32,64,128]{2,1,0:T(8,128)S(1)} %bitcast.19), channel_id=1, replica_groups=mesh['tm'=4,'det'=8] {'tm','det'}, dimensions={0} | all-to-all | bytes 2097152 | tf_op jit(solution)/shard_map/all_to_all | solution.py:291
  93.3 0.9 shard_map.60
  94.2 1.4 %collective-permute-start.12 = (f32[8,4096]{1,0:T(8,128)S(1)}, f32[8,4096]{1,0:T(8,128)S(1)}, u32[]{:S(2)}, u32[]{:S(2)}) collective-permute-start(f32[8,4096]{1,0:T(8,128)S(1)} %get-tuple-element.29), channel_id=1, source_target_pairs={{0,24},{8,16},{16,8},{24,0},{1,25},{9,17},{17,9},{25,1},{2,26},{10... | collective-permute-start | bytes 393224 | tf_op jit(solution)/shard_map/ppermute | solution.py:234
  95.5 0.9 collective-permute-start.13
  96.4 2.2 %collective-permute-start.14 = (f32[8,4096]{1,0:T(8,128)S(1)}, f32[8,4096]{1,0:T(8,128)S(1)}, u32[]{:S(2)}, u32[]{:S(2)}) collective-permute-start(f32[8,4096]{1,0:T(8,128)S(1)} %get-tuple-element.31), channel_id=1, source_target_pairs={{0,8},{8,0},{16,24},{24,16},{1,9},{9,1},{17,25},{25,17},{2,10},{10... | collective-permute-start | bytes 393224 | tf_op jit(solution)/shard_map/ppermute | solution.py:234
  98.6 0.9 shard_map.59
  99.5 1.3 %collective-permute-start.9 = (f32[8,4096]{1,0:T(8,128)S(1)}, f32[8,4096]{1,0:T(8,128)S(1)}, u32[]{:S(2)}, u32[]{:S(2)}) collective-permute-start(f32[8,4096]{1,0:T(8,128)S(1)} %get-tuple-element.25), channel_id=1, source_target_pairs={{0,24},{8,16},{16,8},{24,0},{1,25},{9,17},{17,9},{25,1},{2,26},{10... | collective-permute-start | bytes 393224 | tf_op jit(solution)/shard_map/ppermute | solution.py:234
  101.0 1.4 %collective-permute-done.12.refs_0_ = f32[8,4096]{1,0:T(8,128)S(1)} collective-permute-done((f32[8,4096]{1,0:T(8,128)S(1)}, f32[8,4096]{1,0:T(8,128)S(1)}, u32[]{:S(2)}, u32[]{:S(2)}) %collective-permute-start.12) | collective-permute-done | bytes 131104 | tf_op jit(solution)/shard_map/ppermute | solution.py:234
  102.4 6.1 %collective-permute-start.11 = (f32[8,4096]{1,0:T(8,128)S(1)}, f32[8,4096]{1,0:T(8,128)S(1)}, u32[]{:S(2)}, u32[]{:S(2)}) collective-permute-start(f32[8,4096]{1,0:T(8,128)S(1)} %get-tuple-element.27), channel_id=1, source_target_pairs={{0,8},{8,0},{16,24},{24,16},{1,9},{9,1},{17,25},{25,17},{2,10},{10... | collective-permute-start | bytes 393224 | tf_op jit(solution)/shard_map/ppermute | solution.py:234
  108.5 6.3 %collective-permute-done.13.refs_1_ = f32[8,4096]{1,0:T(8,128)S(1)} collective-permute-done((f32[8,4096]{1,0:T(8,128)S(1)}, f32[8,4096]{1,0:T(8,128)S(1)}, u32[]{:S(2)}, u32[]{:S(2)}) %collective-permute-start.13) | collective-permute-done | bytes 131104 | tf_op jit(solution)/shard_map/ppermute | solution.py:234
  114.8 0.8 shard_map.61.refs_4_
  115.6 4.0 %collective-permute-done.10.refs_1_ = f32[8,4096]{1,0:T(8,128)S(1)} collective-permute-done((f32[8,4096]{1,0:T(8,128)S(1)}, f32[8,4096]{1,0:T(8,128)S(1)}, u32[]{:S(2)}, u32[]{:S(2)}) %collective-permute-start.10) | collective-permute-done | bytes 131104 | tf_op jit(solution)/shard_map/ppermute | solution.py:234
  (37 shorter events, 5.1 us)
Async XLA Ops:
  0.0 7.2 %copy-start = (f32[1,128,512]{2,1,0:T(8,128)S(1)}, f32[1,128,512]{2,1,0:T(8,128)}, u32[]{:S(2)}) copy-start(f32[1,128,512]{2,1,0:T(8,128)} %param.6) | copy-start | bytes 786436
  0.0 1.3 %copy-start.3 = (f32[64,4096]{1,0:T(8,128)S(1)}, f32[64,4096]{1,0:T(8,128)}, u32[]{:S(2)}) copy-start(f32[64,4096]{1,0:T(8,128)} %param.5) | copy-start | bytes 3145732
  1.3 29.0 %copy-start.2 = (bf16[512,512]{1,0:T(8,128)(2,1)S(1)}, bf16[512,512]{1,0:T(8,128)(2,1)}, u32[]{:S(2)}) copy-start(bf16[512,512]{1,0:T(8,128)(2,1)} %constant.20.clone.refs_5_.refs_2_) | copy-start | bytes 1572868
  1.3 29.0 %copy-start.4 = (f32[2,32,256]{2,1,0:T(8,128)S(1)}, f32[2,32,256]{2,1,0:T(8,128)}, u32[]{:S(2)}) copy-start(f32[2,32,256]{2,1,0:T(8,128)} %constant.19.clone.refs_4_.refs_1_) | copy-start | bytes 196612
  1.4 28.9 %copy-start.1 = (bf16[512,512]{1,0:T(8,128)(2,1)S(1)}, bf16[512,512]{1,0:T(8,128)(2,1)}, u32[]{:S(2)}) copy-start(bf16[512,512]{1,0:T(8,128)(2,1)} %constant.21.clone.refs_6_.refs_3_) | copy-start | bytes 1572868
  1.4 12.4 %collective-permute-start = (f32[16,4096]{1,0:T(8,128)S(1)}, f32[16,4096]{1,0:T(8,128)S(1)}, u32[]{:S(2)}, u32[]{:S(2)}) collective-permute-start(f32[16,4096]{1,0:T(8,128)S(1)} %get-tuple-element.19), channel_id=1, source_target_pairs={{0,24},{8,16},{16,8},{24,0},{1,25},{9,17},{17,9},{25,1},{2,26},{10... | collective-permute-start | bytes 786440 | tf_op jit(solution)/shard_map/ppermute | solution.py:234
  6.5 23.7 %collective-permute-start.1 = (f32[16,4096]{1,0:T(8,128)S(1)}, f32[16,4096]{1,0:T(8,128)S(1)}, u32[]{:S(2)}, u32[]{:S(2)}) collective-permute-start(f32[16,4096]{1,0:T(8,128)S(1)} %get-tuple-element.20), channel_id=1, source_target_pairs={{0,16},{8,24},{16,0},{24,8},{1,17},{9,25},{17,1},{25,9},{2,18},{10... | collective-permute-start | bytes 786440 | tf_op jit(solution)/shard_map/ppermute | solution.py:234
  6.5 23.7 %collective-permute-start.2 = (f32[16,4096]{1,0:T(8,128)S(1)}, f32[16,4096]{1,0:T(8,128)S(1)}, u32[]{:S(2)}, u32[]{:S(2)}) collective-permute-start(f32[16,4096]{1,0:T(8,128)S(1)} %get-tuple-element.21), channel_id=1, source_target_pairs={{0,8},{8,0},{16,24},{24,16},{1,9},{9,1},{17,25},{25,17},{2,10},{10... | collective-permute-start | bytes 786440 | tf_op jit(solution)/shard_map/ppermute | solution.py:234
  7.2 29.4 %collective-permute-start.4 = (f32[64,256]{1,0:T(8,128)S(1)}, f32[64,256]{1,0:T(8,128)S(1)}, u32[]{:S(2)}, u32[]{:S(2)}) collective-permute-start(f32[64,256]{1,0:T(8,128)S(1)} %get-tuple-element.33), channel_id=1, source_target_pairs={{16,4},{17,28},{18,12},{19,20},{20,21},{21,13},{22,29},{23,5},{24,... | collective-permute-start | bytes 196616 | tf_op jit(solution)/shard_map/ppermute | solution.py:253
  7.9 28.7 %collective-permute-start.3 = (f32[64,256]{1,0:T(8,128)S(1)}, f32[64,256]{1,0:T(8,128)S(1)}, u32[]{:S(2)}, u32[]{:S(2)}) collective-permute-start(f32[64,256]{1,0:T(8,128)S(1)} %get-tuple-element.34), channel_id=1, source_target_pairs={{0,0},{1,24},{2,8},{3,16},{4,17},{5,9},{6,25},{7,1},{8,2},{9,26},{... | collective-permute-start | bytes 196616 | tf_op jit(solution)/shard_map/ppermute | solution.py:252
  32.5 30.3 %all-to-all-start = ((f32[32,64,128]{2,1,0:T(8,128)}), f32[32,64,128]{2,1,0:T(8,128)S(1)}, u32[]{:S(2)}, u32[]{:S(2)}) async-start(f32[32,64,128]{2,1,0:T(8,128)} %bitcast.1), calls=%async_computation | async-start | bytes 2097152 | tf_op jit(solution)/shard_map/all_to_all | solution.py:291
  36.6 16.0 %collective-permute-start.7 = (f32[64,512]{1,0:T(8,128)S(1)}, f32[64,512]{1,0:T(8,128)S(1)}, u32[]{:S(2)}, u32[]{:S(2)}) collective-permute-start(f32[64,512]{1,0:T(8,128)S(1)} %constant_dynamic-update-slice_fusion), channel_id=1, source_target_pairs={{0,6},{1,7},{2,4},{3,5},{4,2},{5,3},{6,0},{7,1},{8,14},{9,15},{10,... | collective-permute-start | bytes 393224 | tf_op jit(solution)/shard_map/ppermute | solution.py:234
  39.3 14.5 %collective-permute-start.6 = (f32[64,512]{1,0:T(8,128)S(1)}, f32[64,512]{1,0:T(8,128)S(1)}, u32[]{:S(2)}, u32[]{:S(2)}) collective-permute-start(f32[64,512]{1,0:T(8,128)S(1)} %constant_dynamic-update-slice_fusion), channel_id=1, source_target_pairs={{0,4},{1,5},{2,6},{3,7},{4,0},{5,1},{6,2},{7,3},{8,12},{9,13},{10,... | collective-permute-start | bytes 393224 | tf_op jit(solution)/shard_map/ppermute | solution.py:234
  39.9 15.0 %collective-permute-start.5 = (f32[64,512]{1,0:T(8,128)S(1)}, f32[64,512]{1,0:T(8,128)S(1)}, u32[]{:S(2)}, u32[]{:S(2)}) collective-permute-start(f32[64,512]{1,0:T(8,128)S(1)} %constant_dynamic-update-slice_fusion), channel_id=1, source_target_pairs={{0,2},{1,3},{2,0},{3,1},{4,6},{5,7},{6,4},{7,5},{8,10},{9,11},{10,... | collective-permute-start | bytes 393224 | tf_op jit(solution)/shard_map/ppermute | solution.py:234
  55.0 2.0 %collective-permute-start.8 = (f32[4,64,512]{2,1,0:T(8,128)S(1)}, f32[4,64,512]{2,1,0:T(8,128)S(1)}, u32[]{:S(2)}, u32[]{:S(2)}) collective-permute-start(f32[4,64,512]{2,1,0:T(8,128)S(1)} %pad_maximum_fusion), channel_id=1, source_target_pairs={{0,1},{1,0},{2,3},{3,2},{4,5},{5,4},{6,7},{7,6},{8,9},{9,8},{10,11... | collective-permute-start | bytes 1572872 | tf_op jit(solution)/shard_map/ppermute | solution.py:234
  94.2 8.3 %collective-permute-start.12 = (f32[8,4096]{1,0:T(8,128)S(1)}, f32[8,4096]{1,0:T(8,128)S(1)}, u32[]{:S(2)}, u32[]{:S(2)}) collective-permute-start(f32[8,4096]{1,0:T(8,128)S(1)} %get-tuple-element.29), channel_id=1, source_target_pairs={{0,24},{8,16},{16,8},{24,0},{1,25},{9,17},{17,9},{25,1},{2,26},{10... | collective-permute-start | bytes 393224 | tf_op jit(solution)/shard_map/ppermute | solution.py:234
  95.5 19.3 %collective-permute-start.13 = (f32[8,4096]{1,0:T(8,128)S(1)}, f32[8,4096]{1,0:T(8,128)S(1)}, u32[]{:S(2)}, u32[]{:S(2)}) collective-permute-start(f32[8,4096]{1,0:T(8,128)S(1)} %get-tuple-element.30), channel_id=1, source_target_pairs={{0,16},{8,24},{16,0},{24,8},{1,17},{9,25},{17,1},{25,9},{2,18},{10... | collective-permute-start | bytes 393224 | tf_op jit(solution)/shard_map/ppermute | solution.py:234
  96.4 18.3 %collective-permute-start.14 = (f32[8,4096]{1,0:T(8,128)S(1)}, f32[8,4096]{1,0:T(8,128)S(1)}, u32[]{:S(2)}, u32[]{:S(2)}) collective-permute-start(f32[8,4096]{1,0:T(8,128)S(1)} %get-tuple-element.31), channel_id=1, source_target_pairs={{0,8},{8,0},{16,24},{24,16},{1,9},{9,1},{17,25},{25,17},{2,10},{10... | collective-permute-start | bytes 393224 | tf_op jit(solution)/shard_map/ppermute | solution.py:234
  99.5 16.1 %collective-permute-start.9 = (f32[8,4096]{1,0:T(8,128)S(1)}, f32[8,4096]{1,0:T(8,128)S(1)}, u32[]{:S(2)}, u32[]{:S(2)}) collective-permute-start(f32[8,4096]{1,0:T(8,128)S(1)} %get-tuple-element.25), channel_id=1, source_target_pairs={{0,24},{8,16},{16,8},{24,0},{1,25},{9,17},{17,9},{25,1},{2,26},{10... | collective-permute-start | bytes 393224 | tf_op jit(solution)/shard_map/ppermute | solution.py:234
  100.8 18.8 %collective-permute-start.10 = (f32[8,4096]{1,0:T(8,128)S(1)}, f32[8,4096]{1,0:T(8,128)S(1)}, u32[]{:S(2)}, u32[]{:S(2)}) collective-permute-start(f32[8,4096]{1,0:T(8,128)S(1)} %get-tuple-element.26), channel_id=1, source_target_pairs={{0,16},{8,24},{16,0},{24,8},{1,17},{9,25},{17,1},{25,9},{2,18},{10... | collective-permute-start | bytes 393224 | tf_op jit(solution)/shard_map/ppermute | solution.py:234
  102.4 17.2 %collective-permute-start.11 = (f32[8,4096]{1,0:T(8,128)S(1)}, f32[8,4096]{1,0:T(8,128)S(1)}, u32[]{:S(2)}, u32[]{:S(2)}) collective-permute-start(f32[8,4096]{1,0:T(8,128)S(1)} %get-tuple-element.27), channel_id=1, source_target_pairs={{0,8},{8,0},{16,24},{24,16},{1,9},{9,1},{17,25},{25,17},{2,10},{10... | collective-permute-start | bytes 393224 | tf_op jit(solution)/shard_map/ppermute | solution.py:234

commit v15 on v14

--- a/solution.py
+++ b/solution.py
@@ -112,7 +112,7 @@
     span = x_ref.shape[-1]
     _, groups, chunks, pieces, dets, width = stage_ref.shape
     per = span // n2
-    for step, block in enumerate(reversed(blocks)):
+    for step, block in zip(farthest_first(planes), blocks):
         x_ref[here ^ step] = block[...]
     copies = []
     for chunk in range(chunks):
@@ -171,8 +171,8 @@
     out_ref, sem = refs[-2:]
     planes = out_ref.shape[0]
     copies = [
-        pltpu.make_async_copy(refs[planes - 1 - step], out_ref.at[here ^ step, chunk], sem.at[step])
-        for step in range(planes)
+        pltpu.make_async_copy(block, out_ref.at[here ^ step, chunk], sem.at[step])
+        for step, block in zip(half_first(planes), refs)
     ]
     for copy in copies:
         copy.start()
@@ -234,8 +234,16 @@
     return lax.ppermute(value, axis, [(place, place ^ mask) for place in range(lax.axis_size(axis))])
 
 
-def trade(parts):
-    return [swap(parts[step], "tm", step) for step in reversed(range(1, len(parts)))] + [parts[0]]
+def farthest_first(planes):
+    return list(reversed(range(planes)))
+
+
+def half_first(planes):
+    return sorted(range(1, planes), key=lambda step: 2 * step != planes) + [0]
+
+
+def trade(parts, order):
+    return [swap(parts[step], "tm", step) if step else parts[step] for step in order(len(parts))]
 
 
 def plane_factor(factor, planes, groups):
@@ -292,7 +300,7 @@
 
     (spectrum,) = call(
         bind(forward_kernel, n1, n2, planes), [array(*layout)],
-        [(planes, own, span), (chunks, n1 * dets, 2 * n2), layout, dma(chunks)], flops, *trade(parts), *tables, out_space=pl.ANY,
+        [(planes, own, span), (chunks, n1 * dets, 2 * n2), layout, dma(chunks)], flops, *trade(parts, farthest_first), *tables, out_space=pl.ANY,
     )
     sides = plane_factor(factor, planes, groups)
     f_high, f_low = band_factor(sides, groups)
@@ -310,7 +318,7 @@
             [(planes, dets, span), (n1 * dets, 2 * n2)], flops // chunks, back, *tables,
         )
         result = call(
-            bind(place_kernel, chunk), [array(planes, chunks, dets, span)], [dma(planes)], 0, *trade(parts), *result,
+            bind(place_kernel, chunk), [array(planes, chunks, dets, span)], [dma(planes)], 0, *trade(parts, half_first), *result,
             spaces=[pl.ANY] * (planes + len(result)), out_space=pl.ANY, aliases={planes: 0} if result else None,
         )
     return result[0].reshape(rows, span)

time: 121 us -> 119 us (0.983)
  starting transfers between devices: 26.8 us -> 21.1 us
  waiting for transfers between devices: 55.7 us -> 59.6 us
    ppermute x13, starting transfers between devices: 21.4 us -> 15.8 us  [swap(): lax.ppermute(value, axis, [(place, place ^ mask) for place in range(lax.a...]
    ppermute x13, waiting for transfers between devices: 50 us -> 53.9 us  [swap(): lax.ppermute(value, axis, [(place, place ^ mask) for place in range(lax.a...]
  transfers between devices with their start and end apart: 16 -> 16, of which waited for: 10 -> 9; matrix products, arithmetic and copies ran while one was open for 0% -> 0% of each run, Pallas kernels for 3% -> 3%
where the time goes in v15:
time: 119 us
  waiting for transfers between devices  59.6 us (50%)
  blocking collectives  29.7 us (25%)
  starting transfers between devices  21.1 us (18%)
  Pallas kernels  6.71 us (6%)
  local copies, waits for them, and re-layouts  1.4 us (1%)
    ppermute x13, waiting for transfers between devices, swap(): lax.ppermute(value, axis, [(place, place ^ mask) for place in range(lax.a...  53.9 us
    all_to_all x1, blocking collectives, exchange(): lax.all_to_all(value, ('tm', 'det'), split_axis=0, concat_axis=0, tiled=T...  29.7 us
    ppermute x13, starting transfers between devices, swap(): lax.ppermute(value, axis, [(place, place ^ mask) for place in range(lax.a...  15.8 us
    pallas_call x8, Pallas kernels, call(): pl.pallas_call(kernel, out_shape=outs, in_specs=[pl.BlockSpec(memory_spac...  6.71 us
    all_to_all x1, waiting for transfers between devices, exchange(): lax.all_to_all(value, ('tm', 'det'), split_axis=0, concat_axis=0, tiled=T...  5.69 us
    all_to_all x1, starting transfers between devices, exchange(): lax.all_to_all(value, ('tm', 'det'), split_axis=0, concat_axis=0, tiled=T...  4.03 us
  transfers between devices with their start and end apart: 16, of which 9 were waited for; matrix products, arithmetic and copies ran while one was open for 0% of the time, Pallas kernels for 3%

profile of v15, /device:TPU:0, one launch (start us, length us, event | category | flops | bytes accessed | tf_op | source)
XLA Modules:
  0.0 118.8 jit_solution(8139469800481979136)
XLA Ops:
  0.0 1.3 %copy-done.3 = f32[64,4096]{1,0:T(8,128)S(1)} copy-done((f32[64,4096]{1,0:T(8,128)S(1)}, f32[64,4096]{1,0:T(8,128)}, u32[]{:S(2)}) %copy-start.3) | copy-done | bytes 1048600
  1.4 5.1 %collective-permute-start = (f32[16,4096]{1,0:T(8,128)S(1)}, f32[16,4096]{1,0:T(8,128)S(1)}, u32[]{:S(2)}, u32[]{:S(2)}) collective-permute-start(f32[16,4096]{1,0:T(8,128)S(1)} %get-tuple-element.19), channel_id=1, source_target_pairs={{0,24},{8,16},{16,8},{24,0},{1,25},{9,17},{17,9},{25,1},{2,26},{10... | collective-permute-start | bytes 786440 | tf_op jit(solution)/shard_map/ppermute | solution.py:234
  8.5 5.3 %collective-permute-done.refs_0_ = f32[16,4096]{1,0:T(8,128)S(1)} collective-permute-done((f32[16,4096]{1,0:T(8,128)S(1)}, f32[16,4096]{1,0:T(8,128)S(1)}, u32[]{:S(2)}, u32[]{:S(2)}) %collective-permute-start) | collective-permute-done | bytes 262176 | tf_op jit(solution)/shard_map/ppermute | solution.py:234
  13.8 16.4 %collective-permute-done.1.refs_1_ = f32[16,4096]{1,0:T(8,128)S(1)} collective-permute-done((f32[16,4096]{1,0:T(8,128)S(1)}, f32[16,4096]{1,0:T(8,128)S(1)}, u32[]{:S(2)}, u32[]{:S(2)}) %collective-permute-start.1) | collective-permute-done | bytes 262176 | tf_op jit(solution)/shard_map/ppermute | solution.py:234
  30.3 2.3 %shard_map.56 = f32[4,8,2,4,8,128]{5,4,3,2,1,0:T(8,128)} custom-call(f32[16,4096]{1,0:T(8,128)S(1)} %collective-permute-done.refs_0_, f32[16,4096]{1,0:T(8,128)S(1)} %collective-permute-done.1.refs_1_, f32[16,4096]{1,0:T(8,128)S(1)} %collective-permute-done.2.refs_2_, f32[16,4096]{1,0:T(8,128)S(1)} %get-tuple-element.22.refs_3_, ...), custom_call_target="tpu_custom_call" | custom-call | flops 805306368 | bytes 3211264 | tf_op jit(solution)/shard_map/pallas_call | solution.py:213
  32.5 4.0 %all-to-all-start = ((f32[32,64,128]{2,1,0:T(8,128)}), f32[32,64,128]{2,1,0:T(8,128)S(1)}, u32[]{:S(2)}, u32[]{:S(2)}) async-start(f32[32,64,128]{2,1,0:T(8,128)} %bitcast.1), calls=%async_computation | async-start | bytes 2097152 | tf_op jit(solution)/shard_map/all_to_all | solution.py:299
  36.6 2.7 %collective-permute-start.7 = (f32[64,512]{1,0:T(8,128)S(1)}, f32[64,512]{1,0:T(8,128)S(1)}, u32[]{:S(2)}, u32[]{:S(2)}) collective-permute-start(f32[64,512]{1,0:T(8,128)S(1)} %constant_dynamic-update-slice_fusion), channel_id=1, source_target_pairs={{0,6},{1,7},{2,4},{3,5},{4,2},{5,3},{6,0},{7,1},{8,14},{9,15},{10,... | collective-permute-start | bytes 393224 | tf_op jit(solution)/shard_map/ppermute | solution.py:234
  40.2 12.4 %collective-permute-done.7 = f32[64,512]{1,0:T(8,128)S(1)} collective-permute-done((f32[64,512]{1,0:T(8,128)S(1)}, f32[64,512]{1,0:T(8,128)S(1)}, u32[]{:S(2)}, u32[]{:S(2)}) %collective-permute-start.7) | collective-permute-done | bytes 131104 | tf_op jit(solution)/shard_map/ppermute | solution.py:234
  52.6 1.3 %collective-permute-done.6 = f32[64,512]{1,0:T(8,128)S(1)} collective-permute-done((f32[64,512]{1,0:T(8,128)S(1)}, f32[64,512]{1,0:T(8,128)S(1)}, u32[]{:S(2)}, u32[]{:S(2)}) %collective-permute-start.6) | collective-permute-done | bytes 131104 | tf_op jit(solution)/shard_map/ppermute | solution.py:234
  53.9 1.0 collective-permute-done.5
  55.1 1.8 %collective-permute-done.8 = f32[4,64,512]{2,1,0:T(8,128)S(1)} collective-permute-done((f32[4,64,512]{2,1,0:T(8,128)S(1)}, f32[4,64,512]{2,1,0:T(8,128)S(1)}, u32[]{:S(2)}, u32[]{:S(2)}) %collective-permute-start.8) | collective-permute-done | bytes 524320 | tf_op jit(solution)/shard_map/ppermute | solution.py:234
  57.1 5.7 %all-to-all-done = f32[32,64,128]{2,1,0:T(8,128)S(1)} async-done(((f32[32,64,128]{2,1,0:T(8,128)}), f32[32,64,128]{2,1,0:T(8,128)S(1)}, u32[]{:S(2)}, u32[]{:S(2)}) %all-to-all-start) | async-done | bytes 1048608 | tf_op jit(solution)/shard_map/all_to_all | solution.py:299
  62.8 0.8 shard_map.58
  63.6 29.7 %all_to_all.10 = f32[32,64,128]{2,1,0:T(8,128)S(1)} all-to-all(f32[32,64,128]{2,1,0:T(8,128)S(1)} %bitcast.19), channel_id=1, replica_groups=mesh['tm'=4,'det'=8] {'tm','det'}, dimensions={0} | all-to-all | bytes 2097152 | tf_op jit(solution)/shard_map/all_to_all | solution.py:299
  93.3 0.9 shard_map.60
  94.2 0.8 collective-permute-start.12
  95.0 1.1 collective-permute-start.13
  96.1 2.5 %collective-permute-start.14 = (f32[8,4096]{1,0:T(8,128)S(1)}, f32[8,4096]{1,0:T(8,128)S(1)}, u32[]{:S(2)}, u32[]{:S(2)}) collective-permute-start(f32[8,4096]{1,0:T(8,128)S(1)} %get-tuple-element.31), channel_id=1, source_target_pairs={{0,24},{8,16},{16,8},{24,0},{1,25},{9,17},{17,9},{25,1},{2,26},{10... | collective-permute-start | bytes 393224 | tf_op jit(solution)/shard_map/ppermute | solution.py:234
  98.6 0.9 shard_map.59
  99.6 1.8 %collective-permute-start.10 = (f32[8,4096]{1,0:T(8,128)S(1)}, f32[8,4096]{1,0:T(8,128)S(1)}, u32[]{:S(2)}, u32[]{:S(2)}) collective-permute-start(f32[8,4096]{1,0:T(8,128)S(1)} %get-tuple-element.26), channel_id=1, source_target_pairs={{0,8},{8,0},{16,24},{24,16},{1,9},{9,1},{17,25},{25,17},{2,10},{10... | collective-permute-start | bytes 393224 | tf_op jit(solution)/shard_map/ppermute | solution.py:234
  101.4 7.4 %collective-permute-done.12.refs_0_ = f32[8,4096]{1,0:T(8,128)S(1)} collective-permute-done((f32[8,4096]{1,0:T(8,128)S(1)}, f32[8,4096]{1,0:T(8,128)S(1)}, u32[]{:S(2)}, u32[]{:S(2)}) %collective-permute-start.12) | collective-permute-done | bytes 131104 | tf_op jit(solution)/shard_map/ppermute | solution.py:234
  108.8 0.8 shard_map.61.refs_4_
  109.7 8.3 %collective-permute-done.9.refs_0_ = f32[8,4096]{1,0:T(8,128)S(1)} collective-permute-done((f32[8,4096]{1,0:T(8,128)S(1)}, f32[8,4096]{1,0:T(8,128)S(1)}, u32[]{:S(2)}, u32[]{:S(2)}) %collective-permute-start.9) | collective-permute-done | bytes 131104 | tf_op jit(solution)/shard_map/ppermute | solution.py:234
  117.9 0.8 shard_map.62
  (37 shorter events, 3.4 us)
Async XLA Ops:
  0.0 7.2 %copy-start = (f32[1,128,512]{2,1,0:T(8,128)S(1)}, f32[1,128,512]{2,1,0:T(8,128)}, u32[]{:S(2)}) copy-start(f32[1,128,512]{2,1,0:T(8,128)} %param.6) | copy-start | bytes 786436
  0.0 1.3 %copy-start.3 = (f32[64,4096]{1,0:T(8,128)S(1)}, f32[64,4096]{1,0:T(8,128)}, u32[]{:S(2)}) copy-start(f32[64,4096]{1,0:T(8,128)} %param.5) | copy-start | bytes 3145732
  1.3 29.0 %copy-start.2 = (bf16[512,512]{1,0:T(8,128)(2,1)S(1)}, bf16[512,512]{1,0:T(8,128)(2,1)}, u32[]{:S(2)}) copy-start(bf16[512,512]{1,0:T(8,128)(2,1)} %constant.20.clone.refs_5_.refs_2_) | copy-start | bytes 1572868
  1.3 29.0 %copy-start.4 = (f32[2,32,256]{2,1,0:T(8,128)S(1)}, f32[2,32,256]{2,1,0:T(8,128)}, u32[]{:S(2)}) copy-start(f32[2,32,256]{2,1,0:T(8,128)} %constant.19.clone.refs_4_.refs_1_) | copy-start | bytes 196612
  1.4 28.9 %copy-start.1 = (bf16[512,512]{1,0:T(8,128)(2,1)S(1)}, bf16[512,512]{1,0:T(8,128)(2,1)}, u32[]{:S(2)}) copy-start(bf16[512,512]{1,0:T(8,128)(2,1)} %constant.21.clone.refs_6_.refs_3_) | copy-start | bytes 1572868
  1.4 12.4 %collective-permute-start = (f32[16,4096]{1,0:T(8,128)S(1)}, f32[16,4096]{1,0:T(8,128)S(1)}, u32[]{:S(2)}, u32[]{:S(2)}) collective-permute-start(f32[16,4096]{1,0:T(8,128)S(1)} %get-tuple-element.19), channel_id=1, source_target_pairs={{0,24},{8,16},{16,8},{24,0},{1,25},{9,17},{17,9},{25,1},{2,26},{10... | collective-permute-start | bytes 786440 | tf_op jit(solution)/shard_map/ppermute | solution.py:234
  6.5 23.7 %collective-permute-start.1 = (f32[16,4096]{1,0:T(8,128)S(1)}, f32[16,4096]{1,0:T(8,128)S(1)}, u32[]{:S(2)}, u32[]{:S(2)}) collective-permute-start(f32[16,4096]{1,0:T(8,128)S(1)} %get-tuple-element.20), channel_id=1, source_target_pairs={{0,16},{8,24},{16,0},{24,8},{1,17},{9,25},{17,1},{25,9},{2,18},{10... | collective-permute-start | bytes 786440 | tf_op jit(solution)/shard_map/ppermute | solution.py:234
  6.5 23.7 %collective-permute-start.2 = (f32[16,4096]{1,0:T(8,128)S(1)}, f32[16,4096]{1,0:T(8,128)S(1)}, u32[]{:S(2)}, u32[]{:S(2)}) collective-permute-start(f32[16,4096]{1,0:T(8,128)S(1)} %get-tuple-element.21), channel_id=1, source_target_pairs={{0,8},{8,0},{16,24},{24,16},{1,9},{9,1},{17,25},{25,17},{2,10},{10... | collective-permute-start | bytes 786440 | tf_op jit(solution)/shard_map/ppermute | solution.py:234
  7.2 29.4 %collective-permute-start.4 = (f32[64,256]{1,0:T(8,128)S(1)}, f32[64,256]{1,0:T(8,128)S(1)}, u32[]{:S(2)}, u32[]{:S(2)}) collective-permute-start(f32[64,256]{1,0:T(8,128)S(1)} %get-tuple-element.33), channel_id=1, source_target_pairs={{16,4},{17,28},{18,12},{19,20},{20,21},{21,13},{22,29},{23,5},{24,... | collective-permute-start | bytes 196616 | tf_op jit(solution)/shard_map/ppermute | solution.py:261
  7.9 28.7 %collective-permute-start.3 = (f32[64,256]{1,0:T(8,128)S(1)}, f32[64,256]{1,0:T(8,128)S(1)}, u32[]{:S(2)}, u32[]{:S(2)}) collective-permute-start(f32[64,256]{1,0:T(8,128)S(1)} %get-tuple-element.34), channel_id=1, source_target_pairs={{0,0},{1,24},{2,8},{3,16},{4,17},{5,9},{6,25},{7,1},{8,2},{9,26},{... | collective-permute-start | bytes 196616 | tf_op jit(solution)/shard_map/ppermute | solution.py:260
  32.5 30.3 %all-to-all-start = ((f32[32,64,128]{2,1,0:T(8,128)}), f32[32,64,128]{2,1,0:T(8,128)S(1)}, u32[]{:S(2)}, u32[]{:S(2)}) async-start(f32[32,64,128]{2,1,0:T(8,128)} %bitcast.1), calls=%async_computation | async-start | bytes 2097152 | tf_op jit(solution)/shard_map/all_to_all | solution.py:299
  36.6 16.0 %collective-permute-start.7 = (f32[64,512]{1,0:T(8,128)S(1)}, f32[64,512]{1,0:T(8,128)S(1)}, u32[]{:S(2)}, u32[]{:S(2)}) collective-permute-start(f32[64,512]{1,0:T(8,128)S(1)} %constant_dynamic-update-slice_fusion), channel_id=1, source_target_pairs={{0,6},{1,7},{2,4},{3,5},{4,2},{5,3},{6,0},{7,1},{8,14},{9,15},{10,... | collective-permute-start | bytes 393224 | tf_op jit(solution)/shard_map/ppermute | solution.py:234
  39.4 14.5 %collective-permute-start.6 = (f32[64,512]{1,0:T(8,128)S(1)}, f32[64,512]{1,0:T(8,128)S(1)}, u32[]{:S(2)}, u32[]{:S(2)}) collective-permute-start(f32[64,512]{1,0:T(8,128)S(1)} %constant_dynamic-update-slice_fusion), channel_id=1, source_target_pairs={{0,4},{1,5},{2,6},{3,7},{4,0},{5,1},{6,2},{7,3},{8,12},{9,13},{10,... | collective-permute-start | bytes 393224 | tf_op jit(solution)/shard_map/ppermute | solution.py:234
  39.9 15.0 %collective-permute-start.5 = (f32[64,512]{1,0:T(8,128)S(1)}, f32[64,512]{1,0:T(8,128)S(1)}, u32[]{:S(2)}, u32[]{:S(2)}) collective-permute-start(f32[64,512]{1,0:T(8,128)S(1)} %constant_dynamic-update-slice_fusion), channel_id=1, source_target_pairs={{0,2},{1,3},{2,0},{3,1},{4,6},{5,7},{6,4},{7,5},{8,10},{9,11},{10,... | collective-permute-start | bytes 393224 | tf_op jit(solution)/shard_map/ppermute | solution.py:234
  55.0 2.0 %collective-permute-start.8 = (f32[4,64,512]{2,1,0:T(8,128)S(1)}, f32[4,64,512]{2,1,0:T(8,128)S(1)}, u32[]{:S(2)}, u32[]{:S(2)}) collective-permute-start(f32[4,64,512]{2,1,0:T(8,128)S(1)} %pad_maximum_fusion), channel_id=1, source_target_pairs={{0,1},{1,0},{2,3},{3,2},{4,5},{5,4},{6,7},{7,6},{8,9},{9,8},{10,11... | collective-permute-start | bytes 1572872 | tf_op jit(solution)/shard_map/ppermute | solution.py:234
  94.2 14.7 %collective-permute-start.12 = (f32[8,4096]{1,0:T(8,128)S(1)}, f32[8,4096]{1,0:T(8,128)S(1)}, u32[]{:S(2)}, u32[]{:S(2)}) collective-permute-start(f32[8,4096]{1,0:T(8,128)S(1)} %get-tuple-element.29), channel_id=1, source_target_pairs={{0,16},{8,24},{16,0},{24,8},{1,17},{9,25},{17,1},{25,9},{2,18},{10... | collective-permute-start | bytes 393224 | tf_op jit(solution)/shard_map/ppermute | solution.py:234
  95.0 13.8 %collective-permute-start.13 = (f32[8,4096]{1,0:T(8,128)S(1)}, f32[8,4096]{1,0:T(8,128)S(1)}, u32[]{:S(2)}, u32[]{:S(2)}) collective-permute-start(f32[8,4096]{1,0:T(8,128)S(1)} %get-tuple-element.30), channel_id=1, source_target_pairs={{0,8},{8,0},{16,24},{24,16},{1,9},{9,1},{17,25},{25,17},{2,10},{10... | collective-permute-start | bytes 393224 | tf_op jit(solution)/shard_map/ppermute | solution.py:234
  96.1 12.7 %collective-permute-start.14 = (f32[8,4096]{1,0:T(8,128)S(1)}, f32[8,4096]{1,0:T(8,128)S(1)}, u32[]{:S(2)}, u32[]{:S(2)}) collective-permute-start(f32[8,4096]{1,0:T(8,128)S(1)} %get-tuple-element.31), channel_id=1, source_target_pairs={{0,24},{8,16},{16,8},{24,0},{1,25},{9,17},{17,9},{25,1},{2,26},{10... | collective-permute-start | bytes 393224 | tf_op jit(solution)/shard_map/ppermute | solution.py:234
  99.5 18.4 %collective-permute-start.9 = (f32[8,4096]{1,0:T(8,128)S(1)}, f32[8,4096]{1,0:T(8,128)S(1)}, u32[]{:S(2)}, u32[]{:S(2)}) collective-permute-start(f32[8,4096]{1,0:T(8,128)S(1)} %get-tuple-element.25), channel_id=1, source_target_pairs={{0,16},{8,24},{16,0},{24,8},{1,17},{9,25},{17,1},{25,9},{2,18},{10... | collective-permute-start | bytes 393224 | tf_op jit(solution)/shard_map/ppermute | solution.py:234
  99.6 18.3 %collective-permute-start.10 = (f32[8,4096]{1,0:T(8,128)S(1)}, f32[8,4096]{1,0:T(8,128)S(1)}, u32[]{:S(2)}, u32[]{:S(2)}) collective-permute-start(f32[8,4096]{1,0:T(8,128)S(1)} %get-tuple-element.26), channel_id=1, source_target_pairs={{0,8},{8,0},{16,24},{24,16},{1,9},{9,1},{17,25},{25,17},{2,10},{10... | collective-permute-start | bytes 393224 | tf_op jit(solution)/shard_map/ppermute | solution.py:234
  108.8 9.1 %collective-permute-start.11 = (f32[8,4096]{1,0:T(8,128)S(1)}, f32[8,4096]{1,0:T(8,128)S(1)}, u32[]{:S(2)}, u32[]{:S(2)}) collective-permute-start(f32[8,4096]{1,0:T(8,128)S(1)} %get-tuple-element.27), channel_id=1, source_target_pairs={{0,24},{8,16},{16,8},{24,0},{1,25},{9,17},{17,9},{25,1},{2,26},{10... | collective-permute-start | bytes 393224 | tf_op jit(solution)/shard_map/ppermute | solution.py:234

commit v16 on v15

--- a/solution.py
+++ b/solution.py
@@ -13,7 +13,7 @@
 LANES = 128
 VMEM_LIMIT = 48 * 1024 * 1024
 CHUNKS = 2
-FACTOR_WORK = 7 * 10**9
+FACTOR_WORK = 74 * 10**8
 
 
 def band_of(plane, planes):
@@ -110,7 +110,7 @@
     blocks, (turn_ref, high_ref, low_ref) = refs[:planes], refs[planes : planes + 3]
     out_ref, x_ref, mid_ref, stage_ref, sem = refs[-5:]
     span = x_ref.shape[-1]
-    _, groups, chunks, pieces, dets, width = stage_ref.shape
+    groups, _, chunks, pieces, dets, width = stage_ref.shape
     per = span // n2
     for step, block in zip(farthest_first(planes), blocks):
         x_ref[here ^ step] = block[...]
@@ -133,7 +133,7 @@
         spectrum = product(split(mid_ref[chunk]), (high_ref[...], low_ref[...]))
         for plane in range(planes):
             value = spectrum[:, plane * width : (plane + 1) * width]
-            stage_ref[plane, :, chunk] = value.reshape(groups, pieces, dets, width)
+            stage_ref[:, plane, chunk] = value.reshape(groups, pieces, dets, width)
         copies.append(pltpu.make_async_copy(stage_ref.at[:, :, chunk], out_ref.at[:, :, chunk], sem.at[chunk]))
         copies[-1].start()
     for copy in copies:
@@ -144,10 +144,10 @@
     here = lax.axis_index("tm")
     outs, (x_ref, mid_ref) = refs[:-2], refs[-2:]
     _, dets, span = x_ref.shape
-    planes, _, _, _, _, width = y_ref.shape
+    _, planes, _, _, _, width = y_ref.shape
     per = span // n2
     scale = 1.0 / (n1 * n2)
-    bins = jnp.concatenate([y_ref[plane, :, chunk].reshape(n1 * dets, width) for plane in range(planes)], axis=1)
+    bins = jnp.concatenate([y_ref[:, plane, chunk].reshape(n1 * dets, width) for plane in range(planes)], axis=1)
     mid_ref[...] = product(split(bins), (high_ref[...], low_ref[...]), ((1,), (1,)))
     for rows, lane in tiles(dets, n2):
         parts = []
@@ -190,12 +190,12 @@
 
 
 def mix_kernel(x_ref, f_high, f_low, out_ref, x_mid, y_mid):
-    planes, groups, chunks, pieces, dets, width = out_ref.shape
+    groups, planes, chunks, pieces, dets, width = out_ref.shape
     places = []
-    for plane, group, chunk, piece in np.ndindex(planes, groups, chunks, pieces):
+    for group, plane, chunk, piece in np.ndindex(groups, planes, chunks, pieces):
         start = ((group * planes + plane) * chunks + chunk) * dets
         rows, lanes = slice(start, start + dets), slice(piece * width, (piece + 1) * width)
-        places.append(((plane, group, chunk, piece), (rows, lanes)))
+        places.append(((group, plane, chunk, piece), (rows, lanes)))
     for source, target in places:
         x_mid[target] = x_ref[source]
     x_high, x_low = split(x_mid[...])
@@ -292,11 +292,11 @@
         slice_kernel, [array(own, span)] * planes, [dma(planes)], 0, noise.reshape(planes, own, span), spaces=[pl.ANY],
         out_space=pl.ANY,
     )
-    layout = (planes, groups, chunks, pieces, dets, LANES)
+    layout = (groups, planes, chunks, pieces, dets, LANES)
 
     def exchange(value):
-        value = value.reshape(planes * groups, pieces * own, LANES)
-        return lax.all_to_all(value, ("tm", "det"), split_axis=0, concat_axis=0, tiled=True).reshape(layout)
+        value = value.reshape(groups * planes, pieces * own, LANES)
+        return lax.all_to_all(value, ("det", "tm"), split_axis=0, concat_axis=0, tiled=True).reshape(layout)
 
     (spectrum,) = call(
         bind(forward_kernel, n1, n2, planes), [array(*layout)],

time: 119 us -> 118 us (level)
  waiting for transfers between devices: 59.6 us -> 50.7 us
  starting transfers between devices: 21.1 us -> 29.2 us
    ppermute x13, waiting for transfers between devices: 53.9 us -> 45.6 us  [swap(): lax.ppermute(value, axis, [(place, place ^ mask) for place in range(lax.a...]
    ppermute x13, starting transfers between devices: 15.8 us -> 23.8 us  [swap(): lax.ppermute(value, axis, [(place, place ^ mask) for place in range(lax.a...]
where the time goes in v16:
time: 118 us
  waiting for transfers between devices  50.7 us (43%)
  blocking collectives  29.3 us (25%)
  starting transfers between devices  29.2 us (25%)
  Pallas kernels  6.7 us (6%)
  local copies, waits for them, and re-layouts  1.4 us (1%)
    ppermute x13, waiting for transfers between devices, swap(): lax.ppermute(value, axis, [(place, place ^ mask) for place in range(lax.a...  45.6 us
    all_to_all x1, blocking collectives, exchange(): lax.all_to_all(value, ('det', 'tm'), split_axis=0, concat_axis=0, tiled=T...  29.3 us
    ppermute x13, starting transfers between devices, swap(): lax.ppermute(value, axis, [(place, place ^ mask) for place in range(lax.a...  23.8 us
    pallas_call x8, Pallas kernels, call(): pl.pallas_call(kernel, out_shape=outs, in_specs=[pl.BlockSpec(memory_spac...  6.7 us
    all_to_all x1, waiting for transfers between devices, exchange(): lax.all_to_all(value, ('det', 'tm'), split_axis=0, concat_axis=0, tiled=T...  5.05 us
    all_to_all x1, starting transfers between devices, exchange(): lax.all_to_all(value, ('det', 'tm'), split_axis=0, concat_axis=0, tiled=T...  4.03 us
  transfers between devices with their start and end apart: 16, of which 9 were waited for; matrix products, arithmetic and copies ran while one was open for 0% of the time, Pallas kernels for 3%

profile of v16, /device:TPU:0, one launch (start us, length us, event | category | flops | bytes accessed | tf_op | source)
XLA Modules:
  0.0 117.6 jit_solution(2315714442024755645)
XLA Ops:
  0.0 1.3 %copy-done.3 = f32[64,4096]{1,0:T(8,128)S(1)} copy-done((f32[64,4096]{1,0:T(8,128)S(1)}, f32[64,4096]{1,0:T(8,128)}, u32[]{:S(2)}) %copy-start.3) | copy-done | bytes 1048600
  1.4 5.1 %collective-permute-start = (f32[16,4096]{1,0:T(8,128)S(1)}, f32[16,4096]{1,0:T(8,128)S(1)}, u32[]{:S(2)}, u32[]{:S(2)}) collective-permute-start(f32[16,4096]{1,0:T(8,128)S(1)} %get-tuple-element.19), channel_id=1, source_target_pairs={{0,24},{8,16},{16,8},{24,0},{1,25},{9,17},{17,9},{25,1},{2,26},{10... | collective-permute-start | bytes 786440 | tf_op jit(solution)/shard_map/ppermute | solution.py:234
  8.5 5.3 %collective-permute-done.refs_0_ = f32[16,4096]{1,0:T(8,128)S(1)} collective-permute-done((f32[16,4096]{1,0:T(8,128)S(1)}, f32[16,4096]{1,0:T(8,128)S(1)}, u32[]{:S(2)}, u32[]{:S(2)}) %collective-permute-start) | collective-permute-done | bytes 262176 | tf_op jit(solution)/shard_map/ppermute | solution.py:234
  13.8 16.4 %collective-permute-done.1.refs_1_ = f32[16,4096]{1,0:T(8,128)S(1)} collective-permute-done((f32[16,4096]{1,0:T(8,128)S(1)}, f32[16,4096]{1,0:T(8,128)S(1)}, u32[]{:S(2)}, u32[]{:S(2)}) %collective-permute-start.1) | collective-permute-done | bytes 262176 | tf_op jit(solution)/shard_map/ppermute | solution.py:234
  30.3 2.3 %shard_map.56 = f32[8,4,2,4,8,128]{5,4,3,2,1,0:T(8,128)} custom-call(f32[16,4096]{1,0:T(8,128)S(1)} %collective-permute-done.refs_0_, f32[16,4096]{1,0:T(8,128)S(1)} %collective-permute-done.1.refs_1_, f32[16,4096]{1,0:T(8,128)S(1)} %collective-permute-done.2.refs_2_, f32[16,4096]{1,0:T(8,128)S(1)} %get-tuple-element.22.refs_3_, ...), custom_call_target="tpu_custom_call" | custom-call | flops 805306368 | bytes 3211264 | tf_op jit(solution)/shard_map/pallas_call | solution.py:213
  32.5 4.0 %all-to-all-start = ((f32[32,64,128]{2,1,0:T(8,128)}), f32[32,64,128]{2,1,0:T(8,128)S(1)}, u32[]{:S(2)}, u32[]{:S(2)}) async-start(f32[32,64,128]{2,1,0:T(8,128)} %bitcast.1), calls=%async_computation | async-start | bytes 2097152 | tf_op jit(solution)/shard_map/all_to_all | solution.py:299
  36.6 2.7 %collective-permute-start.7 = (f32[64,512]{1,0:T(8,128)S(1)}, f32[64,512]{1,0:T(8,128)S(1)}, u32[]{:S(2)}, u32[]{:S(2)}) collective-permute-start(f32[64,512]{1,0:T(8,128)S(1)} %constant_dynamic-update-slice_fusion), channel_id=1, source_target_pairs={{0,6},{1,7},{2,4},{3,5},{4,2},{5,3},{6,0},{7,1},{8,14},{9,15},{10,... | collective-permute-start | bytes 393224 | tf_op jit(solution)/shard_map/ppermute | solution.py:234
  40.2 11.9 %collective-permute-done.7 = f32[64,512]{1,0:T(8,128)S(1)} collective-permute-done((f32[64,512]{1,0:T(8,128)S(1)}, f32[64,512]{1,0:T(8,128)S(1)}, u32[]{:S(2)}, u32[]{:S(2)}) %collective-permute-start.7) | collective-permute-done | bytes 131104 | tf_op jit(solution)/shard_map/ppermute | solution.py:234
  52.1 1.5 %collective-permute-done.6 = f32[64,512]{1,0:T(8,128)S(1)} collective-permute-done((f32[64,512]{1,0:T(8,128)S(1)}, f32[64,512]{1,0:T(8,128)S(1)}, u32[]{:S(2)}, u32[]{:S(2)}) %collective-permute-start.6) | collective-permute-done | bytes 131104 | tf_op jit(solution)/shard_map/ppermute | solution.py:234
  53.6 0.8 collective-permute-done.5
  54.6 1.8 %collective-permute-done.8 = f32[4,64,512]{2,1,0:T(8,128)S(1)} collective-permute-done((f32[4,64,512]{2,1,0:T(8,128)S(1)}, f32[4,64,512]{2,1,0:T(8,128)S(1)}, u32[]{:S(2)}, u32[]{:S(2)}) %collective-permute-start.8) | collective-permute-done | bytes 524320 | tf_op jit(solution)/shard_map/ppermute | solution.py:234
  56.6 5.1 %all-to-all-done = f32[32,64,128]{2,1,0:T(8,128)S(1)} async-done(((f32[32,64,128]{2,1,0:T(8,128)}), f32[32,64,128]{2,1,0:T(8,128)S(1)}, u32[]{:S(2)}, u32[]{:S(2)}) %all-to-all-start) | async-done | bytes 1048608 | tf_op jit(solution)/shard_map/all_to_all | solution.py:299
  62.4 29.3 %all_to_all.10 = f32[32,64,128]{2,1,0:T(8,128)S(1)} all-to-all(f32[32,64,128]{2,1,0:T(8,128)S(1)} %bitcast.19), channel_id=1, replica_groups=mesh['tm'=4,'det'=8] {'det','tm'}, dimensions={0} | all-to-all | bytes 2097152 | tf_op jit(solution)/shard_map/all_to_all | solution.py:299
  91.7 0.9 shard_map.60
  92.6 2.3 %collective-permute-start.12 = (f32[8,4096]{1,0:T(8,128)S(1)}, f32[8,4096]{1,0:T(8,128)S(1)}, u32[]{:S(2)}, u32[]{:S(2)}) collective-permute-start(f32[8,4096]{1,0:T(8,128)S(1)} %get-tuple-element.29), channel_id=1, source_target_pairs={{0,16},{8,24},{16,0},{24,8},{1,17},{9,25},{17,1},{25,9},{2,18},{10... | collective-permute-start | bytes 393224 | tf_op jit(solution)/shard_map/ppermute | solution.py:234
  95.0 1.5 %collective-permute-start.13 = (f32[8,4096]{1,0:T(8,128)S(1)}, f32[8,4096]{1,0:T(8,128)S(1)}, u32[]{:S(2)}, u32[]{:S(2)}) collective-permute-start(f32[8,4096]{1,0:T(8,128)S(1)} %get-tuple-element.30), channel_id=1, source_target_pairs={{0,8},{8,0},{16,24},{24,16},{1,9},{9,1},{17,25},{25,17},{2,10},{10... | collective-permute-start | bytes 393224 | tf_op jit(solution)/shard_map/ppermute | solution.py:234
  96.5 1.7 %collective-permute-start.14 = (f32[8,4096]{1,0:T(8,128)S(1)}, f32[8,4096]{1,0:T(8,128)S(1)}, u32[]{:S(2)}, u32[]{:S(2)}) collective-permute-start(f32[8,4096]{1,0:T(8,128)S(1)} %get-tuple-element.31), channel_id=1, source_target_pairs={{0,24},{8,16},{16,8},{24,0},{1,25},{9,17},{17,9},{25,1},{2,26},{10... | collective-permute-start | bytes 393224 | tf_op jit(solution)/shard_map/ppermute | solution.py:234
  98.2 0.9 shard_map.59
  99.7 2.1 %collective-permute-start.10 = (f32[8,4096]{1,0:T(8,128)S(1)}, f32[8,4096]{1,0:T(8,128)S(1)}, u32[]{:S(2)}, u32[]{:S(2)}) collective-permute-start(f32[8,4096]{1,0:T(8,128)S(1)} %get-tuple-element.26), channel_id=1, source_target_pairs={{0,8},{8,0},{16,24},{24,16},{1,9},{9,1},{17,25},{25,17},{2,10},{10... | collective-permute-start | bytes 393224 | tf_op jit(solution)/shard_map/ppermute | solution.py:234
  101.8 2.6 %collective-permute-done.12.refs_0_ = f32[8,4096]{1,0:T(8,128)S(1)} collective-permute-done((f32[8,4096]{1,0:T(8,128)S(1)}, f32[8,4096]{1,0:T(8,128)S(1)}, u32[]{:S(2)}, u32[]{:S(2)}) %collective-permute-start.12) | collective-permute-done | bytes 131104 | tf_op jit(solution)/shard_map/ppermute | solution.py:234
  104.4 6.2 %collective-permute-start.11 = (f32[8,4096]{1,0:T(8,128)S(1)}, f32[8,4096]{1,0:T(8,128)S(1)}, u32[]{:S(2)}, u32[]{:S(2)}) collective-permute-start(f32[8,4096]{1,0:T(8,128)S(1)} %get-tuple-element.27), channel_id=1, source_target_pairs={{0,24},{8,16},{16,8},{24,0},{1,25},{9,17},{17,9},{25,1},{2,26},{10... | collective-permute-start | bytes 393224 | tf_op jit(solution)/shard_map/ppermute | solution.py:234
  110.5 0.8 shard_map.61.refs_4_
  111.4 5.4 %collective-permute-done.9.refs_0_ = f32[8,4096]{1,0:T(8,128)S(1)} collective-permute-done((f32[8,4096]{1,0:T(8,128)S(1)}, f32[8,4096]{1,0:T(8,128)S(1)}, u32[]{:S(2)}, u32[]{:S(2)}) %collective-permute-start.9) | collective-permute-done | bytes 131104 | tf_op jit(solution)/shard_map/ppermute | solution.py:234
  116.7 0.8 shard_map.62
  (37 shorter events, 4.7 us)
Async XLA Ops:
  0.0 7.2 %copy-start = (f32[1,128,512]{2,1,0:T(8,128)S(1)}, f32[1,128,512]{2,1,0:T(8,128)}, u32[]{:S(2)}) copy-start(f32[1,128,512]{2,1,0:T(8,128)} %param.6) | copy-start | bytes 786436
  0.0 1.3 %copy-start.3 = (f32[64,4096]{1,0:T(8,128)S(1)}, f32[64,4096]{1,0:T(8,128)}, u32[]{:S(2)}) copy-start(f32[64,4096]{1,0:T(8,128)} %param.5) | copy-start | bytes 3145732
  1.3 29.0 %copy-start.2 = (bf16[512,512]{1,0:T(8,128)(2,1)S(1)}, bf16[512,512]{1,0:T(8,128)(2,1)}, u32[]{:S(2)}) copy-start(bf16[512,512]{1,0:T(8,128)(2,1)} %constant.20.clone.refs_5_.refs_2_) | copy-start | bytes 1572868
  1.3 29.0 %copy-start.4 = (f32[2,32,256]{2,1,0:T(8,128)S(1)}, f32[2,32,256]{2,1,0:T(8,128)}, u32[]{:S(2)}) copy-start(f32[2,32,256]{2,1,0:T(8,128)} %constant.19.clone.refs_4_.refs_1_) | copy-start | bytes 196612
  1.4 28.9 %copy-start.1 = (bf16[512,512]{1,0:T(8,128)(2,1)S(1)}, bf16[512,512]{1,0:T(8,128)(2,1)}, u32[]{:S(2)}) copy-start(bf16[512,512]{1,0:T(8,128)(2,1)} %constant.21.clone.refs_6_.refs_3_) | copy-start | bytes 1572868
  1.4 12.4 %collective-permute-start = (f32[16,4096]{1,0:T(8,128)S(1)}, f32[16,4096]{1,0:T(8,128)S(1)}, u32[]{:S(2)}, u32[]{:S(2)}) collective-permute-start(f32[16,4096]{1,0:T(8,128)S(1)} %get-tuple-element.19), channel_id=1, source_target_pairs={{0,24},{8,16},{16,8},{24,0},{1,25},{9,17},{17,9},{25,1},{2,26},{10... | collective-permute-start | bytes 786440 | tf_op jit(solution)/shard_map/ppermute | solution.py:234
  6.5 23.7 %collective-permute-start.1 = (f32[16,4096]{1,0:T(8,128)S(1)}, f32[16,4096]{1,0:T(8,128)S(1)}, u32[]{:S(2)}, u32[]{:S(2)}) collective-permute-start(f32[16,4096]{1,0:T(8,128)S(1)} %get-tuple-element.20), channel_id=1, source_target_pairs={{0,16},{8,24},{16,0},{24,8},{1,17},{9,25},{17,1},{25,9},{2,18},{10... | collective-permute-start | bytes 786440 | tf_op jit(solution)/shard_map/ppermute | solution.py:234
  6.5 23.7 %collective-permute-start.2 = (f32[16,4096]{1,0:T(8,128)S(1)}, f32[16,4096]{1,0:T(8,128)S(1)}, u32[]{:S(2)}, u32[]{:S(2)}) collective-permute-start(f32[16,4096]{1,0:T(8,128)S(1)} %get-tuple-element.21), channel_id=1, source_target_pairs={{0,8},{8,0},{16,24},{24,16},{1,9},{9,1},{17,25},{25,17},{2,10},{10... | collective-permute-start | bytes 786440 | tf_op jit(solution)/shard_map/ppermute | solution.py:234
  7.2 29.4 %collective-permute-start.4 = (f32[64,256]{1,0:T(8,128)S(1)}, f32[64,256]{1,0:T(8,128)S(1)}, u32[]{:S(2)}, u32[]{:S(2)}) collective-permute-start(f32[64,256]{1,0:T(8,128)S(1)} %get-tuple-element.33), channel_id=1, source_target_pairs={{16,4},{17,28},{18,12},{19,20},{20,21},{21,13},{22,29},{23,5},{24,... | collective-permute-start | bytes 196616 | tf_op jit(solution)/shard_map/ppermute | solution.py:261
  7.9 28.7 %collective-permute-start.3 = (f32[64,256]{1,0:T(8,128)S(1)}, f32[64,256]{1,0:T(8,128)S(1)}, u32[]{:S(2)}, u32[]{:S(2)}) collective-permute-start(f32[64,256]{1,0:T(8,128)S(1)} %get-tuple-element.34), channel_id=1, source_target_pairs={{0,0},{1,24},{2,8},{3,16},{4,17},{5,9},{6,25},{7,1},{8,2},{9,26},{... | collective-permute-start | bytes 196616 | tf_op jit(solution)/shard_map/ppermute | solution.py:260
  32.5 29.1 %all-to-all-start = ((f32[32,64,128]{2,1,0:T(8,128)}), f32[32,64,128]{2,1,0:T(8,128)S(1)}, u32[]{:S(2)}, u32[]{:S(2)}) async-start(f32[32,64,128]{2,1,0:T(8,128)} %bitcast.1), calls=%async_computation | async-start | bytes 2097152 | tf_op jit(solution)/shard_map/all_to_all | solution.py:299
  36.6 15.5 %collective-permute-start.7 = (f32[64,512]{1,0:T(8,128)S(1)}, f32[64,512]{1,0:T(8,128)S(1)}, u32[]{:S(2)}, u32[]{:S(2)}) collective-permute-start(f32[64,512]{1,0:T(8,128)S(1)} %constant_dynamic-update-slice_fusion), channel_id=1, source_target_pairs={{0,6},{1,7},{2,4},{3,5},{4,2},{5,3},{6,0},{7,1},{8,14},{9,15},{10,... | collective-permute-start | bytes 393224 | tf_op jit(solution)/shard_map/ppermute | solution.py:234
  39.4 14.2 %collective-permute-start.6 = (f32[64,512]{1,0:T(8,128)S(1)}, f32[64,512]{1,0:T(8,128)S(1)}, u32[]{:S(2)}, u32[]{:S(2)}) collective-permute-start(f32[64,512]{1,0:T(8,128)S(1)} %constant_dynamic-update-slice_fusion), channel_id=1, source_target_pairs={{0,4},{1,5},{2,6},{3,7},{4,0},{5,1},{6,2},{7,3},{8,12},{9,13},{10,... | collective-permute-start | bytes 393224 | tf_op jit(solution)/shard_map/ppermute | solution.py:234
  39.9 14.5 %collective-permute-start.5 = (f32[64,512]{1,0:T(8,128)S(1)}, f32[64,512]{1,0:T(8,128)S(1)}, u32[]{:S(2)}, u32[]{:S(2)}) collective-permute-start(f32[64,512]{1,0:T(8,128)S(1)} %constant_dynamic-update-slice_fusion), channel_id=1, source_target_pairs={{0,2},{1,3},{2,0},{3,1},{4,6},{5,7},{6,4},{7,5},{8,10},{9,11},{10,... | collective-permute-start | bytes 393224 | tf_op jit(solution)/shard_map/ppermute | solution.py:234
  54.4 2.0 %collective-permute-start.8 = (f32[4,64,512]{2,1,0:T(8,128)S(1)}, f32[4,64,512]{2,1,0:T(8,128)S(1)}, u32[]{:S(2)}, u32[]{:S(2)}) collective-permute-start(f32[4,64,512]{2,1,0:T(8,128)S(1)} %pad_maximum_fusion), channel_id=1, source_target_pairs={{0,1},{1,0},{2,3},{3,2},{4,5},{5,4},{6,7},{7,6},{8,9},{9,8},{10,11... | collective-permute-start | bytes 1572872 | tf_op jit(solution)/shard_map/ppermute | solution.py:234
  92.6 11.7 %collective-permute-start.12 = (f32[8,4096]{1,0:T(8,128)S(1)}, f32[8,4096]{1,0:T(8,128)S(1)}, u32[]{:S(2)}, u32[]{:S(2)}) collective-permute-start(f32[8,4096]{1,0:T(8,128)S(1)} %get-tuple-element.29), channel_id=1, source_target_pairs={{0,16},{8,24},{16,0},{24,8},{1,17},{9,25},{17,1},{25,9},{2,18},{10... | collective-permute-start | bytes 393224 | tf_op jit(solution)/shard_map/ppermute | solution.py:234
  95.0 15.6 %collective-permute-start.13 = (f32[8,4096]{1,0:T(8,128)S(1)}, f32[8,4096]{1,0:T(8,128)S(1)}, u32[]{:S(2)}, u32[]{:S(2)}) collective-permute-start(f32[8,4096]{1,0:T(8,128)S(1)} %get-tuple-element.30), channel_id=1, source_target_pairs={{0,8},{8,0},{16,24},{24,16},{1,9},{9,1},{17,25},{25,17},{2,10},{10... | collective-permute-start | bytes 393224 | tf_op jit(solution)/shard_map/ppermute | solution.py:234
  96.5 14.1 %collective-permute-start.14 = (f32[8,4096]{1,0:T(8,128)S(1)}, f32[8,4096]{1,0:T(8,128)S(1)}, u32[]{:S(2)}, u32[]{:S(2)}) collective-permute-start(f32[8,4096]{1,0:T(8,128)S(1)} %get-tuple-element.31), channel_id=1, source_target_pairs={{0,24},{8,16},{16,8},{24,0},{1,25},{9,17},{17,9},{25,1},{2,26},{10... | collective-permute-start | bytes 393224 | tf_op jit(solution)/shard_map/ppermute | solution.py:234
  99.0 17.7 %collective-permute-start.9 = (f32[8,4096]{1,0:T(8,128)S(1)}, f32[8,4096]{1,0:T(8,128)S(1)}, u32[]{:S(2)}, u32[]{:S(2)}) collective-permute-start(f32[8,4096]{1,0:T(8,128)S(1)} %get-tuple-element.25), channel_id=1, source_target_pairs={{0,16},{8,24},{16,0},{24,8},{1,17},{9,25},{17,1},{25,9},{2,18},{10... | collective-permute-start | bytes 393224 | tf_op jit(solution)/shard_map/ppermute | solution.py:234
  99.7 17.0 %collective-permute-start.10 = (f32[8,4096]{1,0:T(8,128)S(1)}, f32[8,4096]{1,0:T(8,128)S(1)}, u32[]{:S(2)}, u32[]{:S(2)}) collective-permute-start(f32[8,4096]{1,0:T(8,128)S(1)} %get-tuple-element.26), channel_id=1, source_target_pairs={{0,8},{8,0},{16,24},{24,16},{1,9},{9,1},{17,25},{25,17},{2,10},{10... | collective-permute-start | bytes 393224 | tf_op jit(solution)/shard_map/ppermute | solution.py:234
  104.4 12.4 %collective-permute-start.11 = (f32[8,4096]{1,0:T(8,128)S(1)}, f32[8,4096]{1,0:T(8,128)S(1)}, u32[]{:S(2)}, u32[]{:S(2)}) collective-permute-start(f32[8,4096]{1,0:T(8,128)S(1)} %get-tuple-element.27), channel_id=1, source_target_pairs={{0,24},{8,16},{16,8},{24,0},{1,25},{9,17},{17,9},{25,1},{2,26},{10... | collective-permute-start | bytes 393224 | tf_op jit(solution)/shard_map/ppermute | solution.py:234

commit v17 on v16

--- a/solution.py
+++ b/solution.py
@@ -166,13 +166,12 @@
         out[...] = x_ref[here ^ step]
 
 
-def place_kernel(chunk, *refs):
+def place_kernel(spots, *refs):
     here = lax.axis_index("tm")
     out_ref, sem = refs[-2:]
-    planes = out_ref.shape[0]
     copies = [
-        pltpu.make_async_copy(block, out_ref.at[here ^ step, chunk], sem.at[step])
-        for step, block in zip(half_first(planes), refs)
+        pltpu.make_async_copy(block, out_ref.at[here ^ step, chunk], sem.at[at])
+        for at, ((chunk, step), block) in enumerate(zip(spots, refs))
     ]
     for copy in copies:
         copy.start()
@@ -311,15 +310,26 @@
         2 * 3 * count * count * pieces * LANES, exchange(spectrum), f_high, f_low,
     )
     back = exchange(mixed)
+    arrived = [
+        trade(
+            call(
+                bind(inverse_kernel, n1, n2, chunk), [array(dets, span)] * planes,
+                [(planes, dets, span), (n1 * dets, 2 * n2)], flops // chunks, back, *tables,
+            ),
+            half_first,
+        )
+        for chunk in range(chunks)
+    ]
+    places = [[(chunk, step) for step in half_first(planes)] for chunk in range(chunks)]
+    if chunks > 1:
+        places[0].append(places[-1].pop())
+        arrived[0].append(arrived[-1].pop())
     result = []
-    for chunk in range(chunks):
-        parts = call(
-            bind(inverse_kernel, n1, n2, chunk), [array(dets, span)] * planes,
-            [(planes, dets, span), (n1 * dets, 2 * n2)], flops // chunks, back, *tables,
-        )
+    for blocks, spots in zip(arrived, places):
+        count = len(blocks)
         result = call(
-            bind(place_kernel, chunk), [array(planes, chunks, dets, span)], [dma(planes)], 0, *trade(parts, half_first), *result,
-            spaces=[pl.ANY] * (planes + len(result)), out_space=pl.ANY, aliases={planes: 0} if result else None,
+            bind(place_kernel, spots), [array(planes, chunks, dets, span)], [dma(count)], 0, *blocks, *result,
+            spaces=[pl.ANY] * (count + len(result)), out_space=pl.ANY, aliases={count: 0} if result else None,
         )
     return result[0].reshape(rows, span)
 

time: 118 us -> 118 us (level)
  transfers between devices with their start and end apart: 16 -> 16, of which waited for: 9 -> 9; matrix products, arithmetic and copies ran while one was open for 0% -> 0% of each run, Pallas kernels for 3% -> 4%
where the time goes in v17:
time: 118 us; the launch traced here: 117 us
  waiting for transfers between devices  50.6 us (43%)
  blocking collectives  29.3 us (25%)
  starting transfers between devices  29.2 us (25%)
  Pallas kernels  6.7 us (6%)
  local copies, waits for them, and re-layouts  1.4 us (1%)
    ppermute x13, waiting for transfers between devices, swap(): lax.ppermute(value, axis, [(place, place ^ mask) for place in range(lax.a...  45.6 us
    all_to_all x1, blocking collectives, exchange(): lax.all_to_all(value, ('det', 'tm'), split_axis=0, concat_axis=0, tiled=T...  29.3 us
    ppermute x13, starting transfers between devices, swap(): lax.ppermute(value, axis, [(place, place ^ mask) for place in range(lax.a...  23.8 us
    pallas_call x8, Pallas kernels, call(): pl.pallas_call(kernel, out_shape=outs, in_specs=[pl.BlockSpec(memory_spac...  6.7 us
    all_to_all x1, waiting for transfers between devices, exchange(): lax.all_to_all(value, ('det', 'tm'), split_axis=0, concat_axis=0, tiled=T...  5.05 us
    all_to_all x1, starting transfers between devices, exchange(): lax.all_to_all(value, ('det', 'tm'), split_axis=0, concat_axis=0, tiled=T...  4.03 us
  transfers between devices with their start and end apart: 16, of which 9 were waited for; matrix products, arithmetic and copies ran while one was open for 0% of the time, Pallas kernels for 4%

profile of v17, /device:TPU:0, one launch (start us, length us, event | category | flops | bytes accessed | tf_op | source)
XLA Modules:
  0.0 117.5 jit_solution(16814442309353950700)
XLA Ops:
  0.0 1.3 %copy-done.3 = f32[64,4096]{1,0:T(8,128)S(1)} copy-done((f32[64,4096]{1,0:T(8,128)S(1)}, f32[64,4096]{1,0:T(8,128)}, u32[]{:S(2)}) %copy-start.3) | copy-done | bytes 1048600
  1.4 5.1 %collective-permute-start = (f32[16,4096]{1,0:T(8,128)S(1)}, f32[16,4096]{1,0:T(8,128)S(1)}, u32[]{:S(2)}, u32[]{:S(2)}) collective-permute-start(f32[16,4096]{1,0:T(8,128)S(1)} %get-tuple-element.19), channel_id=1, source_target_pairs={{0,24},{8,16},{16,8},{24,0},{1,25},{9,17},{17,9},{25,1},{2,26},{10... | collective-permute-start | bytes 786440 | tf_op jit(solution)/shard_map/ppermute | solution.py:233
  8.5 5.3 %collective-permute-done.refs_0_ = f32[16,4096]{1,0:T(8,128)S(1)} collective-permute-done((f32[16,4096]{1,0:T(8,128)S(1)}, f32[16,4096]{1,0:T(8,128)S(1)}, u32[]{:S(2)}, u32[]{:S(2)}) %collective-permute-start) | collective-permute-done | bytes 262176 | tf_op jit(solution)/shard_map/ppermute | solution.py:233
  13.8 16.4 %collective-permute-done.1.refs_1_ = f32[16,4096]{1,0:T(8,128)S(1)} collective-permute-done((f32[16,4096]{1,0:T(8,128)S(1)}, f32[16,4096]{1,0:T(8,128)S(1)}, u32[]{:S(2)}, u32[]{:S(2)}) %collective-permute-start.1) | collective-permute-done | bytes 262176 | tf_op jit(solution)/shard_map/ppermute | solution.py:233
  30.3 2.3 %shard_map.56 = f32[8,4,2,4,8,128]{5,4,3,2,1,0:T(8,128)} custom-call(f32[16,4096]{1,0:T(8,128)S(1)} %collective-permute-done.refs_0_, f32[16,4096]{1,0:T(8,128)S(1)} %collective-permute-done.1.refs_1_, f32[16,4096]{1,0:T(8,128)S(1)} %collective-permute-done.2.refs_2_, f32[16,4096]{1,0:T(8,128)S(1)} %get-tuple-element.22.refs_3_, ...), custom_call_target="tpu_custom_call" | custom-call | flops 805306368 | bytes 3211264 | tf_op jit(solution)/shard_map/pallas_call | solution.py:212
  32.5 4.0 %all-to-all-start = ((f32[32,64,128]{2,1,0:T(8,128)}), f32[32,64,128]{2,1,0:T(8,128)S(1)}, u32[]{:S(2)}, u32[]{:S(2)}) async-start(f32[32,64,128]{2,1,0:T(8,128)} %bitcast.1), calls=%async_computation | async-start | bytes 2097152 | tf_op jit(solution)/shard_map/all_to_all | solution.py:298
  36.6 2.7 %collective-permute-start.7 = (f32[64,512]{1,0:T(8,128)S(1)}, f32[64,512]{1,0:T(8,128)S(1)}, u32[]{:S(2)}, u32[]{:S(2)}) collective-permute-start(f32[64,512]{1,0:T(8,128)S(1)} %constant_dynamic-update-slice_fusion), channel_id=1, source_target_pairs={{0,6},{1,7},{2,4},{3,5},{4,2},{5,3},{6,0},{7,1},{8,14},{9,15},{10,... | collective-permute-start | bytes 393224 | tf_op jit(solution)/shard_map/ppermute | solution.py:233
  40.2 11.9 %collective-permute-done.7 = f32[64,512]{1,0:T(8,128)S(1)} collective-permute-done((f32[64,512]{1,0:T(8,128)S(1)}, f32[64,512]{1,0:T(8,128)S(1)}, u32[]{:S(2)}, u32[]{:S(2)}) %collective-permute-start.7) | collective-permute-done | bytes 131104 | tf_op jit(solution)/shard_map/ppermute | solution.py:233
  52.1 1.5 %collective-permute-done.6 = f32[64,512]{1,0:T(8,128)S(1)} collective-permute-done((f32[64,512]{1,0:T(8,128)S(1)}, f32[64,512]{1,0:T(8,128)S(1)}, u32[]{:S(2)}, u32[]{:S(2)}) %collective-permute-start.6) | collective-permute-done | bytes 131104 | tf_op jit(solution)/shard_map/ppermute | solution.py:233
  53.6 0.8 collective-permute-done.5
  54.6 1.8 %collective-permute-done.8 = f32[4,64,512]{2,1,0:T(8,128)S(1)} collective-permute-done((f32[4,64,512]{2,1,0:T(8,128)S(1)}, f32[4,64,512]{2,1,0:T(8,128)S(1)}, u32[]{:S(2)}, u32[]{:S(2)}) %collective-permute-start.8) | collective-permute-done | bytes 524320 | tf_op jit(solution)/shard_map/ppermute | solution.py:233
  56.6 5.1 %all-to-all-done = f32[32,64,128]{2,1,0:T(8,128)S(1)} async-done(((f32[32,64,128]{2,1,0:T(8,128)}), f32[32,64,128]{2,1,0:T(8,128)S(1)}, u32[]{:S(2)}, u32[]{:S(2)}) %all-to-all-start) | async-done | bytes 1048608 | tf_op jit(solution)/shard_map/all_to_all | solution.py:298
  61.6 0.8 shard_map.58
  62.4 29.3 %all_to_all.10 = f32[32,64,128]{2,1,0:T(8,128)S(1)} all-to-all(f32[32,64,128]{2,1,0:T(8,128)S(1)} %bitcast.19), channel_id=1, replica_groups=mesh['tm'=4,'det'=8] {'det','tm'}, dimensions={0} | all-to-all | bytes 2097152 | tf_op jit(solution)/shard_map/all_to_all | solution.py:298
  91.7 0.9 shard_map.60
  92.6 2.3 %collective-permute-start.12 = (f32[8,4096]{1,0:T(8,128)S(1)}, f32[8,4096]{1,0:T(8,128)S(1)}, u32[]{:S(2)}, u32[]{:S(2)}) collective-permute-start(f32[8,4096]{1,0:T(8,128)S(1)} %get-tuple-element.28), channel_id=1, source_target_pairs={{0,16},{8,24},{16,0},{24,8},{1,17},{9,25},{17,1},{25,9},{2,18},{10... | collective-permute-start | bytes 393224 | tf_op jit(solution)/shard_map/ppermute | solution.py:233
  95.0 1.5 %collective-permute-start.13 = (f32[8,4096]{1,0:T(8,128)S(1)}, f32[8,4096]{1,0:T(8,128)S(1)}, u32[]{:S(2)}, u32[]{:S(2)}) collective-permute-start(f32[8,4096]{1,0:T(8,128)S(1)} %get-tuple-element.29), channel_id=1, source_target_pairs={{0,8},{8,0},{16,24},{24,16},{1,9},{9,1},{17,25},{25,17},{2,10},{10... | collective-permute-start | bytes 393224 | tf_op jit(solution)/shard_map/ppermute | solution.py:233
  96.5 0.9 shard_map.59
  97.4 1.8 %collective-permute-start.14 = (f32[8,4096]{1,0:T(8,128)S(1)}, f32[8,4096]{1,0:T(8,128)S(1)}, u32[]{:S(2)}, u32[]{:S(2)}) collective-permute-start(f32[8,4096]{1,0:T(8,128)S(1)} %get-tuple-element.30), channel_id=1, source_target_pairs={{0,24},{8,16},{16,8},{24,0},{1,25},{9,17},{17,9},{25,1},{2,26},{10... | collective-permute-start | bytes 393224 | tf_op jit(solution)/shard_map/ppermute | solution.py:233
  99.8 2.0 %collective-permute-start.10 = (f32[8,4096]{1,0:T(8,128)S(1)}, f32[8,4096]{1,0:T(8,128)S(1)}, u32[]{:S(2)}, u32[]{:S(2)}) collective-permute-start(f32[8,4096]{1,0:T(8,128)S(1)} %get-tuple-element.26), channel_id=1, source_target_pairs={{0,8},{8,0},{16,24},{24,16},{1,9},{9,1},{17,25},{25,17},{2,10},{10... | collective-permute-start | bytes 393224 | tf_op jit(solution)/shard_map/ppermute | solution.py:233
  101.8 2.6 %collective-permute-done.12.refs_0_ = f32[8,4096]{1,0:T(8,128)S(1)} collective-permute-done((f32[8,4096]{1,0:T(8,128)S(1)}, f32[8,4096]{1,0:T(8,128)S(1)}, u32[]{:S(2)}, u32[]{:S(2)}) %collective-permute-start.12) | collective-permute-done | bytes 131104 | tf_op jit(solution)/shard_map/ppermute | solution.py:233
  104.4 6.2 %collective-permute-start.11 = (f32[8,4096]{1,0:T(8,128)S(1)}, f32[8,4096]{1,0:T(8,128)S(1)}, u32[]{:S(2)}, u32[]{:S(2)}) collective-permute-start(f32[8,4096]{1,0:T(8,128)S(1)} %get-tuple-element.27), channel_id=1, source_target_pairs={{0,24},{8,16},{16,8},{24,0},{1,25},{9,17},{17,9},{25,1},{2,26},{10... | collective-permute-start | bytes 393224 | tf_op jit(solution)/shard_map/ppermute | solution.py:233
  110.5 0.9 shard_map.61.refs_3_
  111.4 5.3 %collective-permute-done.9.refs_0_ = f32[8,4096]{1,0:T(8,128)S(1)} collective-permute-done((f32[8,4096]{1,0:T(8,128)S(1)}, f32[8,4096]{1,0:T(8,128)S(1)}, u32[]{:S(2)}, u32[]{:S(2)}) %collective-permute-start.9) | collective-permute-done | bytes 131104 | tf_op jit(solution)/shard_map/ppermute | solution.py:233
  (37 shorter events, 4.7 us)
Async XLA Ops:
  0.0 7.2 %copy-start = (f32[1,128,512]{2,1,0:T(8,128)S(1)}, f32[1,128,512]{2,1,0:T(8,128)}, u32[]{:S(2)}) copy-start(f32[1,128,512]{2,1,0:T(8,128)} %param.6) | copy-start | bytes 786436
  0.0 1.3 %copy-start.3 = (f32[64,4096]{1,0:T(8,128)S(1)}, f32[64,4096]{1,0:T(8,128)}, u32[]{:S(2)}) copy-start(f32[64,4096]{1,0:T(8,128)} %param.5) | copy-start | bytes 3145732
  1.3 29.0 %copy-start.2 = (bf16[512,512]{1,0:T(8,128)(2,1)S(1)}, bf16[512,512]{1,0:T(8,128)(2,1)}, u32[]{:S(2)}) copy-start(bf16[512,512]{1,0:T(8,128)(2,1)} %constant.20.clone.refs_5_.refs_2_) | copy-start | bytes 1572868
  1.3 29.0 %copy-start.4 = (f32[2,32,256]{2,1,0:T(8,128)S(1)}, f32[2,32,256]{2,1,0:T(8,128)}, u32[]{:S(2)}) copy-start(f32[2,32,256]{2,1,0:T(8,128)} %constant.19.clone.refs_4_.refs_1_) | copy-start | bytes 196612
  1.4 28.9 %copy-start.1 = (bf16[512,512]{1,0:T(8,128)(2,1)S(1)}, bf16[512,512]{1,0:T(8,128)(2,1)}, u32[]{:S(2)}) copy-start(bf16[512,512]{1,0:T(8,128)(2,1)} %constant.21.clone.refs_6_.refs_3_) | copy-start | bytes 1572868
  1.4 12.4 %collective-permute-start = (f32[16,4096]{1,0:T(8,128)S(1)}, f32[16,4096]{1,0:T(8,128)S(1)}, u32[]{:S(2)}, u32[]{:S(2)}) collective-permute-start(f32[16,4096]{1,0:T(8,128)S(1)} %get-tuple-element.19), channel_id=1, source_target_pairs={{0,24},{8,16},{16,8},{24,0},{1,25},{9,17},{17,9},{25,1},{2,26},{10... | collective-permute-start | bytes 786440 | tf_op jit(solution)/shard_map/ppermute | solution.py:233
  6.5 23.7 %collective-permute-start.1 = (f32[16,4096]{1,0:T(8,128)S(1)}, f32[16,4096]{1,0:T(8,128)S(1)}, u32[]{:S(2)}, u32[]{:S(2)}) collective-permute-start(f32[16,4096]{1,0:T(8,128)S(1)} %get-tuple-element.20), channel_id=1, source_target_pairs={{0,16},{8,24},{16,0},{24,8},{1,17},{9,25},{17,1},{25,9},{2,18},{10... | collective-permute-start | bytes 786440 | tf_op jit(solution)/shard_map/ppermute | solution.py:233
  6.5 23.7 %collective-permute-start.2 = (f32[16,4096]{1,0:T(8,128)S(1)}, f32[16,4096]{1,0:T(8,128)S(1)}, u32[]{:S(2)}, u32[]{:S(2)}) collective-permute-start(f32[16,4096]{1,0:T(8,128)S(1)} %get-tuple-element.21), channel_id=1, source_target_pairs={{0,8},{8,0},{16,24},{24,16},{1,9},{9,1},{17,25},{25,17},{2,10},{10... | collective-permute-start | bytes 786440 | tf_op jit(solution)/shard_map/ppermute | solution.py:233
  7.2 29.4 %collective-permute-start.4 = (f32[64,256]{1,0:T(8,128)S(1)}, f32[64,256]{1,0:T(8,128)S(1)}, u32[]{:S(2)}, u32[]{:S(2)}) collective-permute-start(f32[64,256]{1,0:T(8,128)S(1)} %get-tuple-element.33), channel_id=1, source_target_pairs={{16,4},{17,28},{18,12},{19,20},{20,21},{21,13},{22,29},{23,5},{24,... | collective-permute-start | bytes 196616 | tf_op jit(solution)/shard_map/ppermute | solution.py:260
  7.9 28.7 %collective-permute-start.3 = (f32[64,256]{1,0:T(8,128)S(1)}, f32[64,256]{1,0:T(8,128)S(1)}, u32[]{:S(2)}, u32[]{:S(2)}) collective-permute-start(f32[64,256]{1,0:T(8,128)S(1)} %get-tuple-element.34), channel_id=1, source_target_pairs={{0,0},{1,24},{2,8},{3,16},{4,17},{5,9},{6,25},{7,1},{8,2},{9,26},{... | collective-permute-start | bytes 196616 | tf_op jit(solution)/shard_map/ppermute | solution.py:259
  32.5 29.1 %all-to-all-start = ((f32[32,64,128]{2,1,0:T(8,128)}), f32[32,64,128]{2,1,0:T(8,128)S(1)}, u32[]{:S(2)}, u32[]{:S(2)}) async-start(f32[32,64,128]{2,1,0:T(8,128)} %bitcast.1), calls=%async_computation | async-start | bytes 2097152 | tf_op jit(solution)/shard_map/all_to_all | solution.py:298
  36.6 15.5 %collective-permute-start.7 = (f32[64,512]{1,0:T(8,128)S(1)}, f32[64,512]{1,0:T(8,128)S(1)}, u32[]{:S(2)}, u32[]{:S(2)}) collective-permute-start(f32[64,512]{1,0:T(8,128)S(1)} %constant_dynamic-update-slice_fusion), channel_id=1, source_target_pairs={{0,6},{1,7},{2,4},{3,5},{4,2},{5,3},{6,0},{7,1},{8,14},{9,15},{10,... | collective-permute-start | bytes 393224 | tf_op jit(solution)/shard_map/ppermute | solution.py:233
  39.4 14.2 %collective-permute-start.6 = (f32[64,512]{1,0:T(8,128)S(1)}, f32[64,512]{1,0:T(8,128)S(1)}, u32[]{:S(2)}, u32[]{:S(2)}) collective-permute-start(f32[64,512]{1,0:T(8,128)S(1)} %constant_dynamic-update-slice_fusion), channel_id=1, source_target_pairs={{0,4},{1,5},{2,6},{3,7},{4,0},{5,1},{6,2},{7,3},{8,12},{9,13},{10,... | collective-permute-start | bytes 393224 | tf_op jit(solution)/shard_map/ppermute | solution.py:233
  39.9 14.5 %collective-permute-start.5 = (f32[64,512]{1,0:T(8,128)S(1)}, f32[64,512]{1,0:T(8,128)S(1)}, u32[]{:S(2)}, u32[]{:S(2)}) collective-permute-start(f32[64,512]{1,0:T(8,128)S(1)} %constant_dynamic-update-slice_fusion), channel_id=1, source_target_pairs={{0,2},{1,3},{2,0},{3,1},{4,6},{5,7},{6,4},{7,5},{8,10},{9,11},{10,... | collective-permute-start | bytes 393224 | tf_op jit(solution)/shard_map/ppermute | solution.py:233
  54.4 2.0 %collective-permute-start.8 = (f32[4,64,512]{2,1,0:T(8,128)S(1)}, f32[4,64,512]{2,1,0:T(8,128)S(1)}, u32[]{:S(2)}, u32[]{:S(2)}) collective-permute-start(f32[4,64,512]{2,1,0:T(8,128)S(1)} %pad_maximum_fusion), channel_id=1, source_target_pairs={{0,1},{1,0},{2,3},{3,2},{4,5},{5,4},{6,7},{7,6},{8,9},{9,8},{10,11... | collective-permute-start | bytes 1572872 | tf_op jit(solution)/shard_map/ppermute | solution.py:233
  92.6 11.7 %collective-permute-start.12 = (f32[8,4096]{1,0:T(8,128)S(1)}, f32[8,4096]{1,0:T(8,128)S(1)}, u32[]{:S(2)}, u32[]{:S(2)}) collective-permute-start(f32[8,4096]{1,0:T(8,128)S(1)} %get-tuple-element.28), channel_id=1, source_target_pairs={{0,16},{8,24},{16,0},{24,8},{1,17},{9,25},{17,1},{25,9},{2,18},{10... | collective-permute-start | bytes 393224 | tf_op jit(solution)/shard_map/ppermute | solution.py:233
  95.0 15.6 %collective-permute-start.13 = (f32[8,4096]{1,0:T(8,128)S(1)}, f32[8,4096]{1,0:T(8,128)S(1)}, u32[]{:S(2)}, u32[]{:S(2)}) collective-permute-start(f32[8,4096]{1,0:T(8,128)S(1)} %get-tuple-element.29), channel_id=1, source_target_pairs={{0,8},{8,0},{16,24},{24,16},{1,9},{9,1},{17,25},{25,17},{2,10},{10... | collective-permute-start | bytes 393224 | tf_op jit(solution)/shard_map/ppermute | solution.py:233
  97.4 13.2 %collective-permute-start.14 = (f32[8,4096]{1,0:T(8,128)S(1)}, f32[8,4096]{1,0:T(8,128)S(1)}, u32[]{:S(2)}, u32[]{:S(2)}) collective-permute-start(f32[8,4096]{1,0:T(8,128)S(1)} %get-tuple-element.30), channel_id=1, source_target_pairs={{0,24},{8,16},{16,8},{24,0},{1,25},{9,17},{17,9},{25,1},{2,26},{10... | collective-permute-start | bytes 393224 | tf_op jit(solution)/shard_map/ppermute | solution.py:233
  99.1 17.6 %collective-permute-start.9 = (f32[8,4096]{1,0:T(8,128)S(1)}, f32[8,4096]{1,0:T(8,128)S(1)}, u32[]{:S(2)}, u32[]{:S(2)}) collective-permute-start(f32[8,4096]{1,0:T(8,128)S(1)} %get-tuple-element.25), channel_id=1, source_target_pairs={{0,16},{8,24},{16,0},{24,8},{1,17},{9,25},{17,1},{25,9},{2,18},{10... | collective-permute-start | bytes 393224 | tf_op jit(solution)/shard_map/ppermute | solution.py:233
  99.8 17.0 %collective-permute-start.10 = (f32[8,4096]{1,0:T(8,128)S(1)}, f32[8,4096]{1,0:T(8,128)S(1)}, u32[]{:S(2)}, u32[]{:S(2)}) collective-permute-start(f32[8,4096]{1,0:T(8,128)S(1)} %get-tuple-element.26), channel_id=1, source_target_pairs={{0,8},{8,0},{16,24},{24,16},{1,9},{9,1},{17,25},{25,17},{2,10},{10... | collective-permute-start | bytes 393224 | tf_op jit(solution)/shard_map/ppermute | solution.py:233
  104.4 12.4 %collective-permute-start.11 = (f32[8,4096]{1,0:T(8,128)S(1)}, f32[8,4096]{1,0:T(8,128)S(1)}, u32[]{:S(2)}, u32[]{:S(2)}) collective-permute-start(f32[8,4096]{1,0:T(8,128)S(1)} %get-tuple-element.27), channel_id=1, source_target_pairs={{0,24},{8,16},{16,8},{24,0},{1,25},{9,17},{17,9},{25,1},{2,26},{10... | collective-permute-start | bytes 393224 | tf_op jit(solution)/shard_map/ppermute | solution.py:233

commit v18 on v16

--- a/solution.py
+++ b/solution.py
@@ -189,7 +189,7 @@
         high_ref[place], low_ref[place] = split(factor_ref[share])
 
 
-def mix_kernel(x_ref, f_high, f_low, out_ref, x_mid, y_mid):
+def mix_kernel(x_ref, f_high, f_low, out_ref, x_mid):
     groups, planes, chunks, pieces, dets, width = out_ref.shape
     places = []
     for group, plane, chunk, piece in np.ndindex(groups, planes, chunks, pieces):
@@ -202,9 +202,10 @@
     half = f_high.shape[0] // 2
     for part in range(2):
         rows, reach = slice(part * half, (part + 1) * half), (part + 1) * half
-        y_mid[rows] = product((f_high[rows, :reach], f_low[rows, :reach]), (x_high[:reach], x_low[:reach]))
-    for target, source in places:
-        out_ref[target] = y_mid[source]
+        value = product((f_high[rows, :reach], f_low[rows, :reach]), (x_high[:reach], x_low[:reach]))
+        for target, (place, lanes) in places:
+            if place.start // half == part:
+                out_ref[target] = value[place.start - part * half : place.stop - part * half, lanes]
 
 
 def call(kernel, outs, scratch, flops, *args, spaces=None, out_space=pltpu.VMEM, aliases=None):
@@ -307,7 +308,7 @@
 
     count = f_high.shape[0]
     (mixed,) = call(
-        mix_kernel, [array(*layout)], [(count, pieces * LANES)] * 2,
+        mix_kernel, [array(*layout)], [(count, pieces * LANES)],
         2 * 3 * count * count * pieces * LANES, exchange(spectrum), f_high, f_low,
     )
     back = exchange(mixed)

time: 118 us -> 118 us (level)
  no operation moved by 1% of the time
where the time goes in v18:
time: 118 us
  waiting for transfers between devices  50.7 us (43%)
  blocking collectives  29.3 us (25%)
  starting transfers between devices  29.2 us (25%)
  Pallas kernels  6.7 us (6%)
  local copies, waits for them, and re-layouts  1.4 us (1%)
    ppermute x13, waiting for transfers between devices, swap(): lax.ppermute(value, axis, [(place, place ^ mask) for place in range(lax.a...  45.6 us
    all_to_all x1, blocking collectives, exchange(): lax.all_to_all(value, ('det', 'tm'), split_axis=0, concat_axis=0, tiled=T...  29.3 us
    ppermute x13, starting transfers between devices, swap(): lax.ppermute(value, axis, [(place, place ^ mask) for place in range(lax.a...  23.8 us
    pallas_call x8, Pallas kernels, call(): pl.pallas_call(kernel, out_shape=outs, in_specs=[pl.BlockSpec(memory_spac...  6.7 us
    all_to_all x1, waiting for transfers between devices, exchange(): lax.all_to_all(value, ('det', 'tm'), split_axis=0, concat_axis=0, tiled=T...  5.05 us
    all_to_all x1, starting transfers between devices, exchange(): lax.all_to_all(value, ('det', 'tm'), split_axis=0, concat_axis=0, tiled=T...  4.03 us
  transfers between devices with their start and end apart: 16, of which 9 were waited for; matrix products, arithmetic and copies ran while one was open for 0% of the time, Pallas kernels for 3%

profile of v18, /device:TPU:0, one launch (start us, length us, event | category | flops | bytes accessed | tf_op | source)
XLA Modules:
  0.0 117.6 jit_solution(2315714442024755645)
XLA Ops:
  0.0 1.3 %copy-done.3 = f32[64,4096]{1,0:T(8,128)S(1)} copy-done((f32[64,4096]{1,0:T(8,128)S(1)}, f32[64,4096]{1,0:T(8,128)}, u32[]{:S(2)}) %copy-start.3) | copy-done | bytes 1048600
  1.4 5.1 %collective-permute-start = (f32[16,4096]{1,0:T(8,128)S(1)}, f32[16,4096]{1,0:T(8,128)S(1)}, u32[]{:S(2)}, u32[]{:S(2)}) collective-permute-start(f32[16,4096]{1,0:T(8,128)S(1)} %get-tuple-element.19), channel_id=1, source_target_pairs={{0,24},{8,16},{16,8},{24,0},{1,25},{9,17},{17,9},{25,1},{2,26},{10... | collective-permute-start | bytes 786440 | tf_op jit(solution)/shard_map/ppermute | solution.py:235
  8.5 5.3 %collective-permute-done.refs_0_ = f32[16,4096]{1,0:T(8,128)S(1)} collective-permute-done((f32[16,4096]{1,0:T(8,128)S(1)}, f32[16,4096]{1,0:T(8,128)S(1)}, u32[]{:S(2)}, u32[]{:S(2)}) %collective-permute-start) | collective-permute-done | bytes 262176 | tf_op jit(solution)/shard_map/ppermute | solution.py:235
  13.8 16.4 %collective-permute-done.1.refs_1_ = f32[16,4096]{1,0:T(8,128)S(1)} collective-permute-done((f32[16,4096]{1,0:T(8,128)S(1)}, f32[16,4096]{1,0:T(8,128)S(1)}, u32[]{:S(2)}, u32[]{:S(2)}) %collective-permute-start.1) | collective-permute-done | bytes 262176 | tf_op jit(solution)/shard_map/ppermute | solution.py:235
  30.3 2.3 %shard_map.56 = f32[8,4,2,4,8,128]{5,4,3,2,1,0:T(8,128)} custom-call(f32[16,4096]{1,0:T(8,128)S(1)} %collective-permute-done.refs_0_, f32[16,4096]{1,0:T(8,128)S(1)} %collective-permute-done.1.refs_1_, f32[16,4096]{1,0:T(8,128)S(1)} %collective-permute-done.2.refs_2_, f32[16,4096]{1,0:T(8,128)S(1)} %get-tuple-element.22.refs_3_, ...), custom_call_target="tpu_custom_call" | custom-call | flops 805306368 | bytes 3211264 | tf_op jit(solution)/shard_map/pallas_call | solution.py:214
  32.5 4.0 %all-to-all-start = ((f32[32,64,128]{2,1,0:T(8,128)}), f32[32,64,128]{2,1,0:T(8,128)S(1)}, u32[]{:S(2)}, u32[]{:S(2)}) async-start(f32[32,64,128]{2,1,0:T(8,128)} %bitcast.1), calls=%async_computation | async-start | bytes 2097152 | tf_op jit(solution)/shard_map/all_to_all | solution.py:300
  36.6 2.7 %collective-permute-start.7 = (f32[64,512]{1,0:T(8,128)S(1)}, f32[64,512]{1,0:T(8,128)S(1)}, u32[]{:S(2)}, u32[]{:S(2)}) collective-permute-start(f32[64,512]{1,0:T(8,128)S(1)} %constant_dynamic-update-slice_fusion), channel_id=1, source_target_pairs={{0,6},{1,7},{2,4},{3,5},{4,2},{5,3},{6,0},{7,1},{8,14},{9,15},{10,... | collective-permute-start | bytes 393224 | tf_op jit(solution)/shard_map/ppermute | solution.py:235
  40.2 11.9 %collective-permute-done.7 = f32[64,512]{1,0:T(8,128)S(1)} collective-permute-done((f32[64,512]{1,0:T(8,128)S(1)}, f32[64,512]{1,0:T(8,128)S(1)}, u32[]{:S(2)}, u32[]{:S(2)}) %collective-permute-start.7) | collective-permute-done | bytes 131104 | tf_op jit(solution)/shard_map/ppermute | solution.py:235
  52.1 1.5 %collective-permute-done.6 = f32[64,512]{1,0:T(8,128)S(1)} collective-permute-done((f32[64,512]{1,0:T(8,128)S(1)}, f32[64,512]{1,0:T(8,128)S(1)}, u32[]{:S(2)}, u32[]{:S(2)}) %collective-permute-start.6) | collective-permute-done | bytes 131104 | tf_op jit(solution)/shard_map/ppermute | solution.py:235
  53.6 0.8 collective-permute-done.5
  54.6 1.8 %collective-permute-done.8 = f32[4,64,512]{2,1,0:T(8,128)S(1)} collective-permute-done((f32[4,64,512]{2,1,0:T(8,128)S(1)}, f32[4,64,512]{2,1,0:T(8,128)S(1)}, u32[]{:S(2)}, u32[]{:S(2)}) %collective-permute-start.8) | collective-permute-done | bytes 524320 | tf_op jit(solution)/shard_map/ppermute | solution.py:235
  56.6 5.1 %all-to-all-done = f32[32,64,128]{2,1,0:T(8,128)S(1)} async-done(((f32[32,64,128]{2,1,0:T(8,128)}), f32[32,64,128]{2,1,0:T(8,128)S(1)}, u32[]{:S(2)}, u32[]{:S(2)}) %all-to-all-start) | async-done | bytes 1048608 | tf_op jit(solution)/shard_map/all_to_all | solution.py:300
  62.4 29.3 %all_to_all.10 = f32[32,64,128]{2,1,0:T(8,128)S(1)} all-to-all(f32[32,64,128]{2,1,0:T(8,128)S(1)} %bitcast.19), channel_id=1, replica_groups=mesh['tm'=4,'det'=8] {'det','tm'}, dimensions={0} | all-to-all | bytes 2097152 | tf_op jit(solution)/shard_map/all_to_all | solution.py:300
  91.7 0.9 shard_map.60
  92.6 2.3 %collective-permute-start.12 = (f32[8,4096]{1,0:T(8,128)S(1)}, f32[8,4096]{1,0:T(8,128)S(1)}, u32[]{:S(2)}, u32[]{:S(2)}) collective-permute-start(f32[8,4096]{1,0:T(8,128)S(1)} %get-tuple-element.29), channel_id=1, source_target_pairs={{0,16},{8,24},{16,0},{24,8},{1,17},{9,25},{17,1},{25,9},{2,18},{10... | collective-permute-start | bytes 393224 | tf_op jit(solution)/shard_map/ppermute | solution.py:235
  95.0 1.5 %collective-permute-start.13 = (f32[8,4096]{1,0:T(8,128)S(1)}, f32[8,4096]{1,0:T(8,128)S(1)}, u32[]{:S(2)}, u32[]{:S(2)}) collective-permute-start(f32[8,4096]{1,0:T(8,128)S(1)} %get-tuple-element.30), channel_id=1, source_target_pairs={{0,8},{8,0},{16,24},{24,16},{1,9},{9,1},{17,25},{25,17},{2,10},{10... | collective-permute-start | bytes 393224 | tf_op jit(solution)/shard_map/ppermute | solution.py:235
  96.5 1.7 %collective-permute-start.14 = (f32[8,4096]{1,0:T(8,128)S(1)}, f32[8,4096]{1,0:T(8,128)S(1)}, u32[]{:S(2)}, u32[]{:S(2)}) collective-permute-start(f32[8,4096]{1,0:T(8,128)S(1)} %get-tuple-element.31), channel_id=1, source_target_pairs={{0,24},{8,16},{16,8},{24,0},{1,25},{9,17},{17,9},{25,1},{2,26},{10... | collective-permute-start | bytes 393224 | tf_op jit(solution)/shard_map/ppermute | solution.py:235
  98.2 0.9 shard_map.59
  99.7 2.1 %collective-permute-start.10 = (f32[8,4096]{1,0:T(8,128)S(1)}, f32[8,4096]{1,0:T(8,128)S(1)}, u32[]{:S(2)}, u32[]{:S(2)}) collective-permute-start(f32[8,4096]{1,0:T(8,128)S(1)} %get-tuple-element.26), channel_id=1, source_target_pairs={{0,8},{8,0},{16,24},{24,16},{1,9},{9,1},{17,25},{25,17},{2,10},{10... | collective-permute-start | bytes 393224 | tf_op jit(solution)/shard_map/ppermute | solution.py:235
  101.8 2.6 %collective-permute-done.12.refs_0_ = f32[8,4096]{1,0:T(8,128)S(1)} collective-permute-done((f32[8,4096]{1,0:T(8,128)S(1)}, f32[8,4096]{1,0:T(8,128)S(1)}, u32[]{:S(2)}, u32[]{:S(2)}) %collective-permute-start.12) | collective-permute-done | bytes 131104 | tf_op jit(solution)/shard_map/ppermute | solution.py:235
  104.4 6.2 %collective-permute-start.11 = (f32[8,4096]{1,0:T(8,128)S(1)}, f32[8,4096]{1,0:T(8,128)S(1)}, u32[]{:S(2)}, u32[]{:S(2)}) collective-permute-start(f32[8,4096]{1,0:T(8,128)S(1)} %get-tuple-element.27), channel_id=1, source_target_pairs={{0,24},{8,16},{16,8},{24,0},{1,25},{9,17},{17,9},{25,1},{2,26},{10... | collective-permute-start | bytes 393224 | tf_op jit(solution)/shard_map/ppermute | solution.py:235
  110.5 0.8 shard_map.61.refs_4_
  111.4 5.4 %collective-permute-done.9.refs_0_ = f32[8,4096]{1,0:T(8,128)S(1)} collective-permute-done((f32[8,4096]{1,0:T(8,128)S(1)}, f32[8,4096]{1,0:T(8,128)S(1)}, u32[]{:S(2)}, u32[]{:S(2)}) %collective-permute-start.9) | collective-permute-done | bytes 131104 | tf_op jit(solution)/shard_map/ppermute | solution.py:235
  116.7 0.8 shard_map.62
  (37 shorter events, 4.7 us)
Async XLA Ops:
  0.0 7.2 %copy-start = (f32[1,128,512]{2,1,0:T(8,128)S(1)}, f32[1,128,512]{2,1,0:T(8,128)}, u32[]{:S(2)}) copy-start(f32[1,128,512]{2,1,0:T(8,128)} %param.6) | copy-start | bytes 786436
  0.0 1.3 %copy-start.3 = (f32[64,4096]{1,0:T(8,128)S(1)}, f32[64,4096]{1,0:T(8,128)}, u32[]{:S(2)}) copy-start(f32[64,4096]{1,0:T(8,128)} %param.5) | copy-start | bytes 3145732
  1.3 29.0 %copy-start.2 = (bf16[512,512]{1,0:T(8,128)(2,1)S(1)}, bf16[512,512]{1,0:T(8,128)(2,1)}, u32[]{:S(2)}) copy-start(bf16[512,512]{1,0:T(8,128)(2,1)} %constant.20.clone.refs_5_.refs_2_) | copy-start | bytes 1572868
  1.3 29.0 %copy-start.4 = (f32[2,32,256]{2,1,0:T(8,128)S(1)}, f32[2,32,256]{2,1,0:T(8,128)}, u32[]{:S(2)}) copy-start(f32[2,32,256]{2,1,0:T(8,128)} %constant.19.clone.refs_4_.refs_1_) | copy-start | bytes 196612
  1.4 28.9 %copy-start.1 = (bf16[512,512]{1,0:T(8,128)(2,1)S(1)}, bf16[512,512]{1,0:T(8,128)(2,1)}, u32[]{:S(2)}) copy-start(bf16[512,512]{1,0:T(8,128)(2,1)} %constant.21.clone.refs_6_.refs_3_) | copy-start | bytes 1572868
  1.4 12.4 %collective-permute-start = (f32[16,4096]{1,0:T(8,128)S(1)}, f32[16,4096]{1,0:T(8,128)S(1)}, u32[]{:S(2)}, u32[]{:S(2)}) collective-permute-start(f32[16,4096]{1,0:T(8,128)S(1)} %get-tuple-element.19), channel_id=1, source_target_pairs={{0,24},{8,16},{16,8},{24,0},{1,25},{9,17},{17,9},{25,1},{2,26},{10... | collective-permute-start | bytes 786440 | tf_op jit(solution)/shard_map/ppermute | solution.py:235
  6.5 23.7 %collective-permute-start.1 = (f32[16,4096]{1,0:T(8,128)S(1)}, f32[16,4096]{1,0:T(8,128)S(1)}, u32[]{:S(2)}, u32[]{:S(2)}) collective-permute-start(f32[16,4096]{1,0:T(8,128)S(1)} %get-tuple-element.20), channel_id=1, source_target_pairs={{0,16},{8,24},{16,0},{24,8},{1,17},{9,25},{17,1},{25,9},{2,18},{10... | collective-permute-start | bytes 786440 | tf_op jit(solution)/shard_map/ppermute | solution.py:235
  6.5 23.7 %collective-permute-start.2 = (f32[16,4096]{1,0:T(8,128)S(1)}, f32[16,4096]{1,0:T(8,128)S(1)}, u32[]{:S(2)}, u32[]{:S(2)}) collective-permute-start(f32[16,4096]{1,0:T(8,128)S(1)} %get-tuple-element.21), channel_id=1, source_target_pairs={{0,8},{8,0},{16,24},{24,16},{1,9},{9,1},{17,25},{25,17},{2,10},{10... | collective-permute-start | bytes 786440 | tf_op jit(solution)/shard_map/ppermute | solution.py:235
  7.2 29.4 %collective-permute-start.4 = (f32[64,256]{1,0:T(8,128)S(1)}, f32[64,256]{1,0:T(8,128)S(1)}, u32[]{:S(2)}, u32[]{:S(2)}) collective-permute-start(f32[64,256]{1,0:T(8,128)S(1)} %get-tuple-element.33), channel_id=1, source_target_pairs={{16,4},{17,28},{18,12},{19,20},{20,21},{21,13},{22,29},{23,5},{24,... | collective-permute-start | bytes 196616 | tf_op jit(solution)/shard_map/ppermute | solution.py:262
  7.9 28.7 %collective-permute-start.3 = (f32[64,256]{1,0:T(8,128)S(1)}, f32[64,256]{1,0:T(8,128)S(1)}, u32[]{:S(2)}, u32[]{:S(2)}) collective-permute-start(f32[64,256]{1,0:T(8,128)S(1)} %get-tuple-element.34), channel_id=1, source_target_pairs={{0,0},{1,24},{2,8},{3,16},{4,17},{5,9},{6,25},{7,1},{8,2},{9,26},{... | collective-permute-start | bytes 196616 | tf_op jit(solution)/shard_map/ppermute | solution.py:261
  32.5 29.1 %all-to-all-start = ((f32[32,64,128]{2,1,0:T(8,128)}), f32[32,64,128]{2,1,0:T(8,128)S(1)}, u32[]{:S(2)}, u32[]{:S(2)}) async-start(f32[32,64,128]{2,1,0:T(8,128)} %bitcast.1), calls=%async_computation | async-start | bytes 2097152 | tf_op jit(solution)/shard_map/all_to_all | solution.py:300
  36.6 15.5 %collective-permute-start.7 = (f32[64,512]{1,0:T(8,128)S(1)}, f32[64,512]{1,0:T(8,128)S(1)}, u32[]{:S(2)}, u32[]{:S(2)}) collective-permute-start(f32[64,512]{1,0:T(8,128)S(1)} %constant_dynamic-update-slice_fusion), channel_id=1, source_target_pairs={{0,6},{1,7},{2,4},{3,5},{4,2},{5,3},{6,0},{7,1},{8,14},{9,15},{10,... | collective-permute-start | bytes 393224 | tf_op jit(solution)/shard_map/ppermute | solution.py:235
  39.4 14.2 %collective-permute-start.6 = (f32[64,512]{1,0:T(8,128)S(1)}, f32[64,512]{1,0:T(8,128)S(1)}, u32[]{:S(2)}, u32[]{:S(2)}) collective-permute-start(f32[64,512]{1,0:T(8,128)S(1)} %constant_dynamic-update-slice_fusion), channel_id=1, source_target_pairs={{0,4},{1,5},{2,6},{3,7},{4,0},{5,1},{6,2},{7,3},{8,12},{9,13},{10,... | collective-permute-start | bytes 393224 | tf_op jit(solution)/shard_map/ppermute | solution.py:235
  39.9 14.5 %collective-permute-start.5 = (f32[64,512]{1,0:T(8,128)S(1)}, f32[64,512]{1,0:T(8,128)S(1)}, u32[]{:S(2)}, u32[]{:S(2)}) collective-permute-start(f32[64,512]{1,0:T(8,128)S(1)} %constant_dynamic-update-slice_fusion), channel_id=1, source_target_pairs={{0,2},{1,3},{2,0},{3,1},{4,6},{5,7},{6,4},{7,5},{8,10},{9,11},{10,... | collective-permute-start | bytes 393224 | tf_op jit(solution)/shard_map/ppermute | solution.py:235
  54.4 2.0 %collective-permute-start.8 = (f32[4,64,512]{2,1,0:T(8,128)S(1)}, f32[4,64,512]{2,1,0:T(8,128)S(1)}, u32[]{:S(2)}, u32[]{:S(2)}) collective-permute-start(f32[4,64,512]{2,1,0:T(8,128)S(1)} %pad_maximum_fusion), channel_id=1, source_target_pairs={{0,1},{1,0},{2,3},{3,2},{4,5},{5,4},{6,7},{7,6},{8,9},{9,8},{10,11... | collective-permute-start | bytes 1572872 | tf_op jit(solution)/shard_map/ppermute | solution.py:235
  92.6 11.7 %collective-permute-start.12 = (f32[8,4096]{1,0:T(8,128)S(1)}, f32[8,4096]{1,0:T(8,128)S(1)}, u32[]{:S(2)}, u32[]{:S(2)}) collective-permute-start(f32[8,4096]{1,0:T(8,128)S(1)} %get-tuple-element.29), channel_id=1, source_target_pairs={{0,16},{8,24},{16,0},{24,8},{1,17},{9,25},{17,1},{25,9},{2,18},{10... | collective-permute-start | bytes 393224 | tf_op jit(solution)/shard_map/ppermute | solution.py:235
  95.0 15.6 %collective-permute-start.13 = (f32[8,4096]{1,0:T(8,128)S(1)}, f32[8,4096]{1,0:T(8,128)S(1)}, u32[]{:S(2)}, u32[]{:S(2)}) collective-permute-start(f32[8,4096]{1,0:T(8,128)S(1)} %get-tuple-element.30), channel_id=1, source_target_pairs={{0,8},{8,0},{16,24},{24,16},{1,9},{9,1},{17,25},{25,17},{2,10},{10... | collective-permute-start | bytes 393224 | tf_op jit(solution)/shard_map/ppermute | solution.py:235
  96.5 14.1 %collective-permute-start.14 = (f32[8,4096]{1,0:T(8,128)S(1)}, f32[8,4096]{1,0:T(8,128)S(1)}, u32[]{:S(2)}, u32[]{:S(2)}) collective-permute-start(f32[8,4096]{1,0:T(8,128)S(1)} %get-tuple-element.31), channel_id=1, source_target_pairs={{0,24},{8,16},{16,8},{24,0},{1,25},{9,17},{17,9},{25,1},{2,26},{10... | collective-permute-start | bytes 393224 | tf_op jit(solution)/shard_map/ppermute | solution.py:235
  99.0 17.7 %collective-permute-start.9 = (f32[8,4096]{1,0:T(8,128)S(1)}, f32[8,4096]{1,0:T(8,128)S(1)}, u32[]{:S(2)}, u32[]{:S(2)}) collective-permute-start(f32[8,4096]{1,0:T(8,128)S(1)} %get-tuple-element.25), channel_id=1, source_target_pairs={{0,16},{8,24},{16,0},{24,8},{1,17},{9,25},{17,1},{25,9},{2,18},{10... | collective-permute-start | bytes 393224 | tf_op jit(solution)/shard_map/ppermute | solution.py:235
  99.7 17.0 %collective-permute-start.10 = (f32[8,4096]{1,0:T(8,128)S(1)}, f32[8,4096]{1,0:T(8,128)S(1)}, u32[]{:S(2)}, u32[]{:S(2)}) collective-permute-start(f32[8,4096]{1,0:T(8,128)S(1)} %get-tuple-element.26), channel_id=1, source_target_pairs={{0,8},{8,0},{16,24},{24,16},{1,9},{9,1},{17,25},{25,17},{2,10},{10... | collective-permute-start | bytes 393224 | tf_op jit(solution)/shard_map/ppermute | solution.py:235
  104.4 12.4 %collective-permute-start.11 = (f32[8,4096]{1,0:T(8,128)S(1)}, f32[8,4096]{1,0:T(8,128)S(1)}, u32[]{:S(2)}, u32[]{:S(2)}) collective-permute-start(f32[8,4096]{1,0:T(8,128)S(1)} %get-tuple-element.27), channel_id=1, source_target_pairs={{0,24},{8,16},{16,8},{24,0},{1,25},{9,17},{17,9},{25,1},{2,26},{10... | collective-permute-start | bytes 393224 | tf_op jit(solution)/shard_map/ppermute | solution.py:235
